TPU v7x, 32 devices: a whole 2x2x4 slice. The times are simulated.
32 devices in a mesh: dp: 32 (over z, y, x, core).
Axes of the slice: x: 2, y: 2, z: 4, core: 2. Of those that a mesh axis runs over, the one named last changes fastest.
Arguments:
- tokens: bfloat16 [32768, 768], P('dp'), may hold values from -6 to 6
- lengths: int32 [128, 5], P('dp'), may hold values from 0 to 197, as said below
- attn_gain: bfloat16 [768], P('dp'), may hold values from 0.25 to 1.75
- attn_shift: bfloat16 [768], P('dp'), may hold values from -1.25 to 1.25
- query_weight: bfloat16 [768, 768], P('dp'), may hold values from -0.21875 to 0.21875
- query_bias: bfloat16 [768], P('dp'), may hold values from -1.25 to 1.25
- key_weight: bfloat16 [768, 768], P('dp'), may hold values from -0.21875 to 0.21875
- value_weight: bfloat16 [768, 768], P('dp'), may hold values from -0.21875 to 0.21875
- value_bias: bfloat16 [768], P('dp'), may hold values from -1.25 to 1.25
- out_weight: bfloat16 [768, 768], P('dp'), may hold values from -0.875 to 0.875
- out_bias: bfloat16 [768], P('dp'), may hold values from -1.25 to 1.25
- mlp_gain: bfloat16 [768], P('dp'), may hold values from 0.25 to 1.75
- mlp_shift: bfloat16 [768], P('dp'), may hold values from -1.25 to 1.25
- up_weight: bfloat16 [768, 3072], P('dp'), may hold values from -0.21875 to 0.21875
- up_bias: bfloat16 [3072], P('dp'), may hold values from -1.25 to 1.25
- down_weight: bfloat16 [3072, 768], P('dp'), may hold values from -0.109375 to 0.109375
- down_bias: bfloat16 [768], P('dp'), may hold values from -1.25 to 1.25
- grad_out: bfloat16 [32768, 768], P('dp'), may hold values from -6 to 6
Outputs:
- block_out: bfloat16 [32768, 768], P('dp')
- grad_tokens: bfloat16 [32768, 768], P('dp')
- grad_attn_gain: float32 [768], P('dp')
- grad_attn_shift: float32 [768], P('dp')
- grad_query_weight: float32 [768, 768], P('dp')
- grad_query_bias: float32 [768], P('dp')
- grad_key_weight: float32 [768, 768], P('dp')
- grad_value_weight: float32 [768, 768], P('dp')
- grad_value_bias: float32 [768], P('dp')
- grad_out_weight: float32 [768, 768], P('dp')
- grad_out_bias: float32 [768], P('dp')
- grad_mlp_gain: float32 [768], P('dp')
- grad_mlp_shift: float32 [768], P('dp')
- grad_up_weight: float32 [768, 3072], P('dp')
- grad_up_bias: float32 [3072], P('dp')
- grad_down_weight: float32 [3072, 768], P('dp')
- grad_down_bias: float32 [768], P('dp')
Inputs may be any that keep to these rules, and one draw needn't show every extreme that they name: `lengths`: row t lists the images packed into the t-th block of 256 rows, in order: either one image of 197 tokens followed by one of 50, or one to 5 images of 50 tokens; remaining entries are 0, and the rows after the images are padding. Images never cross a block's end.
All inputs are finite; a program needn't handle non-finite values.
Results may differ from a plain program's by a relative error of at most 0.013.
Values may be sent and summed in bfloat16 or wider, within the bound.
No kernel may reach another device: no remote copies, remote signals or barrier semaphores. Data moves between devices by JAX's collectives and lax.ppermute only.
A program may use at most 192 MiB of HBM per device.

v0:
```python
import jax
import jax.numpy as jnp
from jax import lax
from jax.sharding import PartitionSpec as P

HEADS = 12
HEAD_DIM = 64


epsilon = 1e-06
masked_score = -1e30


def segment_ids(lengths, block_rows):
    bounds = jnp.cumsum(lengths, axis=1)
    row_index = jnp.arange(block_rows, dtype=jnp.int32)
    return jnp.sum((row_index[None, :, None] >= bounds[:, None, :]).astype(jnp.int32), axis=2)


def layer_norm(rows, gain, shift):
    centered = rows - jnp.mean(rows, axis=-1, keepdims=True)
    inverse = lax.rsqrt(jnp.mean(centered * centered, axis=-1, keepdims=True) + epsilon)
    return centered * inverse * gain + shift


def widen(vector):
    return vector.astype(jnp.float32)


def matmul(left, right):
    return jnp.dot(left, right, preferred_element_type=jnp.float32)


def weight_grad(rows, grads):
    return lax.dot_general(
        rows, grads, (((0,), (0,)), ((), ())), preferred_element_type=jnp.float32
    )


def input_grad(grads, weight):
    return lax.dot_general(
        grads, weight, (((1,), (1,)), ((), ())), preferred_element_type=jnp.float32
    )


def scores_of(queries, key_rows, segment):
    scores = jnp.einsum(
        "tqhd,tkhd->thqk", queries, key_rows, preferred_element_type=jnp.float32
    ) * HEAD_DIM ** (-0.5)
    same_image = (segment[:, :, None] == segment[:, None, :])[:, None]
    return jnp.where(same_image, scores, masked_score)


def attend_block(packed):
    queries, key_rows, value_rows, segment = packed
    scores = scores_of(queries, key_rows, segment)
    row_max = jnp.max(scores, axis=-1, keepdims=True)
    weights = jnp.exp(scores - row_max)
    totals = jnp.sum(weights, axis=-1, keepdims=True)
    probs = (weights / totals).astype(jnp.bfloat16)
    mixed = jnp.einsum("thqk,tkhd->tqhd", probs, value_rows, preferred_element_type=jnp.float32)
    return (mixed.astype(jnp.bfloat16), row_max + jnp.log(totals))


def attend_back(packed):
    queries, key_rows, value_rows, segment, log_total, grad_mixed = packed
    probs = jnp.exp(scores_of(queries, key_rows, segment) - log_total)
    grad_probs = jnp.einsum(
        "tqhd,tkhd->thqk", grad_mixed, value_rows, preferred_element_type=jnp.float32
    )
    grad_values = jnp.einsum(
        "thqk,tqhd->tkhd",
        probs.astype(jnp.bfloat16),
        grad_mixed,
        preferred_element_type=jnp.float32,
    )
    grad_scores = (
        probs * (grad_probs - jnp.sum(probs * grad_probs, axis=-1, keepdims=True))
    ).astype(jnp.bfloat16)
    scale_factor = HEAD_DIM ** (-0.5)
    grad_queries = (
        jnp.einsum("thqk,tkhd->tqhd", grad_scores, key_rows, preferred_element_type=jnp.float32)
        * scale_factor
    )
    grad_keys = (
        jnp.einsum("thqk,tqhd->tkhd", grad_scores, queries, preferred_element_type=jnp.float32)
        * scale_factor
    )
    return (
        grad_queries.astype(jnp.bfloat16),
        grad_keys.astype(jnp.bfloat16),
        grad_values.astype(jnp.bfloat16),
    )


def body(
    tokens,
    lengths,
    attn_gain,
    attn_shift,
    query_weight,
    query_bias,
    key_weight,
    value_weight,
    value_bias,
    out_weight,
    out_bias,
    mlp_gain,
    mlp_shift,
    up_weight,
    up_bias,
    down_weight,
    down_bias,
    grad_out,
):
    whole = (
        lax.all_gather(attn_gain, "dp", axis=0, tiled=True),
        lax.all_gather(attn_shift, "dp", axis=0, tiled=True),
        lax.all_gather(query_weight, "dp", axis=0, tiled=True),
        lax.all_gather(query_bias, "dp", axis=0, tiled=True),
        lax.all_gather(key_weight, "dp", axis=0, tiled=True),
        lax.all_gather(value_weight, "dp", axis=0, tiled=True),
        lax.all_gather(value_bias, "dp", axis=0, tiled=True),
        lax.all_gather(out_weight, "dp", axis=0, tiled=True),
        lax.all_gather(out_bias, "dp", axis=0, tiled=True),
        lax.all_gather(mlp_gain, "dp", axis=0, tiled=True),
        lax.all_gather(mlp_shift, "dp", axis=0, tiled=True),
        lax.all_gather(up_weight, "dp", axis=0, tiled=True),
        lax.all_gather(up_bias, "dp", axis=0, tiled=True),
        lax.all_gather(down_weight, "dp", axis=0, tiled=True),
        lax.all_gather(down_bias, "dp", axis=0, tiled=True),
    )
    (
        attn_gain_all,
        attn_shift_all,
        query_all,
        query_bias_all,
        key_all,
        value_all,
        value_bias_all,
        out_all,
        out_bias_all,
        mlp_gain_all,
        mlp_shift_all,
        up_all,
        up_bias_all,
        down_all,
        down_bias_all,
    ) = whole
    tile_count = lengths.shape[0]
    slot_count = lengths.shape[1]
    tile_rows = tokens.shape[0] // tile_count
    segment = segment_ids(lengths, tile_rows)
    block_tiles = 1
    for number in range(1, tile_count + 1):
        if tile_count % number == 0 and number * tile_rows <= 512:
            block_tiles = number
    grouped = (tile_count // block_tiles, block_tiles, tile_rows, HEADS, HEAD_DIM)
    rows_in = tokens.astype(jnp.float32)
    normed_one, pull_one = jax.vjp(layer_norm, rows_in, widen(attn_gain_all), widen(attn_shift_all))
    normed_one = normed_one.astype(jnp.bfloat16)
    queries = (matmul(normed_one, query_all) + widen(query_bias_all)).astype(jnp.bfloat16)
    key_rows = matmul(normed_one, key_all).astype(jnp.bfloat16)
    value_rows = (matmul(normed_one, value_all) + widen(value_bias_all)).astype(jnp.bfloat16)
    packed = (
        queries.reshape(grouped),
        key_rows.reshape(grouped),
        value_rows.reshape(grouped),
        segment.reshape(grouped[:3]),
    )
    mixed, log_total = lax.map(attend_block, packed)
    mixed = mixed.reshape(tokens.shape)
    resid = rows_in + matmul(mixed, out_all) + widen(out_bias_all)
    normed_two, pull_two = jax.vjp(layer_norm, resid, widen(mlp_gain_all), widen(mlp_shift_all))
    normed_two = normed_two.astype(jnp.bfloat16)
    up_pre = matmul(normed_two, up_all) + widen(up_bias_all)
    activated, pull_gelu = jax.vjp(jax.nn.gelu, up_pre)
    activated = activated.astype(jnp.bfloat16)
    block_out = (resid + matmul(activated, down_all) + widen(down_bias_all)).astype(jnp.bfloat16)
    query_back, key_back, value_back, out_back, up_back, down_back = (
        lax.all_gather(query_weight, "dp", axis=0, tiled=True),
        lax.all_gather(key_weight, "dp", axis=0, tiled=True),
        lax.all_gather(value_weight, "dp", axis=0, tiled=True),
        lax.all_gather(out_weight, "dp", axis=0, tiled=True),
        lax.all_gather(up_weight, "dp", axis=0, tiled=True),
        lax.all_gather(down_weight, "dp", axis=0, tiled=True),
    )
    valid = (segment < slot_count).reshape(-1, 1)
    cotangent = jnp.where(valid, grad_out, jnp.zeros_like(grad_out))
    grad_down_weight = weight_grad(activated, cotangent)
    grad_down_bias = jnp.sum(cotangent, axis=0, dtype=jnp.float32)
    (grad_up,) = pull_gelu(input_grad(cotangent, down_back))
    grad_up = grad_up.astype(jnp.bfloat16)
    grad_up_weight = weight_grad(normed_two, grad_up)
    grad_up_bias = jnp.sum(grad_up, axis=0, dtype=jnp.float32)
    grad_resid, grad_mlp_gain, grad_mlp_shift = pull_two(input_grad(grad_up, up_back))
    grad_resid = grad_resid + cotangent.astype(jnp.float32)
    grad_attn = grad_resid.astype(jnp.bfloat16)
    grad_out_weight = weight_grad(mixed, grad_attn)
    grad_out_bias = jnp.sum(grad_attn, axis=0, dtype=jnp.float32)
    grad_mixed = input_grad(grad_attn, out_back).astype(jnp.bfloat16)
    grad_queries, grad_keys, grad_values = lax.map(
        attend_back, packed + (log_total, grad_mixed.reshape(grouped))
    )
    grad_queries = grad_queries.reshape(tokens.shape)
    grad_keys = grad_keys.reshape(tokens.shape)
    grad_values = grad_values.reshape(tokens.shape)
    grad_query_weight = weight_grad(normed_one, grad_queries)
    grad_query_bias = jnp.sum(grad_queries, axis=0, dtype=jnp.float32)
    grad_key_weight = weight_grad(normed_one, grad_keys)
    grad_value_weight = weight_grad(normed_one, grad_values)
    grad_value_bias = jnp.sum(grad_values, axis=0, dtype=jnp.float32)
    grad_one = (
        input_grad(grad_queries, query_back)
        + input_grad(grad_keys, key_back)
        + input_grad(grad_values, value_back)
    )
    grad_rows, grad_attn_gain, grad_attn_shift = pull_one(grad_one)
    grad_tokens = (grad_resid + grad_rows).astype(jnp.bfloat16)
    shares = tuple(
        (
            lax.psum_scatter(grad_attn_gain, "dp", scatter_dimension=0, tiled=True),
            lax.psum_scatter(grad_attn_shift, "dp", scatter_dimension=0, tiled=True),
            lax.psum_scatter(grad_query_weight, "dp", scatter_dimension=0, tiled=True),
            lax.psum_scatter(grad_query_bias, "dp", scatter_dimension=0, tiled=True),
            lax.psum_scatter(grad_key_weight, "dp", scatter_dimension=0, tiled=True),
            lax.psum_scatter(grad_value_weight, "dp", scatter_dimension=0, tiled=True),
            lax.psum_scatter(grad_value_bias, "dp", scatter_dimension=0, tiled=True),
            lax.psum_scatter(grad_out_weight, "dp", scatter_dimension=0, tiled=True),
            lax.psum_scatter(grad_out_bias, "dp", scatter_dimension=0, tiled=True),
            lax.psum_scatter(grad_mlp_gain, "dp", scatter_dimension=0, tiled=True),
            lax.psum_scatter(grad_mlp_shift, "dp", scatter_dimension=0, tiled=True),
            lax.psum_scatter(grad_up_weight, "dp", scatter_dimension=0, tiled=True),
            lax.psum_scatter(grad_up_bias, "dp", scatter_dimension=0, tiled=True),
            lax.psum_scatter(grad_down_weight, "dp", scatter_dimension=0, tiled=True),
            lax.psum_scatter(grad_down_bias, "dp", scatter_dimension=0, tiled=True),
        )
    )
    return (block_out, grad_tokens) + shares


def solution(mesh):
    placed = (
        P("dp", None),
        P("dp", None),
        P("dp"),
        P("dp"),
        P("dp", None),
        P("dp"),
        P("dp", None),
        P("dp", None),
        P("dp"),
        P("dp", None),
        P("dp"),
        P("dp"),
        P("dp"),
        P("dp", None),
        P("dp"),
        P("dp", None),
        P("dp"),
        P("dp", None),
    )
    return jax.shard_map(
        body,
        mesh=mesh,
        in_specs=placed,
        out_specs=(
            P("dp", None),
            P("dp", None),
            P("dp"),
            P("dp"),
            P("dp", None),
            P("dp"),
            P("dp", None),
            P("dp", None),
            P("dp"),
            P("dp", None),
            P("dp"),
            P("dp"),
            P("dp"),
            P("dp", None),
            P("dp"),
            P("dp", None),
            P("dp"),
        ),
        check_vma=False,
    )
```

profile of v0, /device:TPU:0, one launch (start us, length us, event | category | flops | bytes accessed | tf_op | source)
XLA Modules:
  0.0 1121.2 jit_solution(15699823041103515415)
XLA Ops:
  19.9 42.8 %all-reduce.19 = (bf16[768]{0:T(1024)(128)(2,1)S(1)}, bf16[768]{0:T(1024)(128)(2,1)S(1)}, bf16[768]{0:T(1024)(128)(2,1)S(1)}, bf16[768]{0:T(1024)(128)(2,1)S(1)}...) all-reduce(bf16[768]{0:T(1024)(128)(2,1)S(1)} %dynamic-update-slice, ...), channel_id=1, replica_groups=mesh['dp'=32] {'dp'}, use_global_device_ids=true, to_apply=%add.2 | all-reduce | flops 9216 | bytes 36864
  70.7 52.9 %all-gather.7.cloned.1.call-done = bf16[768,768]{1,0:T(8,128)(2,1)} async-done(((bf16[24,768]{1,0:T(8,128)(2,1)}), bf16[768,768]{1,0:T(8,128)(2,1)}) %all-gather.7.cloned.1.call-update) | async-done | bytes 1179664 | tf_op jit(solution)/shard_map/all_gather | solution.py:122
  123.6 4.1 add_convert_fusion.4
  135.1 3.8 reshape.177
  141.8 37.7 %all-gather.11.cloned.1.call-done = bf16[768,768]{1,0:T(8,128)(2,1)} async-done(((bf16[24,768]{1,0:T(8,128)(2,1)}), bf16[768,768]{1,0:T(8,128)(2,1)}) %all-gather.11.cloned.1.call-update) | async-done | bytes 1179664 | tf_op jit(solution)/shard_map/all_gather | solution.py:121
  179.5 4.6 convolution_convert_fusion.1
  186.7 3.8 reshape.180
  195.6 16.1 %while.26 = (s32[]{:T(128)}, bf16[2,2,256,12,64]{2,1,0,4,3:T(2,128)(2,1)}, f32[2,2,12,256,1]{3,2,1,4,0:T(8,128)S(1)}, bf16[2,2,256,12,64]{2,4,3,1,0:T(8,128)(2,1...) while((s32[]{:T(128)}, ...), condition=%wide.region_7.8_spmd, body=%wide.region_4.7_spmd.sunk | while | flops 422045696 | bytes 43236544 | solution.py:171
  215.5 19.7 %all-gather.13.cloned.1.call-done = bf16[768,768]{1,0:T(8,128)(2,1)} async-done(((bf16[24,768]{1,0:T(8,128)(2,1)}), bf16[768,768]{1,0:T(8,128)(2,1)}) %all-gather.13.cloned.1.call-update) | async-done | bytes 1179664 | tf_op jit(solution)/shard_map/all_gather | solution.py:124
  235.3 5.5 fusion.96
  243.0 57.6 %all-gather.15.cloned.1.call-done = bf16[768,3072]{1,0:T(8,128)(2,1)} async-done(((bf16[24,3072]{1,0:T(8,128)(2,1)}), bf16[768,3072]{1,0:T(8,128)(2,1)}) %all-gather.15.cloned.1.call-update) | async-done | bytes 4718608 | tf_op jit(solution)/shard_map/all_gather | solution.py:128
  300.6 11.1 fusion.83
  311.7 54.2 %all-gather.17.cloned.1.call-done = bf16[3072,768]{1,0:T(8,128)(2,1)} async-done(((bf16[96,768]{1,0:T(8,128)(2,1)}), bf16[3072,768]{1,0:T(8,128)(2,1)}) %all-gather.17.cloned.1.call-update) | async-done | bytes 4718608 | tf_op jit(solution)/shard_map/all_gather | solution.py:130
  365.9 17.7 %convert_reduce_fusion = (f32[3072]{0:T(1024)}, bf16[1024,3072]{1,0:T(8,128)(2,1)S(1)}) fusion(f32[1024,3072]{1,0:T(8,128)} %fusion.83, f32[3072]{0:T(1024)S(1)} %convert_element_type.131, bf16[3072,768]{1,0:T(8,128)(2,1)} %all-gather.17.cloned.1.call-done, bf16[1024,768]{0,1:T(8,128)(2,1)} %copy.128, pred[1024]{0:T(1024)(128)(4,1)S(1)} %lt.21), kind=kOutput, calls=%fused_computation.74 | convolution fusion | flops 4904973312 | bytes 25191424 | tf_op jit(solution)/shard_map/dot_general | solution.py:41
  383.6 7.3 fusion.97
  394.5 4.5 multiply_reduce_fusion.1
  408.9 4.0 convolution_convert_fusion
  415.5 3.8 reshape.182
  421.6 33.1 %while.27 = (s32[]{:T(128)}, bf16[2,2,256,12,64]{2,4,3,1,0:T(8,128)(2,1)}, bf16[2,2,256,12,64]{2,1,0,4,3:T(2,128)(2,1)}, bf16[2,2,256,12,64]{2,4,3,1,0:T(8,128)(...) while((s32[]{:T(128)}, ...), condition=%wide.region_14.15_spmd, body=%wide.region_12.14_spmd.sunk | while | flops 1032316928 | bytes 96657728 | solution.py:202
  460.3 4.4 fusion.88
  468.9 4.4 fusion.86
  478.8 4.5 fusion.84
  483.4 13.9 %fusion.74 = f32[3072,768]{1,0:T(8,128)} fusion(bf16[1024,768]{0,1:T(8,128)(2,1)S(1)} %copy-done.9, pred[1024]{0:T(1024)(128)(4,1)S(1)} %lt.21, f32[1024,3072]{1,0:T(8,128)} %fusion.83, f32[3072]{0:T(1024)S(1)} %convert_element_type.131), kind=kOutput, calls=%fused_computation.111 | convolution fusion | flops 4864081920 | bytes 23606272 | tf_op jit(solution)/shard_map/dot_general | solution.py:35
  497.9 10.7 fusion.82
  509.3 12.3 %add_convert_fusion.1 = bf16[1024,768]{0,1:T(8,128)(2,1)} fusion(f32[1024,768]{0,1:T(8,128)} %get-tuple-element.318, bf16[3072,768]{1,0:T(8,128)(2,1)} %all-gather.17.cloned.1.call-done, f32[768]{0:T(1024)S(1)} %convert_element_type.133, f32[1024,3072]{1,0:T(8,128)} %fusion.83, f32[3072]{0:T(1024)S(1)} %convert_element_type.131), kind=kOutput, calls=%fused_computation.102 | convolution fusion | flops 4865654784 | bytes 22035456 | tf_op jit(solution)/shard_map/dot_general | solution.py:31
  536.7 40.8 %all-reduce.18 = (f32[768]{0:T(1024)S(1)}, f32[768]{0:T(1024)S(1)}, f32[768]{0:T(1024)S(1)}, f32[768]{0:T(1024)S(1)}, f32[768]{0:T(1024)S(1)}, /*index=5*/f32[76...) all-reduce(f32[768]{0:T(1024)S(1)} %get-tuple-element.252, ...), channel_id=2, replica_groups=mesh['dp'=32] {'dp'}, use_global_device_ids=true, to_apply=%region_18.19.clone | all-reduce | flops 9216 | bytes 73728
  582.2 5.7 add_convert_fusion
  591.0 31.6 %reduce-scatter.7.cloned.1.call-done = f32[24,768]{1,0:T(8,128)} async-done(((f32[768,768]{1,0:T(8,128)}), f32[24,768]{1,0:T(8,128)}) %reduce-scatter.7.cloned.1.call-update) | async-done | bytes 73744 | tf_op jit(solution)/shard_map/reduce_scatter | solution.py:224
  622.6 104.0 %reduce-scatter.9.cloned.1.call-done = f32[24,768]{1,0:T(8,128)} async-done(((f32[768,768]{1,0:T(8,128)}), f32[24,768]{1,0:T(8,128)}) %reduce-scatter.9.cloned.1.call-update) | async-done | bytes 73744 | tf_op jit(solution)/shard_map/reduce_scatter | solution.py:226
  726.6 104.6 %reduce-scatter.11.cloned.1.call-done = f32[24,768]{1,0:T(8,128)} async-done(((f32[768,768]{1,0:T(8,128)}), f32[24,768]{1,0:T(8,128)}) %reduce-scatter.11.cloned.1.call-update) | async-done | bytes 73744 | tf_op jit(solution)/shard_map/reduce_scatter | solution.py:227
  831.2 141.0 %reduce-scatter.17.cloned.1.call-done = f32[96,768]{1,0:T(8,128)} async-done(((f32[3072,768]{1,0:T(8,128)}), f32[96,768]{1,0:T(8,128)}) %reduce-scatter.17.cloned.1.call-update) | async-done | bytes 294928 | tf_op jit(solution)/shard_map/reduce_scatter | solution.py:235
  972.2 142.0 %reduce-scatter.15.cloned.1.call-done = f32[24,3072]{1,0:T(8,128)} async-done(((f32[768,3072]{1,0:T(8,128)}), f32[24,3072]{1,0:T(8,128)}) %reduce-scatter.15.cloned.1.call-update) | async-done | bytes 294928 | tf_op jit(solution)/shard_map/reduce_scatter | solution.py:233
  (262 shorter events, 150.5 us)
Async XLA Ops:
  7.2 60.5 %all-gather.9.cloned.1.call-start = ((), (), s32[]{:S(2)}) async-start(), calls=%async_computation.7 | async-start | bytes 1216512 | tf_op jit(solution)/shard_map/all_gather | solution.py:119
  7.9 115.7 %all-gather.7.cloned.1.call-start = ((), (), s32[]{:S(2)}) async-start(), calls=%async_computation.6 | async-start | bytes 1216512 | tf_op jit(solution)/shard_map/all_gather | solution.py:122
  8.7 170.8 %all-gather.11.cloned.1.call-start = ((), (), s32[]{:S(2)}) async-start(), calls=%async_computation.8 | async-start | bytes 1216512 | tf_op jit(solution)/shard_map/all_gather | solution.py:121
  9.4 225.8 %all-gather.13.cloned.1.call-start = ((), (), s32[]{:S(2)}) async-start(), calls=%async_computation.9 | async-start | bytes 1216512 | tf_op jit(solution)/shard_map/all_gather | solution.py:124
  10.0 290.6 %all-gather.15.cloned.1.call-start = ((), (), s32[]{:S(2)}) async-start(), calls=%async_computation.10 | async-start | bytes 4866048 | tf_op jit(solution)/shard_map/all_gather | solution.py:128
  10.6 355.3 %all-gather.17.cloned.1.call-start = ((), (), s32[]{:S(2)}) async-start(), calls=%async_computation.11 | async-start | bytes 4866048 | tf_op jit(solution)/shard_map/all_gather | solution.py:130
  11.1 579.8 %reduce-scatter.13.cloned.1.call-start = ((), (), s32[]{:S(2)}) async-start(), calls=%async_computation.15 | async-start | bytes 2433024 | tf_op jit(solution)/shard_map/reduce_scatter | solution.py:229
  62.7 116.8 %copy-start.28 = (f32[768]{0:T(1024)}, f32[768]{0:T(1024)S(1)}, u32[]{:S(2)}) copy-start(f32[768]{0:T(1024)S(1)} %convert_element_type.118) | copy-start | bytes 9220
  62.7 116.8 %copy-start.40 = (f32[768]{0:T(1024)}, f32[768]{0:T(1024)S(1)}, u32[]{:S(2)}) copy-start(f32[768]{0:T(1024)S(1)} %convert_element_type.119) | copy-start | bytes 9220
  62.7 237.9 %copy-start.24 = (f32[768]{0:T(1024)}, f32[768]{0:T(1024)S(1)}, u32[]{:S(2)}) copy-start(f32[768]{0:T(1024)S(1)} %convert_element_type.129) | copy-start | bytes 9220
  64.6 59.0 %copy-start.1 = (bf16[1024,768]{0,1:T(8,128)(2,1)}, bf16[1024,768]{0,1:T(8,128)(2,1)S(1)}, u32[]{:S(2)}) copy-start(bf16[1024,768]{0,1:T(8,128)(2,1)S(1)} %copy.118) | copy-start | bytes 4718596
  64.9 114.6 %copy-start.26 = (f32[1024]{0:T(1024)}, f32[1024]{0:T(1024)S(1)}, u32[]{:S(2)}) copy-start(f32[1024]{0:T(1024)S(1)} %broadcast_multiply_fusion.1) | copy-start | bytes 12292
  65.4 5.3 copy-start.34
  65.4 114.1 %copy-start.30 = (f32[1024]{0:T(1024)}, f32[1024]{0:T(1024)S(1)}, u32[]{:S(2)}) copy-start(f32[1024]{0:T(1024)S(1)} %fusion.78) | copy-start | bytes 12292
  365.9 17.7 %copy-start.18 = (bf16[768,3072]{1,0:T(8,128)(2,1)S(1)}, bf16[768,3072]{1,0:T(8,128)(2,1)}, u32[]{:S(2)}) copy-start(bf16[768,3072]{1,0:T(8,128)(2,1)} %all-gather.15.cloned.1.call-done) | copy-start | bytes 14155780
  383.6 7.3 copy-start.46
  394.5 4.5 copy-start.5
  399.1 4.5 copy-start.8
  419.4 203.2 %reduce-scatter.7.cloned.1.call-start = ((), (), s32[]{:S(2)}) async-start(), calls=%async_computation.12 | async-start | bytes 2433024 | tf_op jit(solution)/shard_map/reduce_scatter | solution.py:224
  454.7 5.5 copy-start.2
  454.7 5.5 copy-start.27
  454.7 5.5 copy-start.29
  454.7 5.5 copy-start.31
  454.7 5.5 copy-start.41
  464.7 261.9 %reduce-scatter.9.cloned.1.call-start = ((), (), s32[]{:S(2)}) async-start(), calls=%async_computation.13 | async-start | bytes 2433024 | tf_op jit(solution)/shard_map/reduce_scatter | solution.py:226
  473.3 357.8 %reduce-scatter.11.cloned.1.call-start = ((), (), s32[]{:S(2)}) async-start(), calls=%async_computation.14 | async-start | bytes 2433024 | tf_op jit(solution)/shard_map/reduce_scatter | solution.py:227
  478.8 4.6 copy-start.9
  483.3 488.8 %reduce-scatter.17.cloned.1.call-start = ((), (), s32[]{:S(2)}) async-start(), calls=%async_computation.17 | async-start | bytes 9732096 | tf_op jit(solution)/shard_map/reduce_scatter | solution.py:235
  497.3 616.8 %reduce-scatter.15.cloned.1.call-start = ((), (), s32[]{:S(2)}) async-start(), calls=%async_computation.16 | async-start | bytes 9732096 | tf_op jit(solution)/shard_map/reduce_scatter | solution.py:233
  526.6 3.3 copy-start.20
  526.6 3.3 copy-start.44
  533.7 48.4 %copy-start.33 = (f32[1024]{0:T(1024)S(1)}, f32[1024]{0:T(1024)}, u32[]{:S(2)}) copy-start(f32[1024]{0:T(1024)} %copy-done.32) | copy-start | bytes 12292
  (36 other events, 65.9 us)
Sparse Core Ops, SparseCore 0:
  10.9 56.7 all-gather.8
  70.6 52.9 all-gather.6
  126.5 52.9 all-gather.10
  182.3 52.9 all-gather.12
  238.0 62.5 all-gather.14
  303.4 62.4 all-gather.16
  419.5 97.8 reduce-scatter.12
  524.1 98.4 reduce-scatter.6
  628.4 98.0 reduce-scatter.8
  733.1 97.9 reduce-scatter.10
  837.7 134.4 reduce-scatter.16
  979.5 134.5 reduce-scatter.14
where the time goes:
time: 1130 us; the launch traced here: 1120 us
  waiting for transfers between devices  750 us (66%)
  matrix products  142 us (13%)
  local copies, waits for them, and re-layouts  100 us (9%)
  blocking collectives  83.6 us (7%)
  other arithmetic  29.2 us (3%)
  between operations  15 us (1%)
    reduce_scatter x1, waiting for transfers between devices, body(): lax.psum_scatter(grad_up_weight, 'dp', scatter_dimension=0, tiled=True)  142 us
    reduce_scatter x1, waiting for transfers between devices, body(): lax.psum_scatter(grad_down_weight, 'dp', scatter_dimension=0, tiled=True)  141 us
    reduce_scatter x1, waiting for transfers between devices, body(): lax.psum_scatter(grad_value_weight, 'dp', scatter_dimension=0, tiled=True)  105 us
    reduce_scatter x1, waiting for transfers between devices, body(): lax.psum_scatter(grad_key_weight, 'dp', scatter_dimension=0, tiled=True)  104 us
    unnamed x2, blocking collectives  83.6 us
    all_gather x1, waiting for transfers between devices, body(): lax.all_gather(up_weight, 'dp', axis=0, tiled=True)  57.6 us
    all_gather x1, waiting for transfers between devices, body(): lax.all_gather(down_weight, 'dp', axis=0, tiled=True)  54.2 us
    all_gather x1, waiting for transfers between devices, body(): lax.all_gather(value_weight, 'dp', axis=0, tiled=True)  52.9 us
  transfers between devices with their start and end apart: 12, of which 11 were waited for; matrix products, arithmetic and copies ran while one was open for 18% of the time, Pallas kernels for 0%

commit v1 on v0

v1 whole, which is shorter than its diff:
```python
import jax
import jax.numpy as jnp
from jax import lax
from jax.experimental import pallas as pl
from jax.experimental.pallas import tpu as pltpu
from jax.sharding import PartitionSpec as P

HEADS = 12
HEAD_DIM = 64
PAIRS = 6
LANES = 128
EPS = 1e-06
MASKED = -1e30
SCALE = HEAD_DIM**-0.5
GELU_C = 0.7978845608028654
GELU_A = 0.044715
VMEM = 56 * 1024 * 1024
F32 = jnp.float32
BF16 = jnp.bfloat16


def dot_nn(left, right):
    return lax.dot_general(left, right, (((1,), (0,)), ((), ())), preferred_element_type=F32)


def dot_nt(left, right):
    return lax.dot_general(left, right, (((1,), (1,)), ((), ())), preferred_element_type=F32)


def dot_tn(left, right):
    return lax.dot_general(left, right, (((0,), (0,)), ((), ())), preferred_element_type=F32)


def normalize(rows):
    centered = rows - jnp.mean(rows, axis=-1, keepdims=True)
    inverse = lax.rsqrt(jnp.mean(centered * centered, axis=-1, keepdims=True) + EPS)
    return centered * inverse, inverse


def norm_back(grads, gain, hat, inverse):
    scaled = grads * gain
    mean = jnp.mean(scaled, axis=-1, keepdims=True)
    mean_hat = jnp.mean(scaled * hat, axis=-1, keepdims=True)
    return inverse * (scaled - mean - hat * mean_hat)


def column_sum(rows):
    return jnp.sum(rows, axis=0, keepdims=True)


def segments(lengths_ref, tile, slots, rows, axis):
    shape = (rows, 1) if axis == 0 else (1, rows)
    index = lax.broadcasted_iota(jnp.int32, shape, axis)
    segment = jnp.zeros(shape, jnp.int32)
    bound = 0
    for slot in range(slots):
        bound = bound + lengths_ref[tile, slot]
        segment = segment + (index >= bound).astype(jnp.int32)
    return segment


def mask_bias(lengths_ref, tile, slots, rows):
    same = segments(lengths_ref, tile, slots, rows, 0) == segments(lengths_ref, tile, slots, rows, 1)
    return jnp.where(same, 0.0, MASKED).astype(F32)


def half_of(pair, side):
    lane = lax.broadcasted_iota(jnp.int32, pair.shape, 1)
    keep = lane < HEAD_DIM if side == 0 else lane >= HEAD_DIM
    return jnp.where(keep, pair, jnp.zeros_like(pair))


def attention_forward(lengths_ref, x_ref, grad_ref, vec_ref, wq_ref, wk_ref, wv_ref, wo_ref,
                      n1_ref, q_ref, k_ref, v_ref, mixed_ref, lse_ref, resid_ref, n2_ref, cot_ref, dsum_ref):
    tile = pl.program_id(0)
    rows = x_ref.shape[0]
    slots = lengths_ref.shape[1]
    x = x_ref[...].astype(F32)
    hat, _ = normalize(x)
    n1 = (hat * vec_ref[0:1, :] + vec_ref[1:2, :]).astype(BF16)
    n1_ref[...] = n1
    q_ref[...] = (dot_nn(n1, wq_ref[...]) + vec_ref[2:3, :]).astype(BF16) * jnp.asarray(SCALE, BF16)
    k_ref[...] = dot_nn(n1, wk_ref[...]).astype(BF16)
    v_ref[...] = (dot_nn(n1, wv_ref[...]) + vec_ref[3:4, :]).astype(BF16)
    bias = mask_bias(lengths_ref, tile, slots, rows)
    lane = lax.broadcasted_iota(jnp.int32, (rows, LANES), 1)
    lse = jnp.zeros((rows, LANES), F32)
    for pair in range(PAIRS):
        cols = pl.ds(pair * LANES, LANES)
        qp, kp, vp = q_ref[:, cols], k_ref[:, cols], v_ref[:, cols]
        total = None
        for side in range(2):
            scores = dot_nt(half_of(qp, side), kp) + bias
            top = jnp.max(scores, axis=-1, keepdims=True)
            weights = jnp.exp(scores - top)
            sums = jnp.sum(weights, axis=-1, keepdims=True)
            probs = (weights * (1.0 / sums)).astype(BF16)
            part = dot_nn(probs, half_of(vp, side))
            total = part if total is None else total + part
            lse = jnp.where(lane == 2 * pair + side, top + jnp.log(sums), lse)
        mixed_ref[:, cols] = total.astype(BF16)
    lse_ref[...] = lse
    resid = x + (dot_nn(mixed_ref[...], wo_ref[...]) + vec_ref[4:5, :])
    resid_ref[...] = resid
    hat_two, _ = normalize(resid)
    n2_ref[...] = (hat_two * vec_ref[5:6, :] + vec_ref[6:7, :]).astype(BF16)
    valid = segments(lengths_ref, tile, slots, rows, 0) < slots
    cot = jnp.where(valid, grad_ref[...].astype(F32), 0.0)
    cot_ref[...] = cot.astype(BF16)

    @pl.when(tile == 0)
    def _():
        dsum_ref[...] = jnp.zeros_like(dsum_ref)

    dsum_ref[0:1, :] += column_sum(cot)


def mlp_up(n2_ref, cot_ref, wup_ref, bup_ref, act_ref, slope_ref, dwd_ref):
    pre = dot_nn(n2_ref[...], wup_ref[...]) + bup_ref[...]
    square = pre * pre
    tanh = jnp.tanh(pre * (GELU_C + (GELU_C * GELU_A) * square))
    half = 0.5 + 0.5 * tanh
    act = (pre * half).astype(BF16)
    inner = GELU_C + (3.0 * GELU_C * GELU_A) * square
    slope_ref[...] = (half + (0.5 * pre) * (1.0 - tanh * tanh) * inner).astype(BF16)
    act_ref[...] = act
    dwd_ref[...] = dot_tn(act, cot_ref[...]).astype(BF16)


def mlp_down(n2_ref, cot_ref, resid_ref, vec_ref, act_ref, slope_ref, wup_ref, wdown_ref,
             out_ref, gresid_ref, gattn_ref, dwu_ref, dbu_ref, dsum_ref, out_acc, grad_acc):
    step = pl.program_id(0)

    @pl.when(step == 0)
    def _():
        out_acc[...] = jnp.zeros_like(out_acc)
        grad_acc[...] = jnp.zeros_like(grad_acc)

    cot = cot_ref[...]
    wdown = wdown_ref[...]
    grad_up = (dot_nt(cot, wdown) * slope_ref[...].astype(F32)).astype(BF16)
    dbu_ref[...] = column_sum(grad_up.astype(F32))
    dwu_ref[...] = dot_tn(n2_ref[...], grad_up).astype(BF16)
    out_acc[...] += dot_nn(act_ref[...], wdown)
    grad_acc[...] += dot_nt(grad_up, wup_ref[...])

    @pl.when(step == pl.num_programs(0) - 1)
    def _():
        block = 256
        dsum_ref[...] = jnp.zeros_like(dsum_ref)

        @pl.loop(0, cot_ref.shape[0] // block)
        def _(index):
            at = pl.ds(pl.multiple_of(index * block, block), block)
            resid = resid_ref[at, :]
            out_ref[at, :] = (resid + (out_acc[at, :] + vec_ref[7:8, :])).astype(BF16)
            hat, inverse = normalize(resid)
            grad_two = grad_acc[at, :]
            gresid = cot_ref[at, :].astype(F32) + norm_back(grad_two, vec_ref[5:6, :], hat, inverse)
            gresid_ref[at, :] = gresid
            gattn = gresid.astype(BF16)
            gattn_ref[at, :] = gattn
            dsum_ref[0:1, :] += column_sum(gattn.astype(F32))
            dsum_ref[1:2, :] += column_sum(grad_two * hat)
            dsum_ref[2:3, :] += column_sum(grad_two)


def attention_backward(lengths_ref, q_ref, k_ref, v_ref, lse_ref, gattn_ref, wo_ref,
                       dq_ref, dk_ref, dv_ref, dsum_ref, gmix_ref):
    tile = pl.program_id(0)
    rows = q_ref.shape[0]
    gmix_ref[...] = dot_nt(gattn_ref[...], wo_ref[...]).astype(BF16)
    bias = mask_bias(lengths_ref, tile, lengths_ref.shape[1], rows)
    for pair in range(PAIRS):
        cols = pl.ds(pair * LANES, LANES)
        qp, kp, vp, gp = q_ref[:, cols], k_ref[:, cols], v_ref[:, cols], gmix_ref[:, cols]
        dq = dk = dv = None
        for side in range(2):
            head = 2 * pair + side
            qh, kh, gh = half_of(qp, side), half_of(kp, side), half_of(gp, side)
            probs = jnp.exp(dot_nt(qh, kp) + bias - lse_ref[:, head : head + 1])
            grad_probs = dot_nt(gh, vp)
            dot = jnp.sum(probs * grad_probs, axis=-1, keepdims=True)
            grad_scores = (probs * (grad_probs - dot)).astype(BF16)
            one_q = dot_nn(grad_scores, kh)
            one_k = dot_tn(grad_scores, qh)
            one_v = dot_tn(probs.astype(BF16), gh)
            dq = one_q if dq is None else dq + one_q
            dk = one_k if dk is None else dk + one_k
            dv = one_v if dv is None else dv + one_v
        dq_ref[:, cols] = (dq * SCALE).astype(BF16)
        dk_ref[:, cols] = dk.astype(BF16)
        dv_ref[:, cols] = dv.astype(BF16)

    @pl.when(tile == 0)
    def _():
        dsum_ref[...] = jnp.zeros_like(dsum_ref)

    dsum_ref[0:1, :] += column_sum(dq_ref[...].astype(F32))
    dsum_ref[1:2, :] += column_sum(dv_ref[...].astype(F32))


def weight_grads(n1_ref, mixed_ref, dq_ref, dk_ref, dv_ref, gattn_ref, wq_out, wk_out, wv_out, wo_out):
    n1 = n1_ref[...]
    wq_out[...] = dot_tn(n1, dq_ref[...]).astype(BF16)
    wk_out[...] = dot_tn(n1, dk_ref[...]).astype(BF16)
    wv_out[...] = dot_tn(n1, dv_ref[...]).astype(BF16)
    wo_out[...] = dot_tn(mixed_ref[...], gattn_ref[...]).astype(BF16)


def tokens_backward(x_ref, gresid_ref, vec_ref, dq_ref, dk_ref, dv_ref, wq_ref, wk_ref, wv_ref, gtok_ref, dsum_ref):
    grad_one = dot_nt(dq_ref[...], wq_ref[...]) + dot_nt(dk_ref[...], wk_ref[...]) + dot_nt(dv_ref[...], wv_ref[...])
    hat, inverse = normalize(x_ref[...].astype(F32))
    gtok_ref[...] = (gresid_ref[...] + norm_back(grad_one, vec_ref[0:1, :], hat, inverse)).astype(BF16)

    @pl.when(pl.program_id(0) == 0)
    def _():
        dsum_ref[...] = jnp.zeros_like(dsum_ref)

    dsum_ref[0:1, :] += column_sum(grad_one * hat)
    dsum_ref[1:2, :] += column_sum(grad_one)


def rows_spec(block, width):
    return pl.BlockSpec((block, width), lambda i: (i, 0))


def cols_spec(height, block):
    return pl.BlockSpec((height, block), lambda i: (0, i))


def whole_spec(shape):
    return pl.BlockSpec(shape, lambda i: (0,) * len(shape), pipeline_mode=pl.Buffered(1))


def kept_spec(shape):
    return pl.BlockSpec(shape, lambda i: (0,) * len(shape))


SMEM = pl.BlockSpec(memory_space=pltpu.SMEM)


def call(kernel, grid, ins, outs, scratch, name, flops, *args):
    out_specs = tuple(spec for spec, _ in outs)
    out_shape = tuple(shape for _, shape in outs)
    moved = sum(a.size * a.dtype.itemsize for a in args) + sum(s.size * s.dtype.itemsize for s in out_shape)
    return pl.pallas_call(
        kernel,
        grid=grid,
        in_specs=ins,
        out_specs=out_specs,
        out_shape=out_shape,
        scratch_shapes=scratch,
        compiler_params=pltpu.CompilerParams(vmem_limit_bytes=VMEM, dimension_semantics=("arbitrary",) * len(grid)),
        cost_estimate=pl.CostEstimate(flops=flops, bytes_accessed=moved, transcendentals=0),
        name=name,
    )(*args)


def shaped(*shape, dtype=BF16):
    return jax.ShapeDtypeStruct(shape, dtype)


def body(tokens, lengths, attn_gain, attn_shift, query_weight, query_bias, key_weight, value_weight, value_bias,
         out_weight, out_bias, mlp_gain, mlp_shift, up_weight, up_bias, down_weight, down_bias, grad_out):
    count = lax.axis_size("dp")
    rows, width = tokens.shape
    tiles = lengths.shape[0]
    tile = rows // tiles
    hidden = up_bias.shape[0] * count
    own = width // count
    folds = hidden // width
    vectors = (attn_gain, attn_shift, query_bias, value_bias, out_bias, mlp_gain, mlp_shift, down_bias)
    flat = jnp.concatenate(vectors + (up_bias,))
    packed = jnp.concatenate(
        (
            query_weight,
            key_weight,
            value_weight,
            out_weight,
            up_weight.reshape(own, folds, width).transpose(1, 0, 2).reshape(own * folds, width),
            down_weight,
            jnp.pad(flat.reshape(1, -1), ((0, 7), (0, width - flat.size))),
        ),
        axis=0,
    )
    whole = lax.all_gather(packed, "dp", axis=0, tiled=True).reshape(count, -1, width)

    def part(index):
        return whole[:, index * own : (index + 1) * own, :].reshape(width, width)

    wq, wk, wv, wo = (part(index) for index in range(4))
    wup = whole[:, 4 * own : (4 + folds) * own, :].reshape(count, folds, own, width).transpose(0, 2, 1, 3)
    wup = wup.reshape(width, hidden)
    wdown = whole[:, (4 + folds) * own : (4 + 2 * folds) * own, :].reshape(hidden, width)
    last = whole[:, (4 + 2 * folds) * own, : flat.size].astype(F32)
    vec = last[:, : 8 * own].reshape(count, 8, own).transpose(1, 0, 2).reshape(8, width)
    bup = last[:, 8 * own :].reshape(1, hidden)

    tile_rows = rows_spec(tile, width)
    square = whole_spec((width, width))
    vec_spec = whole_spec((8, width))
    sums = (kept_spec((8, width)), shaped(8, width, dtype=F32))
    low_rows = (tile_rows, shaped(rows, width))
    high_rows = (tile_rows, shaped(rows, width, dtype=F32))
    lse_spec = rows_spec(tile, LANES)
    mac = 2 * rows * width * width
    n1, q, k, v, mixed, lse, resid, n2, cot, sum_down = call(
        attention_forward, (tiles,), [SMEM, tile_rows, tile_rows, vec_spec, square, square, square, square],
        [low_rows] * 5 + [(lse_spec, shaped(rows, LANES, dtype=F32)), high_rows, low_rows, low_rows, sums],
        [], "attention_forward", 6 * mac, lengths, tokens, grad_out, vec, wq, wk, wv, wo)
    block = min(384, hidden)
    steps = hidden // block
    full_rows = whole_spec((rows, width))
    act, slope, d_down = call(
        mlp_up, (steps,), [full_rows, full_rows, cols_spec(width, block), cols_spec(1, block)],
        [(cols_spec(rows, block), shaped(rows, hidden))] * 2 + [(rows_spec(block, width), shaped(hidden, width))],
        [], "mlp_up", 2 * folds * mac, n2, cot, wup, bup)
    out, gresid, gattn, d_up, sum_up, sum_two = call(
        mlp_down, (steps,),
        [full_rows, full_rows, full_rows, vec_spec, cols_spec(rows, block), cols_spec(rows, block),
         cols_spec(width, block), rows_spec(block, width)],
        [(kept_spec((rows, width)), shaped(rows, width)), (kept_spec((rows, width)), shaped(rows, width, dtype=F32)),
         (kept_spec((rows, width)), shaped(rows, width)), (cols_spec(width, block), shaped(width, hidden)),
         (cols_spec(1, block), shaped(1, hidden, dtype=F32)), sums],
        [pltpu.VMEM((rows, width), F32), pltpu.VMEM((rows, width), F32)],
        "mlp_down", 4 * folds * mac, n2, cot, resid, vec, act, slope, wup, wdown)
    dq, dk, dv, sum_qv = call(
        attention_backward, (tiles,), [SMEM, tile_rows, tile_rows, tile_rows, lse_spec, tile_rows, square],
        [low_rows] * 3 + [sums], [pltpu.VMEM((tile, width), BF16)],
        "attention_backward", 4 * mac, lengths, q, k, v, lse, gattn, wo)
    side = width // 2
    d_q, d_k, d_v, d_o = call(
        weight_grads, (2,), [full_rows] * 2 + [cols_spec(rows, side)] * 4,
        [(cols_spec(width, side), shaped(width, width))] * 4, [],
        "weight_grads", 4 * mac, n1, mixed, dq, dk, dv, gattn)
    gtok, sum_one = call(
        tokens_backward, (tiles,),
        [tile_rows, tile_rows, vec_spec, tile_rows, tile_rows, tile_rows, square, square, square],
        [low_rows, sums], [], "tokens_backward", 3 * mac, tokens, gresid, vec, dq, dk, dv, wq, wk, wv)

    vec_grads = jnp.concatenate(
        (sum_one[0:2], sum_qv[0:2], sum_two[0:3], sum_down[0:1]), axis=0)
    vec_grads = vec_grads.reshape(8, count, own).transpose(1, 0, 2).reshape(count, 8 * own)
    flat_grads = jnp.concatenate((vec_grads, sum_up.reshape(count, folds * own)), axis=1).astype(BF16)
    flat_grads = jnp.pad(flat_grads.reshape(count, 1, -1), ((0, 0), (0, 7), (0, width - flat.size)))
    grads = jnp.concatenate(
        (
            d_q.reshape(count, own, width),
            d_k.reshape(count, own, width),
            d_v.reshape(count, own, width),
            d_o.reshape(count, own, width),
            d_up.reshape(count, own, folds, width).transpose(0, 2, 1, 3).reshape(count, folds * own, width),
            d_down.reshape(count, folds * own, width),
            flat_grads,
        ),
        axis=1,
    )
    share = lax.psum_scatter(grads.reshape(-1, width), "dp", scatter_dimension=0, tiled=True).astype(F32)
    g_q, g_k, g_v, g_o = (share[index * own : (index + 1) * own] for index in range(4))
    g_up = share[4 * own : (4 + folds) * own].reshape(folds, own, width).transpose(1, 0, 2).reshape(own, hidden)
    g_down = share[(4 + folds) * own : (4 + 2 * folds) * own]
    g_vec = share[(4 + 2 * folds) * own]
    g_gain, g_shift, g_qb, g_vb, g_ob, g_mg, g_ms, g_db = (g_vec[index * own : (index + 1) * own] for index in range(8))
    g_ub = g_vec[8 * own : 8 * own + folds * own]
    return (out, gtok, g_gain, g_shift, g_q, g_qb, g_k, g_v, g_vb, g_o, g_ob, g_mg, g_ms, g_up, g_ub, g_down, g_db)


def solution(mesh):
    rows, flat = P("dp", None), P("dp")
    return jax.shard_map(
        body,
        mesh=mesh,
        in_specs=(rows, rows, flat, flat, rows, flat, rows, rows, flat, rows, flat, flat, flat, rows, flat, rows, flat, rows),
        out_specs=(rows, rows, flat, flat, rows, flat, rows, rows, flat, rows, flat, flat, flat, rows, flat, rows, flat),
        check_vma=False,
    )
```

time: 1130 us -> 482 us (0.43)
  waiting for transfers between devices: 750 us -> 271 us
  matrix products: 142 us -> 0 us
  Pallas kernels: 0 us -> 125 us
  blocking collectives: 83.6 us -> 0 us
  local copies, waits for them, and re-layouts: 100 us -> 68.7 us
  other arithmetic: 29.2 us -> 2.03 us
    reduce_scatter x6 -> x1, waiting for transfers between devices: 523 us -> 163 us  [body(): lax.psum_scatter(grads.reshape(-1, width), 'dp', scatter_dimension=0, til...]
    dot_general x32 -> x0, matrix products: 142 us -> none  [the longest x6 40.8 us: weight_grad(): lax.dot_general(rows, grads, (((0,), (0,)), ((), ())), preferred_element_...]
    pallas_call x0 -> x6, Pallas kernels: none -> 125 us  [call(): pl.pallas_call(kernel, grid=grid, in_specs=ins, out_specs=out_specs, out_...]
    all_gather x6 -> x1, waiting for transfers between devices: 223 us -> 108 us  [body(): lax.all_gather(packed, 'dp', axis=0, tiled=True).reshape(count, -1, width)]
    unnamed x2 -> x0, blocking collectives: 83.6 us -> none
    while x41 -> x0, local copies, waits for them, and re-layouts: 21.7 us -> none
    slice x0 -> x13, local copies, waits for them, and re-layouts: none -> 21 us  [the longest x1 8 us: body(): whole[:, (4 + folds) * own:(4 + 2 * folds) * own, :].reshape(hidden, width)]
    reduce_sum x11 -> x0, other arithmetic: 18.1 us -> none  [the longest x2 5.84 us: layer_norm(): return centered * inverse * gain + shift]
  transfers between devices with their start and end apart: 12 -> 2, of which waited for: 11 -> 2; matrix products, arithmetic and copies ran while one was open for 18% -> 0% of each run, Pallas kernels for 0% -> 0%
where the time goes in v1:
time: 482 us; the launch traced here: 481 us
  waiting for transfers between devices  271 us (56%)
  Pallas kernels  125 us (26%)
  local copies, waits for them, and re-layouts  68.7 us (14%)
  between operations  14.2 us (3%)
    reduce_scatter x1, waiting for transfers between devices, body(): lax.psum_scatter(grads.reshape(-1, width), 'dp', scatter_dimension=0, til...  163 us
    pallas_call x6, Pallas kernels, call(): pl.pallas_call(kernel, grid=grid, in_specs=ins, out_specs=out_specs, out_...  125 us
    all_gather x1, waiting for transfers between devices, body(): lax.all_gather(packed, 'dp', axis=0, tiled=True).reshape(count, -1, width)  108 us
    unnamed x25, local copies, waits for them, and re-layouts  20.4 us
    reshape x2, local copies, waits for them, and re-layouts, body(): d_up.reshape(count, own, folds, width).transpose(0, 2, 1, 3)  13 us
  transfers between devices with their start and end apart: 2, of which 2 were waited for; matrix products, arithmetic and copies ran while one was open for 0% of the time, Pallas kernels for 0%

profile of v1, /device:TPU:0, one launch (start us, length us, event | category | flops | bytes accessed | tf_op | source)
XLA Modules:
  0.0 481.0 jit_solution(2290971242958860731)
XLA Ops:
  7.2 6.1 %concatenate.28 = bf16[288]{0:T(512)(128)(2,1)S(1)} concatenate(bf16[24]{0:T(256)(128)(2,1)} %param.20, bf16[24]{0:T(256)(128)(2,1)} %param.21, bf16[24]{0:T(256)(128)(2,1)} %param.23, bf16[24]{0:T(256)(128)(2,1)} %param.26, bf16[24]{0:T(256)(128)(2,1)} %param.28, bf16[24]{0:T(256)(128)(2,1)} %param.29, bf16[24]{0:T(256)(128)(2,1)} %param.30, bf16[24]{0:T(256)(128)(2,1)} %param.34, ...), dimensions={0} | concatenate | bytes 1152 | tf_op jit(solution)/shard_map/concatenate | solution.py:274
  13.3 0.9 copy.57
  14.3 0.8 constant_dynamic-update-slice_fusion.6
  15.0 0.8 constant_dynamic-update-slice_fusion.5
  15.8 0.8 constant_dynamic-update-slice_fusion.4
  16.6 0.8 constant_dynamic-update-slice_fusion.3
  17.4 0.9 constant_dynamic-update-slice_fusion.1
  19.2 107.7 %all-gather.2.cloned.1.call-done = bf16[9472,768]{1,0:T(8,128)(2,1)} async-done(((bf16[296,768]{1,0:T(8,128)(2,1)}), bf16[9472,768]{1,0:T(8,128)(2,1)}) %all-gather.2.cloned.1.call-update) | async-done | bytes 14549008 | tf_op jit(solution)/shard_map/all_gather | solution.py:287
  126.9 1.0 slice.162
  128.0 4.5 fusion.9
  132.5 8.0 %fusion.8 = (bf16[32,96,768]{2,1,0:T(8,128)(2,1)}, bf16[32,96,768]{2,1,0:T(8,128)(2,1)}) fusion(bf16[32,296,768]{2,1,0:T(8,128)(2,1)} %bitcast.62), kind=kLoop, calls=%fused_computation.40 | loop fusion | bytes 18874368 | tf_op jit(solution)/shard_map/slice | solution.py:295
  142.0 4.7 copy.43
  146.7 3.2 copy.52
  149.9 22.6 %attention_forward.1 = (bf16[1024,768]{1,0:T(8,128)(2,1)}, bf16[1024,768]{1,0:T(8,128)(2,1)}, bf16[1024,768]{1,0:T(8,128)(2,1)}, bf16[1024,768]{1,0:T(8,128)(2,1...) custom-call(s32[4,5]{1,0:T(4,128)} %lengths_ref.3, ...), custom_call_target="tpu_custom_call" | custom-call | flops 7247757312 | bytes 22593616 | tf_op jit(solution)/shard_map/attention_forward/pallas_call | solution.py:247
  173.3 20.7 %mlp_up.1 = (bf16[1024,3072]{1,0:T(8,128)(2,1)}, bf16[1024,3072]{1,0:T(8,128)(2,1)}, bf16[3072,768]{1,0:T(8,128)(2,1)}) custom-call(bf16[1024,768]{1,0:T(8,128)(2,1)} %get-tuple-element.46.n2_ref, bf16[1024,768]{1,0:T(8,128)(2,1)} %get-tuple-element.47.cot_ref, bf16[768,3072]{1,0:T(8,128)(2,1)} %bitcast.66, f32[1,3072]{1,0:T(1,128)} %reshape.169.bup_ref), custom_call_target="tpu_custom_call" | custom-call | flops 9663676416 | bytes 25178112 | tf_op jit(solution)/shard_map/mlp_up/pallas_call | solution.py:247
  194.0 37.9 %mlp_down.1 = (bf16[1024,768]{1,0:T(8,128)(2,1)}, f32[1024,768]{1,0:T(8,128)}, bf16[1024,768]{1,0:T(8,128)(2,1)}, bf16[768,3072]{1,0:T(8,128)(2,1)}, f32[1,3072]{1,0:T(1,128)}, /*index=5*/f32[8,768]{1,0:T(8,128)}) custom-call(bf16[1024,768]{1,0:T(8,128)(2,1)} %get-tuple-element.46.n2_ref, bf16[1024,768]{1,0:T(8,128)(2,1)} %get-tuple-element.47.cot_ref, ...), custom_call_target="tpu_custom_call" | custom-call | flops 19327352832 | bytes 39383040 | tf_op jit(solution)/shard_map/mlp_down/pallas_call | solution.py:247
  232.0 22.8 %attention_backward.1 = (bf16[1024,768]{1,0:T(8,128)(2,1)}, bf16[1024,768]{1,0:T(8,128)(2,1)}, bf16[1024,768]{1,0:T(8,128)(2,1)}, f32[8,768]{1,0:T(8,128)}) custom-call(s32[4,5]{1,0:T(4,128)} %lengths_ref.3, bf16[1024,768]{1,0:T(8,128)(2,1)} %get-tuple-element.53.q_ref, bf16[1024,768]{1,0:T(8,128)(2,1)} %get-tuple-element.54.k_ref, ...), custom_call_target="tpu_custom_call" | custom-call | flops 4831838208 | bytes 12738640 | tf_op jit(solution)/shard_map/attention_backward/pallas_call | solution.py:247
  255.5 10.0 %tokens_backward.1 = (bf16[1024,768]{1,0:T(8,128)(2,1)}, f32[8,768]{1,0:T(8,128)}) custom-call(bf16[1024,768]{1,0:T(8,128)(2,1)} %x_ref.3, f32[1024,768]{1,0:T(8,128)} %get-tuple-element.52.gresid_ref, f32[8,768]{1,0:T(8,128)} %reshape.162.vec_ref, bf16[1024,768]{1,0:T(8,128)(2,1)} %get-tuple-element.58.dq_ref, bf16[1024,768]{1,0:T(8,128)(2,1)} %get-tuple-element.59.dk_ref, ...), custom_call_target="tpu_custom_call" | custom-call | flops 3623878656 | bytes 14598144 | tf_op jit(solution)/shard_map/tokens_backward/pallas_call | solution.py:247
  267.4 9.8 %reshape.175 = bf16[32,24,4,768]{3,2,1,0:T(4,128)(2,1)} reshape(bf16[768,3072]{1,0:T(8,128)(2,1)} %get-tuple-element.68) | data formatting | bytes 9437184 | tf_op jit(solution)/shard_map/reshape | solution.py:353
  277.2 3.2 copy.44
  280.4 10.9 %weight_grads.1 = (bf16[768,768]{1,0:T(8,128)(2,1)}, bf16[768,768]{1,0:T(8,128)(2,1)}, bf16[768,768]{1,0:T(8,128)(2,1)}, bf16[768,768]{1,0:T(8,128)(2,1)}) custom-call(bf16[1024,768]{1,0:T(8,128)(2,1)} %get-tuple-element.62.n1_ref, bf16[1024,768]{1,0:T(8,128)(2,1)} %get-tuple-element.63.mixed_ref, bf16[1024,768]{1,0:T(8,128)(2,1)} %get-tuple-element.58.dq_ref, ...), custom_call_target="tpu_custom_call" | custom-call | flops 4831838208 | bytes 14155776 | tf_op jit(solution)/shard_map/weight_grads/pallas_call | solution.py:247
  291.3 2.6 constant_dynamic-update-slice_fusion.12
  293.9 2.4 constant_dynamic-update-slice_fusion.11
  296.3 1.1 constant_dynamic-update-slice_fusion.10
  297.4 1.1 constant_dynamic-update-slice_fusion.9
  298.6 2.5 constant_dynamic-update-slice_fusion.8
  301.2 2.5 constant_dynamic-update-slice_fusion.7
  303.8 0.9 fusion.6
  304.7 163.2 %reduce-scatter.2.cloned.1.call-done = bf16[296,768]{1,0:T(8,128)(2,1)} async-done(((bf16[9472,768]{1,0:T(8,128)(2,1)}), bf16[296,768]{1,0:T(8,128)(2,1)}) %reduce-scatter.2.cloned.1.call-update) | async-done | bytes 454672 | tf_op jit(solution)/shard_map/reduce_scatter | solution.py:359
  467.9 1.1 convert_element_type.23
  470.1 1.7 fusion.10
  472.6 1.5 fusion.11
  (40 shorter events, 8.0 us)
Async XLA Ops:
  7.2 119.7 %all-gather.2.cloned.1.call-start = ((), (), s32[]{:S(2)}) async-start(), calls=%async_computation.1 | async-start | bytes 15003648 | tf_op jit(solution)/shard_map/all_gather | solution.py:287
  18.3 0.8 copy-start.2
  19.1 448.8 %reduce-scatter.2.cloned.1.call-start = ((), (), s32[]{:S(2)}) async-start(), calls=%async_computation.2 | async-start | bytes 15003648 | tf_op jit(solution)/shard_map/reduce_scatter | solution.py:359
  255.5 11.4 %copy-start.3 = (f32[1,3072]{1,0:T(1,128)S(1)}, f32[1,3072]{1,0:T(1,128)}, u32[]{:S(2)}) copy-start(f32[1,3072]{1,0:T(1,128)} %get-tuple-element.74) | copy-start | bytes 36868
  291.3 5.0 %copy-start.1 = (bf16[768,768]{1,0:T(8,128)(2,1)S(1)}, bf16[768,768]{1,0:T(8,128)(2,1)}, u32[]{:S(2)}) copy-start(bf16[768,768]{1,0:T(8,128)(2,1)} %get-tuple-element.66) | copy-start | bytes 3538948
  291.3 6.1 %copy-start = (bf16[768,768]{1,0:T(8,128)(2,1)S(1)}, bf16[768,768]{1,0:T(8,128)(2,1)}, u32[]{:S(2)}) copy-start(bf16[768,768]{1,0:T(8,128)(2,1)} %get-tuple-element.67) | copy-start | bytes 3538948
  297.4 3.6 slice-start
  298.6 2.6 slice-start.1
Sparse Core Ops, SparseCore 0:
  19.2 107.6 all-gather.1
  304.8 163.0 reduce-scatter.1

commit v2 on v1

v2 whole, which is shorter than its diff:
```python
import functools

import jax
import jax.numpy as jnp
from jax import lax
from jax.experimental import pallas as pl
from jax.experimental.pallas import tpu as pltpu
from jax.sharding import PartitionSpec as P

HEADS = 12
HEAD_DIM = 64
PAIRS = 6
LANES = 128
CHIPS = 16
EPS = 1e-06
MASKED = -1e30
SCALE = HEAD_DIM**-0.5
GELU_C = 0.7978845608028654
GELU_A = 0.044715
VMEM = 56 * 1024 * 1024
F32 = jnp.float32
BF16 = jnp.bfloat16


def dot_nn(left, right):
    return lax.dot_general(left, right, (((1,), (0,)), ((), ())), preferred_element_type=F32)


def dot_nt(left, right):
    return lax.dot_general(left, right, (((1,), (1,)), ((), ())), preferred_element_type=F32)


def dot_tn(left, right):
    return lax.dot_general(left, right, (((0,), (0,)), ((), ())), preferred_element_type=F32)


def normalize(rows):
    centered = rows - jnp.mean(rows, axis=-1, keepdims=True)
    inverse = lax.rsqrt(jnp.mean(centered * centered, axis=-1, keepdims=True) + EPS)
    return centered * inverse, inverse


def norm_back(grads, gain, hat, inverse):
    scaled = grads * gain
    mean = jnp.mean(scaled, axis=-1, keepdims=True)
    mean_hat = jnp.mean(scaled * hat, axis=-1, keepdims=True)
    return inverse * (scaled - mean - hat * mean_hat)


def column_sum(rows):
    return jnp.sum(rows, axis=0, keepdims=True)


def segments(lengths_ref, tile, slots, rows, axis):
    shape = (rows, 1) if axis == 0 else (1, rows)
    index = lax.broadcasted_iota(jnp.int32, shape, axis)
    segment = jnp.zeros(shape, jnp.int32)
    bound = 0
    for slot in range(slots):
        bound = bound + lengths_ref[tile, slot]
        segment = segment + (index >= bound).astype(jnp.int32)
    return segment


def mask_bias(lengths_ref, tile, slots, rows):
    same = segments(lengths_ref, tile, slots, rows, 0) == segments(lengths_ref, tile, slots, rows, 1)
    return jnp.where(same, 0.0, MASKED).astype(F32)


def half_of(pair, side):
    lane = lax.broadcasted_iota(jnp.int32, pair.shape, 1)
    keep = lane < HEAD_DIM if side == 0 else lane >= HEAD_DIM
    return jnp.where(keep, pair, jnp.zeros_like(pair))


def fetch_weights(me, sources, weight_refs, parts_ref, sem):
    core, chip = me & 1, me >> 1
    side = sources[0].shape[2]
    each = weight_refs[0].shape[0] // CHIPS
    for index, source in enumerate(sources):
        half = core if index < 4 else 1 - core
        cols = pl.ds(pl.multiple_of(half * side, LANES), side)
        for layer in range(4):
            owner = chip ^ (4 * layer + index % 4)
            rows = pl.ds(pl.multiple_of(owner * each, 16), each)
            for number, ref in enumerate(weight_refs):
                pltpu.make_async_copy(
                    source.at[layer, pl.ds(number * each, each), :], ref.at[rows, cols], sem.at[number]
                ).start()
            pltpu.make_async_copy(
                source.at[layer, pl.ds(3 * each, 16), :], parts_ref.at[2 * owner + half], sem.at[3]
            ).start()


def project(me_ref, x_ref, *refs):
    sources = refs[:8]
    n1_ref, q_ref, k_ref, v_ref, wq_ref, wk_ref, wv_ref, vec_ref, bup_ref, parts_ref, sem = refs[8:]
    weights = (wq_ref, wk_ref, wv_ref)

    @pl.when(pl.program_id(0) == 0)
    def _():
        fetch_weights(me_ref[0], sources, weights, parts_ref, sem)
        for number, ref in enumerate(weights + (parts_ref,)):
            pltpu.make_async_copy(ref, ref, sem.at[number]).wait()
        count, _, side = parts_ref.shape
        parts = [parts_ref[device].astype(F32) for device in range(count)]
        group = count // 2
        vec_ref[...] = jnp.concatenate((sum(parts[:group]), sum(parts[group:])), axis=1)
        blocks = bup_ref.shape[1] // side
        group = count // blocks
        for block in range(blocks):
            rows = sum(parts[block * group : (block + 1) * group])
            bup_ref[:, block * side : (block + 1) * side] = rows[8:9]

    project_rows(x_ref, vec_ref, wq_ref, wk_ref, wv_ref, n1_ref, q_ref, k_ref, v_ref)


def project_rows(x_ref, vec_ref, wq_ref, wk_ref, wv_ref, n1_ref, q_ref, k_ref, v_ref):
    hat, _ = normalize(x_ref[...].astype(F32))
    n1 = (hat * vec_ref[0:1, :] + vec_ref[1:2, :]).astype(BF16)
    n1_ref[...] = n1
    q_ref[...] = (dot_nn(n1, wq_ref[...]) + vec_ref[2:3, :]).astype(BF16) * jnp.asarray(SCALE, BF16)
    k_ref[...] = dot_nn(n1, wk_ref[...]).astype(BF16)
    v_ref[...] = (dot_nn(n1, wv_ref[...]) + vec_ref[3:4, :]).astype(BF16)


def attention_forward(lengths_ref, grad_ref, q_ref, k_ref, v_ref, mixed_ref, lse_ref, cot_ref, dsum_ref):
    tile = pl.program_id(0)
    rows = q_ref.shape[0]
    slots = lengths_ref.shape[1]
    bias = mask_bias(lengths_ref, tile, slots, rows)
    lane = lax.broadcasted_iota(jnp.int32, (rows, LANES), 1)
    lse = jnp.zeros((rows, LANES), F32)
    for pair in range(PAIRS):
        cols = pl.ds(pair * LANES, LANES)
        qp, kp, vp = q_ref[:, cols], k_ref[:, cols], v_ref[:, cols]
        total = None
        for side in range(2):
            scores = dot_nt(half_of(qp, side), kp) + bias
            top = jnp.max(scores, axis=-1, keepdims=True)
            weights = jnp.exp(scores - top)
            sums = jnp.sum(weights, axis=-1, keepdims=True)
            probs = (weights * (1.0 / sums)).astype(BF16)
            part = dot_nn(probs, half_of(vp, side))
            total = part if total is None else total + part
            lse = jnp.where(lane == 2 * pair + side, top + jnp.log(sums), lse)
        mixed_ref[:, cols] = total.astype(BF16)
    lse_ref[...] = lse
    valid = segments(lengths_ref, tile, slots, rows, 0) < slots
    cot = jnp.where(valid, grad_ref[...].astype(F32), 0.0)
    cot_ref[...] = cot.astype(BF16)

    @pl.when(tile == 0)
    def _():
        dsum_ref[...] = jnp.zeros_like(dsum_ref)

    dsum_ref[0:1, :] += column_sum(cot)


def up_block(ref):
    return ref[...].reshape(-1, ref.shape[-1])


def down_block(ref):
    return jnp.concatenate([ref[:, half].reshape(-1, ref.shape[-1]) for half in range(2)], axis=1)


def mlp_up(me_ref, x_ref, mixed_ref, vec_ref, wo_ref, cot_ref, wup_ref, bup_ref,
           resid_ref, n2_ref, act_ref, slope_ref, send_ref, keep_ref):
    step = pl.program_id(0)
    me = me_ref[0]

    @pl.when(step == 0)
    def _():
        weight = down_block(wo_ref)
        block = 256

        @pl.loop(0, x_ref.shape[0] // block)
        def _(index):
            at = pl.ds(pl.multiple_of(index * block, block), block)
            resid = x_ref[at, :].astype(F32) + (dot_nn(mixed_ref[at, :], weight) + vec_ref[4:5, :])
            resid_ref[at, :] = resid
            hat, _ = normalize(resid)
            n2_ref[at, :] = (hat * vec_ref[5:6, :] + vec_ref[6:7, :]).astype(BF16)

    pre = dot_nn(n2_ref[...], up_block(wup_ref)) + bup_ref[...]
    square = pre * pre
    tanh = jnp.tanh(pre * (GELU_C + (GELU_C * GELU_A) * square))
    half = 0.5 + 0.5 * tanh
    act = (pre * half).astype(BF16)
    inner = GELU_C + (3.0 * GELU_C * GELU_A) * square
    slope_ref[...] = (half + (0.5 * pre) * (1.0 - tanh * tanh) * inner).astype(BF16)
    act_ref[...] = act
    grad_weight = dot_tn(act, cot_ref[...])
    first = (me & 1) == 0
    side = send_ref.shape[3]
    low, high = grad_weight[:, :side], grad_weight[:, side:]
    keep = jnp.where(first, low, high).astype(BF16)
    send = jnp.where(first, high, low).astype(BF16)
    deep = send_ref.shape[2]
    chips = keep.shape[0] // deep
    for index in range(chips):
        chip = (step * chips + index) ^ (me >> 1)
        keep_ref[chip & 3, chip >> 2] = keep[index * deep : (index + 1) * deep]
        send_ref[chip & 3, chip >> 2] = send[index * deep : (index + 1) * deep]


def spread(me, rows, put):
    layer, plane = me >> 3, (me >> 1) & 3
    each = rows.shape[0] // CHIPS
    for chip in range(CHIPS):
        put((chip & 3) ^ plane, (chip >> 2) ^ layer, rows[chip * each : (chip + 1) * each].astype(BF16))


def mlp_down(me_ref, n2_ref, cot_ref, resid_ref, vec_ref, mixed_ref, act_ref, slope_ref, wup_ref, wdown_ref,
             out_ref, gresid_ref, gattn_ref, send_ref, keep_ref, dbu_ref, dsum_ref, out_acc, grad_acc):
    step = pl.program_id(0)
    steps = pl.num_programs(0)
    me = me_ref[0]
    half_steps = steps // 2

    @pl.when(step == 0)
    def _():
        out_acc[...] = jnp.zeros_like(out_acc)
        grad_acc[...] = jnp.zeros_like(grad_acc)

    cot = cot_ref[...]
    wdown = down_block(wdown_ref)
    grad_up = (dot_nt(cot, wdown) * slope_ref[...].astype(F32)).astype(BF16)
    dbu_ref[...] = column_sum(grad_up.astype(F32))
    grad_weight = dot_tn(n2_ref[...], grad_up)
    each = grad_weight.shape[0] // CHIPS

    def put_in(ref, fold, rows):
        base = pl.multiple_of(fold * each, 16)

        def put(plane, layer, piece):
            ref[plane, layer, pl.ds(base, each), :] = piece

        spread(me, rows, put)

    @pl.when(step < half_steps)
    def _():
        put_in(send_ref, step, grad_weight)

    @pl.when(step >= half_steps)
    def _():
        put_in(keep_ref, step - half_steps, grad_weight)

    out_acc[...] += dot_nn(act_ref[...], wdown)
    grad_acc[...] += dot_nt(grad_up, up_block(wup_ref))

    @pl.when(step == steps - 1)
    def _():
        block = 256
        dsum_ref[...] = jnp.zeros_like(dsum_ref)

        @pl.loop(0, cot_ref.shape[0] // block)
        def _(index):
            at = pl.ds(pl.multiple_of(index * block, block), block)
            resid = resid_ref[at, :]
            out_ref[at, :] = (resid + (out_acc[at, :] + vec_ref[7:8, :])).astype(BF16)
            hat, inverse = normalize(resid)
            grad_two = grad_acc[at, :]
            gresid = cot_ref[at, :].astype(F32) + norm_back(grad_two, vec_ref[5:6, :], hat, inverse)
            gresid_ref[at, :] = gresid
            gattn = gresid.astype(BF16)
            gattn_ref[at, :] = gattn
            dsum_ref[0:1, :] += column_sum(gattn.astype(F32))
            dsum_ref[1:2, :] += column_sum(grad_two * hat)
            dsum_ref[2:3, :] += column_sum(grad_two)

        side = send_ref.shape[3]
        grad_out = dot_tn(mixed_ref[...], gattn_ref[...])
        first = (me & 1) == 0
        low, high = grad_out[:, :side], grad_out[:, side:]
        put_in(send_ref, half_steps, jnp.where(first, high, low))
        put_in(keep_ref, half_steps, jnp.where(first, low, high))


def attention_backward(lengths_ref, q_ref, k_ref, v_ref, lse_ref, gattn_ref, wo_ref,
                       dq_ref, dk_ref, dv_ref, dsum_ref, gmix_ref):
    tile = pl.program_id(0)
    rows = q_ref.shape[0]
    gmix_ref[...] = dot_nt(gattn_ref[...], down_block(wo_ref)).astype(BF16)
    bias = mask_bias(lengths_ref, tile, lengths_ref.shape[1], rows)
    for pair in range(PAIRS):
        cols = pl.ds(pair * LANES, LANES)
        qp, kp, vp, gp = q_ref[:, cols], k_ref[:, cols], v_ref[:, cols], gmix_ref[:, cols]
        dq = dk = dv = None
        for side in range(2):
            head = 2 * pair + side
            qh, kh, gh = half_of(qp, side), half_of(kp, side), half_of(gp, side)
            probs = jnp.exp(dot_nt(qh, kp) + bias - lse_ref[:, head : head + 1])
            grad_probs = dot_nt(gh, vp)
            dot = jnp.sum(probs * grad_probs, axis=-1, keepdims=True)
            grad_scores = (probs * (grad_probs - dot)).astype(BF16)
            one_q = dot_nn(grad_scores, kh)
            one_k = dot_tn(grad_scores, qh)
            one_v = dot_tn(probs.astype(BF16), gh)
            dq = one_q if dq is None else dq + one_q
            dk = one_k if dk is None else dk + one_k
            dv = one_v if dv is None else dv + one_v
        dq_ref[:, cols] = (dq * SCALE).astype(BF16)
        dk_ref[:, cols] = dk.astype(BF16)
        dv_ref[:, cols] = dv.astype(BF16)

    @pl.when(tile == 0)
    def _():
        dsum_ref[...] = jnp.zeros_like(dsum_ref)

    dsum_ref[0:1, :] += column_sum(dq_ref[...].astype(F32))
    dsum_ref[1:2, :] += column_sum(dv_ref[...].astype(F32))


def weight_grads(me_ref, n1_ref, dq_ref, dk_ref, dv_ref, sum_one_ref, sum_qv_ref, sum_two_ref, sum_down_ref,
                 sum_up_ref, send_ref, keep_ref):
    step = pl.program_id(0)
    me = me_ref[0]
    n1 = n1_ref[...]
    results = [dot_tn(n1, ref[...]) for ref in (dq_ref, dk_ref, dv_ref)]
    each = n1.shape[1] // CHIPS
    side = send_ref.shape[3]
    vecs = jnp.concatenate((sum_one_ref[0:2], sum_qv_ref[0:2], sum_two_ref[0:3], sum_down_ref[0:1]), axis=0)

    def put_in(ref):
        for number, result in enumerate(results):
            def put(plane, layer, rows):
                ref[plane, layer, number * each : (number + 1) * each, :] = rows

            spread(me, result, put)
        for chip in range(CHIPS):
            half = chip // (CHIPS // 2)
            block = chip * (sum_up_ref.shape[1] // side) // CHIPS
            last = jnp.broadcast_to(sum_up_ref[:, block * side : (block + 1) * side], (8, side))
            rows = jnp.concatenate((vecs[:, half * side : (half + 1) * side], last), axis=0)
            ref[(chip & 3) ^ ((me >> 1) & 3), (chip >> 2) ^ (me >> 3), 3 * each :, :] = rows.astype(BF16)

    @pl.when(step == 0)
    def _():
        put_in(send_ref)

    @pl.when(step == 1)
    def _():
        put_in(keep_ref)


def tokens_backward(x_ref, gresid_ref, vec_ref, dq_ref, dk_ref, dv_ref, wq_ref, wk_ref, wv_ref, gtok_ref, dsum_ref):
    grad_one = dot_nt(dq_ref[...], wq_ref[...]) + dot_nt(dk_ref[...], wk_ref[...]) + dot_nt(dv_ref[...], wv_ref[...])
    hat, inverse = normalize(x_ref[...].astype(F32))
    gtok_ref[...] = (gresid_ref[...] + norm_back(grad_one, vec_ref[0:1, :], hat, inverse)).astype(BF16)

    @pl.when(pl.program_id(0) == 0)
    def _():
        dsum_ref[...] = jnp.zeros_like(dsum_ref)

    dsum_ref[0:1, :] += column_sum(grad_one * hat)
    dsum_ref[1:2, :] += column_sum(grad_one)


def rows_spec(block, width):
    return pl.BlockSpec((block, width), lambda i, *me: (i, 0))


def cols_spec(height, block):
    return pl.BlockSpec((height, block), lambda i, *me: (0, i))


def whole_spec(shape):
    return pl.BlockSpec(shape, lambda *i: (0,) * len(shape), pipeline_mode=pl.Buffered(1))


def kept_spec(shape):
    return pl.BlockSpec(shape, lambda *i: (0,) * len(shape))


SMEM = pl.BlockSpec(memory_space=pltpu.SMEM)


def call(kernel, grid, ins, outs, scratch, name, flops, *args):
    out_specs = tuple(spec for spec, _ in outs)
    out_shape = tuple(shape for _, shape in outs)
    return pl.pallas_call(
        kernel,
        grid=grid,
        in_specs=ins,
        out_specs=out_specs,
        out_shape=out_shape,
        scratch_shapes=scratch,
        compiler_params=pltpu.CompilerParams(vmem_limit_bytes=VMEM, dimension_semantics=("arbitrary",) * len(grid)),
        name=name,
    )(*args)


def call_with(me, kernel, steps, ins, outs, scratch, name, flops, *args):
    out_shape = tuple(shape for _, shape in outs)
    return pl.pallas_call(
        kernel,
        grid_spec=pltpu.PrefetchScalarGridSpec(
            num_scalar_prefetch=1, grid=(steps,), in_specs=ins, out_specs=tuple(spec for spec, _ in outs),
            scratch_shapes=scratch),
        out_shape=out_shape,
        compiler_params=pltpu.CompilerParams(vmem_limit_bytes=VMEM, dimension_semantics=("arbitrary",)),
        name=name,
    )(me, *args)


def shaped(*shape, dtype=BF16):
    return jax.ShapeDtypeStruct(shape, dtype)


def flipped(count, change):
    pairs = []
    for source in range(count):
        core, chip = source & 1, source >> 1
        core, chip = change(core, chip)
        pairs.append((source, 2 * chip + core))
    return pairs


def swap(array, change):
    return lax.ppermute(array, "dp", flipped(lax.axis_size("dp"), change))


def other_core(core, chip):
    return core ^ 1, chip


def other_plane(distance):
    return lambda core, chip: (core, chip ^ distance)


def other_layer(distance):
    return lambda core, chip: (core, chip ^ (4 * distance))


def split_shards(core_ref, q_ref, k_ref, v_ref, o_ref, u_ref, d_ref, keep_ref, send_ref):
    own, width = q_ref.shape
    side = width // 2
    first = core_ref[0] == 0

    def put(index, low, high):
        keep_ref[index] = jnp.where(first, low, high).astype(BF16)
        send_ref[index] = jnp.where(first, high, low).astype(BF16)

    for index, ref in enumerate((q_ref, k_ref, v_ref, o_ref)):
        rows = ref[...].astype(F32)
        put(index, rows[:, :side], rows[:, side:])
    up = u_ref[...].astype(F32)
    folds = up.shape[1] // width
    for part in range(folds):
        low = part * side
        high = (folds + part) * side
        put(4 + part, up[:, low : low + side], up[:, high : high + side])
    down = d_ref[...].astype(F32)
    for part in range(folds):
        rows = down[part * own : (part + 1) * own]
        put(4 + folds + part, rows[:, :side], rows[:, side:])


def join_shards(me_ref, keep_ref, take_ref, *refs):
    vectors, (near_ref, far_ref) = refs[:-2], refs[-2:]
    me = me_ref[0]
    first = (me & 1) == 0
    parts, own, side = keep_ref.shape
    folds = (parts - 4) // 2
    keep = keep_ref[...].astype(F32)
    take = take_ref[...].astype(F32)

    def joined(index):
        low = jnp.where(first, keep[index], take[index])
        high = jnp.where(first, take[index], keep[index])
        return jnp.concatenate((low, high), axis=0).astype(BF16)

    for index in range(3):
        near_ref[2 * own * index : 2 * own * (index + 1), :] = joined(index)
    for index in range(folds):
        far_ref[2 * own * index : 2 * own * (index + 1), :] = joined(4 + index)
    base = 2 * folds * own
    near = keep[4 + folds :].reshape(folds * own, side)
    other = take[4 + folds :].reshape(folds * own, side)
    far_ref[base : base + folds * own, :] = jnp.where(first, near, other).astype(BF16)
    far_ref[base + folds * own : 2 * base, :] = jnp.where(first, other, near).astype(BF16)
    far_ref[2 * base :, :] = joined(3)
    rows = []
    for ref in vectors:
        flat = ref[...].astype(F32).reshape(1, -1)
        rows.append(jnp.concatenate((flat, jnp.zeros((1, side - flat.shape[1]), F32)), axis=1))
    rows.append(jnp.zeros((16 - len(rows), side), F32))
    rows = jnp.concatenate(rows, axis=0)
    short = pltpu.roll(rows, own * lax.rem(me, side // own), 1)
    long = pltpu.roll(rows, folds * own * lax.rem(me, side // (folds * own)), 1)
    index = lax.broadcasted_iota(jnp.int32, rows.shape, 0)
    near_ref[6 * own :, :] = jnp.where(index < 8, short, long).astype(BF16)


def across_layers(shard):
    return jnp.stack([shard] + [swap(shard, other_layer(distance)) for distance in (1, 2, 3)])


def after(arrays, *others):
    return lax.optimization_barrier((arrays, others))[0]


def small_call(kernel, args, outs, name, scratch=(), ins=None):
    return pl.pallas_call(
        kernel,
        in_specs=ins,
        out_specs=tuple(spec for spec, _ in outs),
        out_shape=tuple(shape for _, shape in outs),
        scratch_shapes=list(scratch),
        compiler_params=pltpu.CompilerParams(vmem_limit_bytes=VMEM),
        name=name,
    )(*args)


VMEM_SPEC = pl.BlockSpec(memory_space=pltpu.VMEM)
ANY_SPEC = pl.BlockSpec(memory_space=pl.ANY)


def gather_by_hand(me, weights, vectors):
    count = lax.axis_size("dp")
    own, width = weights[0].shape
    side = width // 2
    folds = weights[5].shape[0] // own
    halves = (VMEM_SPEC, shaped(4 + 2 * folds, own, side))
    keep, send = small_call(split_shards, (me & 1, *weights), [halves, halves], "split_shards", ins=[SMEM] + [VMEM_SPEC] * 6)
    take = swap(send, other_core)
    near, far = small_call(
        join_shards, (me, keep, take, *vectors),
        [(VMEM_SPEC, shaped(6 * own + 16, side)), (VMEM_SPEC, shaped((4 * folds + 2) * own, side))], "join_shards",
        ins=[SMEM] + [VMEM_SPEC] * (2 + len(vectors)))
    far = lax.all_gather(far, "dp", axis=0, tiled=True).reshape(count // 2, 2, (4 * folds + 2) * own, side)
    near = across_layers(near)
    near = [near] + [swap(near, other_plane(distance)) for distance in (1, 2, 3)]
    return near + [swap(piece, other_core) for piece in near], far


def gather_plain(weights, vectors):
    squares, up_weight, down_weight = weights[:4], weights[4], weights[5]
    count = lax.axis_size("dp")
    own, width = squares[0].shape
    folds = down_weight.shape[0] // own
    hidden = up_weight.shape[1]
    side = width // 2
    flat = jnp.concatenate(vectors)
    packed = jnp.concatenate(
        (
            *squares,
            up_weight.reshape(own, folds, width).transpose(1, 0, 2).reshape(own * folds, width),
            down_weight,
            jnp.pad(flat.reshape(1, -1), ((0, 7), (0, width - flat.size))),
        ),
        axis=0,
    )
    whole = lax.all_gather(packed, "dp", axis=0, tiled=True).reshape(count, -1, width)
    square_all = [whole[:, index * own : (index + 1) * own, :].reshape(width, width) for index in range(4)]
    wup = whole[:, 4 * own : (4 + folds) * own, :].reshape(count, folds, own, width).transpose(0, 2, 1, 3)
    wup = wup.reshape(CHIPS, width // CHIPS, 2, folds, side).transpose(0, 2, 3, 1, 4).reshape(CHIPS, 2, -1, side)
    wdown = whole[:, (4 + folds) * own : (4 + 2 * folds) * own, :]
    wdown = wdown.reshape(CHIPS, hidden // CHIPS, 2, side).transpose(0, 2, 1, 3)
    last = whole[:, (4 + 2 * folds) * own, : flat.size].astype(F32)
    vec = last[:, : 8 * own].reshape(count, 8, own).transpose(1, 0, 2).reshape(8, width)
    bup = last[:, 8 * own :].reshape(1, hidden)
    wo = square_all[3].reshape(CHIPS, width // CHIPS, 2, side).transpose(0, 2, 1, 3)
    return (*square_all[:3], jnp.concatenate((wup, wdown, wo), axis=2), jnp.pad(vec, ((0, 8), (0, 0))), bup)


def merge_planes(keep_ref, take_ref, own_ref, *send_refs):
    for plane in range(4):
        whole = keep_ref[plane].astype(F32) + take_ref[plane].astype(F32)
        if plane == 0:
            own_ref[...] = whole
        else:
            send_refs[plane - 1][...] = whole.astype(BF16)


def merge_layers(own_ref, a_ref, b_ref, c_ref, rest_ref, *send_refs):
    for layer in range(4):
        whole = own_ref[layer] + a_ref[layer].astype(F32) + b_ref[layer].astype(F32) + c_ref[layer].astype(F32)
        if layer == 0:
            rest_ref[...] = whole
        else:
            send_refs[layer - 1][...] = whole.astype(BF16)


def merge_last(parts, core_ref, rest_ref, a_ref, b_ref, c_ref, keep_ref, send_ref, *flat_refs):
    whole = rest_ref[...] + a_ref[...].astype(F32) + b_ref[...].astype(F32) + c_ref[...].astype(F32)
    first = core_ref[0] == 0
    base = 0
    at = 0
    for size in parts:
        low = whole[base : base + size]
        high = whole[base + size : base + 2 * size]
        keep_ref[at : at + size, :] = jnp.where(first, low, high)
        send_ref[at : at + size, :] = jnp.where(first, high, low)
        base += 2 * size
        at += size
    if flat_refs:
        flat_refs[0][...] = whole[base:]


def finish_hidden(core_ref, keep_ref, take_ref, down_ref, up_ref, out_ref):
    first = core_ref[0] == 0
    keep, take = keep_ref[...], take_ref[...]
    left, right = jnp.where(first, keep, take), jnp.where(first, take, keep)
    side = keep.shape[1]
    deep = down_ref.shape[0]
    down_ref[:, :side] = left[:deep]
    down_ref[:, side:] = right[:deep]
    own, hidden = up_ref.shape
    folds = hidden // (2 * side)
    for fold in range(folds):
        rows = slice(deep + fold * own, deep + (fold + 1) * own)
        up_ref[:, fold * side : (fold + 1) * side] = left[rows]
        up_ref[:, (folds + fold) * side : (folds + fold + 1) * side] = right[rows]
    rows = slice(deep + folds * own, deep + (folds + 1) * own)
    out_ref[:, :side] = left[rows]
    out_ref[:, side:] = right[rows]


def finish_square(me_ref, keep_ref, take_ref, flat_ref, *refs):
    me = me_ref[0]
    first = (me & 1) == 0
    keep, take = keep_ref[...], take_ref[...]
    left, right = jnp.where(first, keep, take), jnp.where(first, take, keep)
    side = keep.shape[1]
    own = refs[0].shape[0]
    for number, ref in enumerate(refs[:3]):
        ref[:, :side] = left[number * own : (number + 1) * own]
        ref[:, side:] = right[number * own : (number + 1) * own]
    flat = flat_ref[...]
    long = refs[-1].shape[0]
    short_turn = lax.rem(side - own * lax.rem(me, side // own), side)
    long_turn = lax.rem(side - long * lax.rem(me, side // long), side)
    short = pltpu.roll(flat, short_turn, 1)
    for number, ref in enumerate(refs[3:-1]):
        ref[...] = short[number, :own]
    refs[-1][...] = pltpu.roll(flat, long_turn, 1)[8, :long]


def scatter_core(send):
    return swap(send, other_core)


def scatter_planes(keep, take):
    planes, layers, rows, side = keep.shape
    block = pl.BlockSpec((planes, 1, rows, side), lambda i: (0, i, 0, 0))
    out = pl.BlockSpec((1, rows, side), lambda i: (i, 0, 0))
    own, *sends = call(
        merge_planes, (layers,), [block, block],
        [(out, shaped(layers, rows, side, dtype=F32))] + [(out, shaped(layers, rows, side))] * 3, [], "merge_planes", 0,
        keep, take)
    return [own] + [swap(piece, other_plane(r + 1)) for r, piece in enumerate(sends)]


def scatter_layers(pieces):
    rows, side = pieces[0].shape[1:]
    rest, *sends = small_call(
        merge_layers, pieces, [(VMEM_SPEC, shaped(rows, side, dtype=F32))] + [(VMEM_SPEC, shaped(rows, side))] * 3,
        "merge_layers", ins=[VMEM_SPEC] * 4)
    return [rest] + [swap(piece, other_layer(r + 1)) for r, piece in enumerate(sends)]


def scatter_last(core, pieces, parts):
    rows, side = pieces[0].shape
    half = sum(parts)
    outs = [(VMEM_SPEC, shaped(half, side, dtype=F32))] * 2
    if rows > 2 * half:
        outs.append((VMEM_SPEC, shaped(rows - 2 * half, side, dtype=F32)))
    return small_call(
        functools.partial(merge_last, parts), (core, *pieces), outs, "merge_last", ins=[SMEM] + [VMEM_SPEC] * 4)


def reduce_plain(down_pair, up_pair, square_pair, flat):
    def whole(pair):
        return jnp.stack(pair).transpose(2, 1, 3, 0, 4)

    def squares(rows, parts, each):
        side = rows.shape[-1]
        return rows.reshape(CHIPS, parts, each, 2 * side).transpose(1, 0, 2, 3).reshape(parts, CHIPS * each, 2 * side)

    def scattered(array, axis):
        return lax.psum_scatter(array, "dp", scatter_dimension=axis, tiled=True).astype(F32)

    down, up, square = whole(down_pair), whole(up_pair), whole(square_pair)
    layers, planes, deep, _, side = down.shape
    each = up.shape[2] - deep
    folds = deep // each
    out = squares(up[:, :, deep:], 1, each)
    up = up[:, :, :deep].reshape(CHIPS, folds, each, 2, side).transpose(0, 2, 3, 1, 4)
    square = squares(square[:, :, : 3 * each], 3, each)
    return (
        scattered(down.reshape(CHIPS * deep, 2 * side), 0),
        scattered(up.reshape(CHIPS * each, 2 * folds * side), 0),
        *scattered(jnp.concatenate((square, out), axis=0), 1),
        lax.psum_scatter(flat, "dp", scatter_dimension=0, tiled=True).reshape(-1),
    )


def body(tokens, lengths, attn_gain, attn_shift, query_weight, query_bias, key_weight, value_weight, value_bias,
         out_weight, out_bias, mlp_gain, mlp_shift, up_weight, up_bias, down_weight, down_bias, grad_out):
    count = lax.axis_size("dp")
    rows, width = tokens.shape
    tiles = lengths.shape[0]
    tile = rows // tiles
    hidden = up_bias.shape[0] * count
    own = width // count
    folds = hidden // width
    vectors = (attn_gain, attn_shift, query_bias, value_bias, out_bias, mlp_gain, mlp_shift, down_bias, up_bias)
    by_hand = count == 2 * CHIPS
    me = lax.axis_index("dp").astype(jnp.int32).reshape(1) if by_hand else jnp.zeros((1,), jnp.int32)
    core = me & 1
    weights = (query_weight, key_weight, value_weight, out_weight, up_weight, down_weight)

    tile_rows = rows_spec(tile, width)
    square = whole_spec((width, width))
    vec_spec = whole_spec((16, width))
    sums = (kept_spec((8, width)), shaped(8, width, dtype=F32))
    low_rows = (tile_rows, shaped(rows, width))
    lse_spec = rows_spec(tile, LANES)
    mac = 2 * rows * width * width
    kept_square = (kept_spec((width, width)), shaped(width, width))
    side = width // 2
    if by_hand:
        near, far = gather_by_hand(me, weights, vectors)
        n1, q, k, v, wq, wk, wv, vec, bup = call_with(
            me, project, tiles, [rows_spec(tile, width)] + [ANY_SPEC] * 8,
            [low_rows] * 4 + [kept_square] * 3
            + [(kept_spec((16, width)), shaped(16, width, dtype=F32)), (kept_spec((1, hidden)), shaped(1, hidden, dtype=F32))],
            [pltpu.VMEM((count, 16, side), BF16), pltpu.SemaphoreType.DMA((4,))], "project", 3 * mac, tokens, *near)
    else:
        wq, wk, wv, far, vec, bup = gather_plain(weights, vectors)
        n1, q, k, v = call(
            project_rows, (tiles,), [tile_rows, vec_spec, square, square, square], [low_rows] * 4,
            [], "project", 3 * mac, tokens, vec, wq, wk, wv)
    mixed, lse, cot, sum_down = call(
        attention_forward, (tiles,), [SMEM, tile_rows, tile_rows, tile_rows, tile_rows],
        [low_rows, (lse_spec, shaped(rows, LANES, dtype=F32)), low_rows, sums],
        [], "attention_forward", mac, lengths, grad_out, q, k, v)

    steps = hidden // side
    each = width // CHIPS
    deep = hidden // CHIPS
    full_rows = whole_spec((rows, width))
    kept_low = (kept_spec((rows, width)), shaped(rows, width))
    kept_high = (kept_spec((rows, width)), shaped(rows, width, dtype=F32))

    def pair_of(count):
        return (kept_spec((4, CHIPS // 4, count, side)), shaped(4, CHIPS // 4, count, side))

    def up_spec(at):
        return pl.BlockSpec(
            (CHIPS, 1, each, side), lambda i, me: (0, at(i, me) // folds, lax.rem(at(i, me), folds), 0))

    def down_spec(at):
        return pl.BlockSpec((side // deep, 2, deep, side), lambda i, me: (at(i, me), 0, 1, 0))

    out_spec = pl.BlockSpec((CHIPS, 2, each, side), lambda *i: (0, 0, 2 * folds, 0), pipeline_mode=pl.Buffered(1))

    def hidden_spec(height, at):
        return pl.BlockSpec((height, side), lambda i, me: (0, at(i, me)))

    def in_turn(i, me):
        return i

    def send_first(i, me):
        return ((i // folds) ^ 1 ^ (me[0] & 1)) * folds + lax.rem(i, folds)

    hidden_rows = (hidden_spec(rows, in_turn), shaped(rows, hidden))
    resid, n2, act, slope, down_send, down_keep = call_with(
        me, mlp_up, steps,
        [full_rows, full_rows, vec_spec, out_spec, full_rows, up_spec(in_turn), hidden_spec(1, in_turn)],
        [kept_high, kept_low, hidden_rows, hidden_rows, pair_of(deep), pair_of(deep)],
        [], "mlp_up", 2 * folds * mac, tokens, mixed, vec, far, cot, far, bup)

    out, gresid, gattn, up_send, up_keep, sum_up, sum_two = call_with(
        me, mlp_down, steps,
        [full_rows, full_rows, full_rows, vec_spec, full_rows, hidden_spec(rows, send_first),
         hidden_spec(rows, send_first), up_spec(send_first), down_spec(send_first)],
        [kept_low, kept_high, kept_low, pair_of(deep + each), pair_of(deep + each),
         (hidden_spec(1, send_first), shaped(1, hidden, dtype=F32)), sums],
        [pltpu.VMEM((rows, width), F32), pltpu.VMEM((rows, width), F32)],
        "mlp_down", 4 * folds * mac, n2, cot, resid, vec, mixed, act, slope, far, far)
    if by_hand:
        down_take = after(scatter_core(down_send), gattn)
        down_planes = scatter_planes(down_keep, down_take)
        up_take = scatter_core(up_send)
        gattn = after(gattn, down_planes[0])
    dq, dk, dv, sum_qv = call(
        attention_backward, (tiles,), [SMEM, tile_rows, tile_rows, tile_rows, lse_spec, tile_rows, out_spec],
        [low_rows] * 3 + [sums], [pltpu.VMEM((tile, width), BF16)],
        "attention_backward", 4 * mac, lengths, q, k, v, lse, gattn, far)
    if by_hand:
        up_take, down_planes = after((up_take, down_planes), dq)
        down_layers = scatter_layers(down_planes)
        up_planes = scatter_planes(up_keep, up_take)
        gresid = after(gresid, down_layers[0], up_planes[0])
    gtok, sum_one = call(
        tokens_backward, (tiles,),
        [tile_rows, tile_rows, vec_spec, tile_rows, tile_rows, tile_rows, square, square, square],
        [low_rows, sums], [], "tokens_backward", 3 * mac, tokens, gresid, vec, dq, dk, dv, wq, wk, wv)
    if by_hand:
        up_planes, down_layers = after((up_planes, down_layers), sum_one)
        up_layers = scatter_layers(up_planes)
        down_keep, down_send = scatter_last(core, down_layers, (folds * own,))
        n1 = after(n1, up_layers[0], down_keep)

    half_cols = pl.BlockSpec((rows, side), lambda i, me: (0, (me[0] & 1) ^ 1 ^ i))
    sum_spec = whole_spec((8, width))
    square_send, square_keep = call_with(
        me, weight_grads, 2, [full_rows] + [half_cols] * 3 + [sum_spec] * 4 + [whole_spec((1, hidden))],
        [pair_of(3 * each + 16)] * 2, [],
        "weight_grads", 3 * mac, n1, dq, dk, dv, sum_one, sum_qv, sum_two, sum_down, sum_up)
    if by_hand:
        square_take = scatter_core(square_send)
        up_layers = after(up_layers, square_send)
        up_keep, up_send = scatter_last(core, up_layers, (own,) * (folds + 1))
        hidden_keep = jnp.concatenate((down_keep, up_keep), axis=0)
        hidden_take = scatter_core(jnp.concatenate((down_send, up_send), axis=0))
        square_planes = scatter_planes(square_keep, square_take)
        hidden_take = after(hidden_take, square_planes[0])
        g_down, g_up, g_o = small_call(
            finish_hidden, (core, hidden_keep, hidden_take),
            [(VMEM_SPEC, shaped(folds * own, width, dtype=F32)), (VMEM_SPEC, shaped(own, hidden, dtype=F32)),
             (VMEM_SPEC, shaped(own, width, dtype=F32))], "finish_hidden", ins=[SMEM] + [VMEM_SPEC] * 2)
        square_layers = scatter_layers(square_planes)
        square_keep, square_send, flat = scatter_last(core, square_layers, (own,) * 3)
        square_take = scatter_core(square_send)
        g_q, g_k, g_v, *g_flat, g_ub = small_call(
            finish_square, (me, square_keep, square_take, flat),
            [(VMEM_SPEC, shaped(own, width, dtype=F32))] * 3 + [(VMEM_SPEC, shaped(own, dtype=F32))] * 8
            + [(VMEM_SPEC, shaped(folds * own, dtype=F32))], "finish_square", ins=[SMEM] + [VMEM_SPEC] * 3)
    else:
        flat = jnp.concatenate((sum_one[0:2], sum_qv[0:2], sum_two[0:3], sum_down[0:1]), axis=0)
        flat = flat.reshape(8, count, own).transpose(1, 0, 2).reshape(count, 8 * own)
        flat = jnp.concatenate((flat, sum_up.reshape(count, folds * own)), axis=1)
        g_down, g_up, g_q, g_k, g_v, g_o, flat = reduce_plain(
            (down_keep, down_send), (up_keep, up_send), (square_keep, square_send), flat)
        g_flat = [flat[index * own : (index + 1) * own] for index in range(8)]
        g_ub = flat[8 * own :]
    g_gain, g_shift, g_qb, g_vb, g_ob, g_mg, g_ms, g_db = g_flat
    return (out, gtok, g_gain, g_shift, g_q, g_qb, g_k, g_v, g_vb, g_o, g_ob, g_mg, g_ms, g_up, g_ub, g_down, g_db)


def solution(mesh):
    rows, flat = P("dp", None), P("dp")
    return jax.shard_map(
        body,
        mesh=mesh,
        in_specs=(rows, rows, flat, flat, rows, flat, rows, rows, flat, rows, flat, flat, flat, rows, flat, rows, flat, rows),
        out_specs=(rows, rows, flat, flat, rows, flat, rows, rows, flat, rows, flat, flat, flat, rows, flat, rows, flat),
        check_vma=False,
    )
```

time: 482 us -> 345 us (0.72)
  waiting for transfers between devices: 271 us -> 109 us
  local copies, waits for them, and re-layouts: 68.7 us -> 11.6 us
  Pallas kernels: 125 us -> 173 us
  starting transfers between devices: 0.08 us -> 34.7 us
    reduce_scatter x1 -> x0, waiting for transfers between devices: 163 us -> none  [body(): lax.psum_scatter(grads.reshape(-1, width), 'dp', scatter_dimension=0, til...]
    pallas_call x0 -> x14, Pallas kernels: none -> 113 us  [the longest x4 91.4 us: call_with(): pl.pallas_call(kernel, grid_spec=pltpu.PrefetchScalarGridSpec(num_scalar_...]
    ppermute x0 -> x34, waiting for transfers between devices: none -> 86.2 us  [swap(): return lax.ppermute(array, 'dp', flipped(lax.axis_size('dp'), change))]
    all_gather x1, waiting for transfers between devices: 108 us -> 22.4 us  [gather_by_hand(): lax.all_gather(far, 'dp', axis=0, tiled=True)]
    pallas_call x6, Pallas kernels: 125 us -> 59.6 us  [call(): pl.pallas_call(kernel, grid=grid, in_specs=ins, out_specs=out_specs, out_...]
    ppermute x0 -> x34, starting transfers between devices: none -> 34.6 us  [swap(): return lax.ppermute(array, 'dp', flipped(lax.axis_size('dp'), change))]
    slice x13 -> x0, local copies, waits for them, and re-layouts: 21 us -> none  [the longest x1 8 us: body(): whole[:, (4 + folds) * own:(4 + 2 * folds) * own, :].reshape(hidden, width)]
    reshape x10 -> x0, local copies, waits for them, and re-layouts: 20.9 us -> none  [the longest x2 13 us: body(): d_up.reshape(count, own, folds, width).transpose(0, 2, 1, 3)]
  transfers between devices with their start and end apart: 2 -> 35, of which waited for: 2 -> 16; matrix products, arithmetic and copies ran while one was open for 0% -> 1% of each run, Pallas kernels for 0% -> 35%
where the time goes in v2:
time: 345 us; the launch traced here: 344 us
  Pallas kernels  173 us (50%)
  waiting for transfers between devices  109 us (32%)
  starting transfers between devices  34.7 us (10%)
  between operations  14.4 us (4%)
  local copies, waits for them, and re-layouts  11.6 us (3%)
    pallas_call x4, Pallas kernels, call_with(): pl.pallas_call(kernel, grid_spec=pltpu.PrefetchScalarGridSpec(num_scalar_...  91.4 us
    ppermute x34, waiting for transfers between devices, swap(): return lax.ppermute(array, 'dp', flipped(lax.axis_size('dp'), change))  86.2 us
    pallas_call x6, Pallas kernels, call(): pl.pallas_call(kernel, grid=grid, in_specs=ins, out_specs=out_specs, out_...  59.6 us
    ppermute x34, starting transfers between devices, swap(): return lax.ppermute(array, 'dp', flipped(lax.axis_size('dp'), change))  34.6 us
    all_gather x1, waiting for transfers between devices, gather_by_hand(): lax.all_gather(far, 'dp', axis=0, tiled=True)  22.4 us
    pallas_call x10, Pallas kernels, small_call(): pl.pallas_call(kernel, in_specs=ins, out_specs=tuple((spec for spec, _ in...  21.6 us
    unnamed x76, local copies, waits for them, and re-layouts  11.6 us
  transfers between devices with their start and end apart: 35, of which 16 were waited for; matrix products, arithmetic and copies ran while one was open for 1% of the time, Pallas kernels for 35%

profile of v2, /device:TPU:0, one launch (start us, length us, event | category | flops | bytes accessed | tf_op | source)
XLA Modules:
  0.0 344.4 jit_solution(3275142898678901839)
XLA Ops:
  11.6 2.0 join_shards.1
  13.6 5.0 %collective-permute-start.3 = (bf16[160,384]{1,0:T(8,128)(2,1)}, bf16[160,384]{1,0:T(8,128)(2,1)S(1)}, u32[]{:S(2)}, u32[]{:S(2)}) collective-permute-start(bf16[160,384]{1,0:T(8,128)(2,1)} %get-tuple-element.125), channel_id=1, source_target_pairs={{0,24},{1,25},{2,26},{3,27},{4,28},{5,29},{6,30},{7,31},{8,16},{9,... | collective-permute-start | bytes 368648 | tf_op jit(solution)/shard_map/ppermute | solution.py:422
  19.3 3.8 %collective-permute-done.3 = bf16[160,384]{1,0:T(8,128)(2,1)S(1)} collective-permute-done((bf16[160,384]{1,0:T(8,128)(2,1)}, bf16[160,384]{1,0:T(8,128)(2,1)S(1)}, u32[]{:S(2)}, u32[]{:S(2)}) %collective-permute-start.3) | collective-permute-done | bytes 122912 | tf_op jit(solution)/shard_map/ppermute | solution.py:422
  23.1 8.9 %collective-permute-done.2 = bf16[160,384]{1,0:T(8,128)(2,1)S(1)} collective-permute-done((bf16[160,384]{1,0:T(8,128)(2,1)}, bf16[160,384]{1,0:T(8,128)(2,1)S(1)}, u32[]{:S(2)}, u32[]{:S(2)}) %collective-permute-start.2) | collective-permute-done | bytes 122912 | tf_op jit(solution)/shard_map/ppermute | solution.py:422
  33.0 2.5 collective-permute-start.6
  36.5 13.6 %collective-permute-done.6.refs_3_ = bf16[4,160,384]{2,1,0:T(8,128)(2,1)S(1)} collective-permute-done((bf16[4,160,384]{2,1,0:T(8,128)(2,1)S(1)}, bf16[4,160,384]{2,1,0:T(8,128)(2,1)S(1)}, u32[]{:S(2)}, u32[]{:S(2)}) %collective-permute-start.6) | collective-permute-done | bytes 491552 | tf_op jit(solution)/shard_map/ppermute | solution.py:422
  50.1 9.1 %collective-permute-done.5.refs_2_ = bf16[4,160,384]{2,1,0:T(8,128)(2,1)S(1)} collective-permute-done((bf16[4,160,384]{2,1,0:T(8,128)(2,1)S(1)}, bf16[4,160,384]{2,1,0:T(8,128)(2,1)S(1)}, u32[]{:S(2)}, u32[]{:S(2)}) %collective-permute-start.5) | collective-permute-done | bytes 491552 | tf_op jit(solution)/shard_map/ppermute | solution.py:422
  59.4 4.7 %collective-permute-done.4.refs_1_ = bf16[4,160,384]{2,1,0:T(8,128)(2,1)S(1)} collective-permute-done((bf16[4,160,384]{2,1,0:T(8,128)(2,1)S(1)}, bf16[4,160,384]{2,1,0:T(8,128)(2,1)S(1)}, u32[]{:S(2)}, u32[]{:S(2)}) %collective-permute-start.4) | collective-permute-done | bytes 491552 | tf_op jit(solution)/shard_map/ppermute | solution.py:422
  66.8 10.1 %project.1 = (bf16[1024,768]{1,0:T(8,128)(2,1)}, bf16[1024,768]{1,0:T(8,128)(2,1)}, bf16[1024,768]{1,0:T(8,128)(2,1)}, bf16[1024,768]{1,0:T(8,128)(2,1)}, bf16[7...) custom-call(s32[1]{0:T(128)} %bitcast.me_ref, ...), custom_call_target="tpu_custom_call" | custom-call | tf_op jit(solution)/shard_map/project/pallas_call | solution.py:397
  76.9 13.5 %attention_forward.1 = (bf16[1024,768]{1,0:T(8,128)(2,1)}, f32[1024,128]{1,0:T(8,128)}, bf16[1024,768]{1,0:T(8,128)(2,1)}, f32[8,768]{1,0:T(8,128)}) custom-call(s32[4,5]{1,0:T(4,128)} %lengths_ref.3, bf16[1024,768]{1,0:T(8,128)(2,1)} %grad_ref.1, bf16[1024,768]{1,0:T(8,128)(2,1)} %get-tuple-element.126.q_ref, bf16[1024,768]{1,0:T(8,128)(2,1)} %get-tuple-element.127.k_ref, ...), custom_call_target="tpu_custom_call" | custom-call | tf_op jit(solution)/shard_map/attention_forward/pallas_call | solution.py:383
  90.3 22.4 %all-gather.2.cloned.1.call-done = bf16[13824,384]{1,0:T(8,128)(2,1)} async-done(((bf16[432,384]{1,0:T(8,128)(2,1)}), bf16[13824,384]{1,0:T(8,128)(2,1)}) %all-gather.2.cloned.1.call-update) | async-done | bytes 10616848 | tf_op jit(solution)/shard_map/all_gather | solution.py:533
  112.7 27.2 %mlp_up.1 = (f32[1024,768]{1,0:T(8,128)}, bf16[1024,768]{1,0:T(8,128)(2,1)}, bf16[1024,3072]{1,0:T(8,128)(2,1)}, bf16[1024,3072]{1,0:T(8,128)(2,1)}, bf16[4,4,19...) custom-call(s32[1]{0:T(128)} %bitcast.me_ref, bf16[1024,768]{1,0:T(8,128)(2,1)} %x_ref.5, ...), custom_call_target="tpu_custom_call" | custom-call | tf_op jit(solution)/shard_map/mlp_up/pallas_call | solution.py:397
  140.2 44.0 %mlp_down.1 = (bf16[1024,768]{1,0:T(8,128)(2,1)}, f32[1024,768]{1,0:T(8,128)}, bf16[1024,768]{1,0:T(8,128)(2,1)}, bf16[4,4,240,384]{3,2,1,0:T(8,128)(2,1)}, bf16...) custom-call(s32[1]{0:T(128)} %bitcast.me_ref, bf16[1024,768]{1,0:T(8,128)(2,1)} %get-tuple-element.134.n2_ref, ...), custom_call_target="tpu_custom_call" | custom-call | tf_op jit(solution)/shard_map/mlp_down/pallas_call | solution.py:397
  186.1 4.5 %merge_planes.3 = (f32[4,192,384]{2,1,0:T(8,128)}, bf16[4,192,384]{2,1,0:T(8,128)(2,1)}, bf16[4,192,384]{2,1,0:T(8,128)(2,1)}, bf16[4,192,384]{2,1,0:T(8,128)(2,1)}) custom-call(bf16[4,4,192,384]{3,2,1,0:T(8,128)(2,1)} %get-tuple-element.141.keep_ref, bf16[4,4,192,384]{3,2,1,0:T(8,128)(2,1)} %copy-done.1), custom_call_target="tpu_custom_call" | custom-call | tf_op jit(solution)/shard_map/merge_planes/pallas_call | solution.py:383
  194.0 22.4 %attention_backward.1 = (bf16[1024,768]{1,0:T(8,128)(2,1)}, bf16[1024,768]{1,0:T(8,128)(2,1)}, bf16[1024,768]{1,0:T(8,128)(2,1)}, f32[8,768]{1,0:T(8,128)}) custom-call(s32[4,5]{1,0:T(4,128)} %lengths_ref.3, bf16[1024,768]{1,0:T(8,128)(2,1)} %get-tuple-element.126.q_ref, bf16[1024,768]{1,0:T(8,128)(2,1)} %get-tuple-element.127.k_ref, ...), custom_call_target="tpu_custom_call" | custom-call | tf_op jit(solution)/shard_map/attention_backward/pallas_call | solution.py:383
  216.5 3.6 %collective-permute-done.14.b_ref = bf16[4,192,384]{2,1,0:T(8,128)(2,1)S(1)} collective-permute-done((bf16[4,192,384]{2,1,0:T(8,128)(2,1)}, bf16[4,192,384]{2,1,0:T(8,128)(2,1)S(1)}, u32[]{:S(2)}, u32[]{:S(2)}) %collective-permute-start.14) | collective-permute-done | bytes 589856 | tf_op jit(solution)/shard_map/ppermute | solution.py:422
  221.8 5.0 %merge_planes.4 = (f32[4,240,384]{2,1,0:T(8,128)}, bf16[4,240,384]{2,1,0:T(8,128)(2,1)}, bf16[4,240,384]{2,1,0:T(8,128)(2,1)}, bf16[4,240,384]{2,1,0:T(8,128)(2,1)}) custom-call(bf16[4,4,240,384]{3,2,1,0:T(8,128)(2,1)} %get-tuple-element.157.keep_ref, bf16[4,4,240,384]{3,2,1,0:T(8,128)(2,1)} %copy-done), custom_call_target="tpu_custom_call" | custom-call | tf_op jit(solution)/shard_map/merge_planes/pallas_call | solution.py:383
  230.3 2.7 merge_layers.3
  235.3 3.9 %collective-permute-done.19.a_ref = bf16[192,384]{1,0:T(8,128)(2,1)S(1)} collective-permute-done((bf16[192,384]{1,0:T(8,128)(2,1)}, bf16[192,384]{1,0:T(8,128)(2,1)S(1)}, u32[]{:S(2)}, u32[]{:S(2)}) %collective-permute-start.19) | collective-permute-done | bytes 147488 | tf_op jit(solution)/shard_map/ppermute | solution.py:422
  241.0 10.0 %tokens_backward.1 = (bf16[1024,768]{1,0:T(8,128)(2,1)}, f32[8,768]{1,0:T(8,128)}) custom-call(bf16[1024,768]{1,0:T(8,128)(2,1)} %x_ref.5, f32[1024,768]{1,0:T(8,128)} %get-tuple-element.160.gresid_ref, f32[16,768]{1,0:T(8,128)} %get-tuple-element.130.vec_ref, bf16[1024,768]{1,0:T(8,128)(2,1)} %get-tuple-element.151.dq_ref, ...), custom_call_target="tpu_custom_call" | custom-call | tf_op jit(solution)/shard_map/tokens_backward/pallas_call | solution.py:383
  251.0 9.6 %collective-permute-done.17.b_ref = bf16[4,240,384]{2,1,0:T(8,128)(2,1)S(1)} collective-permute-done((bf16[4,240,384]{2,1,0:T(8,128)(2,1)}, bf16[4,240,384]{2,1,0:T(8,128)(2,1)S(1)}, u32[]{:S(2)}, u32[]{:S(2)}) %collective-permute-start.17) | collective-permute-done | bytes 737312 | tf_op jit(solution)/shard_map/ppermute | solution.py:422
  261.8 3.0 merge_layers.4
  264.8 1.9 merge_last.3
  266.7 10.1 %weight_grads.1 = (bf16[4,4,160,384]{3,2,1,0:T(8,128)(2,1)}, bf16[4,4,160,384]{3,2,1,0:T(8,128)(2,1)}) custom-call(s32[1]{0:T(128)} %bitcast.me_ref, bf16[1024,768]{1,0:T(8,128)(2,1)} %get-tuple-element.185.n1_ref, bf16[1024,768]{1,0:T(8,128)(2,1)} %get-tuple-element.151.dq_ref, bf16[1024,768]{1,0:T(8,128)(2,1)} %get-tuple-element.161.dk_ref, ...), custom_call_target="tpu_custom_call" | custom-call | tf_op jit(solution)/shard_map/weight_grads/pallas_call | solution.py:397
  278.2 2.8 collective-permute-done.22.take_ref
  282.3 4.3 %merge_planes.5 = (f32[4,160,384]{2,1,0:T(8,128)}, bf16[4,160,384]{2,1,0:T(8,128)(2,1)}, bf16[4,160,384]{2,1,0:T(8,128)(2,1)}, bf16[4,160,384]{2,1,0:T(8,128)(2,1)}) custom-call(bf16[4,4,160,384]{3,2,1,0:T(8,128)(2,1)} %get-tuple-element.190.keep_ref, bf16[4,4,160,384]{3,2,1,0:T(8,128)(2,1)} %copy-done.2), custom_call_target="tpu_custom_call" | custom-call | tf_op jit(solution)/shard_map/merge_planes/pallas_call | solution.py:383
  293.9 11.8 %collective-permute-done.31.b_ref = bf16[240,384]{1,0:T(8,128)(2,1)S(1)} collective-permute-done((bf16[240,384]{1,0:T(8,128)(2,1)S(1)}, bf16[240,384]{1,0:T(8,128)(2,1)S(1)}, u32[]{:S(2)}, u32[]{:S(2)}) %collective-permute-start.31) | collective-permute-done | bytes 184352 | tf_op jit(solution)/shard_map/ppermute | solution.py:422
  307.0 2.0 merge_last.5
  312.8 2.5 merge_layers.5
  317.6 2.1 collective-permute-start.28
  319.7 2.6 collective-permute-done.26.a_ref
  322.3 7.0 %collective-permute-done.27.b_ref = bf16[160,384]{1,0:T(8,128)(2,1)S(1)} collective-permute-done((bf16[160,384]{1,0:T(8,128)(2,1)}, bf16[160,384]{1,0:T(8,128)(2,1)S(1)}, u32[]{:S(2)}, u32[]{:S(2)}) %collective-permute-start.27) | collective-permute-done | bytes 122912 | tf_op jit(solution)/shard_map/ppermute | solution.py:422
  (138 shorter events, 51.6 us)
Async XLA Ops:
  7.2 105.5 %all-gather.2.cloned.1.call-start = ((), (), s32[]{:S(2)}) async-start(), calls=%async_computation | async-start | bytes 10948608 | tf_op jit(solution)/shard_map/all_gather | solution.py:533
  13.6 9.5 %collective-permute-start.3 = (bf16[160,384]{1,0:T(8,128)(2,1)}, bf16[160,384]{1,0:T(8,128)(2,1)S(1)}, u32[]{:S(2)}, u32[]{:S(2)}) collective-permute-start(bf16[160,384]{1,0:T(8,128)(2,1)} %get-tuple-element.125), channel_id=1, source_target_pairs={{0,24},{1,25},{2,26},{3,27},{4,28},{5,29},{6,30},{7,31},{8,16},{9,... | collective-permute-start | bytes 368648 | tf_op jit(solution)/shard_map/ppermute | solution.py:422
  18.7 13.3 %collective-permute-start.2 = (bf16[160,384]{1,0:T(8,128)(2,1)}, bf16[160,384]{1,0:T(8,128)(2,1)S(1)}, u32[]{:S(2)}, u32[]{:S(2)}) collective-permute-start(bf16[160,384]{1,0:T(8,128)(2,1)} %get-tuple-element.125), channel_id=1, source_target_pairs={{0,16},{1,17},{2,18},{3,19},{4,20},{5,21},{6,22},{7,23},{8,24},{9,... | collective-permute-start | bytes 368648 | tf_op jit(solution)/shard_map/ppermute | solution.py:422
  18.7 13.3 %collective-permute-start.1 = (bf16[160,384]{1,0:T(8,128)(2,1)}, bf16[160,384]{1,0:T(8,128)(2,1)S(1)}, u32[]{:S(2)}, u32[]{:S(2)}) collective-permute-start(bf16[160,384]{1,0:T(8,128)(2,1)} %get-tuple-element.125), channel_id=1, source_target_pairs={{0,8},{1,9},{2,10},{3,11},{4,12},{5,13},{6,14},{7,15},{8,0},{9,1},... | collective-permute-start | bytes 368648 | tf_op jit(solution)/shard_map/ppermute | solution.py:422
  33.0 17.1 %collective-permute-start.6 = (bf16[4,160,384]{2,1,0:T(8,128)(2,1)S(1)}, bf16[4,160,384]{2,1,0:T(8,128)(2,1)S(1)}, u32[]{:S(2)}, u32[]{:S(2)}) collective-permute-start(bf16[4,160,384]{2,1,0:T(8,128)(2,1)S(1)} %pad_maximum_fusion.refs_0_), channel_id=1, source_target_pairs={{0,6},{1,7},{2,4},{3,5},{4,2},{5,3},{6,0},{7,1},{8,14},{9,15},{10,... | collective-permute-start | bytes 1474568 | tf_op jit(solution)/shard_map/ppermute | solution.py:422
  35.5 23.7 %collective-permute-start.5 = (bf16[4,160,384]{2,1,0:T(8,128)(2,1)S(1)}, bf16[4,160,384]{2,1,0:T(8,128)(2,1)S(1)}, u32[]{:S(2)}, u32[]{:S(2)}) collective-permute-start(bf16[4,160,384]{2,1,0:T(8,128)(2,1)S(1)} %pad_maximum_fusion.refs_0_), channel_id=1, source_target_pairs={{0,4},{1,5},{2,6},{3,7},{4,0},{5,1},{6,2},{7,3},{8,12},{9,13},{10,... | collective-permute-start | bytes 1474568 | tf_op jit(solution)/shard_map/ppermute | solution.py:422
  36.0 28.1 %collective-permute-start.4 = (bf16[4,160,384]{2,1,0:T(8,128)(2,1)S(1)}, bf16[4,160,384]{2,1,0:T(8,128)(2,1)S(1)}, u32[]{:S(2)}, u32[]{:S(2)}) collective-permute-start(bf16[4,160,384]{2,1,0:T(8,128)(2,1)S(1)} %pad_maximum_fusion.refs_0_), channel_id=1, source_target_pairs={{0,2},{1,3},{2,0},{3,1},{4,6},{5,7},{6,4},{7,5},{8,10},{9,11},{10,... | collective-permute-start | bytes 1474568 | tf_op jit(solution)/shard_map/ppermute | solution.py:422
  36.5 27.6 %collective-permute-start.7 = (bf16[4,160,384]{2,1,0:T(8,128)(2,1)S(1)}, bf16[4,160,384]{2,1,0:T(8,128)(2,1)S(1)}, u32[]{:S(2)}, u32[]{:S(2)}) collective-permute-start(bf16[4,160,384]{2,1,0:T(8,128)(2,1)S(1)} %pad_maximum_fusion.refs_0_), channel_id=1, source_target_pairs={{0,1},{1,0},{2,3},{3,2},{4,5},{5,4},{6,7},{7,6},{8,9},{9,8},{10,11... | collective-permute-start | bytes 1474568 | tf_op jit(solution)/shard_map/ppermute | solution.py:422
  50.1 14.0 %collective-permute-start.10 = (bf16[4,160,384]{2,1,0:T(8,128)(2,1)S(1)}, bf16[4,160,384]{2,1,0:T(8,128)(2,1)S(1)}, u32[]{:S(2)}, u32[]{:S(2)}) collective-permute-start(bf16[4,160,384]{2,1,0:T(8,128)(2,1)S(1)} %collective-permute-done.6.refs_3_), channel_id=1, source_target_pairs={{0,1},{1,0},{2,3},{3,2},{4,5},{5,4},{6,7},{7,6},{8,9},{9,8},{10,11... | collective-permute-start | bytes 1474568 | tf_op jit(solution)/shard_map/ppermute | solution.py:422
  59.2 4.9 %collective-permute-start.9 = (bf16[4,160,384]{2,1,0:T(8,128)(2,1)S(1)}, bf16[4,160,384]{2,1,0:T(8,128)(2,1)S(1)}, u32[]{:S(2)}, u32[]{:S(2)}) collective-permute-start(bf16[4,160,384]{2,1,0:T(8,128)(2,1)S(1)} %collective-permute-done.5.refs_2_), channel_id=1, source_target_pairs={{0,1},{1,0},{2,3},{3,2},{4,5},{5,4},{6,7},{7,6},{8,9},{9,8},{10,11... | collective-permute-start | bytes 1474568 | tf_op jit(solution)/shard_map/ppermute | solution.py:422
  139.9 44.7 %collective-permute-start.12 = (bf16[4,4,192,384]{3,2,1,0:T(8,128)(2,1)}, bf16[4,4,192,384]{3,2,1,0:T(8,128)(2,1)S(1)}, u32[]{:S(2)}, u32[]{:S(2)}) collective-permute-start(bf16[4,4,192,384]{3,2,1,0:T(8,128)(2,1)} %get-tuple-element.142), channel_id=1, source_target_pairs={{0,1},{1,0},{2,3},{3,2},{4,5},{5,4},{6,7},{7,6},{8,9},{9,8},{10,11... | collective-permute-start | bytes 7077896 | tf_op jit(solution)/shard_map/ppermute | solution.py:422
  184.2 35.8 %collective-permute-start.11 = (bf16[4,4,240,384]{3,2,1,0:T(8,128)(2,1)}, bf16[4,4,240,384]{3,2,1,0:T(8,128)(2,1)S(1)}, u32[]{:S(2)}, u32[]{:S(2)}) collective-permute-start(bf16[4,4,240,384]{3,2,1,0:T(8,128)(2,1)} %get-tuple-element.140), channel_id=1, source_target_pairs={{0,1},{1,0},{2,3},{3,2},{4,5},{5,4},{6,7},{7,6},{8,9},{9,8},{10,11... | collective-permute-start | bytes 8847368 | tf_op jit(solution)/shard_map/ppermute | solution.py:422
  190.5 25.9 %collective-permute-start.13 = (bf16[4,192,384]{2,1,0:T(8,128)(2,1)}, bf16[4,192,384]{2,1,0:T(8,128)(2,1)S(1)}, u32[]{:S(2)}, u32[]{:S(2)}) collective-permute-start(bf16[4,192,384]{2,1,0:T(8,128)(2,1)} %get-tuple-element.146), channel_id=1, source_target_pairs={{0,2},{1,3},{2,0},{3,1},{4,6},{5,7},{6,4},{7,5},{8,10},{9,11},{10,... | collective-permute-start | bytes 1769480 | tf_op jit(solution)/shard_map/ppermute | solution.py:422
  191.9 28.1 %collective-permute-start.14 = (bf16[4,192,384]{2,1,0:T(8,128)(2,1)}, bf16[4,192,384]{2,1,0:T(8,128)(2,1)S(1)}, u32[]{:S(2)}, u32[]{:S(2)}) collective-permute-start(bf16[4,192,384]{2,1,0:T(8,128)(2,1)} %get-tuple-element.147), channel_id=1, source_target_pairs={{0,4},{1,5},{2,6},{3,7},{4,0},{5,1},{6,2},{7,3},{8,12},{9,13},{10,... | collective-permute-start | bytes 1769480 | tf_op jit(solution)/shard_map/ppermute | solution.py:422
  192.6 27.5 %collective-permute-start.15 = (bf16[4,192,384]{2,1,0:T(8,128)(2,1)}, bf16[4,192,384]{2,1,0:T(8,128)(2,1)S(1)}, u32[]{:S(2)}, u32[]{:S(2)}) collective-permute-start(bf16[4,192,384]{2,1,0:T(8,128)(2,1)} %get-tuple-element.148), channel_id=1, source_target_pairs={{0,6},{1,7},{2,4},{3,5},{4,2},{5,3},{6,0},{7,1},{8,14},{9,15},{10,... | collective-permute-start | bytes 1769480 | tf_op jit(solution)/shard_map/ppermute | solution.py:422
  226.8 24.2 %collective-permute-start.16 = (bf16[4,240,384]{2,1,0:T(8,128)(2,1)}, bf16[4,240,384]{2,1,0:T(8,128)(2,1)S(1)}, u32[]{:S(2)}, u32[]{:S(2)}) collective-permute-start(bf16[4,240,384]{2,1,0:T(8,128)(2,1)} %get-tuple-element.168), channel_id=1, source_target_pairs={{0,2},{1,3},{2,0},{3,1},{4,6},{5,7},{6,4},{7,5},{8,10},{9,11},{10,... | collective-permute-start | bytes 2211848 | tf_op jit(solution)/shard_map/ppermute | solution.py:422
  227.4 33.3 %collective-permute-start.17 = (bf16[4,240,384]{2,1,0:T(8,128)(2,1)}, bf16[4,240,384]{2,1,0:T(8,128)(2,1)S(1)}, u32[]{:S(2)}, u32[]{:S(2)}) collective-permute-start(bf16[4,240,384]{2,1,0:T(8,128)(2,1)} %get-tuple-element.169), channel_id=1, source_target_pairs={{0,4},{1,5},{2,6},{3,7},{4,0},{5,1},{6,2},{7,3},{8,12},{9,13},{10,... | collective-permute-start | bytes 2211848 | tf_op jit(solution)/shard_map/ppermute | solution.py:422
  228.8 31.8 %collective-permute-start.18 = (bf16[4,240,384]{2,1,0:T(8,128)(2,1)}, bf16[4,240,384]{2,1,0:T(8,128)(2,1)S(1)}, u32[]{:S(2)}, u32[]{:S(2)}) collective-permute-start(bf16[4,240,384]{2,1,0:T(8,128)(2,1)} %get-tuple-element.170), channel_id=1, source_target_pairs={{0,6},{1,7},{2,4},{3,5},{4,2},{5,3},{6,0},{7,1},{8,14},{9,15},{10,... | collective-permute-start | bytes 2211848 | tf_op jit(solution)/shard_map/ppermute | solution.py:422
  233.0 6.2 %collective-permute-start.19 = (bf16[192,384]{1,0:T(8,128)(2,1)}, bf16[192,384]{1,0:T(8,128)(2,1)S(1)}, u32[]{:S(2)}, u32[]{:S(2)}) collective-permute-start(bf16[192,384]{1,0:T(8,128)(2,1)} %get-tuple-element.171), channel_id=1, source_target_pairs={{0,8},{1,9},{2,10},{3,11},{4,12},{5,13},{6,14},{7,15},{8,0},{9,1},... | collective-permute-start | bytes 442376 | tf_op jit(solution)/shard_map/ppermute | solution.py:422
  234.2 16.7 %collective-permute-start.20 = (bf16[192,384]{1,0:T(8,128)(2,1)}, bf16[192,384]{1,0:T(8,128)(2,1)S(1)}, u32[]{:S(2)}, u32[]{:S(2)}) collective-permute-start(bf16[192,384]{1,0:T(8,128)(2,1)} %get-tuple-element.172), channel_id=1, source_target_pairs={{0,16},{1,17},{2,18},{3,19},{4,20},{5,21},{6,22},{7,23},{8,24},{9,... | collective-permute-start | bytes 442376 | tf_op jit(solution)/shard_map/ppermute | solution.py:422
  239.1 11.8 %collective-permute-start.21 = (bf16[192,384]{1,0:T(8,128)(2,1)}, bf16[192,384]{1,0:T(8,128)(2,1)S(1)}, u32[]{:S(2)}, u32[]{:S(2)}) collective-permute-start(bf16[192,384]{1,0:T(8,128)(2,1)} %get-tuple-element.173), channel_id=1, source_target_pairs={{0,24},{1,25},{2,26},{3,27},{4,28},{5,29},{6,30},{7,31},{8,16},{9,... | collective-permute-start | bytes 442376 | tf_op jit(solution)/shard_map/ppermute | solution.py:422
  276.8 4.2 %collective-permute-start.22 = (bf16[4,4,160,384]{3,2,1,0:T(8,128)(2,1)}, bf16[4,4,160,384]{3,2,1,0:T(8,128)(2,1)S(1)}, u32[]{:S(2)}, u32[]{:S(2)}) collective-permute-start(bf16[4,4,160,384]{3,2,1,0:T(8,128)(2,1)} %get-tuple-element.191), channel_id=1, source_target_pairs={{0,1},{1,0},{2,3},{3,2},{4,5},{5,4},{6,7},{7,6},{8,9},{9,8},{10,11... | collective-permute-start | bytes 5898248 | tf_op jit(solution)/shard_map/ppermute | solution.py:422
  276.8 15.1 %collective-permute-start.30 = (bf16[240,384]{1,0:T(8,128)(2,1)S(1)}, bf16[240,384]{1,0:T(8,128)(2,1)S(1)}, u32[]{:S(2)}, u32[]{:S(2)}) collective-permute-start(bf16[240,384]{1,0:T(8,128)(2,1)S(1)} %copy-done.37), channel_id=1, source_target_pairs={{0,8},{1,9},{2,10},{3,11},{4,12},{5,13},{6,14},{7,15},{8,0},{9,1},... | collective-permute-start | bytes 552968 | tf_op jit(solution)/shard_map/ppermute | solution.py:422
  286.6 23.5 %collective-permute-start.23 = (bf16[4,160,384]{2,1,0:T(8,128)(2,1)}, bf16[4,160,384]{2,1,0:T(8,128)(2,1)S(1)}, u32[]{:S(2)}, u32[]{:S(2)}) collective-permute-start(bf16[4,160,384]{2,1,0:T(8,128)(2,1)} %get-tuple-element.193), channel_id=1, source_target_pairs={{0,2},{1,3},{2,0},{3,1},{4,6},{5,7},{6,4},{7,5},{8,10},{9,11},{10,... | collective-permute-start | bytes 1474568 | tf_op jit(solution)/shard_map/ppermute | solution.py:422
  288.1 23.7 %collective-permute-start.24 = (bf16[4,160,384]{2,1,0:T(8,128)(2,1)}, bf16[4,160,384]{2,1,0:T(8,128)(2,1)S(1)}, u32[]{:S(2)}, u32[]{:S(2)}) collective-permute-start(bf16[4,160,384]{2,1,0:T(8,128)(2,1)} %get-tuple-element.194), channel_id=1, source_target_pairs={{0,4},{1,5},{2,6},{3,7},{4,0},{5,1},{6,2},{7,3},{8,12},{9,13},{10,... | collective-permute-start | bytes 1474568 | tf_op jit(solution)/shard_map/ppermute | solution.py:422
  288.7 23.2 %collective-permute-start.25 = (bf16[4,160,384]{2,1,0:T(8,128)(2,1)}, bf16[4,160,384]{2,1,0:T(8,128)(2,1)S(1)}, u32[]{:S(2)}, u32[]{:S(2)}) collective-permute-start(bf16[4,160,384]{2,1,0:T(8,128)(2,1)} %get-tuple-element.195), channel_id=1, source_target_pairs={{0,6},{1,7},{2,4},{3,5},{4,2},{5,3},{6,0},{7,1},{8,14},{9,15},{10,... | collective-permute-start | bytes 1474568 | tf_op jit(solution)/shard_map/ppermute | solution.py:422
  290.1 15.5 %collective-permute-start.31 = (bf16[240,384]{1,0:T(8,128)(2,1)S(1)}, bf16[240,384]{1,0:T(8,128)(2,1)S(1)}, u32[]{:S(2)}, u32[]{:S(2)}) collective-permute-start(bf16[240,384]{1,0:T(8,128)(2,1)S(1)} %copy-done.36), channel_id=1, source_target_pairs={{0,16},{1,17},{2,18},{3,19},{4,20},{5,21},{6,22},{7,23},{8,24},{9,... | collective-permute-start | bytes 552968 | tf_op jit(solution)/shard_map/ppermute | solution.py:422
  292.0 13.7 %collective-permute-start.32 = (bf16[240,384]{1,0:T(8,128)(2,1)S(1)}, bf16[240,384]{1,0:T(8,128)(2,1)S(1)}, u32[]{:S(2)}, u32[]{:S(2)}) collective-permute-start(bf16[240,384]{1,0:T(8,128)(2,1)S(1)} %copy-done.35), channel_id=1, source_target_pairs={{0,24},{1,25},{2,26},{3,27},{4,28},{5,29},{6,30},{7,31},{8,16},{9,... | collective-permute-start | bytes 552968 | tf_op jit(solution)/shard_map/ppermute | solution.py:422
  310.0 22.6 %collective-permute-start.33 = (f32[216,384]{1,0:T(8,128)S(1)}, f32[216,384]{1,0:T(8,128)S(1)}, u32[]{:S(2)}, u32[]{:S(2)}) collective-permute-start(f32[216,384]{1,0:T(8,128)S(1)} %pad_maximum_fusion.2), channel_id=1, source_target_pairs={{0,1},{1,0},{2,3},{3,2},{4,5},{5,4},{6,7},{7,6},{8,9},{9,8},{10,11... | collective-permute-start | bytes 995336 | tf_op jit(solution)/shard_map/ppermute | solution.py:422
  315.3 7.0 %collective-permute-start.26 = (bf16[160,384]{1,0:T(8,128)(2,1)}, bf16[160,384]{1,0:T(8,128)(2,1)S(1)}, u32[]{:S(2)}, u32[]{:S(2)}) collective-permute-start(bf16[160,384]{1,0:T(8,128)(2,1)} %get-tuple-element.197), channel_id=1, source_target_pairs={{0,8},{1,9},{2,10},{3,11},{4,12},{5,13},{6,14},{7,15},{8,0},{9,1},... | collective-permute-start | bytes 368648 | tf_op jit(solution)/shard_map/ppermute | solution.py:422
  316.6 12.6 %collective-permute-start.27 = (bf16[160,384]{1,0:T(8,128)(2,1)}, bf16[160,384]{1,0:T(8,128)(2,1)S(1)}, u32[]{:S(2)}, u32[]{:S(2)}) collective-permute-start(bf16[160,384]{1,0:T(8,128)(2,1)} %get-tuple-element.198), channel_id=1, source_target_pairs={{0,16},{1,17},{2,18},{3,19},{4,20},{5,21},{6,22},{7,23},{8,24},{9,... | collective-permute-start | bytes 368648 | tf_op jit(solution)/shard_map/ppermute | solution.py:422
  317.6 11.6 %collective-permute-start.28 = (bf16[160,384]{1,0:T(8,128)(2,1)}, bf16[160,384]{1,0:T(8,128)(2,1)S(1)}, u32[]{:S(2)}, u32[]{:S(2)}) collective-permute-start(bf16[160,384]{1,0:T(8,128)(2,1)} %get-tuple-element.199), channel_id=1, source_target_pairs={{0,24},{1,25},{2,26},{3,27},{4,28},{5,29},{6,30},{7,31},{8,16},{9,... | collective-permute-start | bytes 368648 | tf_op jit(solution)/shard_map/ppermute | solution.py:422
  (41 other events, 287.6 us)
Sparse Core Ops, SparseCore 0:
  13.8 98.8 all-gather.1

commit v3 on v2

v3 whole, which is shorter than its diff:
```python
import functools

import jax
import jax.numpy as jnp
from jax import lax
from jax.experimental import pallas as pl
from jax.experimental.pallas import tpu as pltpu
from jax.sharding import PartitionSpec as P

HEADS = 12
HEAD_DIM = 64
PAIRS = 6
LANES = 128
CHIPS = 16
MERGE_STEPS = 2
LONG = 10**11
SHORT = 6 * 10**9
EPS = 1e-06
MASKED = -1e30
SCALE = HEAD_DIM**-0.5
GELU_C = 0.7978845608028654
GELU_A = 0.044715
VMEM = 64 * 1024 * 1024 - 65536
F32 = jnp.float32
BF16 = jnp.bfloat16


def dot_nn(left, right):
    return lax.dot_general(left, right, (((1,), (0,)), ((), ())), preferred_element_type=F32)


def dot_nt(left, right):
    return lax.dot_general(left, right, (((1,), (1,)), ((), ())), preferred_element_type=F32)


def dot_tn(left, right):
    return lax.dot_general(left, right, (((0,), (0,)), ((), ())), preferred_element_type=F32)


def normalize(rows):
    centered = rows - jnp.mean(rows, axis=-1, keepdims=True)
    inverse = lax.rsqrt(jnp.mean(centered * centered, axis=-1, keepdims=True) + EPS)
    return centered * inverse, inverse


def norm_back(grads, gain, hat, inverse):
    scaled = grads * gain
    mean = jnp.mean(scaled, axis=-1, keepdims=True)
    mean_hat = jnp.mean(scaled * hat, axis=-1, keepdims=True)
    return inverse * (scaled - mean - hat * mean_hat)


def column_sum(rows):
    return jnp.sum(rows, axis=0, keepdims=True)


def segments(lengths_ref, tile, slots, rows, axis):
    shape = (rows, 1) if axis == 0 else (1, rows)
    index = lax.broadcasted_iota(jnp.int32, shape, axis)
    segment = jnp.zeros(shape, jnp.int32)
    bound = 0
    for slot in range(slots):
        bound = bound + lengths_ref[tile, slot]
        segment = segment + (index >= bound).astype(jnp.int32)
    return segment


def mask_bias(lengths_ref, tile, slots, rows):
    same = segments(lengths_ref, tile, slots, rows, 0) == segments(lengths_ref, tile, slots, rows, 1)
    return jnp.where(same, 0.0, MASKED).astype(F32)


def half_of(pair, side):
    lane = lax.broadcasted_iota(jnp.int32, pair.shape, 1)
    keep = lane < HEAD_DIM if side == 0 else lane >= HEAD_DIM
    return jnp.where(keep, pair, jnp.zeros_like(pair))


def fetch_weights(me, sources, weight_refs, parts_ref, sem):
    core, chip = me & 1, me >> 1
    side = sources[0].shape[2]
    each = weight_refs[0].shape[0] // CHIPS
    for index, source in enumerate(sources):
        half = core if index < 4 else 1 - core
        cols = pl.ds(pl.multiple_of(half * side, LANES), side)
        for layer in range(4):
            owner = chip ^ (4 * layer + index % 4)
            rows = pl.ds(pl.multiple_of(owner * each, 16), each)
            for number, ref in enumerate(weight_refs):
                pltpu.make_async_copy(
                    source.at[layer, pl.ds(number * each, each), :], ref.at[rows, cols], sem.at[number]
                ).start()
            pltpu.make_async_copy(
                source.at[layer, pl.ds(4 * each, 16), :], parts_ref.at[2 * owner + half], sem.at[4]
            ).start()


def project(me_ref, x_ref, *refs):
    sources = refs[:8]
    n1_ref, q_ref, k_ref, v_ref, wq_ref, wk_ref, wv_ref, wo_ref, vec_ref, bup_ref, parts_ref, sem = refs[8:]
    weights = (wq_ref, wk_ref, wv_ref, wo_ref)

    @pl.when(pl.program_id(0) == 0)
    def _():
        fetch_weights(me_ref[0], sources, weights, parts_ref, sem)
        for number, ref in enumerate(weights + (parts_ref,)):
            pltpu.make_async_copy(ref, ref, sem.at[number]).wait()
        count, _, side = parts_ref.shape
        parts = [parts_ref[device].astype(F32) for device in range(count)]
        group = count // 2
        vec_ref[...] = jnp.concatenate((sum(parts[:group]), sum(parts[group:])), axis=1)
        blocks = bup_ref.shape[1] // side
        group = count // blocks
        for block in range(blocks):
            rows = sum(parts[block * group : (block + 1) * group])
            bup_ref[:, block * side : (block + 1) * side] = rows[8:9]

    project_rows(x_ref, vec_ref, wq_ref, wk_ref, wv_ref, n1_ref, q_ref, k_ref, v_ref)


def project_rows(x_ref, vec_ref, wq_ref, wk_ref, wv_ref, n1_ref, q_ref, k_ref, v_ref):
    hat, _ = normalize(x_ref[...].astype(F32))
    n1 = (hat * vec_ref[0:1, :] + vec_ref[1:2, :]).astype(BF16)
    n1_ref[...] = n1
    q_ref[...] = (dot_nn(n1, wq_ref[...]) + vec_ref[2:3, :]).astype(BF16) * jnp.asarray(SCALE, BF16)
    k_ref[...] = dot_nn(n1, wk_ref[...]).astype(BF16)
    v_ref[...] = (dot_nn(n1, wv_ref[...]) + vec_ref[3:4, :]).astype(BF16)


def attention_forward(lengths_ref, x_ref, grad_ref, vec_ref, q_ref, k_ref, v_ref, wo_ref,
                      mixed_ref, lse_ref, resid_ref, n2_ref, cot_ref, dsum_ref):
    tile = pl.program_id(0)
    rows = q_ref.shape[0]
    slots = lengths_ref.shape[1]
    bias = mask_bias(lengths_ref, tile, slots, rows)
    lane = lax.broadcasted_iota(jnp.int32, (rows, LANES), 1)
    lse = jnp.zeros((rows, LANES), F32)

    def at(pair):
        return pl.ds(pair * LANES, LANES)

    def scores_of(pair):
        qp, kp = q_ref[:, at(pair)], k_ref[:, at(pair)]
        return [dot_nt(half_of(qp, side), kp) for side in range(2)]

    def softmax_of(scores):
        scores = scores + bias
        top = jnp.max(scores, axis=-1, keepdims=True)
        weights = jnp.exp(scores - top)
        sums = jnp.sum(weights, axis=-1, keepdims=True)
        return (weights * (1.0 / sums)).astype(BF16), top + jnp.log(sums)

    raw = {}
    probs = {}
    for turn in range(PAIRS + 2):
        if turn < PAIRS:
            raw[turn] = scores_of(turn)
        if 0 <= turn - 1 < PAIRS:
            both = [softmax_of(scores) for scores in raw.pop(turn - 1)]
            for side in range(2):
                lse = jnp.where(lane == 2 * (turn - 1) + side, both[side][1], lse)
            probs[turn - 1] = [pair[0] for pair in both]
        if turn >= 2:
            vp = v_ref[:, at(turn - 2)]
            parts = [dot_nn(probs[turn - 2][side], half_of(vp, side)) for side in range(2)]
            mixed_ref[:, at(turn - 2)] = (parts[0] + parts[1]).astype(BF16)
    lse_ref[...] = lse
    resid = x_ref[...].astype(F32) + (dot_nn(mixed_ref[...], wo_ref[...]) + vec_ref[4:5, :])
    resid_ref[...] = resid
    hat, _ = normalize(resid)
    n2_ref[...] = (hat * vec_ref[5:6, :] + vec_ref[6:7, :]).astype(BF16)
    valid = segments(lengths_ref, tile, slots, rows, 0) < slots
    cot = jnp.where(valid, grad_ref[...].astype(F32), 0.0)
    cot_ref[...] = cot.astype(BF16)

    @pl.when(tile == 0)
    def _():
        dsum_ref[...] = jnp.zeros_like(dsum_ref)

    dsum_ref[0:1, :] += column_sum(cot)


def flat_rows(ref):
    return ref[...].reshape(-1, ref.shape[-1])


def spread(me, rows, put):
    layer, plane = me >> 3, (me >> 1) & 3
    each = rows.shape[0] // CHIPS
    for chip in range(CHIPS):
        put((chip & 3) ^ plane, (chip >> 2) ^ layer, rows[chip * each : (chip + 1) * each].astype(BF16))


def mlp(me_ref, n2_ref, cot_ref, resid_ref, vec_ref, bup_ref, wup_ref, wdown_ref,
        out_ref, gtwo_ref, down_send_ref, down_keep_ref, up_send_ref, up_keep_ref, dbu_ref, acc, act_ref, gup_ref):
    step = pl.program_id(0)
    steps = pl.num_programs(0)
    me = me_ref[0]
    block = 256
    chunks = [slice(start, start + block) for start in range(0, n2_ref.shape[0], block)]

    @pl.when(step == 0)
    def _():
        gtwo_ref[...] = jnp.zeros_like(gtwo_ref)
        acc[...] = resid_ref[...] + vec_ref[7:8, :]

    wup = flat_rows(wup_ref)
    wdown = flat_rows(wdown_ref)
    sums = jnp.zeros_like(dbu_ref)
    for at in chunks:
        pre = dot_nn(n2_ref[at, :], wup) + bup_ref[...]
        grad_act = dot_nt(cot_ref[at, :], wdown)
        square = pre * pre
        tanh = jnp.tanh(pre * (GELU_C + (GELU_C * GELU_A) * square))
        half = 0.5 + 0.5 * tanh
        inner = GELU_C + (3.0 * GELU_C * GELU_A) * square
        act_ref[at, :] = (pre * half).astype(BF16)
        gup = (grad_act * (half + (0.5 * pre) * (1.0 - tanh * tanh) * inner)).astype(BF16)
        gup_ref[at, :] = gup
        sums = sums + column_sum(gup.astype(F32))
    dbu_ref[...] = sums
    for at in chunks:
        acc[at, :] += dot_nn(act_ref[at, :], wdown)
        gtwo_ref[at, :] += dot_nt(gup_ref[at, :], wup)

    grad_down = dot_tn(act_ref[...], cot_ref[...])
    first = (me & 1) == 0
    plane = (me >> 1) & 3
    deep = down_send_ref.shape[2]
    for index in range(4):
        low = grad_down[2 * deep * index : 2 * deep * index + deep]
        high = grad_down[2 * deep * index + deep : 2 * deep * (index + 1)]
        down_keep_ref[0, index ^ plane] = jnp.where(first, low, high).astype(BF16)
        down_send_ref[0, index ^ plane] = jnp.where(first, high, low).astype(BF16)

    grad_up = dot_tn(n2_ref[...], gup_ref[...])

    def put_in(ref):
        def put(plane, layer, piece):
            ref[0, layer, plane] = piece

        spread(me, grad_up, put)

    @pl.when(step < steps // 2)
    def _():
        put_in(up_send_ref)

    @pl.when(step >= steps // 2)
    def _():
        put_in(up_keep_ref)

    @pl.when(step == steps - 1)
    def _():
        out_ref[...] = acc[...].astype(BF16)


def attention_backward(lengths_ref, q_ref, k_ref, v_ref, lse_ref, cot_ref, resid_ref, gtwo_ref, vec_ref, wo_ref,
                       grads_ref, gresid_ref, dsum_ref, gmix_ref):
    tile = pl.program_id(0)
    rows = q_ref.shape[0]

    @pl.when(tile == 0)
    def _():
        dsum_ref[...] = jnp.zeros_like(dsum_ref)

    hat, inverse = normalize(resid_ref[...])
    grad_two = gtwo_ref[...]
    gresid = cot_ref[...].astype(F32) + norm_back(grad_two, vec_ref[5:6, :], hat, inverse)
    gresid_ref[...] = gresid
    gattn = gresid.astype(BF16)
    grads_ref[3] = gattn
    dsum_ref[2:3, :] += column_sum(gattn.astype(F32))
    dsum_ref[3:4, :] += column_sum(grad_two * hat)
    dsum_ref[4:5, :] += column_sum(grad_two)
    gmix_ref[...] = dot_nt(gattn, wo_ref[...]).astype(BF16)
    bias = mask_bias(lengths_ref, tile, lengths_ref.shape[1], rows)

    def load(pair):
        cols = pl.ds(pair * LANES, LANES)
        return q_ref[:, cols], k_ref[:, cols], v_ref[:, cols], gmix_ref[:, cols]

    def products_of(pair):
        qp, kp, vp, gp = load(pair)
        return [(dot_nt(half_of(qp, side), kp), dot_nt(half_of(gp, side), vp)) for side in range(2)]

    def softmax_back(pair, products):
        results = []
        for side, (scores, grad_probs) in enumerate(products):
            head = 2 * pair + side
            probs = jnp.exp(scores + bias - lse_ref[:, head : head + 1])
            weighted = probs * grad_probs
            dot = jnp.sum(weighted, axis=-1, keepdims=True)
            results.append((probs.astype(BF16), (weighted - probs * dot).astype(BF16)))
        return results

    def store(pair, results):
        qp, kp, vp, gp = load(pair)
        dq = sum(dot_nn(results[side][1], half_of(kp, side)) for side in range(2))
        dk = sum(dot_tn(results[side][1], half_of(qp, side)) for side in range(2))
        dv = sum(dot_tn(results[side][0], half_of(gp, side)) for side in range(2))
        cols = pl.ds(pair * LANES, LANES)
        grads_ref[0, :, cols] = (dq * SCALE).astype(BF16)
        grads_ref[1, :, cols] = dk.astype(BF16)
        grads_ref[2, :, cols] = dv.astype(BF16)

    raw = {}
    done = {}
    for turn in range(PAIRS + 2):
        if turn < PAIRS:
            raw[turn] = products_of(turn)
        if 0 <= turn - 1 < PAIRS:
            done[turn - 1] = softmax_back(turn - 1, raw.pop(turn - 1))
        if turn >= 2:
            store(turn - 2, done.pop(turn - 2))

    dsum_ref[0:1, :] += column_sum(grads_ref[0].astype(F32))
    dsum_ref[1:2, :] += column_sum(grads_ref[2].astype(F32))


def projections_backward(me_ref, x_ref, gresid_ref, vec_ref, grads_ref, wq_ref, wk_ref, wv_ref, n1_ref, mixed_ref,
                         columns_ref, sum_back_ref, sum_down_ref, sum_up_ref,
                         gtok_ref, dsum_ref, send_ref, keep_ref):
    step = pl.program_id(0)
    tiles = pl.num_programs(0) - 4
    me = me_ref[0]
    first = (me & 1) == 0
    side = send_ref.shape[3]
    each = wq_ref.shape[0] // CHIPS

    @pl.when(step == 0)
    def _():
        dsum_ref[...] = jnp.zeros_like(dsum_ref)

    @pl.when(step < tiles)
    def _():
        grad_one = dot_nt(grads_ref[0], wq_ref[...]) + dot_nt(grads_ref[1], wk_ref[...]) + dot_nt(grads_ref[2], wv_ref[...])
        hat, inverse = normalize(x_ref[...].astype(F32))
        gtok_ref[...] = (gresid_ref[...] + norm_back(grad_one, vec_ref[0:1, :], hat, inverse)).astype(BF16)
        dsum_ref[0:1, :] += column_sum(grad_one * hat)
        dsum_ref[1:2, :] += column_sum(grad_one)

    def run(left, number):
        result = dot_tn(left, columns_ref[0])
        low, high = result[:, :side], result[:, side:]
        rows_at = pl.ds(pl.multiple_of(number * each, 16), each)

        def put_send(plane, layer, rows):
            send_ref[layer, plane, rows_at, :] = rows

        def put_keep(plane, layer, rows):
            keep_ref[layer, plane, rows_at, :] = rows

        spread(me, jnp.where(first, high, low), put_send)
        spread(me, jnp.where(first, low, high), put_keep)

    @pl.when((step >= tiles) & (step < tiles + 3))
    def _():
        run(n1_ref[...], step - tiles)

    @pl.when(step == tiles + 3)
    def _():
        run(mixed_ref[...], 3)
        vecs = jnp.concatenate((dsum_ref[0:2], sum_back_ref[0:5], sum_down_ref[0:1]), axis=0)
        for chip in range(CHIPS):
            half = chip // (CHIPS // 2)
            block = chip * (sum_up_ref.shape[1] // side) // CHIPS
            last = jnp.broadcast_to(sum_up_ref[:, block * side : (block + 1) * side], (8, side))
            rows = jnp.concatenate((vecs[:, half * side : (half + 1) * side], last), axis=0).astype(BF16)
            at = ((chip >> 2) ^ (me >> 3), (chip & 3) ^ ((me >> 1) & 3))
            send_ref[at[0], at[1], 4 * each :, :] = rows
            keep_ref[at[0], at[1], 4 * each :, :] = rows


def rows_spec(block, width):
    return pl.BlockSpec((block, width), lambda i, *me: (i, 0))


def cols_spec(height, block):
    return pl.BlockSpec((height, block), lambda i, *me: (0, i))


def whole_spec(shape):
    return pl.BlockSpec(shape, lambda *i: (0,) * len(shape), pipeline_mode=pl.Buffered(1))


def kept_spec(shape):
    return pl.BlockSpec(shape, lambda *i: (0,) * len(shape))


SMEM = pl.BlockSpec(memory_space=pltpu.SMEM)


def cost(flops):
    return pl.CostEstimate(flops=flops, bytes_accessed=1, transcendentals=0)


def call(kernel, grid, ins, outs, scratch, name, flops, *args):
    out_specs = tuple(spec for spec, _ in outs)
    out_shape = tuple(shape for _, shape in outs)
    return pl.pallas_call(
        kernel,
        grid=grid,
        in_specs=ins,
        out_specs=out_specs,
        out_shape=out_shape,
        scratch_shapes=scratch,
        compiler_params=pltpu.CompilerParams(vmem_limit_bytes=VMEM, dimension_semantics=("arbitrary",) * len(grid)),
        cost_estimate=cost(flops),
        name=name,
    )(*args)


def call_with(me, kernel, steps, ins, outs, scratch, name, flops, *args):
    out_shape = tuple(shape for _, shape in outs)
    return pl.pallas_call(
        kernel,
        grid_spec=pltpu.PrefetchScalarGridSpec(
            num_scalar_prefetch=1, grid=(steps,), in_specs=ins, out_specs=tuple(spec for spec, _ in outs),
            scratch_shapes=scratch),
        out_shape=out_shape,
        compiler_params=pltpu.CompilerParams(vmem_limit_bytes=VMEM, dimension_semantics=("arbitrary",)),
        cost_estimate=cost(0),
        name=name,
    )(me, *args)


def shaped(*shape, dtype=BF16):
    return jax.ShapeDtypeStruct(shape, dtype)


def flipped(count, change):
    pairs = []
    for source in range(count):
        core, chip = source & 1, source >> 1
        core, chip = change(core, chip)
        pairs.append((source, 2 * chip + core))
    return pairs


def swap(array, change):
    return lax.ppermute(array, "dp", flipped(lax.axis_size("dp"), change))


def other_core(core, chip):
    return core ^ 1, chip


def first_plane(core, chip):
    return core, chip ^ (1 + core)


def second_plane(core, chip):
    return core, chip ^ (2 - core)


def other_plane(distance):
    return lambda core, chip: (core, chip ^ distance)


def other_layer(distance):
    return lambda core, chip: (core, chip ^ (4 * distance))


def split_shards(core_ref, q_ref, k_ref, v_ref, o_ref, u_ref, keep_ref, send_ref):
    width = q_ref.shape[1]
    side = width // 2
    first = core_ref[0] == 0

    def put(index, low, high):
        keep_ref[index] = jnp.where(first, low, high).astype(BF16)
        send_ref[index] = jnp.where(first, high, low).astype(BF16)

    for index, ref in enumerate((q_ref, k_ref, v_ref, o_ref)):
        rows = ref[...].astype(F32)
        put(index, rows[:, :side], rows[:, side:])
    up = u_ref[...].astype(F32)
    folds = up.shape[1] // width
    for part in range(folds):
        low = part * side
        high = (folds + part) * side
        put(4 + part, up[:, low : low + side], up[:, high : high + side])


def join_shards(me_ref, keep_ref, take_ref, down_ref, *refs):
    vectors, (near_ref, far_ref) = refs[:-2], refs[-2:]
    me = me_ref[0]
    first = (me & 1) == 0
    parts, own, side = keep_ref.shape
    folds = parts - 4
    keep = keep_ref[...].astype(F32)
    take = take_ref[...].astype(F32)

    def joined(index):
        low = jnp.where(first, keep[index], take[index])
        high = jnp.where(first, take[index], keep[index])
        return jnp.concatenate((low, high), axis=0).astype(BF16)

    for index in range(4):
        near_ref[2 * own * index : 2 * own * (index + 1), :] = joined(index)
    for index in range(folds):
        far_ref[2 * own * (index // 2) : 2 * own * (index // 2 + 1), side * (index % 2) : side * (index % 2 + 1)] = joined(4 + index)
    far_ref[folds * own :, :] = down_ref[...]
    rows = []
    for ref in vectors:
        flat = ref[...].astype(F32).reshape(1, -1)
        rows.append(jnp.concatenate((flat, jnp.zeros((1, side - flat.shape[1]), F32)), axis=1))
    rows.append(jnp.zeros((16 - len(rows), side), F32))
    rows = jnp.concatenate(rows, axis=0)
    short = pltpu.roll(rows, own * lax.rem(me, side // own), 1)
    long = pltpu.roll(rows, folds * own * lax.rem(me, side // (folds * own)), 1)
    index = lax.broadcasted_iota(jnp.int32, rows.shape, 0)
    near_ref[8 * own :, :] = jnp.where(index < 8, short, long).astype(BF16)


def across_layers(shard):
    return jnp.stack([shard] + [swap(shard, other_layer(distance)) for distance in (1, 2, 3)])


def after(arrays, *others):
    return lax.optimization_barrier((arrays, others))[0]


def small_call(kernel, args, outs, name, scratch=(), ins=None, flops=0):
    return pl.pallas_call(
        kernel,
        in_specs=ins,
        out_specs=tuple(spec for spec, _ in outs),
        out_shape=tuple(shape for _, shape in outs),
        scratch_shapes=list(scratch),
        compiler_params=pltpu.CompilerParams(vmem_limit_bytes=VMEM),
        cost_estimate=cost(flops),
        name=name,
    )(*args)


VMEM_SPEC = pl.BlockSpec(memory_space=pltpu.VMEM)
ANY_SPEC = pl.BlockSpec(memory_space=pl.ANY)


def gather_by_hand(me, weights, vectors):
    count = lax.axis_size("dp")
    own, width = weights[0].shape
    side = width // 2
    deep = weights[5].shape[0]
    folds = deep // own
    halves = (VMEM_SPEC, shaped(4 + folds, own, side))
    keep, send = small_call(
        split_shards, (me & 1, *weights[:5]), [halves, halves], "split_shards", ins=[SMEM] + [VMEM_SPEC] * 5)
    take = swap(send, other_core)
    near, far = small_call(
        join_shards, (me, keep, take, weights[5], *vectors),
        [(VMEM_SPEC, shaped(8 * own + 16, side)), (VMEM_SPEC, shaped(2 * deep, width))], "join_shards",
        ins=[SMEM] + [VMEM_SPEC] * (3 + len(vectors)))
    far = lax.all_gather(far, "dp", axis=0, tiled=True).reshape(count // 2, 2, 2 * deep, width)
    near = across_layers(near)
    near = [near] + [swap(near, other_plane(distance)) for distance in (1, 2, 3)]
    return near + [swap(piece, other_core) for piece in near], far


def gather_plain(weights, vectors):
    squares, up_weight, down_weight = weights[:4], weights[4], weights[5]
    count = lax.axis_size("dp")
    own, width = squares[0].shape
    folds = down_weight.shape[0] // own
    hidden = up_weight.shape[1]
    flat = jnp.concatenate(vectors)
    packed = jnp.concatenate(
        (
            *squares,
            up_weight.reshape(own, folds, width).transpose(1, 0, 2).reshape(own * folds, width),
            down_weight,
            jnp.pad(flat.reshape(1, -1), ((0, 7), (0, width - flat.size))),
        ),
        axis=0,
    )
    whole = lax.all_gather(packed, "dp", axis=0, tiled=True).reshape(count, -1, width)
    square_all = [whole[:, index * own : (index + 1) * own, :].reshape(width, width) for index in range(4)]
    wup = whole[:, 4 * own : (4 + folds) * own, :].reshape(count, folds, own, width).transpose(0, 2, 1, 3)
    wup = wup.reshape(CHIPS, width // CHIPS, 2, folds // 2, width).transpose(0, 2, 3, 1, 4).reshape(CHIPS, 2, -1, width)
    wdown = whole[:, (4 + folds) * own : (4 + 2 * folds) * own, :]
    wdown = wdown.reshape(CHIPS, 2, -1, width)
    last = whole[:, (4 + 2 * folds) * own, : flat.size].astype(F32)
    vec = last[:, : 8 * own].reshape(count, 8, own).transpose(1, 0, 2).reshape(8, width)
    bup = last[:, 8 * own :].reshape(1, hidden)
    return (*square_all, jnp.concatenate((wup, wdown), axis=2), jnp.pad(vec, ((0, 8), (0, 0))), bup)


def merge_core(core_ref, keep_ref, take_ref, own_ref, send_ref):
    core = core_ref[0]

    def whole(plane):
        return (keep_ref[:, plane].astype(F32) + take_ref[:, plane].astype(F32)).astype(BF16)

    own_ref[:, 0] = whole(0)
    own_ref[:, 1] = whole(2 - core)
    send_ref[:, 0] = whole(1 + core)
    send_ref[:, 1] = whole(3)


def merge_first(*refs):
    pairs, rest_ref, send_ref = refs[:-2], refs[-2], refs[-1]
    base = 0
    for own_ref, take_ref in zip(pairs[::2], pairs[1::2]):
        for part in range(own_ref.shape[0]):
            at = slice(base, base + own_ref.shape[3])
            rest_ref[:, at, :] = own_ref[part, :, 0].astype(F32) + take_ref[part, :, 0].astype(F32)
            send_ref[:, at, :] = (own_ref[part, :, 1].astype(F32) + take_ref[part, :, 1].astype(F32)).astype(BF16)
            base += own_ref.shape[3]


def merge_second(own_ref, take_ref, rest_ref, *send_refs):
    for layer in range(4):
        whole = own_ref[layer] + take_ref[layer].astype(F32)
        if layer == 0:
            rest_ref[...] = whole
        else:
            send_refs[layer - 1][...] = whole.astype(BF16)


def merge_last(deep, core_ref, rest_ref, a_ref, b_ref, c_ref, *refs):
    whole = rest_ref[...] + a_ref[...].astype(F32) + b_ref[...].astype(F32) + c_ref[...].astype(F32)
    first = core_ref[0] == 0
    if deep:
        refs[0][...] = whole[:deep]
        refs = refs[1:]
    keep_ref, send_ref = refs[:2]
    parts, own, _ = keep_ref.shape
    for part in range(parts):
        low = whole[deep + 2 * own * part : deep + 2 * own * part + own]
        high = whole[deep + 2 * own * part + own : deep + 2 * own * (part + 1)]
        keep_ref[part] = jnp.where(first, low, high)
        send_ref[part] = jnp.where(first, high, low)
    if not deep:
        refs[2][...] = whole[2 * own * parts :]


def finish(me_ref, up_keep_ref, up_take_ref, keep_ref, take_ref, flat_ref, up_ref, *refs):
    me = me_ref[0]
    first = (me & 1) == 0
    side = keep_ref.shape[2]
    width = 2 * side
    squares, flats = refs[:4], refs[4:]
    own = up_ref.shape[0]
    for number, ref in enumerate(squares):
        keep, take = keep_ref[number], take_ref[number]
        ref[:, :side] = jnp.where(first, keep, take)
        ref[:, side:] = jnp.where(first, take, keep)
    parts = up_keep_ref.shape[0]
    for part in range(parts):
        keep, take = up_keep_ref[part], up_take_ref[part]
        up_ref[:, part * width : (part + 1) * width] = jnp.where(first, keep, take)
        up_ref[:, (parts + part) * width : (parts + part + 1) * width] = jnp.where(first, take, keep)
    flat = flat_ref[...]
    long = flats[-1].shape[0]
    short_turn = lax.rem(side - own * lax.rem(me, side // own), side)
    long_turn = lax.rem(side - long * lax.rem(me, side // long), side)
    short = pltpu.roll(flat, short_turn, 1)
    for number, ref in enumerate(flats[:-1]):
        ref[...] = short[number, :own]
    flats[-1][...] = pltpu.roll(flat, long_turn, 1)[8, :long]


def scatter_core(send):
    return swap(send, other_core)


def scatter_first(core, keep, take):
    shape = keep.shape
    planes, rows, side = shape[-3:]
    keep, take = keep.reshape(-1, planes, rows, side), take.reshape(-1, planes, rows, side)
    count = keep.shape[0]
    steps = MERGE_STEPS
    block = pl.BlockSpec((count // steps, planes, rows, side), lambda i: (i, 0, 0, 0))
    half = (pl.BlockSpec((count // steps, 2, rows, side), lambda i: (i, 0, 0, 0)), shaped(count, 2, rows, side))
    own, send = call(merge_core, (steps,), [SMEM, block, block], [half, half], [], "merge_core", 0, core, keep, take)
    parts = (-1, CHIPS // 4, 2, rows, side)
    return own.reshape(parts), swap(send, first_plane).reshape(parts)


def scatter_second(*pairs):
    _, count, _, _, side = pairs[0].shape
    rows = sum(piece.shape[0] * piece.shape[3] for piece in pairs[::2])
    steps = MERGE_STEPS
    ins = [pl.BlockSpec((piece.shape[0], count // steps, *piece.shape[2:]), lambda i: (0, i, 0, 0, 0)) for piece in pairs]
    out = pl.BlockSpec((count // steps, rows, side), lambda i: (i, 0, 0))
    rest, send = call(
        merge_first, (steps,), ins, [(out, shaped(count, rows, side, dtype=F32)), (out, shaped(count, rows, side))], [],
        "merge_first", LONG, *pairs)
    return rest, swap(send, second_plane)


def scatter_layers(own, take):
    _, rows, side = own.shape
    out = shaped(rows, side)
    rest, *sends = small_call(
        merge_second, (own, take), [(VMEM_SPEC, shaped(rows, side, dtype=F32))] + [(VMEM_SPEC, out)] * 3,
        "merge_second", ins=[VMEM_SPEC] * 2)
    return [rest] + [swap(piece, other_layer(r + 1)) for r, piece in enumerate(sends)]


def scatter_last(core, pieces, own, parts, deep):
    rows, side = pieces[0].shape
    outs = [(VMEM_SPEC, shaped(parts, own, side, dtype=F32))] * 2
    if deep:
        outs = [(VMEM_SPEC, shaped(deep, side, dtype=F32))] + outs
    else:
        outs.append((VMEM_SPEC, shaped(rows - 2 * own * parts, side, dtype=F32)))
    return small_call(
        functools.partial(merge_last, deep), (core, *pieces), outs, "merge_last", ins=[SMEM] + [VMEM_SPEC] * 4, flops=SHORT if deep else 0)


def reduce_plain(down_pair, up_pair, square_pair, flat):
    def scattered(array, axis):
        return lax.psum_scatter(array, "dp", scatter_dimension=axis, tiled=True).astype(F32)

    deep, width = down_pair[0].shape[2:]
    down = jnp.stack(down_pair).transpose(1, 2, 0, 3, 4).reshape(-1, width)
    up = jnp.stack(up_pair)
    folds, each = up.shape[1], up.shape[4]
    up = up.transpose(2, 3, 4, 0, 1, 5).reshape(CHIPS * each, 2 * folds * width)
    square = jnp.stack(square_pair).transpose(1, 2, 3, 0, 4)[:, :, : 4 * each]
    square = square.reshape(CHIPS, 4, each, width).transpose(1, 0, 2, 3).reshape(4, CHIPS * each, width)
    return (
        scattered(down, 0),
        scattered(up, 0),
        *scattered(square, 1),
        lax.psum_scatter(flat, "dp", scatter_dimension=0, tiled=True).reshape(-1),
    )


def body(tokens, lengths, attn_gain, attn_shift, query_weight, query_bias, key_weight, value_weight, value_bias,
         out_weight, out_bias, mlp_gain, mlp_shift, up_weight, up_bias, down_weight, down_bias, grad_out):
    count = lax.axis_size("dp")
    rows, width = tokens.shape
    tiles = lengths.shape[0]
    tile = rows // tiles
    hidden = up_bias.shape[0] * count
    own = width // count
    folds = hidden // width
    vectors = (attn_gain, attn_shift, query_bias, value_bias, out_bias, mlp_gain, mlp_shift, down_bias, up_bias)
    by_hand = count == 2 * CHIPS
    me = lax.axis_index("dp").astype(jnp.int32).reshape(1) if by_hand else jnp.zeros((1,), jnp.int32)
    core = me & 1
    weights = (query_weight, key_weight, value_weight, out_weight, up_weight, down_weight)

    tile_rows = rows_spec(tile, width)
    square = whole_spec((width, width))
    vec_spec = whole_spec((16, width))
    sums = (kept_spec((8, width)), shaped(8, width, dtype=F32))
    low_rows = (tile_rows, shaped(rows, width))
    lse_spec = rows_spec(tile, LANES)
    mac = 2 * rows * width * width
    kept_square = (kept_spec((width, width)), shaped(width, width))
    kept_vec = (kept_spec((16, width)), shaped(16, width, dtype=F32))
    kept_hidden = (kept_spec((1, hidden)), shaped(1, hidden, dtype=F32))
    side = width // 2
    if by_hand:
        near, far = gather_by_hand(me, weights, vectors)
        n1, q, k, v, wq, wk, wv, wo, vec, bup = call_with(
            me, project, tiles, [tile_rows] + [ANY_SPEC] * 8, [low_rows] * 4 + [kept_square] * 4 + [kept_vec, kept_hidden],
            [pltpu.VMEM((count, 16, side), BF16), pltpu.SemaphoreType.DMA((5,))], "project", 0, tokens, *near)
    else:
        wq, wk, wv, wo, far, vec, bup = gather_plain(weights, vectors)
        n1, q, k, v = call(
            project_rows, (tiles,), [tile_rows, vec_spec, square, square, square], [low_rows] * 4,
            [], "project", 0, tokens, vec, wq, wk, wv)
    high_rows = (tile_rows, shaped(rows, width, dtype=F32))
    mixed, lse, resid, n2, cot, sum_down = call(
        attention_forward, (tiles,), [SMEM, tile_rows, tile_rows, vec_spec, tile_rows, tile_rows, tile_rows, square],
        [low_rows, (lse_spec, shaped(rows, LANES, dtype=F32)), high_rows, low_rows, low_rows, sums],
        [], "attention_forward", 0, lengths, tokens, grad_out, vec, q, k, v, wo)

    halves = folds // 2
    each = width // CHIPS
    deep = hidden // (2 * CHIPS)
    full_rows = whole_spec((rows, width))
    kept_low = (kept_spec((rows, width)), shaped(rows, width))
    kept_high = (kept_spec((rows, width)), shaped(rows, width, dtype=F32))

    def turn(i, me):
        return ((i // halves) ^ 1 ^ (me[0] & 1)) * halves + lax.rem(i, halves)

    up_spec = pl.BlockSpec((CHIPS, 1, each, width), lambda i, me: (0, turn(i, me) // halves, lax.rem(turn(i, me), halves), 0))
    down_spec = pl.BlockSpec((width // (2 * deep), 2, deep, width), lambda i, me: (turn(i, me), 0, 1, 0))
    hidden_spec = pl.BlockSpec((1, width), lambda i, me: (0, turn(i, me)))
    down_pair = (pl.BlockSpec((1, 4, deep, width), lambda i, me: (turn(i, me) ^ (me[0] >> 3), 0, 0, 0)), shaped(4, 4, deep, width))
    part = (1, CHIPS // 4, 4, each, width)
    up_shape = shaped(halves, *part[1:])
    out, gtwo, down_send, down_keep, up_send, up_keep, sum_up = call_with(
        me, mlp, folds,
        [full_rows, full_rows, full_rows, vec_spec, hidden_spec, up_spec, down_spec],
        [kept_low, kept_high, down_pair, down_pair,
         (pl.BlockSpec(part, lambda i, me: (jnp.minimum(i, halves - 1), 0, 0, 0, 0)), up_shape),
         (pl.BlockSpec(part, lambda i, me: (jnp.maximum(i - halves, 0), 0, 0, 0, 0)), up_shape),
         (hidden_spec, shaped(1, hidden, dtype=F32))],
        [pltpu.VMEM((rows, width), F32), pltpu.VMEM((rows, width), BF16), pltpu.VMEM((rows, width), BF16)],
        "mlp", 6 * folds * mac, n2, cot, resid, vec, bup, far, far)
    if by_hand:
        down_first = scatter_first(core, down_keep, scatter_core(down_send))
        up_first = scatter_first(core, up_keep, scatter_core(up_send))
        gtwo = after(gtwo, down_first[0], up_first[0])
    grads_spec = pl.BlockSpec((4, tile, width), lambda i, *me: (0, i, 0))
    grads, gresid, sum_back = call(
        attention_backward, (tiles,),
        [SMEM, tile_rows, tile_rows, tile_rows, lse_spec, tile_rows, tile_rows, tile_rows, vec_spec, square],
        [(grads_spec, shaped(4, rows, width)), high_rows, sums], [pltpu.VMEM((tile, width), BF16)],
        "attention_backward", 0, lengths, q, k, v, lse, cot, resid, gtwo, vec, wo)
    if by_hand:
        down_first, up_first = after((down_first, up_first), grads)
        hidden_second = scatter_second(*down_first, *up_first)
        gresid = after(gresid, hidden_second[0])
    sum_spec = whole_spec((8, width))
    pair_shape = (CHIPS // 4, 4, 4 * each + 16, side)
    tile_at = pl.BlockSpec((tile, width), lambda i, me: (jnp.minimum(i, tiles - 1), 0))
    tile_grads = pl.BlockSpec((4, tile, width), lambda i, me: (0, jnp.minimum(i, tiles - 1), 0))
    columns = pl.BlockSpec((1, rows, width), lambda i, me: (jnp.maximum(i - tiles, 0), 0, 0))
    gtok, sum_one, square_send, square_keep = call_with(
        me, projections_backward, tiles + 4,
        [tile_at, tile_at, vec_spec, tile_grads, square, square, square, full_rows, full_rows, columns, sum_spec, sum_spec,
         whole_spec((1, hidden))],
        [(tile_at, shaped(rows, width)), sums] + [(kept_spec(pair_shape), shaped(*pair_shape))] * 2, [],
        "projections_backward", 7 * mac,
        tokens, gresid, vec, grads, wq, wk, wv, n1, mixed, grads, sum_back, sum_down, sum_up)
    if by_hand:
        square_send = after(square_send, hidden_second[1])
        square_take = scatter_core(square_send)
        hidden_layers = scatter_layers(*hidden_second)
        square_keep = after(square_keep, hidden_layers[0])
        square_first = scatter_first(core, square_keep, square_take)
        square_second = scatter_second(*square_first)
        hidden_layers = after(hidden_layers, square_second[0])
        g_down, up_keep, up_send = scatter_last(core, hidden_layers, own, halves, deep)
        up_take = scatter_core(up_send)
        square_second = after(square_second, g_down)
        square_layers = scatter_layers(*square_second)
        square_keep, square_send, flat = scatter_last(core, square_layers, own, 4, 0)
        square_take = scatter_core(square_send)
        outs = [(VMEM_SPEC, shaped(own, hidden, dtype=F32))] + [(VMEM_SPEC, shaped(own, width, dtype=F32))] * 4
        outs += [(VMEM_SPEC, shaped(own, dtype=F32))] * 8 + [(VMEM_SPEC, shaped(folds * own, dtype=F32))]
        g_up, g_q, g_k, g_v, g_o, *g_flat, g_ub = small_call(
            finish, (me, up_keep, up_take, square_keep, square_take, flat), outs, "finish", ins=[SMEM] + [VMEM_SPEC] * 5)
    else:
        flat = jnp.concatenate((sum_one[0:2], sum_back[0:5], sum_down[0:1]), axis=0)
        flat = flat.reshape(8, count, own).transpose(1, 0, 2).reshape(count, 8 * own)
        flat = jnp.concatenate((flat, sum_up.reshape(count, folds * own)), axis=1)
        g_down, g_up, g_q, g_k, g_v, g_o, flat = reduce_plain(
            (down_keep, down_send), (up_keep, up_send), (square_keep, square_send), flat)
        g_flat = [flat[index * own : (index + 1) * own] for index in range(8)]
        g_ub = flat[8 * own :]
    g_gain, g_shift, g_qb, g_vb, g_ob, g_mg, g_ms, g_db = g_flat
    return (out, gtok, g_gain, g_shift, g_q, g_qb, g_k, g_v, g_vb, g_o, g_ob, g_mg, g_ms, g_up, g_ub, g_down, g_db)


def solution(mesh):
    rows, flat = P("dp", None), P("dp")
    return jax.shard_map(
        body,
        mesh=mesh,
        in_specs=(rows, rows, flat, flat, rows, flat, rows, rows, flat, rows, flat, flat, flat, rows, flat, rows, flat, rows),
        out_specs=(rows, rows, flat, flat, rows, flat, rows, rows, flat, rows, flat, flat, flat, rows, flat, rows, flat),
        check_vma=False,
    )
```

time: 345 us -> 283 us (0.82)
  Pallas kernels: 173 us -> 137 us
  starting transfers between devices: 34.7 us -> 24.2 us
  local copies, waits for them, and re-layouts: 11.6 us -> 2.07 us
  waiting for transfers between devices: 109 us -> 103 us
    pallas_call x4 -> x3, Pallas kernels: 91.4 us -> 69.9 us  [call_with(): pl.pallas_call(kernel, grid_spec=pltpu.PrefetchScalarGridSpec(num_scalar_...]
    all_gather x1, waiting for transfers between devices: 22.4 us -> 4.18 us  [gather_by_hand(): lax.all_gather(far, 'dp', axis=0, tiled=True)]
    ppermute x34 -> x27, waiting for transfers between devices: 86.2 us -> 99.1 us  [swap(): return lax.ppermute(array, 'dp', flipped(lax.axis_size('dp'), change))]
    ppermute x34 -> x27, starting transfers between devices: 34.6 us -> 24.2 us  [swap(): return lax.ppermute(array, 'dp', flipped(lax.axis_size('dp'), change))]
    unnamed x76 -> x14, local copies, waits for them, and re-layouts: 11.6 us -> 2.07 us
    pallas_call x6 -> x7, Pallas kernels: 59.6 us -> 51.9 us  [call(): pl.pallas_call(kernel, grid=grid, in_specs=ins, out_specs=out_specs, out_...]
    pallas_call x10 -> x7, Pallas kernels: 21.6 us -> 15.4 us  [small_call(): pl.pallas_call(kernel, in_specs=ins, out_specs=tuple((spec for spec, _ in...]
  transfers between devices with their start and end apart: 35 -> 28, of which waited for: 16 -> 17; matrix products, arithmetic and copies ran while one was open for 1% -> 0% of each run, Pallas kernels for 35% -> 29%
where the time goes in v3:
time: 283 us; the launch traced here: 282 us
  Pallas kernels  137 us (48%)
  waiting for transfers between devices  103 us (36%)
  starting transfers between devices  24.2 us (9%)
  between operations  14.2 us (5%)
    ppermute x27, waiting for transfers between devices, swap(): return lax.ppermute(array, 'dp', flipped(lax.axis_size('dp'), change))  99.1 us
    pallas_call x3, Pallas kernels, call_with(): pl.pallas_call(kernel, grid_spec=pltpu.PrefetchScalarGridSpec(num_scalar_...  69.9 us
    pallas_call x7, Pallas kernels, call(): pl.pallas_call(kernel, grid=grid, in_specs=ins, out_specs=out_specs, out_...  51.9 us
    ppermute x27, starting transfers between devices, swap(): return lax.ppermute(array, 'dp', flipped(lax.axis_size('dp'), change))  24.2 us
    pallas_call x7, Pallas kernels, small_call(): pl.pallas_call(kernel, in_specs=ins, out_specs=tuple((spec for spec, _ in...  15.4 us
  transfers between devices with their start and end apart: 28, of which 17 were waited for; matrix products, arithmetic and copies ran while one was open for 0% of the time, Pallas kernels for 29%

profile of v3, /device:TPU:0, one launch (start us, length us, event | category | flops | bytes accessed | tf_op | source)
XLA Modules:
  0.0 282.1 jit_solution(16162321088893831725)
XLA Ops:
  10.8 2.0 join_shards.1
  12.8 5.0 %collective-permute-start.3 = (bf16[208,384]{1,0:T(8,128)(2,1)}, bf16[208,384]{1,0:T(8,128)(2,1)S(1)}, u32[]{:S(2)}, u32[]{:S(2)}) collective-permute-start(bf16[208,384]{1,0:T(8,128)(2,1)} %get-tuple-element.104), channel_id=1, source_target_pairs={{0,24},{1,25},{2,26},{3,27},{4,28},{5,29},{6,30},{7,31},{8,16},{9,... | collective-permute-start | bytes 479240 | tf_op jit(solution)/shard_map/ppermute | solution.py:441
  18.5 4.6 %collective-permute-done.3 = bf16[208,384]{1,0:T(8,128)(2,1)S(1)} collective-permute-done((bf16[208,384]{1,0:T(8,128)(2,1)}, bf16[208,384]{1,0:T(8,128)(2,1)S(1)}, u32[]{:S(2)}, u32[]{:S(2)}) %collective-permute-start.3) | collective-permute-done | bytes 159776 | tf_op jit(solution)/shard_map/ppermute | solution.py:441
  23.1 14.8 %collective-permute-done.2 = bf16[208,384]{1,0:T(8,128)(2,1)S(1)} collective-permute-done((bf16[208,384]{1,0:T(8,128)(2,1)}, bf16[208,384]{1,0:T(8,128)(2,1)S(1)}, u32[]{:S(2)}, u32[]{:S(2)}) %collective-permute-start.2) | collective-permute-done | bytes 159776 | tf_op jit(solution)/shard_map/ppermute | solution.py:441
  38.9 2.5 collective-permute-start.6
  42.5 23.2 %collective-permute-done.6.refs_3_ = bf16[4,208,384]{2,1,0:T(8,128)(2,1)S(1)} collective-permute-done((bf16[4,208,384]{2,1,0:T(8,128)(2,1)S(1)}, bf16[4,208,384]{2,1,0:T(8,128)(2,1)S(1)}, u32[]{:S(2)}, u32[]{:S(2)}) %collective-permute-start.6) | collective-permute-done | bytes 639008 | tf_op jit(solution)/shard_map/ppermute | solution.py:441
  65.6 6.7 %collective-permute-done.5.refs_2_ = bf16[4,208,384]{2,1,0:T(8,128)(2,1)S(1)} collective-permute-done((bf16[4,208,384]{2,1,0:T(8,128)(2,1)S(1)}, bf16[4,208,384]{2,1,0:T(8,128)(2,1)S(1)}, u32[]{:S(2)}, u32[]{:S(2)}) %collective-permute-start.5) | collective-permute-done | bytes 639008 | tf_op jit(solution)/shard_map/ppermute | solution.py:441
  72.4 4.1 %collective-permute-done.4.refs_1_ = bf16[4,208,384]{2,1,0:T(8,128)(2,1)S(1)} collective-permute-done((bf16[4,208,384]{2,1,0:T(8,128)(2,1)S(1)}, bf16[4,208,384]{2,1,0:T(8,128)(2,1)S(1)}, u32[]{:S(2)}, u32[]{:S(2)}) %collective-permute-start.4) | collective-permute-done | bytes 639008 | tf_op jit(solution)/shard_map/ppermute | solution.py:441
  79.5 10.2 %project.1 = (bf16[1024,768]{1,0:T(8,128)(2,1)}, bf16[1024,768]{1,0:T(8,128)(2,1)}, bf16[1024,768]{1,0:T(8,128)(2,1)}, bf16[1024,768]{1,0:T(8,128)(2,1)}, bf16[7...) custom-call(s32[1]{0:T(128)} %bitcast.me_ref, ...), custom_call_target="tpu_custom_call" | custom-call | bytes 1 | tf_op jit(solution)/shard_map/project/pallas_call | solution.py:415
  89.7 14.3 %attention_forward.1 = (bf16[1024,768]{1,0:T(8,128)(2,1)}, f32[1024,128]{1,0:T(8,128)}, f32[1024,768]{1,0:T(8,128)}, bf16[1024,768]{1,0:T(8,128)(2,1)}, bf16[1024,768]{1,0:T(8,128)(2,1)}, /*index=5*/f32[8,768]{1,0:T(8,128)}) custom-call(s32[4,5]{1,0:T(4,128)} %lengths_ref.3, bf16[1024,768]{1,0:T(8,128)(2,1)} %x_ref.5, bf16[1024,768]{1,0:T(8,128)(2,1)} %grad_ref.1, ...), custom_call_target="tpu_custom_call" | custom-call | bytes 1 | tf_op jit(solution)/shard_map/attention_forward/pallas_call | solution.py:400
  104.0 4.2 %all-gather.2.cloned.1.call-done = bf16[6144,768]{1,0:T(8,128)(2,1)} async-done(((bf16[192,768]{1,0:T(8,128)(2,1)}), bf16[6144,768]{1,0:T(8,128)(2,1)}) %all-gather.2.cloned.1.call-update) | async-done | bytes 9437200 | tf_op jit(solution)/shard_map/all_gather | solution.py:554
  108.2 40.4 %mlp.1 = (bf16[1024,768]{1,0:T(8,128)(2,1)}, f32[1024,768]{1,0:T(8,128)}, bf16[4,4,96,768]{3,2,1,0:T(8,128)(2,1)}, bf16[4,4,96,768]{3,2,1,0:T(8,128)(2,1)}, bf16...) custom-call(s32[1]{0:T(128)} %bitcast.me_ref, ...), custom_call_target="tpu_custom_call" | custom-call | bytes 1 | tf_op jit(solution)/shard_map/mlp/pallas_call | solution.py:415
  149.2 4.4 %collective-permute-done.11.take_ref = bf16[4,4,96,768]{3,2,1,0:T(8,128)(2,1)} collective-permute-done((bf16[4,4,96,768]{3,2,1,0:T(8,128)(2,1)}, bf16[4,4,96,768]{3,2,1,0:T(8,128)(2,1)}, u32[]{:S(2)}, u32[]{:S(2)}) %collective-permute-start.11) | collective-permute-done | bytes 2359328 | tf_op jit(solution)/shard_map/ppermute | solution.py:441
  153.5 3.5 %merge_core.3 = (bf16[4,2,96,768]{3,2,1,0:T(8,128)(2,1)}, bf16[4,2,96,768]{3,2,1,0:T(8,128)(2,1)}) custom-call(s32[1]{0:T(128)S(6)} %and.5.core_ref, bf16[4,4,96,768]{3,2,1,0:T(8,128)(2,1)} %get-tuple-element.118.keep_ref, bf16[4,4,96,768]{3,2,1,0:T(8,128)(2,1)} %collective-permute-done.11.take_ref), custom_call_target="tpu_custom_call" | custom-call | bytes 1 | tf_op jit(solution)/shard_map/merge_core/pallas_call | solution.py:400
  158.5 3.6 %merge_core.4 = (bf16[8,2,48,768]{3,2,1,0:T(8,128)(2,1)}, bf16[8,2,48,768]{3,2,1,0:T(8,128)(2,1)}) custom-call(s32[1]{0:T(128)S(6)} %and.5.core_ref, bf16[8,4,48,768]{3,2,1,0:T(8,128)(2,1)} %bitcast.16, bf16[8,4,48,768]{3,2,1,0:T(8,128)(2,1)} %bitcast.8.take_ref), custom_call_target="tpu_custom_call" | custom-call | bytes 1 | tf_op jit(solution)/shard_map/merge_core/pallas_call | solution.py:400
  162.7 20.3 %attention_backward.1 = (bf16[4,1024,768]{2,1,0:T(8,128)(2,1)}, f32[1024,768]{1,0:T(8,128)}, f32[8,768]{1,0:T(8,128)}) custom-call(s32[4,5]{1,0:T(4,128)} %lengths_ref.3, bf16[1024,768]{1,0:T(8,128)(2,1)} %get-tuple-element.106.q_ref, bf16[1024,768]{1,0:T(8,128)(2,1)} %get-tuple-element.107.k_ref, bf16[1024,768]{1,0:T(8,128)(2,1)} %get-tuple-element.108.v_ref, ...), custom_call_target="tpu_custom_call" | custom-call | bytes 1 | tf_op jit(solution)/shard_map/attention_backward/pallas_call | solution.py:400
  183.0 3.2 %collective-permute-done.14 = bf16[8,2,48,768]{3,2,1,0:T(8,128)(2,1)} collective-permute-done((bf16[8,2,48,768]{3,2,1,0:T(8,128)(2,1)}, bf16[8,2,48,768]{3,2,1,0:T(8,128)(2,1)}, u32[]{:S(2)}, u32[]{:S(2)}) %collective-permute-start.14) | collective-permute-done | bytes 1179680 | tf_op jit(solution)/shard_map/ppermute | solution.py:441
  186.2 3.8 %merge_first.2 = (f32[4,192,768]{2,1,0:T(8,128)}, bf16[4,192,768]{2,1,0:T(8,128)(2,1)}) custom-call(bf16[1,4,2,96,768]{4,3,2,1,0:T(8,128)(2,1)} %bitcast.22, bf16[1,4,2,96,768]{4,3,2,1,0:T(8,128)(2,1)} %bitcast.10.refs_1_, bf16[2,4,2,48,768]{4,3,2,1,0:T(8,128)(2,1)} %bitcast.23, bf16[2,4,2,48,768]{4,3,2,1,0:T(8,128)(2,1)} %bitcast.11.refs_3_), custom_call_target="tpu_custom_call" | custom-call | flops 99999997952 | bytes 1 | tf_op jit(solution)/shard_map/merge_first/pallas_call | solution.py:400
  191.5 19.3 %projections_backward.1 = (bf16[1024,768]{1,0:T(8,128)(2,1)}, f32[8,768]{1,0:T(8,128)}, bf16[4,4,208,384]{3,2,1,0:T(8,128)(2,1)}, bf16[4,4,208,384]{3,2,1,0:T(8,128)(2,1)}) custom-call(s32[1]{0:T(128)} %bitcast.me_ref, bf16[1024,768]{1,0:T(8,128)(2,1)} %x_ref.5, f32[1024,768]{1,0:T(8,128)} %get-tuple-element.134.gresid_ref, ...), custom_call_target="tpu_custom_call" | custom-call | bytes 1 | tf_op jit(solution)/shard_map/projections_backward/pallas_call | solution.py:415
  210.8 3.1 %merge_second.2 = (f32[192,768]{1,0:T(8,128)}, bf16[192,768]{1,0:T(8,128)(2,1)}, bf16[192,768]{1,0:T(8,128)(2,1)}, bf16[192,768]{1,0:T(8,128)(2,1)}) custom-call(f32[4,192,768]{2,1,0:T(8,128)} %get-tuple-element.133.own_ref, bf16[4,192,768]{2,1,0:T(8,128)(2,1)} %collective-permute-done.15.take_ref), custom_call_target="tpu_custom_call" | custom-call | bytes 1 | tf_op jit(solution)/shard_map/merge_second/pallas_call | solution.py:524
  214.0 2.0 collective-permute-done.19.take_ref
  216.0 3.7 %merge_core.5 = (bf16[4,2,208,384]{3,2,1,0:T(8,128)(2,1)}, bf16[4,2,208,384]{3,2,1,0:T(8,128)(2,1)}) custom-call(s32[1]{0:T(128)S(6)} %and.5.core_ref, bf16[4,4,208,384]{3,2,1,0:T(8,128)(2,1)} %get-tuple-element.150.keep_ref, bf16[4,4,208,384]{3,2,1,0:T(8,128)(2,1)} %collective-permute-done.19.take_ref), custom_call_target="tpu_custom_call" | custom-call | bytes 1 | tf_op jit(solution)/shard_map/merge_core/pallas_call | solution.py:400
  224.6 12.6 %collective-permute-done.20 = bf16[4,2,208,384]{3,2,1,0:T(8,128)(2,1)} collective-permute-done((bf16[4,2,208,384]{3,2,1,0:T(8,128)(2,1)}, bf16[4,2,208,384]{3,2,1,0:T(8,128)(2,1)}, u32[]{:S(2)}, u32[]{:S(2)}) %collective-permute-start.20) | collective-permute-done | bytes 1277984 | tf_op jit(solution)/shard_map/ppermute | solution.py:441
  237.3 2.7 merge_first.3
  240.5 5.0 %collective-permute-done.17.b_ref = bf16[192,768]{1,0:T(8,128)(2,1)} collective-permute-done((bf16[192,768]{1,0:T(8,128)(2,1)}, bf16[192,768]{1,0:T(8,128)(2,1)}, u32[]{:S(2)}, u32[]{:S(2)}) %collective-permute-start.17) | collective-permute-done | bytes 294944 | tf_op jit(solution)/shard_map/ppermute | solution.py:441
  245.5 2.2 merge_last.2
  247.7 3.0 %collective-permute-done.22.take_ref = bf16[4,208,384]{2,1,0:T(8,128)(2,1)} collective-permute-done((bf16[4,208,384]{2,1,0:T(8,128)(2,1)}, bf16[4,208,384]{2,1,0:T(8,128)(2,1)}, u32[]{:S(2)}, u32[]{:S(2)}) %collective-permute-start.22) | collective-permute-done | bytes 639008 | tf_op jit(solution)/shard_map/ppermute | solution.py:441
  250.7 2.4 merge_second.3
  253.0 2.5 collective-permute-start.23
  257.9 2.8 %collective-permute-done.23.a_ref = bf16[208,384]{1,0:T(8,128)(2,1)} collective-permute-done((bf16[208,384]{1,0:T(8,128)(2,1)}, bf16[208,384]{1,0:T(8,128)(2,1)}, u32[]{:S(2)}, u32[]{:S(2)}) %collective-permute-start.23) | collective-permute-done | bytes 159776 | tf_op jit(solution)/shard_map/ppermute | solution.py:441
  260.7 8.8 %collective-permute-done.24.b_ref = bf16[208,384]{1,0:T(8,128)(2,1)} collective-permute-done((bf16[208,384]{1,0:T(8,128)(2,1)}, bf16[208,384]{1,0:T(8,128)(2,1)}, u32[]{:S(2)}, u32[]{:S(2)}) %collective-permute-start.24) | collective-permute-done | bytes 159776 | tf_op jit(solution)/shard_map/ppermute | solution.py:441
  273.2 2.0 finish.1
  (57 shorter events, 24.9 us)
Async XLA Ops:
  7.2 101.0 %all-gather.2.cloned.1.call-start = ((), (), s32[]{:S(2)}) async-start(), calls=%async_computation | async-start | bytes 9732096 | tf_op jit(solution)/shard_map/all_gather | solution.py:554
  9.0 1.8 collective-permute-start
  12.8 10.2 %collective-permute-start.3 = (bf16[208,384]{1,0:T(8,128)(2,1)}, bf16[208,384]{1,0:T(8,128)(2,1)S(1)}, u32[]{:S(2)}, u32[]{:S(2)}) collective-permute-start(bf16[208,384]{1,0:T(8,128)(2,1)} %get-tuple-element.104), channel_id=1, source_target_pairs={{0,24},{1,25},{2,26},{3,27},{4,28},{5,29},{6,30},{7,31},{8,16},{9,... | collective-permute-start | bytes 479240 | tf_op jit(solution)/shard_map/ppermute | solution.py:441
  17.9 20.0 %collective-permute-start.2 = (bf16[208,384]{1,0:T(8,128)(2,1)}, bf16[208,384]{1,0:T(8,128)(2,1)S(1)}, u32[]{:S(2)}, u32[]{:S(2)}) collective-permute-start(bf16[208,384]{1,0:T(8,128)(2,1)} %get-tuple-element.104), channel_id=1, source_target_pairs={{0,16},{1,17},{2,18},{3,19},{4,20},{5,21},{6,22},{7,23},{8,24},{9,... | collective-permute-start | bytes 479240 | tf_op jit(solution)/shard_map/ppermute | solution.py:441
  17.9 20.0 %collective-permute-start.1 = (bf16[208,384]{1,0:T(8,128)(2,1)}, bf16[208,384]{1,0:T(8,128)(2,1)S(1)}, u32[]{:S(2)}, u32[]{:S(2)}) collective-permute-start(bf16[208,384]{1,0:T(8,128)(2,1)} %get-tuple-element.104), channel_id=1, source_target_pairs={{0,8},{1,9},{2,10},{3,11},{4,12},{5,13},{6,14},{7,15},{8,0},{9,1},... | collective-permute-start | bytes 479240 | tf_op jit(solution)/shard_map/ppermute | solution.py:441
  38.9 3.6 %copy-start = (bf16[4,208,384]{2,1,0:T(8,128)(2,1)}, bf16[4,208,384]{2,1,0:T(8,128)(2,1)S(1)}, u32[]{:S(2)}) copy-start(bf16[4,208,384]{2,1,0:T(8,128)(2,1)S(1)} %pad_maximum_fusion.refs_0_) | copy-start | bytes 1916932
  38.9 26.8 %collective-permute-start.6 = (bf16[4,208,384]{2,1,0:T(8,128)(2,1)S(1)}, bf16[4,208,384]{2,1,0:T(8,128)(2,1)S(1)}, u32[]{:S(2)}, u32[]{:S(2)}) collective-permute-start(bf16[4,208,384]{2,1,0:T(8,128)(2,1)S(1)} %pad_maximum_fusion.refs_0_), channel_id=1, source_target_pairs={{0,6},{1,7},{2,4},{3,5},{4,2},{5,3},{6,0},{7,1},{8,14},{9,15},{10,... | collective-permute-start | bytes 1916936 | tf_op jit(solution)/shard_map/ppermute | solution.py:441
  41.4 30.9 %collective-permute-start.5 = (bf16[4,208,384]{2,1,0:T(8,128)(2,1)S(1)}, bf16[4,208,384]{2,1,0:T(8,128)(2,1)S(1)}, u32[]{:S(2)}, u32[]{:S(2)}) collective-permute-start(bf16[4,208,384]{2,1,0:T(8,128)(2,1)S(1)} %pad_maximum_fusion.refs_0_), channel_id=1, source_target_pairs={{0,4},{1,5},{2,6},{3,7},{4,0},{5,1},{6,2},{7,3},{8,12},{9,13},{10,... | collective-permute-start | bytes 1916936 | tf_op jit(solution)/shard_map/ppermute | solution.py:441
  41.9 34.6 %collective-permute-start.4 = (bf16[4,208,384]{2,1,0:T(8,128)(2,1)S(1)}, bf16[4,208,384]{2,1,0:T(8,128)(2,1)S(1)}, u32[]{:S(2)}, u32[]{:S(2)}) collective-permute-start(bf16[4,208,384]{2,1,0:T(8,128)(2,1)S(1)} %pad_maximum_fusion.refs_0_), channel_id=1, source_target_pairs={{0,2},{1,3},{2,0},{3,1},{4,6},{5,7},{6,4},{7,5},{8,10},{9,11},{10,... | collective-permute-start | bytes 1916936 | tf_op jit(solution)/shard_map/ppermute | solution.py:441
  42.4 34.0 %collective-permute-start.7 = (bf16[4,208,384]{2,1,0:T(8,128)(2,1)S(1)}, bf16[4,208,384]{2,1,0:T(8,128)(2,1)S(1)}, u32[]{:S(2)}, u32[]{:S(2)}) collective-permute-start(bf16[4,208,384]{2,1,0:T(8,128)(2,1)S(1)} %pad_maximum_fusion.refs_0_), channel_id=1, source_target_pairs={{0,1},{1,0},{2,3},{3,2},{4,5},{5,4},{6,7},{7,6},{8,9},{9,8},{10,11... | collective-permute-start | bytes 1916936 | tf_op jit(solution)/shard_map/ppermute | solution.py:441
  65.6 10.9 %copy-start.1 = (bf16[4,208,384]{2,1,0:T(8,128)(2,1)}, bf16[4,208,384]{2,1,0:T(8,128)(2,1)S(1)}, u32[]{:S(2)}) copy-start(bf16[4,208,384]{2,1,0:T(8,128)(2,1)S(1)} %collective-permute-done.6.refs_3_) | copy-start | bytes 1916932
  65.6 10.9 %collective-permute-start.10 = (bf16[4,208,384]{2,1,0:T(8,128)(2,1)S(1)}, bf16[4,208,384]{2,1,0:T(8,128)(2,1)S(1)}, u32[]{:S(2)}, u32[]{:S(2)}) collective-permute-start(bf16[4,208,384]{2,1,0:T(8,128)(2,1)S(1)} %collective-permute-done.6.refs_3_), channel_id=1, source_target_pairs={{0,1},{1,0},{2,3},{3,2},{4,5},{5,4},{6,7},{7,6},{8,9},{9,8},{10,11... | collective-permute-start | bytes 1916936 | tf_op jit(solution)/shard_map/ppermute | solution.py:441
  72.4 4.2 %copy-start.2 = (bf16[4,208,384]{2,1,0:T(8,128)(2,1)}, bf16[4,208,384]{2,1,0:T(8,128)(2,1)S(1)}, u32[]{:S(2)}) copy-start(bf16[4,208,384]{2,1,0:T(8,128)(2,1)S(1)} %collective-permute-done.5.refs_2_) | copy-start | bytes 1916932
  72.4 4.2 %collective-permute-start.9 = (bf16[4,208,384]{2,1,0:T(8,128)(2,1)S(1)}, bf16[4,208,384]{2,1,0:T(8,128)(2,1)S(1)}, u32[]{:S(2)}, u32[]{:S(2)}) collective-permute-start(bf16[4,208,384]{2,1,0:T(8,128)(2,1)S(1)} %collective-permute-done.5.refs_2_), channel_id=1, source_target_pairs={{0,1},{1,0},{2,3},{3,2},{4,5},{5,4},{6,7},{7,6},{8,9},{9,8},{10,11... | collective-permute-start | bytes 1916936 | tf_op jit(solution)/shard_map/ppermute | solution.py:441
  76.5 3.0 %collective-permute-start.8 = (bf16[4,208,384]{2,1,0:T(8,128)(2,1)S(1)}, bf16[4,208,384]{2,1,0:T(8,128)(2,1)}, u32[]{:S(2)}, u32[]{:S(2)}) collective-permute-start(bf16[4,208,384]{2,1,0:T(8,128)(2,1)S(1)} %collective-permute-done.4.refs_1_), channel_id=1, source_target_pairs={{0,1},{1,0},{2,3},{3,2},{4,5},{5,4},{6,7},{7,6},{8,9},{9,8},{10,11... | collective-permute-start | bytes 1916936 | tf_op jit(solution)/shard_map/ppermute | solution.py:441
  76.5 1.2 copy-start.5
  148.6 4.9 %collective-permute-start.11 = (bf16[4,4,96,768]{3,2,1,0:T(8,128)(2,1)}, bf16[4,4,96,768]{3,2,1,0:T(8,128)(2,1)}, u32[]{:S(2)}, u32[]{:S(2)}) collective-permute-start(bf16[4,4,96,768]{3,2,1,0:T(8,128)(2,1)} %get-tuple-element.119), channel_id=1, source_target_pairs={{0,1},{1,0},{2,3},{3,2},{4,5},{5,4},{6,7},{7,6},{8,9},{9,8},{10,11... | collective-permute-start | bytes 7077896 | tf_op jit(solution)/shard_map/ppermute | solution.py:441
  148.9 9.6 %collective-permute-start.12 = (bf16[2,4,4,48,768]{4,3,2,1,0:T(8,128)(2,1)}, bf16[2,4,4,48,768]{4,3,2,1,0:T(8,128)(2,1)}, u32[]{:S(2)}, u32[]{:S(2)}) collective-permute-start(bf16[2,4,4,48,768]{4,3,2,1,0:T(8,128)(2,1)} %get-tuple-element.122), channel_id=1, source_target_pairs={{0,1},{1,0},{2,3},{3,2},{4,5},{5,4},{6,7},{7,6},{8,9},{9,8},{10,11... | collective-permute-start | bytes 7077896 | tf_op jit(solution)/shard_map/ppermute | solution.py:441
  157.1 26.0 %collective-permute-start.13 = (bf16[4,2,96,768]{3,2,1,0:T(8,128)(2,1)}, bf16[4,2,96,768]{3,2,1,0:T(8,128)(2,1)}, u32[]{:S(2)}, u32[]{:S(2)}) collective-permute-start(bf16[4,2,96,768]{3,2,1,0:T(8,128)(2,1)} %get-tuple-element.126), channel_id=1, source_target_pairs={{0,2},{1,5},{2,0},{3,7},{4,6},{5,1},{6,4},{7,3},{8,10},{9,13},{10,... | collective-permute-start | bytes 3538952 | tf_op jit(solution)/shard_map/ppermute | solution.py:441
  162.1 24.1 %collective-permute-start.14 = (bf16[8,2,48,768]{3,2,1,0:T(8,128)(2,1)}, bf16[8,2,48,768]{3,2,1,0:T(8,128)(2,1)}, u32[]{:S(2)}, u32[]{:S(2)}) collective-permute-start(bf16[8,2,48,768]{3,2,1,0:T(8,128)(2,1)} %get-tuple-element.127), channel_id=1, source_target_pairs={{0,2},{1,5},{2,0},{3,7},{4,6},{5,1},{6,4},{7,3},{8,10},{9,13},{10,... | collective-permute-start | bytes 3538952 | tf_op jit(solution)/shard_map/ppermute | solution.py:441
  190.0 20.8 %collective-permute-start.15 = (bf16[4,192,768]{2,1,0:T(8,128)(2,1)}, bf16[4,192,768]{2,1,0:T(8,128)(2,1)}, u32[]{:S(2)}, u32[]{:S(2)}) collective-permute-start(bf16[4,192,768]{2,1,0:T(8,128)(2,1)} %get-tuple-element.144), channel_id=1, source_target_pairs={{0,4},{1,3},{2,6},{3,1},{4,0},{5,7},{6,2},{7,5},{8,12},{9,11},{10,... | collective-permute-start | bytes 3538952 | tf_op jit(solution)/shard_map/ppermute | solution.py:441
  210.8 5.2 %collective-permute-start.19 = (bf16[4,4,208,384]{3,2,1,0:T(8,128)(2,1)}, bf16[4,4,208,384]{3,2,1,0:T(8,128)(2,1)}, u32[]{:S(2)}, u32[]{:S(2)}) collective-permute-start(bf16[4,4,208,384]{3,2,1,0:T(8,128)(2,1)} %get-tuple-element.152), channel_id=1, source_target_pairs={{0,1},{1,0},{2,3},{3,2},{4,5},{5,4},{6,7},{7,6},{8,9},{9,8},{10,11... | collective-permute-start | bytes 7667720 | tf_op jit(solution)/shard_map/ppermute | solution.py:441
  219.7 17.6 %collective-permute-start.20 = (bf16[4,2,208,384]{3,2,1,0:T(8,128)(2,1)}, bf16[4,2,208,384]{3,2,1,0:T(8,128)(2,1)}, u32[]{:S(2)}, u32[]{:S(2)}) collective-permute-start(bf16[4,2,208,384]{3,2,1,0:T(8,128)(2,1)} %get-tuple-element.154), channel_id=1, source_target_pairs={{0,2},{1,5},{2,0},{3,7},{4,6},{5,1},{6,4},{7,3},{8,10},{9,13},{10,... | collective-permute-start | bytes 3833864 | tf_op jit(solution)/shard_map/ppermute | solution.py:441
  220.2 20.3 %collective-permute-start.16 = (bf16[192,768]{1,0:T(8,128)(2,1)}, bf16[192,768]{1,0:T(8,128)(2,1)}, u32[]{:S(2)}, u32[]{:S(2)}) collective-permute-start(bf16[192,768]{1,0:T(8,128)(2,1)} %get-tuple-element.146), channel_id=1, source_target_pairs={{0,8},{1,9},{2,10},{3,11},{4,12},{5,13},{6,14},{7,15},{8,0},{9,1},... | collective-permute-start | bytes 884744 | tf_op jit(solution)/shard_map/ppermute | solution.py:441
  221.7 23.8 %collective-permute-start.17 = (bf16[192,768]{1,0:T(8,128)(2,1)}, bf16[192,768]{1,0:T(8,128)(2,1)}, u32[]{:S(2)}, u32[]{:S(2)}) collective-permute-start(bf16[192,768]{1,0:T(8,128)(2,1)} %get-tuple-element.147), channel_id=1, source_target_pairs={{0,16},{1,17},{2,18},{3,19},{4,20},{5,21},{6,22},{7,23},{8,24},{9,... | collective-permute-start | bytes 884744 | tf_op jit(solution)/shard_map/ppermute | solution.py:441
  222.7 22.8 %collective-permute-start.18 = (bf16[192,768]{1,0:T(8,128)(2,1)}, bf16[192,768]{1,0:T(8,128)(2,1)}, u32[]{:S(2)}, u32[]{:S(2)}) collective-permute-start(bf16[192,768]{1,0:T(8,128)(2,1)} %get-tuple-element.148), channel_id=1, source_target_pairs={{0,24},{1,25},{2,26},{3,27},{4,28},{5,29},{6,30},{7,31},{8,16},{9,... | collective-permute-start | bytes 884744 | tf_op jit(solution)/shard_map/ppermute | solution.py:441
  239.9 10.7 %collective-permute-start.22 = (bf16[4,208,384]{2,1,0:T(8,128)(2,1)}, bf16[4,208,384]{2,1,0:T(8,128)(2,1)}, u32[]{:S(2)}, u32[]{:S(2)}) collective-permute-start(bf16[4,208,384]{2,1,0:T(8,128)(2,1)} %get-tuple-element.162), channel_id=1, source_target_pairs={{0,4},{1,3},{2,6},{3,1},{4,0},{5,7},{6,2},{7,5},{8,12},{9,11},{10,... | collective-permute-start | bytes 1916936 | tf_op jit(solution)/shard_map/ppermute | solution.py:441
  253.0 7.7 %collective-permute-start.23 = (bf16[208,384]{1,0:T(8,128)(2,1)}, bf16[208,384]{1,0:T(8,128)(2,1)}, u32[]{:S(2)}, u32[]{:S(2)}) collective-permute-start(bf16[208,384]{1,0:T(8,128)(2,1)} %get-tuple-element.167), channel_id=1, source_target_pairs={{0,8},{1,9},{2,10},{3,11},{4,12},{5,13},{6,14},{7,15},{8,0},{9,1},... | collective-permute-start | bytes 479240 | tf_op jit(solution)/shard_map/ppermute | solution.py:441
  255.5 14.0 %collective-permute-start.24 = (bf16[208,384]{1,0:T(8,128)(2,1)}, bf16[208,384]{1,0:T(8,128)(2,1)}, u32[]{:S(2)}, u32[]{:S(2)}) collective-permute-start(bf16[208,384]{1,0:T(8,128)(2,1)} %get-tuple-element.168), channel_id=1, source_target_pairs={{0,16},{1,17},{2,18},{3,19},{4,20},{5,21},{6,22},{7,23},{8,24},{9,... | collective-permute-start | bytes 479240 | tf_op jit(solution)/shard_map/ppermute | solution.py:441
  256.0 13.6 %collective-permute-start.25 = (bf16[208,384]{1,0:T(8,128)(2,1)}, bf16[208,384]{1,0:T(8,128)(2,1)}, u32[]{:S(2)}, u32[]{:S(2)}) collective-permute-start(bf16[208,384]{1,0:T(8,128)(2,1)} %get-tuple-element.169), channel_id=1, source_target_pairs={{0,24},{1,25},{2,26},{3,27},{4,28},{5,29},{6,30},{7,31},{8,16},{9,... | collective-permute-start | bytes 479240 | tf_op jit(solution)/shard_map/ppermute | solution.py:441
  257.9 13.6 %collective-permute-start.21 = (f32[2,24,768]{2,1,0:T(8,128)}, f32[2,24,768]{2,1,0:T(8,128)}, u32[]{:S(2)}, u32[]{:S(2)}) collective-permute-start(f32[2,24,768]{2,1,0:T(8,128)} %get-tuple-element.161), channel_id=1, source_target_pairs={{0,1},{1,0},{2,3},{3,2},{4,5},{5,4},{6,7},{7,6},{8,9},{9,8},{10,11... | collective-permute-start | bytes 442376 | tf_op jit(solution)/shard_map/ppermute | solution.py:441
  271.5 1.7 collective-permute-start.26
  (3 other events, 2.8 us)
Sparse Core Ops, SparseCore 0:
  12.9 95.2 all-gather.1

commit v4 on v3

--- a/solution.py
+++ b/solution.py
@@ -95,10 +95,12 @@
             ).start()
 
 
-def project(me_ref, x_ref, *refs):
+def project(me_ref, lengths_ref, x_ref, grad_ref, *refs):
     sources = refs[:8]
-    n1_ref, q_ref, k_ref, v_ref, wq_ref, wk_ref, wv_ref, wo_ref, vec_ref, bup_ref, parts_ref, sem = refs[8:]
+    n1_ref, q_ref, k_ref, v_ref, cot_ref, dsum_ref = refs[8:14]
+    wq_ref, wk_ref, wv_ref, wo_ref, vec_ref, bup_ref, parts_ref, sem = refs[14:]
     weights = (wq_ref, wk_ref, wv_ref, wo_ref)
+    core = me_ref[0] & 1
 
     @pl.when(pl.program_id(0) == 0)
     def _():
@@ -106,29 +108,41 @@
         for number, ref in enumerate(weights + (parts_ref,)):
             pltpu.make_async_copy(ref, ref, sem.at[number]).wait()
         count, _, side = parts_ref.shape
-        parts = [parts_ref[device].astype(F32) for device in range(count)]
         group = count // 2
-        vec_ref[...] = jnp.concatenate((sum(parts[:group]), sum(parts[group:])), axis=1)
+        halves = [sum(parts_ref[half * group + index].astype(F32) for index in range(group)) for half in range(2)]
+        vec_ref[...] = jnp.concatenate(halves, axis=1)
         blocks = bup_ref.shape[1] // side
-        group = count // blocks
+        group = CHIPS // blocks
         for block in range(blocks):
-            rows = sum(parts[block * group : (block + 1) * group])
+            rows = sum(parts_ref[2 * (block * group + index) + core].astype(F32) for index in range(group))
             bup_ref[:, block * side : (block + 1) * side] = rows[8:9]
 
-    project_rows(x_ref, vec_ref, wq_ref, wk_ref, wv_ref, n1_ref, q_ref, k_ref, v_ref)
-
-
-def project_rows(x_ref, vec_ref, wq_ref, wk_ref, wv_ref, n1_ref, q_ref, k_ref, v_ref):
+    project_rows(lengths_ref, x_ref, grad_ref, vec_ref, wq_ref, wk_ref, wv_ref, n1_ref, q_ref, k_ref, v_ref, cot_ref, dsum_ref)
+
+
+def project_rows(lengths_ref, x_ref, grad_ref, vec_ref, wq_ref, wk_ref, wv_ref,
+                 n1_ref, q_ref, k_ref, v_ref, cot_ref, dsum_ref):
+    tile = pl.program_id(0)
+    rows = x_ref.shape[0]
+    slots = lengths_ref.shape[1]
     hat, _ = normalize(x_ref[...].astype(F32))
     n1 = (hat * vec_ref[0:1, :] + vec_ref[1:2, :]).astype(BF16)
     n1_ref[...] = n1
     q_ref[...] = (dot_nn(n1, wq_ref[...]) + vec_ref[2:3, :]).astype(BF16) * jnp.asarray(SCALE, BF16)
     k_ref[...] = dot_nn(n1, wk_ref[...]).astype(BF16)
     v_ref[...] = (dot_nn(n1, wv_ref[...]) + vec_ref[3:4, :]).astype(BF16)
-
-
-def attention_forward(lengths_ref, x_ref, grad_ref, vec_ref, q_ref, k_ref, v_ref, wo_ref,
-                      mixed_ref, lse_ref, resid_ref, n2_ref, cot_ref, dsum_ref):
+    valid = segments(lengths_ref, tile, slots, rows, 0) < slots
+    cot = jnp.where(valid, grad_ref[...].astype(F32), 0.0)
+    cot_ref[...] = cot.astype(BF16)
+
+    @pl.when(tile == 0)
+    def _():
+        dsum_ref[...] = jnp.zeros_like(dsum_ref)
+
+    dsum_ref[0:1, :] += column_sum(cot)
+
+
+def attention_forward(lengths_ref, x_ref, vec_ref, q_ref, k_ref, v_ref, wo_ref, mixed_ref, lse_ref, resid_ref, n2_ref):
     tile = pl.program_id(0)
     rows = q_ref.shape[0]
     slots = lengths_ref.shape[1]
@@ -169,15 +183,6 @@
     resid_ref[...] = resid
     hat, _ = normalize(resid)
     n2_ref[...] = (hat * vec_ref[5:6, :] + vec_ref[6:7, :]).astype(BF16)
-    valid = segments(lengths_ref, tile, slots, rows, 0) < slots
-    cot = jnp.where(valid, grad_ref[...].astype(F32), 0.0)
-    cot_ref[...] = cot.astype(BF16)
-
-    @pl.when(tile == 0)
-    def _():
-        dsum_ref[...] = jnp.zeros_like(dsum_ref)
-
-    dsum_ref[0:1, :] += column_sum(cot)
 
 
 def flat_rows(ref):
@@ -191,23 +196,41 @@
         put((chip & 3) ^ plane, (chip >> 2) ^ layer, rows[chip * each : (chip + 1) * each].astype(BF16))
 
 
-def mlp(me_ref, n2_ref, cot_ref, resid_ref, vec_ref, bup_ref, wup_ref, wdown_ref,
-        out_ref, gtwo_ref, down_send_ref, down_keep_ref, up_send_ref, up_keep_ref, dbu_ref, acc, act_ref, gup_ref):
+def mlp(sets, me_ref, *refs):
+    n2_hbm, cot_hbm = refs[:sets], refs[sets : 2 * sets]
+    bup_ref, wup_ref, wdown_ref = refs[2 * sets : 2 * sets + 3]
+    refs = refs[2 * sets + 3 :]
+    out_hbm, gtwo_hbm, refs = refs[:sets], refs[sets : 2 * sets], refs[2 * sets :]
+    down_own, down_send, up_own, up_send, dbu_ref = refs[:5]
+    n2_ref, cot_ref, acc, gacc, act_ref, gup_ref, low_ref, gdown_ref, gupw_ref, in_sem, out_sem, grad_sem = refs[5:]
     step = pl.program_id(0)
-    steps = pl.num_programs(0)
+    last = pl.num_programs(0) - 1
     me = me_ref[0]
-    block = 256
-    chunks = [slice(start, start + block) for start in range(0, n2_ref.shape[0], block)]
+    rows = n2_ref.shape[0] // sets
+
+    def rows_of(index):
+        return pl.ds(pl.multiple_of(index * rows, rows), rows)
 
     @pl.when(step == 0)
     def _():
-        gtwo_ref[...] = jnp.zeros_like(gtwo_ref)
-        acc[...] = resid_ref[...] + vec_ref[7:8, :]
+        for index in range(sets):
+            at = pl.ds(index * rows, rows)
+            pltpu.make_async_copy(n2_hbm[index], n2_ref.at[at, :], in_sem.at[0, index]).start()
+            pltpu.make_async_copy(cot_hbm[index], cot_ref.at[at, :], in_sem.at[1, index]).start()
 
     wup = flat_rows(wup_ref)
     wdown = flat_rows(wdown_ref)
-    sums = jnp.zeros_like(dbu_ref)
-    for at in chunks:
+    dbu_ref[...] = jnp.zeros_like(dbu_ref)
+
+    @pl.loop(0, sets)
+    def _(index):
+        at = rows_of(index)
+
+        @pl.when(step == 0)
+        def _():
+            pltpu.make_async_copy(n2_ref.at[at, :], n2_ref.at[at, :], in_sem.at[0, index]).wait()
+            pltpu.make_async_copy(cot_ref.at[at, :], cot_ref.at[at, :], in_sem.at[1, index]).wait()
+
         pre = dot_nn(n2_ref[at, :], wup) + bup_ref[...]
         grad_act = dot_nt(cot_ref[at, :], wdown)
         square = pre * pre
@@ -217,44 +240,88 @@
         act_ref[at, :] = (pre * half).astype(BF16)
         gup = (grad_act * (half + (0.5 * pre) * (1.0 - tanh * tanh) * inner)).astype(BF16)
         gup_ref[at, :] = gup
-        sums = sums + column_sum(gup.astype(F32))
-    dbu_ref[...] = sums
-    for at in chunks:
-        acc[at, :] += dot_nn(act_ref[at, :], wdown)
-        gtwo_ref[at, :] += dot_nt(gup_ref[at, :], wup)
-
-    grad_down = dot_tn(act_ref[...], cot_ref[...])
-    first = (me & 1) == 0
-    plane = (me >> 1) & 3
-    deep = down_send_ref.shape[2]
-    for index in range(4):
-        low = grad_down[2 * deep * index : 2 * deep * index + deep]
-        high = grad_down[2 * deep * index + deep : 2 * deep * (index + 1)]
-        down_keep_ref[0, index ^ plane] = jnp.where(first, low, high).astype(BF16)
-        down_send_ref[0, index ^ plane] = jnp.where(first, high, low).astype(BF16)
-
-    grad_up = dot_tn(n2_ref[...], gup_ref[...])
-
-    def put_in(ref):
-        def put(plane, layer, piece):
-            ref[0, layer, plane] = piece
-
-        spread(me, grad_up, put)
-
-    @pl.when(step < steps // 2)
-    def _():
-        put_in(up_send_ref)
-
-    @pl.when(step >= steps // 2)
-    def _():
-        put_in(up_keep_ref)
-
-    @pl.when(step == steps - 1)
-    def _():
-        out_ref[...] = acc[...].astype(BF16)
-
-
-def attention_backward(lengths_ref, q_ref, k_ref, v_ref, lse_ref, cot_ref, resid_ref, gtwo_ref, vec_ref, wo_ref,
+        dbu_ref[...] += column_sum(gup.astype(F32))
+
+    @pl.when(step == 0)
+    def _():
+        @pl.loop(0, sets)
+        def _(index):
+            at = rows_of(index)
+            acc[at, :] = dot_nn(act_ref[at, :], wdown)
+            gacc[at, :] = dot_nt(gup_ref[at, :], wup)
+
+    @pl.when((step > 0) & (step < last))
+    def _():
+        @pl.loop(0, sets)
+        def _(index):
+            at = rows_of(index)
+            acc[at, :] += dot_nn(act_ref[at, :], wdown)
+            gacc[at, :] += dot_nt(gup_ref[at, :], wup)
+
+    def results():
+        for index in range(sets):
+            at = pl.ds(index * rows, rows)
+            yield pltpu.make_async_copy(low_ref.at[0, at, :], out_hbm[index], out_sem.at[0, index])
+            source = low_ref.at[1, at, :] if index else gacc.at[at, :]
+            yield pltpu.make_async_copy(source, gtwo_hbm[index], out_sem.at[1, index])
+
+    @pl.when(step == last)
+    def _():
+        @pl.loop(0, sets)
+        def _(index):
+            at = rows_of(index)
+            low_ref[0, at, :] = (acc[at, :] + dot_nn(act_ref[at, :], wdown)).astype(BF16)
+            total = gacc[at, :] + dot_nt(gup_ref[at, :], wup)
+            gacc[at, :] = total
+            low_ref[1, at, :] = total.astype(BF16)
+
+        for copy in results():
+            copy.start()
+
+    slot = lax.rem(step, 2)
+    gdown_ref[slot] = dot_tn(act_ref[...], cot_ref[...]).astype(BF16)
+    deep = down_own.shape[2]
+    count = gdown_ref.shape[1] // deep
+    for index in range(count):
+        chip = step * count + index
+        source = gdown_ref.at[slot, pl.ds(index * deep, deep), :]
+        keep_or_send(me, chip & 3, (chip >> 2) ^ (me >> 3), source, down_own, down_send, grad_sem, 0)
+
+    gupw_ref[slot] = dot_tn(n2_ref[...], gup_ref[...]).astype(BF16)
+    each = gupw_ref.shape[1] // CHIPS
+    for chip in range(CHIPS):
+        source = gupw_ref.at[slot, pl.ds(chip * each, each), :]
+        keep_or_send(
+            me, chip & 3, (chip >> 2) ^ (me >> 3), source, up_own.at[step], up_send.at[step], grad_sem, 2)
+
+    @pl.when(step == last)
+    def _():
+        for copy in results():
+            copy.wait()
+        for number, ref in enumerate((down_own, down_send, up_own, up_send)):
+            pltpu.make_async_copy(ref, ref, grad_sem.at[number]).wait()
+
+
+def keep_or_send(me, plane, layer, source, own_ref, send_ref, sem, number):
+    core = me & 1
+    relative = plane ^ ((me >> 1) & 3)
+    mine = (relative == 0) | (relative == 2 - core)
+
+    @pl.when(mine)
+    def _():
+        pltpu.make_async_copy(source, own_ref.at[layer, jnp.where(relative == 0, 0, 1)], sem.at[number]).start()
+
+    @pl.when(jnp.logical_not(mine))
+    def _():
+        pltpu.make_async_copy(source, send_ref.at[layer, jnp.where(relative == 3, 1, 0)], sem.at[number + 1]).start()
+
+
+def add_rows(resid_ref, vec_ref, a_ref, b_ref, out_ref):
+    total = resid_ref[...] + (a_ref[...].astype(F32) + b_ref[...].astype(F32) + vec_ref[7:8, :])
+    out_ref[...] = total.astype(BF16)
+
+
+def attention_backward(lengths_ref, q_ref, k_ref, v_ref, lse_ref, cot_ref, resid_ref, gtwo_ref, gother_ref, vec_ref, wo_ref,
                        grads_ref, gresid_ref, dsum_ref, gmix_ref):
     tile = pl.program_id(0)
     rows = q_ref.shape[0]
@@ -264,7 +331,7 @@
         dsum_ref[...] = jnp.zeros_like(dsum_ref)
 
     hat, inverse = normalize(resid_ref[...])
-    grad_two = gtwo_ref[...]
+    grad_two = gtwo_ref[...] + gother_ref[...].astype(F32)
     gresid = cot_ref[...].astype(F32) + norm_back(grad_two, vec_ref[5:6, :], hat, inverse)
     gresid_ref[...] = gresid
     gattn = gresid.astype(BF16)
@@ -365,10 +432,10 @@
             half = chip // (CHIPS // 2)
             block = chip * (sum_up_ref.shape[1] // side) // CHIPS
             last = jnp.broadcast_to(sum_up_ref[:, block * side : (block + 1) * side], (8, side))
-            rows = jnp.concatenate((vecs[:, half * side : (half + 1) * side], last), axis=0).astype(BF16)
+            short = vecs[:, half * side : (half + 1) * side]
             at = ((chip >> 2) ^ (me >> 3), (chip & 3) ^ ((me >> 1) & 3))
-            send_ref[at[0], at[1], 4 * each :, :] = rows
-            keep_ref[at[0], at[1], 4 * each :, :] = rows
+            keep_ref[at[0], at[1], 4 * each :, :] = jnp.concatenate((short, last), axis=0).astype(BF16)
+            send_ref[at[0], at[1], 4 * each :, :] = jnp.concatenate((short, jnp.zeros_like(last)), axis=0).astype(BF16)
 
 
 def rows_spec(block, width):
@@ -474,11 +541,15 @@
         rows = ref[...].astype(F32)
         put(index, rows[:, :side], rows[:, side:])
     up = u_ref[...].astype(F32)
-    folds = up.shape[1] // width
-    for part in range(folds):
-        low = part * side
-        high = (folds + part) * side
-        put(4 + part, up[:, low : low + side], up[:, high : high + side])
+    hidden = up.shape[1]
+    deep = hidden // (2 * CHIPS)
+    halves = [
+        jnp.concatenate([up[:, start : start + deep] for start in range(half * deep, hidden, 2 * deep)], axis=1)
+        for half in range(2)
+    ]
+    for part in range(hidden // width):
+        at = slice(part * side, (part + 1) * side)
+        put(4 + part, halves[0][:, at], halves[1][:, at])
 
 
 def join_shards(me_ref, keep_ref, take_ref, down_ref, *refs):
@@ -507,7 +578,7 @@
     rows.append(jnp.zeros((16 - len(rows), side), F32))
     rows = jnp.concatenate(rows, axis=0)
     short = pltpu.roll(rows, own * lax.rem(me, side // own), 1)
-    long = pltpu.roll(rows, folds * own * lax.rem(me, side // (folds * own)), 1)
+    long = pltpu.roll(rows, folds * own * lax.rem(me >> 1, side // (folds * own)), 1)
     index = lax.broadcasted_iota(jnp.int32, rows.shape, 0)
     near_ref[8 * own :, :] = jnp.where(index < 8, short, long).astype(BF16)
 
@@ -576,12 +647,12 @@
     whole = lax.all_gather(packed, "dp", axis=0, tiled=True).reshape(count, -1, width)
     square_all = [whole[:, index * own : (index + 1) * own, :].reshape(width, width) for index in range(4)]
     wup = whole[:, 4 * own : (4 + folds) * own, :].reshape(count, folds, own, width).transpose(0, 2, 1, 3)
-    wup = wup.reshape(CHIPS, width // CHIPS, 2, folds // 2, width).transpose(0, 2, 3, 1, 4).reshape(CHIPS, 2, -1, width)
+    wup = wup.reshape(CHIPS, width // CHIPS, 2, CHIPS // 2, 2, -1).transpose(0, 4, 2, 1, 3, 5).reshape(CHIPS, 2, -1, width)
     wdown = whole[:, (4 + folds) * own : (4 + 2 * folds) * own, :]
     wdown = wdown.reshape(CHIPS, 2, -1, width)
     last = whole[:, (4 + 2 * folds) * own, : flat.size].astype(F32)
     vec = last[:, : 8 * own].reshape(count, 8, own).transpose(1, 0, 2).reshape(8, width)
-    bup = last[:, 8 * own :].reshape(1, hidden)
+    bup = last[:, 8 * own :].reshape(CHIPS, 2, -1).transpose(1, 0, 2).reshape(2, 1, -1)
     return (*square_all, jnp.concatenate((wup, wdown), axis=2), jnp.pad(vec, ((0, 8), (0, 0))), bup)
 
 
@@ -646,14 +717,18 @@
         ref[:, :side] = jnp.where(first, keep, take)
         ref[:, side:] = jnp.where(first, take, keep)
     parts = up_keep_ref.shape[0]
+    deep = parts * width // CHIPS
     for part in range(parts):
         keep, take = up_keep_ref[part], up_take_ref[part]
-        up_ref[:, part * width : (part + 1) * width] = jnp.where(first, keep, take)
-        up_ref[:, (parts + part) * width : (parts + part + 1) * width] = jnp.where(first, take, keep)
+        low, high = jnp.where(first, keep, take), jnp.where(first, take, keep)
+        pieces = []
+        for start in range(0, width, deep):
+            pieces += [low[:, start : start + deep], high[:, start : start + deep]]
+        up_ref[:, 2 * width * part : 2 * width * (part + 1)] = jnp.concatenate(pieces, axis=1)
     flat = flat_ref[...]
     long = flats[-1].shape[0]
     short_turn = lax.rem(side - own * lax.rem(me, side // own), side)
-    long_turn = lax.rem(side - long * lax.rem(me, side // long), side)
+    long_turn = lax.rem(side - long * lax.rem(me >> 1, side // long), side)
     short = pltpu.roll(flat, short_turn, 1)
     for number, ref in enumerate(flats[:-1]):
         ref[...] = short[number, :own]
@@ -709,15 +784,22 @@
         functools.partial(merge_last, deep), (core, *pieces), outs, "merge_last", ins=[SMEM] + [VMEM_SPEC] * 4, flops=SHORT if deep else 0)
 
 
-def reduce_plain(down_pair, up_pair, square_pair, flat):
+def reduce_plain(down_pairs, up_pairs, square_pair, flat):
     def scattered(array, axis):
         return lax.psum_scatter(array, "dp", scatter_dimension=axis, tiled=True).astype(F32)
 
-    deep, width = down_pair[0].shape[2:]
-    down = jnp.stack(down_pair).transpose(1, 2, 0, 3, 4).reshape(-1, width)
-    up = jnp.stack(up_pair)
-    folds, each = up.shape[1], up.shape[4]
-    up = up.transpose(2, 3, 4, 0, 1, 5).reshape(CHIPS * each, 2 * folds * width)
+    def planes(own, send, core):
+        order = (own[..., 0, :, :], send[..., 0, :, :], own[..., 1, :, :], send[..., 1, :, :])
+        if core == 1:
+            order = (order[0], order[2], order[1], order[3])
+        return jnp.stack(order, axis=-3)
+
+    down = jnp.stack([planes(*pair, core) for core, pair in enumerate(down_pairs)])
+    up = jnp.stack([planes(*pair, core) for core, pair in enumerate(up_pairs)])
+    width = down.shape[-1]
+    each = up.shape[4]
+    down = down.transpose(1, 2, 0, 3, 4).reshape(-1, width)
+    up = up.reshape(2, 2, CHIPS, each, CHIPS // 2, -1).transpose(2, 3, 1, 4, 0, 5).reshape(CHIPS * each, -1)
     square = jnp.stack(square_pair).transpose(1, 2, 3, 0, 4)[:, :, : 4 * each]
     square = square.reshape(CHIPS, 4, each, width).transpose(1, 0, 2, 3).reshape(4, CHIPS * each, width)
     return (
@@ -752,59 +834,74 @@
     mac = 2 * rows * width * width
     kept_square = (kept_spec((width, width)), shaped(width, width))
     kept_vec = (kept_spec((16, width)), shaped(16, width, dtype=F32))
-    kept_hidden = (kept_spec((1, hidden)), shaped(1, hidden, dtype=F32))
+    kept_hidden = (kept_spec((1, hidden // 2)), shaped(1, hidden // 2, dtype=F32))
     side = width // 2
+    lengths_spec = SMEM
+    rows_outs = [low_rows] * 5 + [sums]
     if by_hand:
         near, far = gather_by_hand(me, weights, vectors)
-        n1, q, k, v, wq, wk, wv, wo, vec, bup = call_with(
-            me, project, tiles, [tile_rows] + [ANY_SPEC] * 8, [low_rows] * 4 + [kept_square] * 4 + [kept_vec, kept_hidden],
-            [pltpu.VMEM((count, 16, side), BF16), pltpu.SemaphoreType.DMA((5,))], "project", 0, tokens, *near)
+        n1, q, k, v, cot, sum_down, wq, wk, wv, wo, vec, bup = call_with(
+            me, project, tiles, [lengths_spec, tile_rows, tile_rows] + [ANY_SPEC] * 8,
+            rows_outs + [kept_square] * 4 + [kept_vec, kept_hidden],
+            [pltpu.VMEM((count, 16, side), BF16), pltpu.SemaphoreType.DMA((5,))], "project", 0,
+            lengths, tokens, grad_out, *near)
+        cot_other = swap(cot, other_core)
     else:
         wq, wk, wv, wo, far, vec, bup = gather_plain(weights, vectors)
-        n1, q, k, v = call(
-            project_rows, (tiles,), [tile_rows, vec_spec, square, square, square], [low_rows] * 4,
-            [], "project", 0, tokens, vec, wq, wk, wv)
+        n1, q, k, v, cot, sum_down = call(
+            project_rows, (tiles,), [lengths_spec, tile_rows, tile_rows, vec_spec, square, square, square], rows_outs,
+            [], "project", 0, lengths, tokens, grad_out, vec, wq, wk, wv)
     high_rows = (tile_rows, shaped(rows, width, dtype=F32))
-    mixed, lse, resid, n2, cot, sum_down = call(
-        attention_forward, (tiles,), [SMEM, tile_rows, tile_rows, vec_spec, tile_rows, tile_rows, tile_rows, square],
-        [low_rows, (lse_spec, shaped(rows, LANES, dtype=F32)), high_rows, low_rows, low_rows, sums],
-        [], "attention_forward", 0, lengths, tokens, grad_out, vec, q, k, v, wo)
-
-    halves = folds // 2
+    mixed, lse, resid, n2 = call(
+        attention_forward, (tiles,), [SMEM, tile_rows, vec_spec, tile_rows, tile_rows, tile_rows, square],
+        [low_rows, (lse_spec, shaped(rows, LANES, dtype=F32)), high_rows, low_rows],
+        [], "attention_forward", 0, lengths, tokens, vec, q, k, v, wo)
+
     each = width // CHIPS
     deep = hidden // (2 * CHIPS)
+    blocks = hidden // (2 * width)
     full_rows = whole_spec((rows, width))
-    kept_low = (kept_spec((rows, width)), shaped(rows, width))
-    kept_high = (kept_spec((rows, width)), shaped(rows, width, dtype=F32))
-
-    def turn(i, me):
-        return ((i // halves) ^ 1 ^ (me[0] & 1)) * halves + lax.rem(i, halves)
-
-    up_spec = pl.BlockSpec((CHIPS, 1, each, width), lambda i, me: (0, turn(i, me) // halves, lax.rem(turn(i, me), halves), 0))
-    down_spec = pl.BlockSpec((width // (2 * deep), 2, deep, width), lambda i, me: (turn(i, me), 0, 1, 0))
-    hidden_spec = pl.BlockSpec((1, width), lambda i, me: (0, turn(i, me)))
-    down_pair = (pl.BlockSpec((1, 4, deep, width), lambda i, me: (turn(i, me) ^ (me[0] >> 3), 0, 0, 0)), shaped(4, 4, deep, width))
-    part = (1, CHIPS // 4, 4, each, width)
-    up_shape = shaped(halves, *part[1:])
-    out, gtwo, down_send, down_keep, up_send, up_keep, sum_up = call_with(
-        me, mlp, folds,
-        [full_rows, full_rows, full_rows, vec_spec, hidden_spec, up_spec, down_spec],
-        [kept_low, kept_high, down_pair, down_pair,
-         (pl.BlockSpec(part, lambda i, me: (jnp.minimum(i, halves - 1), 0, 0, 0, 0)), up_shape),
-         (pl.BlockSpec(part, lambda i, me: (jnp.maximum(i - halves, 0), 0, 0, 0, 0)), up_shape),
-         (hidden_spec, shaped(1, hidden, dtype=F32))],
-        [pltpu.VMEM((rows, width), F32), pltpu.VMEM((rows, width), BF16), pltpu.VMEM((rows, width), BF16)],
-        "mlp", 6 * folds * mac, n2, cot, resid, vec, bup, far, far)
+    up_spec = pl.BlockSpec((CHIPS, 1, each, width), lambda i, me: (0, me[0] & 1, i, 0))
+    down_spec = pl.BlockSpec((CHIPS // 2, 1, deep, width), lambda i, me: (i, me[0] & 1, 1, 0))
+    hidden_spec = pl.BlockSpec((1, width), lambda i, me: (0, i))
+    low_out, high_out = (ANY_SPEC, shaped(rows, width)), (ANY_SPEC, shaped(rows, width, dtype=F32))
+    down_part = (ANY_SPEC, shaped(4, 2, deep, width))
+    up_part = (ANY_SPEC, shaped(blocks, 4, 2, each, width))
+
+    def run_mlp(me, tokens_of, bup):
+        sets = len(tokens_of[0])
+        low, high = pltpu.VMEM((sets * rows, width), BF16), pltpu.VMEM((sets * rows, width), F32)
+        weight = pltpu.VMEM((2, width, width), BF16)
+        dma = pltpu.SemaphoreType.DMA((2, sets))
+        return call_with(
+            me, functools.partial(mlp, sets), blocks, [ANY_SPEC] * (2 * sets) + [hidden_spec, up_spec, down_spec],
+            [low_out] * sets + [high_out] + [low_out] * (sets - 1) + [down_part] * 2 + [up_part] * 2
+            + [(hidden_spec, shaped(1, hidden // 2, dtype=F32))],
+            [low, low, high, high, low, low, pltpu.VMEM((2, sets * rows, width), BF16), weight, weight, dma, dma,
+             pltpu.SemaphoreType.DMA((4,))],
+            "mlp", 0, *tokens_of[0], *tokens_of[1], bup, far, far)
+
     if by_hand:
-        down_first = scatter_first(core, down_keep, scatter_core(down_send))
-        up_first = scatter_first(core, up_keep, scatter_core(up_send))
-        gtwo = after(gtwo, down_first[0], up_first[0])
+        cot_other = after(cot_other, mixed)
+        n2_other = swap(n2, other_core)
+        out_own, out_other, gtwo, gtwo_other, down_own, down_send, up_own, up_send, sum_up = run_mlp(
+            me, ((n2, n2_other), (cot, cot_other)), bup)
+        gtwo_take = swap(gtwo_other, other_core)
+        out_take = swap(out_other, other_core)
+        parts = (-1, CHIPS // 4, 2)
+        down_first = [piece.reshape(*parts, deep, width) for piece in (down_own, swap(down_send, first_plane))]
+        up_first = [piece.reshape(*parts, each, width) for piece in (up_own, swap(up_send, first_plane))]
+    else:
+        runs = [run_mlp(me + half, ((n2,), (cot,)), bup[half]) for half in range(2)]
+        (out_own, gtwo), (out_take, gtwo_take) = ((run[0], run[1]) for run in runs)
+        gtwo_take = gtwo_take.astype(BF16)
+        sum_up = jnp.concatenate([run[6] for run in runs], axis=1)
     grads_spec = pl.BlockSpec((4, tile, width), lambda i, *me: (0, i, 0))
     grads, gresid, sum_back = call(
         attention_backward, (tiles,),
-        [SMEM, tile_rows, tile_rows, tile_rows, lse_spec, tile_rows, tile_rows, tile_rows, vec_spec, square],
+        [SMEM, tile_rows, tile_rows, tile_rows, lse_spec, tile_rows, tile_rows, tile_rows, tile_rows, vec_spec, square],
         [(grads_spec, shaped(4, rows, width)), high_rows, sums], [pltpu.VMEM((tile, width), BF16)],
-        "attention_backward", 0, lengths, q, k, v, lse, cot, resid, gtwo, vec, wo)
+        "attention_backward", 0, lengths, q, k, v, lse, cot, resid, gtwo, gtwo_take, vec, wo)
     if by_hand:
         down_first, up_first = after((down_first, up_first), grads)
         hidden_second = scatter_second(*down_first, *up_first)
@@ -817,7 +914,7 @@
     gtok, sum_one, square_send, square_keep = call_with(
         me, projections_backward, tiles + 4,
         [tile_at, tile_at, vec_spec, tile_grads, square, square, square, full_rows, full_rows, columns, sum_spec, sum_spec,
-         whole_spec((1, hidden))],
+         whole_spec((1, sum_up.shape[1]))],
         [(tile_at, shaped(rows, width)), sums] + [(kept_spec(pair_shape), shaped(*pair_shape))] * 2, [],
         "projections_backward", 7 * mac,
         tokens, gresid, vec, grads, wq, wk, wv, n1, mixed, grads, sum_back, sum_down, sum_up)
@@ -827,9 +924,14 @@
         hidden_layers = scatter_layers(*hidden_second)
         square_keep = after(square_keep, hidden_layers[0])
         square_first = scatter_first(core, square_keep, square_take)
+        resid = after(resid, square_first[0])
+        (out,) = call(
+            add_rows, (tiles,), [tile_rows, vec_spec, tile_rows, tile_rows], [low_rows], [], "add_rows", 0,
+            resid, vec, out_own, out_take)
+        square_first = after(square_first, out)
         square_second = scatter_second(*square_first)
         hidden_layers = after(hidden_layers, square_second[0])
-        g_down, up_keep, up_send = scatter_last(core, hidden_layers, own, halves, deep)
+        g_down, up_keep, up_send = scatter_last(core, hidden_layers, own, blocks, deep)
         up_take = scatter_core(up_send)
         square_second = after(square_second, g_down)
         square_layers = scatter_layers(*square_second)
@@ -842,9 +944,13 @@
     else:
         flat = jnp.concatenate((sum_one[0:2], sum_back[0:5], sum_down[0:1]), axis=0)
         flat = flat.reshape(8, count, own).transpose(1, 0, 2).reshape(count, 8 * own)
-        flat = jnp.concatenate((flat, sum_up.reshape(count, folds * own)), axis=1)
+        hidden_sums = sum_up.reshape(2, CHIPS, deep).transpose(1, 0, 2).reshape(count, folds * own)
+        flat = jnp.concatenate((flat, hidden_sums), axis=1)
         g_down, g_up, g_q, g_k, g_v, g_o, flat = reduce_plain(
-            (down_keep, down_send), (up_keep, up_send), (square_keep, square_send), flat)
+            [run[2:4] for run in runs], [run[4:6] for run in runs], (square_keep, square_send), flat)
+        (out,) = call(
+            add_rows, (tiles,), [tile_rows, vec_spec, tile_rows, tile_rows], [low_rows], [], "add_rows", 0,
+            resid, vec, out_own, out_take)
         g_flat = [flat[index * own : (index + 1) * own] for index in range(8)]
         g_ub = flat[8 * own :]
     g_gain, g_shift, g_qb, g_vb, g_ob, g_mg, g_ms, g_db = g_flat

time: 283 us -> 276 us (0.975)
  waiting for transfers between devices: 103 us -> 96.7 us
    all_gather x1, waiting for transfers between devices: 4.18 us -> 0.01 us  [gather_by_hand(): lax.all_gather(far, 'dp', axis=0, tiled=True)]
    pallas_call x7 -> x6, Pallas kernels: 51.9 us -> 48.6 us  [call(): pl.pallas_call(kernel, grid=grid, in_specs=ins, out_specs=out_specs, out_...]
    ppermute x27 -> x29, waiting for transfers between devices: 99.1 us -> 96.7 us  [swap(): return lax.ppermute(array, 'dp', flipped(lax.axis_size('dp'), change))]
    ppermute x27 -> x29, starting transfers between devices: 24.2 us -> 24.8 us  [swap(): return lax.ppermute(array, 'dp', flipped(lax.axis_size('dp'), change))]
  transfers between devices with their start and end apart: 28 -> 30, of which waited for: 17 -> 17; matrix products, arithmetic and copies ran while one was open for 0% -> 0% of each run, Pallas kernels for 29% -> 31%
where the time goes in v4:
time: 276 us; the launch traced here: 274 us
  Pallas kernels  136 us (49%)
  waiting for transfers between devices  96.7 us (35%)
  starting transfers between devices  24.9 us (9%)
  between operations  14.2 us (5%)
    ppermute x29, waiting for transfers between devices, swap(): return lax.ppermute(array, 'dp', flipped(lax.axis_size('dp'), change))  96.7 us
    pallas_call x3, Pallas kernels, call_with(): pl.pallas_call(kernel, grid_spec=pltpu.PrefetchScalarGridSpec(num_scalar_...  71.3 us
    pallas_call x6, Pallas kernels, call(): pl.pallas_call(kernel, grid=grid, in_specs=ins, out_specs=out_specs, out_...  48.6 us
    ppermute x29, starting transfers between devices, swap(): return lax.ppermute(array, 'dp', flipped(lax.axis_size('dp'), change))  24.8 us
    pallas_call x7, Pallas kernels, small_call(): pl.pallas_call(kernel, in_specs=ins, out_specs=tuple((spec for spec, _ in...  15.6 us
  transfers between devices with their start and end apart: 30, of which 17 were waited for; matrix products, arithmetic and copies ran while one was open for 0% of the time, Pallas kernels for 31%

profile of v4, /device:TPU:0, one launch (start us, length us, event | category | flops | bytes accessed | tf_op | source)
XLA Modules:
  0.0 274.5 jit_solution(18035213329362534698)
XLA Ops:
  7.2 1.9 split_shards.1
  10.9 2.0 join_shards.1
  12.9 5.0 %collective-permute-start.3 = (bf16[208,384]{1,0:T(8,128)(2,1)}, bf16[208,384]{1,0:T(8,128)(2,1)S(1)}, u32[]{:S(2)}, u32[]{:S(2)}) collective-permute-start(bf16[208,384]{1,0:T(8,128)(2,1)} %get-tuple-element.105), channel_id=1, source_target_pairs={{0,24},{1,25},{2,26},{3,27},{4,28},{5,29},{6,30},{7,31},{8,16},{9,... | collective-permute-start | bytes 479240 | tf_op jit(solution)/shard_map/ppermute | solution.py:508
  18.6 4.6 %collective-permute-done.3 = bf16[208,384]{1,0:T(8,128)(2,1)S(1)} collective-permute-done((bf16[208,384]{1,0:T(8,128)(2,1)}, bf16[208,384]{1,0:T(8,128)(2,1)S(1)}, u32[]{:S(2)}, u32[]{:S(2)}) %collective-permute-start.3) | collective-permute-done | bytes 159776 | tf_op jit(solution)/shard_map/ppermute | solution.py:508
  23.2 14.8 %collective-permute-done.2 = bf16[208,384]{1,0:T(8,128)(2,1)S(1)} collective-permute-done((bf16[208,384]{1,0:T(8,128)(2,1)}, bf16[208,384]{1,0:T(8,128)(2,1)S(1)}, u32[]{:S(2)}, u32[]{:S(2)}) %collective-permute-start.2) | collective-permute-done | bytes 159776 | tf_op jit(solution)/shard_map/ppermute | solution.py:508
  39.0 2.5 collective-permute-start.6
  42.5 23.2 %collective-permute-done.6.refs_3_ = bf16[4,208,384]{2,1,0:T(8,128)(2,1)S(1)} collective-permute-done((bf16[4,208,384]{2,1,0:T(8,128)(2,1)S(1)}, bf16[4,208,384]{2,1,0:T(8,128)(2,1)S(1)}, u32[]{:S(2)}, u32[]{:S(2)}) %collective-permute-start.6) | collective-permute-done | bytes 639008 | tf_op jit(solution)/shard_map/ppermute | solution.py:508
  65.7 6.7 %collective-permute-done.5.refs_2_ = bf16[4,208,384]{2,1,0:T(8,128)(2,1)S(1)} collective-permute-done((bf16[4,208,384]{2,1,0:T(8,128)(2,1)S(1)}, bf16[4,208,384]{2,1,0:T(8,128)(2,1)S(1)}, u32[]{:S(2)}, u32[]{:S(2)}) %collective-permute-start.5) | collective-permute-done | bytes 639008 | tf_op jit(solution)/shard_map/ppermute | solution.py:508
  72.5 4.1 %collective-permute-done.4.refs_1_ = bf16[4,208,384]{2,1,0:T(8,128)(2,1)S(1)} collective-permute-done((bf16[4,208,384]{2,1,0:T(8,128)(2,1)S(1)}, bf16[4,208,384]{2,1,0:T(8,128)(2,1)S(1)}, u32[]{:S(2)}, u32[]{:S(2)}) %collective-permute-start.4) | collective-permute-done | bytes 639008 | tf_op jit(solution)/shard_map/ppermute | solution.py:508
  79.6 13.0 %project.1 = (bf16[1024,768]{1,0:T(8,128)(2,1)}, bf16[1024,768]{1,0:T(8,128)(2,1)}, bf16[1024,768]{1,0:T(8,128)(2,1)}, bf16[1024,768]{1,0:T(8,128)(2,1)}, bf16[1...) custom-call(s32[1]{0:T(128)} %bitcast.me_ref, ...), custom_call_target="tpu_custom_call" | custom-call | bytes 1 | tf_op jit(solution)/shard_map/project/pallas_call | solution.py:482
  92.8 13.3 %attention_forward.1 = (bf16[1024,768]{1,0:T(8,128)(2,1)}, f32[1024,128]{1,0:T(8,128)}, f32[1024,768]{1,0:T(8,128)}, bf16[1024,768]{1,0:T(8,128)(2,1)}) custom-call(s32[4,5]{1,0:T(4,128)} %lengths_ref.5, bf16[1024,768]{1,0:T(8,128)(2,1)} %x_ref.5, f32[16,768]{1,0:T(8,128)} %get-tuple-element.106.vec_ref, bf16[1024,768]{1,0:T(8,128)(2,1)} %get-tuple-element.107.q_ref, ...), custom_call_target="tpu_custom_call" | custom-call | bytes 1 | tf_op jit(solution)/shard_map/attention_forward/pallas_call | solution.py:467
  106.5 4.0 %collective-permute-done.11.refs_1_ = bf16[1024,768]{1,0:T(8,128)(2,1)} collective-permute-done((bf16[1024,768]{1,0:T(8,128)(2,1)}, bf16[1024,768]{1,0:T(8,128)(2,1)}, u32[]{:S(2)}, u32[]{:S(2)}) %collective-permute-start.11) | collective-permute-done | bytes 1572896 | tf_op jit(solution)/shard_map/ppermute | solution.py:508
  110.5 39.0 %mlp.1 = (bf16[1024,768]{1,0:T(8,128)(2,1)}, bf16[1024,768]{1,0:T(8,128)(2,1)}, f32[1024,768]{1,0:T(8,128)}, bf16[1024,768]{1,0:T(8,128)(2,1)}, bf16[4,2,96,768]...) custom-call(s32[1]{0:T(128)} %bitcast.me_ref, ...), custom_call_target="tpu_custom_call" | custom-call | bytes 1 | tf_op jit(solution)/shard_map/mlp/pallas_call | solution.py:482
  153.3 20.6 %attention_backward.1 = (bf16[4,1024,768]{2,1,0:T(8,128)(2,1)}, f32[1024,768]{1,0:T(8,128)}, f32[8,768]{1,0:T(8,128)}) custom-call(s32[4,5]{1,0:T(4,128)} %lengths_ref.5, bf16[1024,768]{1,0:T(8,128)(2,1)} %get-tuple-element.107.q_ref, bf16[1024,768]{1,0:T(8,128)(2,1)} %get-tuple-element.108.k_ref, bf16[1024,768]{1,0:T(8,128)(2,1)} %get-tuple-element.109.v_ref, ...), custom_call_target="tpu_custom_call" | custom-call | bytes 1 | tf_op jit(solution)/shard_map/attention_backward/pallas_call | solution.py:467
  174.0 5.1 %collective-permute-done.15.refs_3_ = bf16[2,4,2,48,768]{4,3,2,1,0:T(8,128)(2,1)} collective-permute-done((bf16[2,4,2,48,768]{4,3,2,1,0:T(8,128)(2,1)}, bf16[2,4,2,48,768]{4,3,2,1,0:T(8,128)(2,1)}, u32[]{:S(2)}, u32[]{:S(2)}) %collective-permute-start.15) | collective-permute-done | bytes 1179680 | tf_op jit(solution)/shard_map/ppermute | solution.py:508
  179.1 3.8 %merge_first.2 = (f32[4,192,768]{2,1,0:T(8,128)}, bf16[4,192,768]{2,1,0:T(8,128)(2,1)}) custom-call(bf16[1,4,2,96,768]{4,3,2,1,0:T(8,128)(2,1)} %bitcast.17, bf16[1,4,2,96,768]{4,3,2,1,0:T(8,128)(2,1)} %bitcast.7.refs_1_, bf16[2,4,2,48,768]{4,3,2,1,0:T(8,128)(2,1)} %get-tuple-element.129.refs_2_, bf16[2,4,2,48,768]{4,3,2,1,0:T(8,128)(2,1)} %collective-permute-done.15.refs_3_), custom_call_target="tpu_custom_call" | custom-call | flops 99999997952 | bytes 1 | tf_op jit(solution)/shard_map/merge_first/pallas_call | solution.py:467
  184.3 19.3 %projections_backward.1 = (bf16[1024,768]{1,0:T(8,128)(2,1)}, f32[8,768]{1,0:T(8,128)}, bf16[4,4,208,384]{3,2,1,0:T(8,128)(2,1)}, bf16[4,4,208,384]{3,2,1,0:T(8,128)(2,1)}) custom-call(s32[1]{0:T(128)} %bitcast.me_ref, bf16[1024,768]{1,0:T(8,128)(2,1)} %x_ref.5, f32[1024,768]{1,0:T(8,128)} %get-tuple-element.132.gresid_ref, ...), custom_call_target="tpu_custom_call" | custom-call | bytes 1 | tf_op jit(solution)/shard_map/projections_backward/pallas_call | solution.py:482
  204.1 3.1 %merge_second.2 = (f32[192,768]{1,0:T(8,128)}, bf16[192,768]{1,0:T(8,128)(2,1)}, bf16[192,768]{1,0:T(8,128)(2,1)}, bf16[192,768]{1,0:T(8,128)(2,1)}) custom-call(f32[4,192,768]{2,1,0:T(8,128)} %get-tuple-element.131.own_ref, bf16[4,192,768]{2,1,0:T(8,128)(2,1)} %collective-permute-done.16.take_ref), custom_call_target="tpu_custom_call" | custom-call | bytes 1 | tf_op jit(solution)/shard_map/merge_second/pallas_call | solution.py:595
  208.8 3.7 %merge_core.1 = (bf16[4,2,208,384]{3,2,1,0:T(8,128)(2,1)}, bf16[4,2,208,384]{3,2,1,0:T(8,128)(2,1)}) custom-call(s32[1]{0:T(128)S(6)} %and.5.core_ref, bf16[4,4,208,384]{3,2,1,0:T(8,128)(2,1)} %get-tuple-element.143.keep_ref, bf16[4,4,208,384]{3,2,1,0:T(8,128)(2,1)} %collective-permute-done.17.take_ref), custom_call_target="tpu_custom_call" | custom-call | bytes 1 | tf_op jit(solution)/shard_map/merge_core/pallas_call | solution.py:467
  213.2 2.9 %collective-permute-start.20 = (bf16[192,768]{1,0:T(8,128)(2,1)}, bf16[192,768]{1,0:T(8,128)(2,1)}, u32[]{:S(2)}, u32[]{:S(2)}) collective-permute-start(bf16[192,768]{1,0:T(8,128)(2,1)} %get-tuple-element.152), channel_id=1, source_target_pairs={{0,16},{1,17},{2,18},{3,19},{4,20},{5,21},{6,22},{7,23},{8,24},{9,... | collective-permute-start | bytes 884744 | tf_op jit(solution)/shard_map/ppermute | solution.py:508
  217.6 4.6 %add_rows.1 = bf16[1024,768]{1,0:T(8,128)(2,1)} custom-call(f32[1024,768]{1,0:T(8,128)} %get-tuple-element.147.resid_ref, f32[16,768]{1,0:T(8,128)} %get-tuple-element.106.vec_ref, bf16[1024,768]{1,0:T(8,128)(2,1)} %get-tuple-element.148.a_ref, bf16[1024,768]{1,0:T(8,128)(2,1)} %collective-permute-done.18.b_ref), custom_call_target="tpu_custom_call" | custom-call | bytes 1 | tf_op jit(solution)/shard_map/add_rows/pallas_call | solution.py:467
  222.2 7.8 %collective-permute-done.22 = bf16[4,2,208,384]{3,2,1,0:T(8,128)(2,1)} collective-permute-done((bf16[4,2,208,384]{3,2,1,0:T(8,128)(2,1)}, bf16[4,2,208,384]{3,2,1,0:T(8,128)(2,1)}, u32[]{:S(2)}, u32[]{:S(2)}) %collective-permute-start.22) | collective-permute-done | bytes 1277984 | tf_op jit(solution)/shard_map/ppermute | solution.py:508
  230.1 2.7 merge_first.3
  233.3 3.6 %collective-permute-done.20.b_ref = bf16[192,768]{1,0:T(8,128)(2,1)} collective-permute-done((bf16[192,768]{1,0:T(8,128)(2,1)}, bf16[192,768]{1,0:T(8,128)(2,1)}, u32[]{:S(2)}, u32[]{:S(2)}) %collective-permute-start.20) | collective-permute-done | bytes 294944 | tf_op jit(solution)/shard_map/ppermute | solution.py:508
  236.9 2.2 merge_last.2
  239.1 4.3 %collective-permute-done.24.take_ref = bf16[4,208,384]{2,1,0:T(8,128)(2,1)} collective-permute-done((bf16[4,208,384]{2,1,0:T(8,128)(2,1)}, bf16[4,208,384]{2,1,0:T(8,128)(2,1)}, u32[]{:S(2)}, u32[]{:S(2)}) %collective-permute-start.24) | collective-permute-done | bytes 639008 | tf_op jit(solution)/shard_map/ppermute | solution.py:508
  243.4 2.4 merge_second.3
  248.4 1.8 collective-permute-start.27
  250.2 3.2 %collective-permute-done.25.a_ref = bf16[208,384]{1,0:T(8,128)(2,1)} collective-permute-done((bf16[208,384]{1,0:T(8,128)(2,1)}, bf16[208,384]{1,0:T(8,128)(2,1)}, u32[]{:S(2)}, u32[]{:S(2)}) %collective-permute-start.25) | collective-permute-done | bytes 159776 | tf_op jit(solution)/shard_map/ppermute | solution.py:508
  253.4 8.3 %collective-permute-done.26.b_ref = bf16[208,384]{1,0:T(8,128)(2,1)} collective-permute-done((bf16[208,384]{1,0:T(8,128)(2,1)}, bf16[208,384]{1,0:T(8,128)(2,1)}, u32[]{:S(2)}, u32[]{:S(2)}) %collective-permute-start.26) | collective-permute-done | bytes 159776 | tf_op jit(solution)/shard_map/ppermute | solution.py:508
  261.8 2.0 merge_last.3
  265.5 2.1 finish.1
  (60 shorter events, 22.5 us)
Async XLA Ops:
  7.2 103.3 %all-gather.2.cloned.1.call-start = ((), (), s32[]{:S(2)}) async-start(), calls=%async_computation | async-start | bytes 9732096 | tf_op jit(solution)/shard_map/all_gather | solution.py:625
  9.1 1.8 collective-permute-start
  12.9 10.2 %collective-permute-start.3 = (bf16[208,384]{1,0:T(8,128)(2,1)}, bf16[208,384]{1,0:T(8,128)(2,1)S(1)}, u32[]{:S(2)}, u32[]{:S(2)}) collective-permute-start(bf16[208,384]{1,0:T(8,128)(2,1)} %get-tuple-element.105), channel_id=1, source_target_pairs={{0,24},{1,25},{2,26},{3,27},{4,28},{5,29},{6,30},{7,31},{8,16},{9,... | collective-permute-start | bytes 479240 | tf_op jit(solution)/shard_map/ppermute | solution.py:508
  17.9 20.0 %collective-permute-start.2 = (bf16[208,384]{1,0:T(8,128)(2,1)}, bf16[208,384]{1,0:T(8,128)(2,1)S(1)}, u32[]{:S(2)}, u32[]{:S(2)}) collective-permute-start(bf16[208,384]{1,0:T(8,128)(2,1)} %get-tuple-element.105), channel_id=1, source_target_pairs={{0,16},{1,17},{2,18},{3,19},{4,20},{5,21},{6,22},{7,23},{8,24},{9,... | collective-permute-start | bytes 479240 | tf_op jit(solution)/shard_map/ppermute | solution.py:508
  17.9 20.0 %collective-permute-start.1 = (bf16[208,384]{1,0:T(8,128)(2,1)}, bf16[208,384]{1,0:T(8,128)(2,1)S(1)}, u32[]{:S(2)}, u32[]{:S(2)}) collective-permute-start(bf16[208,384]{1,0:T(8,128)(2,1)} %get-tuple-element.105), channel_id=1, source_target_pairs={{0,8},{1,9},{2,10},{3,11},{4,12},{5,13},{6,14},{7,15},{8,0},{9,1},... | collective-permute-start | bytes 479240 | tf_op jit(solution)/shard_map/ppermute | solution.py:508
  39.0 26.8 %collective-permute-start.6 = (bf16[4,208,384]{2,1,0:T(8,128)(2,1)S(1)}, bf16[4,208,384]{2,1,0:T(8,128)(2,1)S(1)}, u32[]{:S(2)}, u32[]{:S(2)}) collective-permute-start(bf16[4,208,384]{2,1,0:T(8,128)(2,1)S(1)} %pad_maximum_fusion.refs_0_), channel_id=1, source_target_pairs={{0,6},{1,7},{2,4},{3,5},{4,2},{5,3},{6,0},{7,1},{8,14},{9,15},{10,... | collective-permute-start | bytes 1916936 | tf_op jit(solution)/shard_map/ppermute | solution.py:508
  41.5 30.9 %collective-permute-start.5 = (bf16[4,208,384]{2,1,0:T(8,128)(2,1)S(1)}, bf16[4,208,384]{2,1,0:T(8,128)(2,1)S(1)}, u32[]{:S(2)}, u32[]{:S(2)}) collective-permute-start(bf16[4,208,384]{2,1,0:T(8,128)(2,1)S(1)} %pad_maximum_fusion.refs_0_), channel_id=1, source_target_pairs={{0,4},{1,5},{2,6},{3,7},{4,0},{5,1},{6,2},{7,3},{8,12},{9,13},{10,... | collective-permute-start | bytes 1916936 | tf_op jit(solution)/shard_map/ppermute | solution.py:508
  42.0 34.6 %collective-permute-start.4 = (bf16[4,208,384]{2,1,0:T(8,128)(2,1)S(1)}, bf16[4,208,384]{2,1,0:T(8,128)(2,1)S(1)}, u32[]{:S(2)}, u32[]{:S(2)}) collective-permute-start(bf16[4,208,384]{2,1,0:T(8,128)(2,1)S(1)} %pad_maximum_fusion.refs_0_), channel_id=1, source_target_pairs={{0,2},{1,3},{2,0},{3,1},{4,6},{5,7},{6,4},{7,5},{8,10},{9,11},{10,... | collective-permute-start | bytes 1916936 | tf_op jit(solution)/shard_map/ppermute | solution.py:508
  42.5 34.0 %collective-permute-start.7 = (bf16[4,208,384]{2,1,0:T(8,128)(2,1)S(1)}, bf16[4,208,384]{2,1,0:T(8,128)(2,1)S(1)}, u32[]{:S(2)}, u32[]{:S(2)}) collective-permute-start(bf16[4,208,384]{2,1,0:T(8,128)(2,1)S(1)} %pad_maximum_fusion.refs_0_), channel_id=1, source_target_pairs={{0,1},{1,0},{2,3},{3,2},{4,5},{5,4},{6,7},{7,6},{8,9},{9,8},{10,11... | collective-permute-start | bytes 1916936 | tf_op jit(solution)/shard_map/ppermute | solution.py:508
  65.7 10.9 %copy-start.1 = (bf16[4,208,384]{2,1,0:T(8,128)(2,1)}, bf16[4,208,384]{2,1,0:T(8,128)(2,1)S(1)}, u32[]{:S(2)}) copy-start(bf16[4,208,384]{2,1,0:T(8,128)(2,1)S(1)} %collective-permute-done.6.refs_3_) | copy-start | bytes 1916932
  65.7 10.9 %collective-permute-start.10 = (bf16[4,208,384]{2,1,0:T(8,128)(2,1)S(1)}, bf16[4,208,384]{2,1,0:T(8,128)(2,1)S(1)}, u32[]{:S(2)}, u32[]{:S(2)}) collective-permute-start(bf16[4,208,384]{2,1,0:T(8,128)(2,1)S(1)} %collective-permute-done.6.refs_3_), channel_id=1, source_target_pairs={{0,1},{1,0},{2,3},{3,2},{4,5},{5,4},{6,7},{7,6},{8,9},{9,8},{10,11... | collective-permute-start | bytes 1916936 | tf_op jit(solution)/shard_map/ppermute | solution.py:508
  72.5 4.2 %copy-start.2 = (bf16[4,208,384]{2,1,0:T(8,128)(2,1)}, bf16[4,208,384]{2,1,0:T(8,128)(2,1)S(1)}, u32[]{:S(2)}) copy-start(bf16[4,208,384]{2,1,0:T(8,128)(2,1)S(1)} %collective-permute-done.5.refs_2_) | copy-start | bytes 1916932
  72.5 4.2 %collective-permute-start.9 = (bf16[4,208,384]{2,1,0:T(8,128)(2,1)S(1)}, bf16[4,208,384]{2,1,0:T(8,128)(2,1)S(1)}, u32[]{:S(2)}, u32[]{:S(2)}) collective-permute-start(bf16[4,208,384]{2,1,0:T(8,128)(2,1)S(1)} %collective-permute-done.5.refs_2_), channel_id=1, source_target_pairs={{0,1},{1,0},{2,3},{3,2},{4,5},{5,4},{6,7},{7,6},{8,9},{9,8},{10,11... | collective-permute-start | bytes 1916936 | tf_op jit(solution)/shard_map/ppermute | solution.py:508
  76.6 3.0 %collective-permute-start.8 = (bf16[4,208,384]{2,1,0:T(8,128)(2,1)S(1)}, bf16[4,208,384]{2,1,0:T(8,128)(2,1)}, u32[]{:S(2)}, u32[]{:S(2)}) collective-permute-start(bf16[4,208,384]{2,1,0:T(8,128)(2,1)S(1)} %collective-permute-done.4.refs_1_), channel_id=1, source_target_pairs={{0,1},{1,0},{2,3},{3,2},{4,5},{5,4},{6,7},{7,6},{8,9},{9,8},{10,11... | collective-permute-start | bytes 1916936 | tf_op jit(solution)/shard_map/ppermute | solution.py:508
  92.6 13.9 %collective-permute-start.12 = (bf16[1024,768]{1,0:T(8,128)(2,1)}, bf16[1024,768]{1,0:T(8,128)(2,1)}, u32[]{:S(2)}, u32[]{:S(2)}) collective-permute-start(bf16[1024,768]{1,0:T(8,128)(2,1)} %get-tuple-element.113.refs_2_.cot_ref), channel_id=1, source_target_pairs={{0,1},{1,0},{2,3},{3,2},{4,5},{5,4},{6,7},{7,6},{8,9},{9,8},{10,11... | collective-permute-start | bytes 4718600 | tf_op jit(solution)/shard_map/ppermute | solution.py:508
  106.1 4.4 %collective-permute-start.11 = (bf16[1024,768]{1,0:T(8,128)(2,1)}, bf16[1024,768]{1,0:T(8,128)(2,1)}, u32[]{:S(2)}, u32[]{:S(2)}) collective-permute-start(bf16[1024,768]{1,0:T(8,128)(2,1)} %get-tuple-element.114.refs_0_), channel_id=1, source_target_pairs={{0,1},{1,0},{2,3},{3,2},{4,5},{5,4},{6,7},{7,6},{8,9},{9,8},{10,11... | collective-permute-start | bytes 4718600 | tf_op jit(solution)/shard_map/ppermute | solution.py:508
  149.5 3.8 %collective-permute-start.13 = (bf16[1024,768]{1,0:T(8,128)(2,1)}, bf16[1024,768]{1,0:T(8,128)(2,1)}, u32[]{:S(2)}, u32[]{:S(2)}) collective-permute-start(bf16[1024,768]{1,0:T(8,128)(2,1)} %get-tuple-element.120), channel_id=1, source_target_pairs={{0,1},{1,0},{2,3},{3,2},{4,5},{5,4},{6,7},{7,6},{8,9},{9,8},{10,11... | collective-permute-start | bytes 4718600 | tf_op jit(solution)/shard_map/ppermute | solution.py:508
  150.0 24.0 %collective-permute-start.14 = (bf16[4,2,96,768]{3,2,1,0:T(8,128)(2,1)}, bf16[4,2,96,768]{3,2,1,0:T(8,128)(2,1)}, u32[]{:S(2)}, u32[]{:S(2)}) collective-permute-start(bf16[4,2,96,768]{3,2,1,0:T(8,128)(2,1)} %get-tuple-element.123), channel_id=1, source_target_pairs={{0,2},{1,5},{2,0},{3,7},{4,6},{5,1},{6,4},{7,3},{8,10},{9,13},{10,... | collective-permute-start | bytes 3538952 | tf_op jit(solution)/shard_map/ppermute | solution.py:508
  151.5 27.6 %collective-permute-start.15 = (bf16[2,4,2,48,768]{4,3,2,1,0:T(8,128)(2,1)}, bf16[2,4,2,48,768]{4,3,2,1,0:T(8,128)(2,1)}, u32[]{:S(2)}, u32[]{:S(2)}) collective-permute-start(bf16[2,4,2,48,768]{4,3,2,1,0:T(8,128)(2,1)} %get-tuple-element.125), channel_id=1, source_target_pairs={{0,2},{1,5},{2,0},{3,7},{4,6},{5,1},{6,4},{7,3},{8,10},{9,13},{10,... | collective-permute-start | bytes 3538952 | tf_op jit(solution)/shard_map/ppermute | solution.py:508
  182.9 20.7 %collective-permute-start.16 = (bf16[4,192,768]{2,1,0:T(8,128)(2,1)}, bf16[4,192,768]{2,1,0:T(8,128)(2,1)}, u32[]{:S(2)}, u32[]{:S(2)}) collective-permute-start(bf16[4,192,768]{2,1,0:T(8,128)(2,1)} %get-tuple-element.141), channel_id=1, source_target_pairs={{0,4},{1,3},{2,6},{3,1},{4,0},{5,7},{6,2},{7,5},{8,12},{9,11},{10,... | collective-permute-start | bytes 3538952 | tf_op jit(solution)/shard_map/ppermute | solution.py:508
  203.6 5.2 %collective-permute-start.17 = (bf16[4,4,208,384]{3,2,1,0:T(8,128)(2,1)}, bf16[4,4,208,384]{3,2,1,0:T(8,128)(2,1)}, u32[]{:S(2)}, u32[]{:S(2)}) collective-permute-start(bf16[4,4,208,384]{3,2,1,0:T(8,128)(2,1)} %get-tuple-element.145), channel_id=1, source_target_pairs={{0,1},{1,0},{2,3},{3,2},{4,5},{5,4},{6,7},{7,6},{8,9},{9,8},{10,11... | collective-permute-start | bytes 7667720 | tf_op jit(solution)/shard_map/ppermute | solution.py:508
  203.6 13.9 %collective-permute-start.18 = (bf16[1024,768]{1,0:T(8,128)(2,1)}, bf16[1024,768]{1,0:T(8,128)(2,1)}, u32[]{:S(2)}, u32[]{:S(2)}) collective-permute-start(bf16[1024,768]{1,0:T(8,128)(2,1)} %get-tuple-element.149), channel_id=1, source_target_pairs={{0,1},{1,0},{2,3},{3,2},{4,5},{5,4},{6,7},{7,6},{8,9},{9,8},{10,11... | collective-permute-start | bytes 4718600 | tf_op jit(solution)/shard_map/ppermute | solution.py:508
  212.5 17.6 %collective-permute-start.22 = (bf16[4,2,208,384]{3,2,1,0:T(8,128)(2,1)}, bf16[4,2,208,384]{3,2,1,0:T(8,128)(2,1)}, u32[]{:S(2)}, u32[]{:S(2)}) collective-permute-start(bf16[4,2,208,384]{3,2,1,0:T(8,128)(2,1)} %get-tuple-element.154), channel_id=1, source_target_pairs={{0,2},{1,5},{2,0},{3,7},{4,6},{5,1},{6,4},{7,3},{8,10},{9,13},{10,... | collective-permute-start | bytes 3833864 | tf_op jit(solution)/shard_map/ppermute | solution.py:508
  213.2 20.2 %collective-permute-start.19 = (bf16[192,768]{1,0:T(8,128)(2,1)}, bf16[192,768]{1,0:T(8,128)(2,1)}, u32[]{:S(2)}, u32[]{:S(2)}) collective-permute-start(bf16[192,768]{1,0:T(8,128)(2,1)} %get-tuple-element.151), channel_id=1, source_target_pairs={{0,8},{1,9},{2,10},{3,11},{4,12},{5,13},{6,14},{7,15},{8,0},{9,1},... | collective-permute-start | bytes 884744 | tf_op jit(solution)/shard_map/ppermute | solution.py:508
  213.2 23.8 %collective-permute-start.20 = (bf16[192,768]{1,0:T(8,128)(2,1)}, bf16[192,768]{1,0:T(8,128)(2,1)}, u32[]{:S(2)}, u32[]{:S(2)}) collective-permute-start(bf16[192,768]{1,0:T(8,128)(2,1)} %get-tuple-element.152), channel_id=1, source_target_pairs={{0,16},{1,17},{2,18},{3,19},{4,20},{5,21},{6,22},{7,23},{8,24},{9,... | collective-permute-start | bytes 884744 | tf_op jit(solution)/shard_map/ppermute | solution.py:508
  216.1 20.9 %collective-permute-start.21 = (bf16[192,768]{1,0:T(8,128)(2,1)}, bf16[192,768]{1,0:T(8,128)(2,1)}, u32[]{:S(2)}, u32[]{:S(2)}) collective-permute-start(bf16[192,768]{1,0:T(8,128)(2,1)} %get-tuple-element.153), channel_id=1, source_target_pairs={{0,24},{1,25},{2,26},{3,27},{4,28},{5,29},{6,30},{7,31},{8,16},{9,... | collective-permute-start | bytes 884744 | tf_op jit(solution)/shard_map/ppermute | solution.py:508
  232.7 10.7 %collective-permute-start.24 = (bf16[4,208,384]{2,1,0:T(8,128)(2,1)}, bf16[4,208,384]{2,1,0:T(8,128)(2,1)}, u32[]{:S(2)}, u32[]{:S(2)}) collective-permute-start(bf16[4,208,384]{2,1,0:T(8,128)(2,1)} %get-tuple-element.164), channel_id=1, source_target_pairs={{0,4},{1,3},{2,6},{3,1},{4,0},{5,7},{6,2},{7,5},{8,12},{9,11},{10,... | collective-permute-start | bytes 1916936 | tf_op jit(solution)/shard_map/ppermute | solution.py:508
  245.8 7.6 %collective-permute-start.25 = (bf16[208,384]{1,0:T(8,128)(2,1)}, bf16[208,384]{1,0:T(8,128)(2,1)}, u32[]{:S(2)}, u32[]{:S(2)}) collective-permute-start(bf16[208,384]{1,0:T(8,128)(2,1)} %get-tuple-element.169), channel_id=1, source_target_pairs={{0,8},{1,9},{2,10},{3,11},{4,12},{5,13},{6,14},{7,15},{8,0},{9,1},... | collective-permute-start | bytes 479240 | tf_op jit(solution)/shard_map/ppermute | solution.py:508
  247.2 14.5 %collective-permute-start.26 = (bf16[208,384]{1,0:T(8,128)(2,1)}, bf16[208,384]{1,0:T(8,128)(2,1)}, u32[]{:S(2)}, u32[]{:S(2)}) collective-permute-start(bf16[208,384]{1,0:T(8,128)(2,1)} %get-tuple-element.170), channel_id=1, source_target_pairs={{0,16},{1,17},{2,18},{3,19},{4,20},{5,21},{6,22},{7,23},{8,24},{9,... | collective-permute-start | bytes 479240 | tf_op jit(solution)/shard_map/ppermute | solution.py:508
  248.4 13.4 %collective-permute-start.27 = (bf16[208,384]{1,0:T(8,128)(2,1)}, bf16[208,384]{1,0:T(8,128)(2,1)}, u32[]{:S(2)}, u32[]{:S(2)}) collective-permute-start(bf16[208,384]{1,0:T(8,128)(2,1)} %get-tuple-element.171), channel_id=1, source_target_pairs={{0,24},{1,25},{2,26},{3,27},{4,28},{5,29},{6,30},{7,31},{8,16},{9,... | collective-permute-start | bytes 479240 | tf_op jit(solution)/shard_map/ppermute | solution.py:508
  250.2 13.5 %collective-permute-start.23 = (f32[2,24,768]{2,1,0:T(8,128)}, f32[2,24,768]{2,1,0:T(8,128)}, u32[]{:S(2)}, u32[]{:S(2)}) collective-permute-start(f32[2,24,768]{2,1,0:T(8,128)} %get-tuple-element.163), channel_id=1, source_target_pairs={{0,1},{1,0},{2,3},{3,2},{4,5},{5,4},{6,7},{7,6},{8,9},{9,8},{10,11... | collective-permute-start | bytes 442376 | tf_op jit(solution)/shard_map/ppermute | solution.py:508
  263.7 1.7 collective-permute-start.28
  (5 other events, 7.5 us)
Sparse Core Ops, SparseCore 0:
  13.0 96.7 all-gather.1

commit v5 on v4

--- a/solution.py
+++ b/solution.py
@@ -15,6 +15,7 @@
 MERGE_STEPS = 2
 LONG = 10**11
 SHORT = 6 * 10**9
+MIDDLE = 115 * 10**8
 EPS = 1e-06
 MASKED = -1e30
 SCALE = HEAD_DIM**-0.5
@@ -84,7 +85,7 @@
         half = core if index < 4 else 1 - core
         cols = pl.ds(pl.multiple_of(half * side, LANES), side)
         for layer in range(4):
-            owner = chip ^ (4 * layer + index % 4)
+            owner = chip ^ (4 * layer + (0, 1 + half, 2 - half, 3)[index % 4])
             rows = pl.ds(pl.multiple_of(owner * each, 16), each)
             for number, ref in enumerate(weight_refs):
                 pltpu.make_async_copy(
@@ -95,10 +96,10 @@
             ).start()
 
 
-def project(me_ref, lengths_ref, x_ref, grad_ref, *refs):
+def project(me_ref, x_ref, *refs):
     sources = refs[:8]
-    n1_ref, q_ref, k_ref, v_ref, cot_ref, dsum_ref = refs[8:14]
-    wq_ref, wk_ref, wv_ref, wo_ref, vec_ref, bup_ref, parts_ref, sem = refs[14:]
+    n1_ref, q_ref, k_ref, v_ref = refs[8:12]
+    wq_ref, wk_ref, wv_ref, wo_ref, vec_ref, bup_ref, parts_ref, sem = refs[12:]
     weights = (wq_ref, wk_ref, wv_ref, wo_ref)
     core = me_ref[0] & 1
 
@@ -117,21 +118,22 @@
             rows = sum(parts_ref[2 * (block * group + index) + core].astype(F32) for index in range(group))
             bup_ref[:, block * side : (block + 1) * side] = rows[8:9]
 
-    project_rows(lengths_ref, x_ref, grad_ref, vec_ref, wq_ref, wk_ref, wv_ref, n1_ref, q_ref, k_ref, v_ref, cot_ref, dsum_ref)
-
-
-def project_rows(lengths_ref, x_ref, grad_ref, vec_ref, wq_ref, wk_ref, wv_ref,
-                 n1_ref, q_ref, k_ref, v_ref, cot_ref, dsum_ref):
-    tile = pl.program_id(0)
-    rows = x_ref.shape[0]
-    slots = lengths_ref.shape[1]
+    project_rows(x_ref, vec_ref, wq_ref, wk_ref, wv_ref, n1_ref, q_ref, k_ref, v_ref)
+
+
+def project_rows(x_ref, vec_ref, wq_ref, wk_ref, wv_ref, n1_ref, q_ref, k_ref, v_ref):
     hat, _ = normalize(x_ref[...].astype(F32))
     n1 = (hat * vec_ref[0:1, :] + vec_ref[1:2, :]).astype(BF16)
     n1_ref[...] = n1
     q_ref[...] = (dot_nn(n1, wq_ref[...]) + vec_ref[2:3, :]).astype(BF16) * jnp.asarray(SCALE, BF16)
     k_ref[...] = dot_nn(n1, wk_ref[...]).astype(BF16)
     v_ref[...] = (dot_nn(n1, wv_ref[...]) + vec_ref[3:4, :]).astype(BF16)
-    valid = segments(lengths_ref, tile, slots, rows, 0) < slots
+
+
+def mask_grads(lengths_ref, grad_ref, cot_ref, dsum_ref):
+    tile = pl.program_id(0)
+    slots = lengths_ref.shape[1]
+    valid = segments(lengths_ref, tile, slots, grad_ref.shape[0], 0) < slots
     cot = jnp.where(valid, grad_ref[...].astype(F32), 0.0)
     cot_ref[...] = cot.astype(BF16)
 
@@ -200,9 +202,9 @@
     n2_hbm, cot_hbm = refs[:sets], refs[sets : 2 * sets]
     bup_ref, wup_ref, wdown_ref = refs[2 * sets : 2 * sets + 3]
     refs = refs[2 * sets + 3 :]
-    out_hbm, gtwo_hbm, refs = refs[:sets], refs[sets : 2 * sets], refs[2 * sets :]
+    act_hbm, gtwo_hbm, refs = refs[:sets], refs[sets : 2 * sets], refs[2 * sets :]
     down_own, down_send, up_own, up_send, dbu_ref = refs[:5]
-    n2_ref, cot_ref, acc, gacc, act_ref, gup_ref, low_ref, gdown_ref, gupw_ref, in_sem, out_sem, grad_sem = refs[5:]
+    n2_ref, cot_ref, gacc, act_ref, gup_ref, low_ref, gdown_ref, gupw_ref, in_sem, act_sem, out_sem, grad_sem = refs[5:]
     step = pl.program_id(0)
     last = pl.num_programs(0) - 1
     me = me_ref[0]
@@ -221,6 +223,8 @@
     wup = flat_rows(wup_ref)
     wdown = flat_rows(wdown_ref)
     dbu_ref[...] = jnp.zeros_like(dbu_ref)
+    slot = lax.rem(step, 2)
+    width = n2_ref.shape[1]
 
     @pl.loop(0, sets)
     def _(index):
@@ -237,7 +241,7 @@
         tanh = jnp.tanh(pre * (GELU_C + (GELU_C * GELU_A) * square))
         half = 0.5 + 0.5 * tanh
         inner = GELU_C + (3.0 * GELU_C * GELU_A) * square
-        act_ref[at, :] = (pre * half).astype(BF16)
+        act_ref[slot, at, :] = (pre * half).astype(BF16)
         gup = (grad_act * (half + (0.5 * pre) * (1.0 - tanh * tanh) * inner)).astype(BF16)
         gup_ref[at, :] = gup
         dbu_ref[...] += column_sum(gup.astype(F32))
@@ -247,7 +251,6 @@
         @pl.loop(0, sets)
         def _(index):
             at = rows_of(index)
-            acc[at, :] = dot_nn(act_ref[at, :], wdown)
             gacc[at, :] = dot_nt(gup_ref[at, :], wup)
 
     @pl.when((step > 0) & (step < last))
@@ -255,31 +258,40 @@
         @pl.loop(0, sets)
         def _(index):
             at = rows_of(index)
-            acc[at, :] += dot_nn(act_ref[at, :], wdown)
             gacc[at, :] += dot_nt(gup_ref[at, :], wup)
 
     def results():
         for index in range(sets):
             at = pl.ds(index * rows, rows)
-            yield pltpu.make_async_copy(low_ref.at[0, at, :], out_hbm[index], out_sem.at[0, index])
-            source = low_ref.at[1, at, :] if index else gacc.at[at, :]
-            yield pltpu.make_async_copy(source, gtwo_hbm[index], out_sem.at[1, index])
+            source = low_ref.at[at, :] if index else gacc.at[at, :]
+            yield pltpu.make_async_copy(source, gtwo_hbm[index], out_sem.at[index])
+
+    def activations(number):
+        for index in range(sets):
+            source = act_ref.at[number, pl.ds(index * rows, rows), :]
+            cols = pl.ds(number * width, width)
+            yield pltpu.make_async_copy(source, act_hbm[index].at[:, cols], act_sem.at[number, index])
+
+    for number in range(act_ref.shape[0]):
+
+        @pl.when(step == number)
+        def _():
+            for copy in activations(number):
+                copy.start()
 
     @pl.when(step == last)
     def _():
         @pl.loop(0, sets)
         def _(index):
             at = rows_of(index)
-            low_ref[0, at, :] = (acc[at, :] + dot_nn(act_ref[at, :], wdown)).astype(BF16)
             total = gacc[at, :] + dot_nt(gup_ref[at, :], wup)
             gacc[at, :] = total
-            low_ref[1, at, :] = total.astype(BF16)
+            low_ref[at, :] = total.astype(BF16)
 
         for copy in results():
             copy.start()
 
-    slot = lax.rem(step, 2)
-    gdown_ref[slot] = dot_tn(act_ref[...], cot_ref[...]).astype(BF16)
+    gdown_ref[slot] = dot_tn(act_ref[slot], cot_ref[...]).astype(BF16)
     deep = down_own.shape[2]
     count = gdown_ref.shape[1] // deep
     for index in range(count):
@@ -298,6 +310,9 @@
     def _():
         for copy in results():
             copy.wait()
+        for number in range(act_ref.shape[0]):
+            for copy in activations(number):
+                copy.wait()
         for number, ref in enumerate((down_own, down_send, up_own, up_send)):
             pltpu.make_async_copy(ref, ref, grad_sem.at[number]).wait()
 
@@ -316,9 +331,13 @@
         pltpu.make_async_copy(source, send_ref.at[layer, jnp.where(relative == 3, 1, 0)], sem.at[number + 1]).start()
 
 
-def add_rows(resid_ref, vec_ref, a_ref, b_ref, out_ref):
-    total = resid_ref[...] + (a_ref[...].astype(F32) + b_ref[...].astype(F32) + vec_ref[7:8, :])
-    out_ref[...] = total.astype(BF16)
+def mlp_out_other(me_ref, act_ref, wdown_ref, out_ref):
+    out_ref[...] = dot_nn(act_ref[...], flat_rows(wdown_ref)).astype(BF16)
+
+
+def mlp_out_own(me_ref, resid_ref, vec_ref, act_ref, take_ref, wdown_ref, out_ref):
+    half = dot_nn(act_ref[...], flat_rows(wdown_ref)) + take_ref[...].astype(F32)
+    out_ref[...] = (resid_ref[...] + (half + vec_ref[7:8, :])).astype(BF16)
 
 
 def attention_backward(lengths_ref, q_ref, k_ref, v_ref, lse_ref, cot_ref, resid_ref, gtwo_ref, gother_ref, vec_ref, wo_ref,
@@ -384,27 +403,12 @@
     dsum_ref[1:2, :] += column_sum(grads_ref[2].astype(F32))
 
 
-def projections_backward(me_ref, x_ref, gresid_ref, vec_ref, grads_ref, wq_ref, wk_ref, wv_ref, n1_ref, mixed_ref,
-                         columns_ref, sum_back_ref, sum_down_ref, sum_up_ref,
-                         gtok_ref, dsum_ref, send_ref, keep_ref):
+def weight_grads(me_ref, n1_ref, mixed_ref, columns_ref, sum_back_ref, sum_down_ref, sum_up_ref, send_ref, keep_ref):
     step = pl.program_id(0)
-    tiles = pl.num_programs(0) - 4
     me = me_ref[0]
     first = (me & 1) == 0
     side = send_ref.shape[3]
-    each = wq_ref.shape[0] // CHIPS
-
-    @pl.when(step == 0)
-    def _():
-        dsum_ref[...] = jnp.zeros_like(dsum_ref)
-
-    @pl.when(step < tiles)
-    def _():
-        grad_one = dot_nt(grads_ref[0], wq_ref[...]) + dot_nt(grads_ref[1], wk_ref[...]) + dot_nt(grads_ref[2], wv_ref[...])
-        hat, inverse = normalize(x_ref[...].astype(F32))
-        gtok_ref[...] = (gresid_ref[...] + norm_back(grad_one, vec_ref[0:1, :], hat, inverse)).astype(BF16)
-        dsum_ref[0:1, :] += column_sum(grad_one * hat)
-        dsum_ref[1:2, :] += column_sum(grad_one)
+    each = n1_ref.shape[1] // CHIPS
 
     def run(left, number):
         result = dot_tn(left, columns_ref[0])
@@ -420,14 +424,15 @@
         spread(me, jnp.where(first, high, low), put_send)
         spread(me, jnp.where(first, low, high), put_keep)
 
-    @pl.when((step >= tiles) & (step < tiles + 3))
-    def _():
-        run(n1_ref[...], step - tiles)
-
-    @pl.when(step == tiles + 3)
+    @pl.when(step < 3)
+    def _():
+        run(n1_ref[...], step)
+
+    @pl.when(step == 3)
     def _():
         run(mixed_ref[...], 3)
-        vecs = jnp.concatenate((dsum_ref[0:2], sum_back_ref[0:5], sum_down_ref[0:1]), axis=0)
+        nothing = jnp.zeros((2, n1_ref.shape[1]), F32)
+        vecs = jnp.concatenate((nothing, sum_back_ref[0:5], sum_down_ref[0:1]), axis=0)
         for chip in range(CHIPS):
             half = chip // (CHIPS // 2)
             block = chip * (sum_up_ref.shape[1] // side) // CHIPS
@@ -436,6 +441,18 @@
             at = ((chip >> 2) ^ (me >> 3), (chip & 3) ^ ((me >> 1) & 3))
             keep_ref[at[0], at[1], 4 * each :, :] = jnp.concatenate((short, last), axis=0).astype(BF16)
             send_ref[at[0], at[1], 4 * each :, :] = jnp.concatenate((short, jnp.zeros_like(last)), axis=0).astype(BF16)
+
+
+def tokens_backward(x_ref, gresid_ref, vec_ref, grads_ref, wq_ref, wk_ref, wv_ref, gtok_ref, dsum_ref):
+    @pl.when(pl.program_id(0) == 0)
+    def _():
+        dsum_ref[...] = jnp.zeros_like(dsum_ref)
+
+    grad_one = dot_nt(grads_ref[0], wq_ref[...]) + dot_nt(grads_ref[1], wk_ref[...]) + dot_nt(grads_ref[2], wv_ref[...])
+    hat, inverse = normalize(x_ref[...].astype(F32))
+    gtok_ref[...] = (gresid_ref[...] + norm_back(grad_one, vec_ref[0:1, :], hat, inverse)).astype(BF16)
+    dsum_ref[0:1, :] += column_sum(grad_one * hat)
+    dsum_ref[1:2, :] += column_sum(grad_one)
 
 
 def rows_spec(block, width):
@@ -608,7 +625,7 @@
 ANY_SPEC = pl.BlockSpec(memory_space=pl.ANY)
 
 
-def gather_by_hand(me, weights, vectors):
+def gather_by_hand(me, weights, vectors, masked):
     count = lax.axis_size("dp")
     own, width = weights[0].shape
     side = width // 2
@@ -624,8 +641,10 @@
         ins=[SMEM] + [VMEM_SPEC] * (3 + len(vectors)))
     far = lax.all_gather(far, "dp", axis=0, tiled=True).reshape(count // 2, 2, 2 * deep, width)
     near = across_layers(near)
-    near = [near] + [swap(near, other_plane(distance)) for distance in (1, 2, 3)]
-    return near + [swap(piece, other_core) for piece in near], far
+    cot, sum_down = masked(near)
+    far_plane = after(swap(near, first_plane), cot)
+    near = [near, far_plane, swap(near, second_plane), swap(far_plane, second_plane)]
+    return near + [swap(piece, other_core) for piece in near], far, cot, sum_down
 
 
 def gather_plain(weights, vectors):
@@ -705,7 +724,7 @@
         refs[2][...] = whole[2 * own * parts :]
 
 
-def finish(me_ref, up_keep_ref, up_take_ref, keep_ref, take_ref, flat_ref, up_ref, *refs):
+def finish(me_ref, up_keep_ref, up_take_ref, keep_ref, take_ref, flat_ref, late_ref, up_ref, *refs):
     me = me_ref[0]
     first = (me & 1) == 0
     side = keep_ref.shape[2]
@@ -725,7 +744,8 @@
         for start in range(0, width, deep):
             pieces += [low[:, start : start + deep], high[:, start : start + deep]]
         up_ref[:, 2 * width * part : 2 * width * (part + 1)] = jnp.concatenate(pieces, axis=1)
-    flat = flat_ref[...]
+    late = jnp.where(me < side // own, late_ref[0:2, :side], late_ref[0:2, side:])
+    flat = jnp.concatenate((late, flat_ref[2:]), axis=0)
     long = flats[-1].shape[0]
     short_turn = lax.rem(side - own * lax.rem(me, side // own), side)
     long_turn = lax.rem(side - long * lax.rem(me >> 1, side // long), side)
@@ -735,11 +755,20 @@
     flats[-1][...] = pltpu.roll(flat, long_turn, 1)[8, :long]
 
 
+def fenced(function, *args):
+    kinds = jax.eval_shape(function, *args)
+
+    def nothing(*_):
+        return jax.tree.map(lambda kind: jnp.zeros(kind.shape, kind.dtype), kinds)
+
+    return lax.cond(lax.axis_index("dp") < lax.axis_size("dp"), function, nothing, *args)
+
+
 def scatter_core(send):
     return swap(send, other_core)
 
 
-def scatter_first(core, keep, take):
+def merge_core_of(core, keep, take):
     shape = keep.shape
     planes, rows, side = shape[-3:]
     keep, take = keep.reshape(-1, planes, rows, side), take.reshape(-1, planes, rows, side)
@@ -748,8 +777,7 @@
     block = pl.BlockSpec((count // steps, planes, rows, side), lambda i: (i, 0, 0, 0))
     half = (pl.BlockSpec((count // steps, 2, rows, side), lambda i: (i, 0, 0, 0)), shaped(count, 2, rows, side))
     own, send = call(merge_core, (steps,), [SMEM, block, block], [half, half], [], "merge_core", 0, core, keep, take)
-    parts = (-1, CHIPS // 4, 2, rows, side)
-    return own.reshape(parts), swap(send, first_plane).reshape(parts)
+    return own.reshape(-1, CHIPS // 4, 2, rows, side), send
 
 
 def scatter_second(*pairs):
@@ -760,7 +788,7 @@
     out = pl.BlockSpec((count // steps, rows, side), lambda i: (i, 0, 0))
     rest, send = call(
         merge_first, (steps,), ins, [(out, shaped(count, rows, side, dtype=F32)), (out, shaped(count, rows, side))], [],
-        "merge_first", LONG, *pairs)
+        "merge_first", 0, *pairs)
     return rest, swap(send, second_plane)
 
 
@@ -836,21 +864,24 @@
     kept_vec = (kept_spec((16, width)), shaped(16, width, dtype=F32))
     kept_hidden = (kept_spec((1, hidden // 2)), shaped(1, hidden // 2, dtype=F32))
     side = width // 2
-    lengths_spec = SMEM
-    rows_outs = [low_rows] * 5 + [sums]
+
+    def masked(*earlier):
+        return call(
+            mask_grads, (tiles,), [SMEM, tile_rows], [low_rows, sums], [], "mask_grads", 0,
+            lengths, after(grad_out, *earlier))
+
     if by_hand:
-        near, far = gather_by_hand(me, weights, vectors)
-        n1, q, k, v, cot, sum_down, wq, wk, wv, wo, vec, bup = call_with(
-            me, project, tiles, [lengths_spec, tile_rows, tile_rows] + [ANY_SPEC] * 8,
-            rows_outs + [kept_square] * 4 + [kept_vec, kept_hidden],
-            [pltpu.VMEM((count, 16, side), BF16), pltpu.SemaphoreType.DMA((5,))], "project", 0,
-            lengths, tokens, grad_out, *near)
+        near, far, cot, sum_down = gather_by_hand(me, weights, vectors, masked)
+        n1, q, k, v, wq, wk, wv, wo, vec, bup = call_with(
+            me, project, tiles, [tile_rows] + [ANY_SPEC] * 8, [low_rows] * 4 + [kept_square] * 4 + [kept_vec, kept_hidden],
+            [pltpu.VMEM((count, 16, side), BF16), pltpu.SemaphoreType.DMA((5,))], "project", 0, tokens, *near)
         cot_other = swap(cot, other_core)
     else:
         wq, wk, wv, wo, far, vec, bup = gather_plain(weights, vectors)
-        n1, q, k, v, cot, sum_down = call(
-            project_rows, (tiles,), [lengths_spec, tile_rows, tile_rows, vec_spec, square, square, square], rows_outs,
-            [], "project", 0, lengths, tokens, grad_out, vec, wq, wk, wv)
+        cot, sum_down = masked()
+        n1, q, k, v = call(
+            project_rows, (tiles,), [tile_rows, vec_spec, square, square, square], [low_rows] * 4,
+            [], "project", 0, tokens, vec, wq, wk, wv)
     high_rows = (tile_rows, shaped(rows, width, dtype=F32))
     mixed, lse, resid, n2 = call(
         attention_forward, (tiles,), [SMEM, tile_rows, vec_spec, tile_rows, tile_rows, tile_rows, square],
@@ -865,8 +896,13 @@
     down_spec = pl.BlockSpec((CHIPS // 2, 1, deep, width), lambda i, me: (i, me[0] & 1, 1, 0))
     hidden_spec = pl.BlockSpec((1, width), lambda i, me: (0, i))
     low_out, high_out = (ANY_SPEC, shaped(rows, width)), (ANY_SPEC, shaped(rows, width, dtype=F32))
+    act_out = (ANY_SPEC, shaped(rows, blocks * width))
     down_part = (ANY_SPEC, shaped(4, 2, deep, width))
     up_part = (ANY_SPEC, shaped(blocks, 4, 2, each, width))
+
+    act_spec = pl.BlockSpec((tile, blocks * width), lambda i, *me: (i, 0))
+    wide_spec = pl.BlockSpec(
+        (CHIPS, 1, deep, width), lambda i, me: (0, me[0] & 1, 1, 0), pipeline_mode=pl.Buffered(1))
 
     def run_mlp(me, tokens_of, bup):
         sets = len(tokens_of[0])
@@ -875,25 +911,24 @@
         dma = pltpu.SemaphoreType.DMA((2, sets))
         return call_with(
             me, functools.partial(mlp, sets), blocks, [ANY_SPEC] * (2 * sets) + [hidden_spec, up_spec, down_spec],
-            [low_out] * sets + [high_out] + [low_out] * (sets - 1) + [down_part] * 2 + [up_part] * 2
+            [act_out] * sets + [high_out] + [low_out] * (sets - 1) + [down_part] * 2 + [up_part] * 2
             + [(hidden_spec, shaped(1, hidden // 2, dtype=F32))],
-            [low, low, high, high, low, low, pltpu.VMEM((2, sets * rows, width), BF16), weight, weight, dma, dma,
-             pltpu.SemaphoreType.DMA((4,))],
+            [low, low, high, pltpu.VMEM((blocks, sets * rows, width), BF16), low, low, weight, weight, dma,
+             pltpu.SemaphoreType.DMA((blocks, sets)), pltpu.SemaphoreType.DMA((sets,)), pltpu.SemaphoreType.DMA((4,))],
             "mlp", 0, *tokens_of[0], *tokens_of[1], bup, far, far)
 
     if by_hand:
         cot_other = after(cot_other, mixed)
         n2_other = swap(n2, other_core)
-        out_own, out_other, gtwo, gtwo_other, down_own, down_send, up_own, up_send, sum_up = run_mlp(
+        act_own, act_other, gtwo, gtwo_other, down_own, down_send, up_own, up_send, sum_up = run_mlp(
             me, ((n2, n2_other), (cot, cot_other)), bup)
         gtwo_take = swap(gtwo_other, other_core)
-        out_take = swap(out_other, other_core)
         parts = (-1, CHIPS // 4, 2)
         down_first = [piece.reshape(*parts, deep, width) for piece in (down_own, swap(down_send, first_plane))]
         up_first = [piece.reshape(*parts, each, width) for piece in (up_own, swap(up_send, first_plane))]
     else:
         runs = [run_mlp(me + half, ((n2,), (cot,)), bup[half]) for half in range(2)]
-        (out_own, gtwo), (out_take, gtwo_take) = ((run[0], run[1]) for run in runs)
+        (act_own, gtwo), (act_other, gtwo_take) = ((run[0], run[1]) for run in runs)
         gtwo_take = gtwo_take.astype(BF16)
         sum_up = jnp.concatenate([run[6] for run in runs], axis=1)
     grads_spec = pl.BlockSpec((4, tile, width), lambda i, *me: (0, i, 0))
@@ -902,55 +937,75 @@
         [SMEM, tile_rows, tile_rows, tile_rows, lse_spec, tile_rows, tile_rows, tile_rows, tile_rows, vec_spec, square],
         [(grads_spec, shaped(4, rows, width)), high_rows, sums], [pltpu.VMEM((tile, width), BF16)],
         "attention_backward", 0, lengths, q, k, v, lse, cot, resid, gtwo, gtwo_take, vec, wo)
-    if by_hand:
-        down_first, up_first = after((down_first, up_first), grads)
-        hidden_second = scatter_second(*down_first, *up_first)
-        gresid = after(gresid, hidden_second[0])
     sum_spec = whole_spec((8, width))
     pair_shape = (CHIPS // 4, 4, 4 * each + 16, side)
-    tile_at = pl.BlockSpec((tile, width), lambda i, me: (jnp.minimum(i, tiles - 1), 0))
-    tile_grads = pl.BlockSpec((4, tile, width), lambda i, me: (0, jnp.minimum(i, tiles - 1), 0))
-    columns = pl.BlockSpec((1, rows, width), lambda i, me: (jnp.maximum(i - tiles, 0), 0, 0))
-    gtok, sum_one, square_send, square_keep = call_with(
-        me, projections_backward, tiles + 4,
-        [tile_at, tile_at, vec_spec, tile_grads, square, square, square, full_rows, full_rows, columns, sum_spec, sum_spec,
-         whole_spec((1, sum_up.shape[1]))],
-        [(tile_at, shaped(rows, width)), sums] + [(kept_spec(pair_shape), shaped(*pair_shape))] * 2, [],
-        "projections_backward", 7 * mac,
-        tokens, gresid, vec, grads, wq, wk, wv, n1, mixed, grads, sum_back, sum_down, sum_up)
+    columns = pl.BlockSpec((1, rows, width), lambda i, me: (i, 0, 0))
+
+    def run_weights(grads):
+        return call_with(
+            me, weight_grads, 4, [full_rows] * 2 + [columns, sum_spec, sum_spec, whole_spec((1, sum_up.shape[1]))],
+            [(kept_spec(pair_shape), shaped(*pair_shape))] * 2, [], "weight_grads", 0,
+            n1, mixed, grads, sum_back, sum_down, sum_up)
+
+    def run_tokens(gresid):
+        return call(
+            tokens_backward, (tiles,), [tile_rows, tile_rows, vec_spec, grads_spec, square, square, square],
+            [low_rows, sums], [], "tokens_backward", MIDDLE, tokens, gresid, vec, grads, wq, wk, wv)
+
     if by_hand:
-        square_send = after(square_send, hidden_second[1])
-        square_take = scatter_core(square_send)
-        hidden_layers = scatter_layers(*hidden_second)
-        square_keep = after(square_keep, hidden_layers[0])
-        square_first = scatter_first(core, square_keep, square_take)
-        resid = after(resid, square_first[0])
-        (out,) = call(
-            add_rows, (tiles,), [tile_rows, vec_spec, tile_rows, tile_rows], [low_rows], [], "add_rows", 0,
-            resid, vec, out_own, out_take)
-        square_first = after(square_first, out)
-        square_second = scatter_second(*square_first)
-        hidden_layers = after(hidden_layers, square_second[0])
+        (out_other,) = call_with(
+            me, mlp_out_other, tiles, [act_spec, wide_spec], [low_rows], [], "mlp_out_other", 0, after(act_other, grads), far)
+        down_first, up_first = after((down_first, up_first), out_other)
+        hidden_rest, hidden_take = scatter_second(*down_first, *up_first)
+
+        def weights_of_chip(grads):
+            square_send, square_keep = run_weights(grads)
+            return merge_core_of(core, square_keep, scatter_core(square_send))
+
+        square_own, square_send = fenced(weights_of_chip, after(grads, hidden_rest))
+        square_take = swap(square_send, first_plane).reshape(square_own.shape)
+        hidden_rest, hidden_take = after((hidden_rest, hidden_take), square_own)
+        hidden_layers = scatter_layers(hidden_rest, hidden_take)
+        gtok, late = run_tokens(after(gresid, hidden_layers[0]))
+        square_take = after(square_take, late)
+        late = late + swap(late, other_core)
+        square_second = scatter_second(square_own, square_take)
+        late = after(late, square_second[0])
+        out_take = after(swap(out_other, other_core), square_second[0])
+        (out,) = call_with(
+            me, mlp_out_own, tiles, [tile_rows, vec_spec, act_spec, tile_rows, wide_spec], [low_rows], [],
+            "mlp_out_own", 0, resid, vec, act_own, out_take, far)
+        late = late + after(swap(late, other_layer(1)), out)
+        hidden_layers = after(hidden_layers, late)
         g_down, up_keep, up_send = scatter_last(core, hidden_layers, own, blocks, deep)
         up_take = scatter_core(up_send)
-        square_second = after(square_second, g_down)
+        late = late + after(swap(late, other_layer(2)), g_down)
+        square_second = after(square_second, g_down, late)
         square_layers = scatter_layers(*square_second)
+        late = late + after(swap(late, other_plane(1)), square_layers[0])
+        late = late + swap(late, other_plane(2))
+        square_layers = after(square_layers, late)
         square_keep, square_send, flat = scatter_last(core, square_layers, own, 4, 0)
         square_take = scatter_core(square_send)
         outs = [(VMEM_SPEC, shaped(own, hidden, dtype=F32))] + [(VMEM_SPEC, shaped(own, width, dtype=F32))] * 4
         outs += [(VMEM_SPEC, shaped(own, dtype=F32))] * 8 + [(VMEM_SPEC, shaped(folds * own, dtype=F32))]
         g_up, g_q, g_k, g_v, g_o, *g_flat, g_ub = small_call(
-            finish, (me, up_keep, up_take, square_keep, square_take, flat), outs, "finish", ins=[SMEM] + [VMEM_SPEC] * 5)
+            finish, (me, up_keep, up_take, square_keep, square_take, flat, late), outs, "finish",
+            ins=[SMEM] + [VMEM_SPEC] * 6)
     else:
+        square_send, square_keep = run_weights(grads)
+        gtok, sum_one = run_tokens(gresid)
         flat = jnp.concatenate((sum_one[0:2], sum_back[0:5], sum_down[0:1]), axis=0)
         flat = flat.reshape(8, count, own).transpose(1, 0, 2).reshape(count, 8 * own)
         hidden_sums = sum_up.reshape(2, CHIPS, deep).transpose(1, 0, 2).reshape(count, folds * own)
         flat = jnp.concatenate((flat, hidden_sums), axis=1)
         g_down, g_up, g_q, g_k, g_v, g_o, flat = reduce_plain(
             [run[2:4] for run in runs], [run[4:6] for run in runs], (square_keep, square_send), flat)
-        (out,) = call(
-            add_rows, (tiles,), [tile_rows, vec_spec, tile_rows, tile_rows], [low_rows], [], "add_rows", 0,
-            resid, vec, out_own, out_take)
+        (out_other,) = call_with(
+            me + 1, mlp_out_other, tiles, [act_spec, wide_spec], [low_rows], [], "mlp_out_other", 0, act_other, far)
+        (out,) = call_with(
+            me, mlp_out_own, tiles, [tile_rows, vec_spec, act_spec, tile_rows, wide_spec], [low_rows], [],
+            "mlp_out_own", 0, resid, vec, act_own, out_other, far)
         g_flat = [flat[index * own : (index + 1) * own] for index in range(8)]
         g_ub = flat[8 * own :]
     g_gain, g_shift, g_qb, g_vb, g_ob, g_mg, g_ms, g_db = g_flat

time: 276 us -> 270 us (0.978)
  waiting for transfers between devices: 96.7 us -> 73.9 us
  other arithmetic: 1.01 us -> 7.29 us
  starting transfers between devices: 24.9 us -> 31.1 us
  Pallas kernels: 136 us -> 142 us
    ppermute x29 -> x34, waiting for transfers between devices: 96.7 us -> 64.7 us  [swap(): return lax.ppermute(array, 'dp', flipped(lax.axis_size('dp'), change))]
    all_gather x1, waiting for transfers between devices: 0.01 us -> 9.22 us  [gather_by_hand(): lax.all_gather(far, 'dp', axis=0, tiled=True)]
    pallas_call x6 -> x7, Pallas kernels: 48.6 us -> 57.8 us  [call(): pl.pallas_call(kernel, grid=grid, in_specs=ins, out_specs=out_specs, out_...]
    ppermute x29 -> x34, starting transfers between devices: 24.8 us -> 31 us  [swap(): return lax.ppermute(array, 'dp', flipped(lax.axis_size('dp'), change))]
    add x0 -> x5, other arithmetic: none -> 5.45 us  [the longest x1 1.37 us: body(): late = late + after(swap(late, other_layer(1)), out)]
    pallas_call x3 -> x5, Pallas kernels: 71.3 us -> 68.6 us  [call_with(): pl.pallas_call(kernel, grid_spec=pltpu.PrefetchScalarGridSpec(num_scalar_...]
  transfers between devices with their start and end apart: 30 -> 35, of which waited for: 17 -> 15; matrix products, arithmetic and copies ran while one was open for 0% -> 3% of each run, Pallas kernels for 31% -> 36%
where the time goes in v5:
time: 270 us; the launch traced here: 269 us
  Pallas kernels  142 us (53%)
  waiting for transfers between devices  73.9 us (27%)
  starting transfers between devices  31.1 us (12%)
  between operations  14.2 us (5%)
  other arithmetic  7.29 us (3%)
    pallas_call x5, Pallas kernels, call_with(): pl.pallas_call(kernel, grid_spec=pltpu.PrefetchScalarGridSpec(num_scalar_...  68.6 us
    ppermute x34, waiting for transfers between devices, swap(): return lax.ppermute(array, 'dp', flipped(lax.axis_size('dp'), change))  64.7 us
    pallas_call x7, Pallas kernels, call(): pl.pallas_call(kernel, grid=grid, in_specs=ins, out_specs=out_specs, out_...  57.8 us
    ppermute x34, starting transfers between devices, swap(): return lax.ppermute(array, 'dp', flipped(lax.axis_size('dp'), change))  31 us
    pallas_call x7, Pallas kernels, small_call(): pl.pallas_call(kernel, in_specs=ins, out_specs=tuple((spec for spec, _ in...  15.6 us
    all_gather x1, waiting for transfers between devices, gather_by_hand(): lax.all_gather(far, 'dp', axis=0, tiled=True)  9.22 us
  transfers between devices with their start and end apart: 35, of which 15 were waited for; matrix products, arithmetic and copies ran while one was open for 3% of the time, Pallas kernels for 36%

profile of v5, /device:TPU:0, one launch (start us, length us, event | category | flops | bytes accessed | tf_op | source)
XLA Modules:
  0.0 269.4 jit_solution(4154224617143145059)
XLA Ops:
  10.9 2.0 join_shards.1
  12.9 3.0 %collective-permute-start.2 = (bf16[208,384]{1,0:T(8,128)(2,1)}, bf16[208,384]{1,0:T(8,128)(2,1)S(1)}, u32[]{:S(2)}, u32[]{:S(2)}) collective-permute-start(bf16[208,384]{1,0:T(8,128)(2,1)} %get-tuple-element.143), channel_id=1, source_target_pairs={{0,8},{1,9},{2,10},{3,11},{4,12},{5,13},{6,14},{7,15},{8,0},{9,1},... | collective-permute-start | bytes 479240 | tf_op jit(solution)/shard_map/ppermute | solution.py:525
  15.9 2.6 collective-permute-start.3
  18.5 4.7 %collective-permute-done.2 = bf16[208,384]{1,0:T(8,128)(2,1)S(1)} collective-permute-done((bf16[208,384]{1,0:T(8,128)(2,1)}, bf16[208,384]{1,0:T(8,128)(2,1)S(1)}, u32[]{:S(2)}, u32[]{:S(2)}) %collective-permute-start.2) | collective-permute-done | bytes 159776 | tf_op jit(solution)/shard_map/ppermute | solution.py:525
  23.3 10.0 %collective-permute-done.3 = bf16[208,384]{1,0:T(8,128)(2,1)S(1)} collective-permute-done((bf16[208,384]{1,0:T(8,128)(2,1)}, bf16[208,384]{1,0:T(8,128)(2,1)S(1)}, u32[]{:S(2)}, u32[]{:S(2)}) %collective-permute-start.3) | collective-permute-done | bytes 159776 | tf_op jit(solution)/shard_map/ppermute | solution.py:525
  38.1 3.8 %mask_grads.1 = (bf16[1024,768]{1,0:T(8,128)(2,1)}, f32[8,768]{1,0:T(8,128)}) custom-call(s32[4,5]{1,0:T(4,128)} %lengths_ref.5, bf16[1024,768]{1,0:T(8,128)(2,1)} %grad_ref), custom_call_target="tpu_custom_call" | custom-call | bytes 1 | tf_op jit(solution)/shard_map/mask_grads/pallas_call | solution.py:484
  42.0 15.9 %collective-permute-done.5.refs_1_ = bf16[4,208,384]{2,1,0:T(8,128)(2,1)} collective-permute-done((bf16[4,208,384]{2,1,0:T(8,128)(2,1)}, bf16[4,208,384]{2,1,0:T(8,128)(2,1)}, u32[]{:S(2)}, u32[]{:S(2)}) %collective-permute-start.5) | collective-permute-done | bytes 639008 | tf_op jit(solution)/shard_map/ppermute | solution.py:525
  58.4 10.1 %collective-permute-done.7.refs_3_ = bf16[4,208,384]{2,1,0:T(8,128)(2,1)S(1)} collective-permute-done((bf16[4,208,384]{2,1,0:T(8,128)(2,1)}, bf16[4,208,384]{2,1,0:T(8,128)(2,1)S(1)}, u32[]{:S(2)}, u32[]{:S(2)}) %collective-permute-start.7) | collective-permute-done | bytes 639008 | tf_op jit(solution)/shard_map/ppermute | solution.py:525
  69.8 2.6 collective-permute-done.11.refs_7_
  72.4 10.2 %project.1 = (bf16[1024,768]{1,0:T(8,128)(2,1)}, bf16[1024,768]{1,0:T(8,128)(2,1)}, bf16[1024,768]{1,0:T(8,128)(2,1)}, bf16[1024,768]{1,0:T(8,128)(2,1)}, bf16[7...) custom-call(s32[1]{0:T(128)} %bitcast.1.me_ref, ...), custom_call_target="tpu_custom_call" | custom-call | bytes 1 | tf_op jit(solution)/shard_map/project/pallas_call | solution.py:499
  82.6 13.3 %attention_forward.1 = (bf16[1024,768]{1,0:T(8,128)(2,1)}, f32[1024,128]{1,0:T(8,128)}, f32[1024,768]{1,0:T(8,128)}, bf16[1024,768]{1,0:T(8,128)(2,1)}) custom-call(s32[4,5]{1,0:T(4,128)} %lengths_ref.5, bf16[1024,768]{1,0:T(8,128)(2,1)} %x_ref.5, f32[16,768]{1,0:T(8,128)} %get-tuple-element.147.vec_ref, bf16[1024,768]{1,0:T(8,128)(2,1)} %get-tuple-element.148.q_ref, ...), custom_call_target="tpu_custom_call" | custom-call | bytes 1 | tf_op jit(solution)/shard_map/attention_forward/pallas_call | solution.py:484
  96.1 3.7 %collective-permute-done.12.refs_1_ = bf16[1024,768]{1,0:T(8,128)(2,1)} collective-permute-done((bf16[1024,768]{1,0:T(8,128)(2,1)}, bf16[1024,768]{1,0:T(8,128)(2,1)}, u32[]{:S(2)}, u32[]{:S(2)}) %collective-permute-start.12) | collective-permute-done | bytes 1572896 | tf_op jit(solution)/shard_map/ppermute | solution.py:525
  99.8 9.2 %all-gather.2.cloned.1.call-done = bf16[6144,768]{1,0:T(8,128)(2,1)} async-done(((bf16[192,768]{1,0:T(8,128)(2,1)}), bf16[6144,768]{1,0:T(8,128)(2,1)}) %all-gather.2.cloned.1.call-update) | async-done | bytes 9437200 | tf_op jit(solution)/shard_map/all_gather | solution.py:642
  109.0 34.3 %mlp.1 = (bf16[1024,1536]{1,0:T(8,128)(2,1)}, bf16[1024,1536]{1,0:T(8,128)(2,1)}, f32[1024,768]{1,0:T(8,128)}, bf16[1024,768]{1,0:T(8,128)(2,1)}, bf16[4,2,96,76...) custom-call(s32[1]{0:T(128)} %bitcast.1.me_ref, ...), custom_call_target="tpu_custom_call" | custom-call | bytes 1 | tf_op jit(solution)/shard_map/mlp/pallas_call | solution.py:499
  147.1 20.7 %attention_backward.1 = (bf16[4,1024,768]{2,1,0:T(8,128)(2,1)}, f32[1024,768]{1,0:T(8,128)}, f32[8,768]{1,0:T(8,128)}) custom-call(s32[4,5]{1,0:T(4,128)} %lengths_ref.5, bf16[1024,768]{1,0:T(8,128)(2,1)} %get-tuple-element.148.q_ref, bf16[1024,768]{1,0:T(8,128)(2,1)} %get-tuple-element.149.k_ref, bf16[1024,768]{1,0:T(8,128)(2,1)} %get-tuple-element.150.v_ref, ...), custom_call_target="tpu_custom_call" | custom-call | bytes 1 | tf_op jit(solution)/shard_map/attention_backward/pallas_call | solution.py:484
  167.8 6.4 %mlp_out_other.1 = bf16[1024,768]{1,0:T(8,128)(2,1)} custom-call(s32[1]{0:T(128)} %bitcast.1.me_ref, bf16[1024,1536]{1,0:T(8,128)(2,1)} %get-tuple-element.164.act_ref, bf16[16,2,192,768]{3,2,1,0:T(8,128)(2,1)} %bitcast.12), custom_call_target="tpu_custom_call" | custom-call | bytes 1 | tf_op jit(solution)/shard_map/mlp_out_other/pallas_call | solution.py:499
  174.3 3.8 %merge_first.2 = (f32[4,192,768]{2,1,0:T(8,128)}, bf16[4,192,768]{2,1,0:T(8,128)(2,1)}) custom-call(bf16[1,4,2,96,768]{4,3,2,1,0:T(8,128)(2,1)} %bitcast.14, bf16[1,4,2,96,768]{4,3,2,1,0:T(8,128)(2,1)} %bitcast.8.refs_1_, bf16[2,4,2,48,768]{4,3,2,1,0:T(8,128)(2,1)} %get-tuple-element.172.refs_2_, bf16[2,4,2,48,768]{4,3,2,1,0:T(8,128)(2,1)} %collective-permute-done.17.refs_3_), custom_call_target="tpu_custom_call" | custom-call | bytes 1 | tf_op jit(solution)/shard_map/merge_first/pallas_call | solution.py:484
  179.5 19.5 %conditional.1 = (bf16[1,4,2,208,384]{4,3,2,1,0:T(8,128)(2,1)}, bf16[4,2,208,384]{3,2,1,0:T(8,128)(2,1)}) conditional(s32[]{:T(128)} %convert_element_type.3, () %tuple.37, (s32[1]{0:T(128)}, bf16[1024,768]{1,0:T(8,128)(2,1)}, bf16[1024,768]{1,0:T(8,128)(2,1)}, bf16[4,1024,768]{2,1,0:T(8,128)(2,1)}, f32[8,768]{1,0:T(8,128)}, ...), branch_computations={%region_0.0_spmd, %region_1.0_spmd} | conditional | bytes 10223674 | solution.py:764
  179.5 10.5 %weight_grads.1 = (bf16[4,4,208,384]{3,2,1,0:T(8,128)(2,1)}, bf16[4,4,208,384]{3,2,1,0:T(8,128)(2,1)}) custom-call(s32[1]{0:T(128)} %get-tuple-element.17.me_ref, bf16[1024,768]{1,0:T(8,128)(2,1)} %get-tuple-element.18.n1_ref, bf16[1024,768]{1,0:T(8,128)(2,1)} %get-tuple-element.19.mixed_ref, bf16[4,1024,768]{2,1,0:T(8,128)(2,1)} %get-tuple-element.20.columns_ref, ...), custom_call_target="tpu_custom_call" | custom-call | bytes 1 | tf_op jit(solution)/shard_map/cond/branch_1_fun/weight_grads/pallas_call | solution.py:499
  190.5 4.8 %collective-permute-done.take_ref = bf16[4,4,208,384]{3,2,1,0:T(8,128)(2,1)} collective-permute-done((bf16[4,4,208,384]{3,2,1,0:T(8,128)(2,1)}, bf16[4,4,208,384]{3,2,1,0:T(8,128)(2,1)}, u32[]{:S(2)}, u32[]{:S(2)}) %collective-permute-start) | collective-permute-done | bytes 2555936 | tf_op jit(solution)/shard_map/cond/branch_1_fun/ppermute | solution.py:525
  195.3 3.7 %merge_core.1 = (bf16[4,2,208,384]{3,2,1,0:T(8,128)(2,1)}, bf16[4,2,208,384]{3,2,1,0:T(8,128)(2,1)}) custom-call(s32[1]{0:T(128)} %get-tuple-element.16.core_ref, bf16[4,4,208,384]{3,2,1,0:T(8,128)(2,1)} %get-tuple-element.24.keep_ref, bf16[4,4,208,384]{3,2,1,0:T(8,128)(2,1)} %collective-permute-done.take_ref), custom_call_target="tpu_custom_call" | custom-call | bytes 1 | tf_op jit(solution)/shard_map/cond/branch_1_fun/merge_core/pallas_call | solution.py:484
  199.6 3.1 %merge_second.2 = (f32[192,768]{1,0:T(8,128)}, bf16[192,768]{1,0:T(8,128)(2,1)}, bf16[192,768]{1,0:T(8,128)(2,1)}, bf16[192,768]{1,0:T(8,128)(2,1)}) custom-call(f32[4,192,768]{2,1,0:T(8,128)} %get-tuple-element.183.own_ref, bf16[4,192,768]{2,1,0:T(8,128)(2,1)} %collective-permute-done.19.take_ref), custom_call_target="tpu_custom_call" | custom-call | bytes 1 | tf_op jit(solution)/shard_map/merge_second/pallas_call | solution.py:612
  202.7 2.6 collective-permute-start.20
  207.7 9.8 %tokens_backward.1 = (bf16[1024,768]{1,0:T(8,128)(2,1)}, f32[8,768]{1,0:T(8,128)}) custom-call(bf16[1024,768]{1,0:T(8,128)(2,1)} %x_ref.5, f32[1024,768]{1,0:T(8,128)} %get-tuple-element.186.gresid_ref, f32[16,768]{1,0:T(8,128)} %get-tuple-element.147.vec_ref, bf16[4,1024,768]{2,1,0:T(8,128)(2,1)} %get-tuple-element.175.grads_ref, ...), custom_call_target="tpu_custom_call" | custom-call | flops 11500000256 | bytes 1 | tf_op jit(solution)/shard_map/tokens_backward/pallas_call | solution.py:484
  217.6 2.7 %merge_first.3 = (f32[4,208,384]{2,1,0:T(8,128)}, bf16[4,208,384]{2,1,0:T(8,128)(2,1)}) custom-call(bf16[1,4,2,208,384]{4,3,2,1,0:T(8,128)(2,1)} %get-tuple-element.179.refs_0_, bf16[1,4,2,208,384]{4,3,2,1,0:T(8,128)(2,1)} %bitcast.9.refs_1_), custom_call_target="tpu_custom_call" | custom-call | bytes 1 | tf_op jit(solution)/shard_map/merge_first/pallas_call | solution.py:484
  224.0 7.2 %mlp_out_own.1 = bf16[1024,768]{1,0:T(8,128)(2,1)} custom-call(s32[1]{0:T(128)} %bitcast.1.me_ref, f32[1024,768]{1,0:T(8,128)} %get-tuple-element.152.resid_ref, f32[16,768]{1,0:T(8,128)} %get-tuple-element.147.vec_ref, bf16[1024,1536]{1,0:T(8,128)(2,1)} %get-tuple-element.158.act_ref, bf16[1024,768]{1,0:T(8,128)(2,1)} %collective-permute-done.15.take_ref, ...), custom_call_target="tpu_custom_call" | custom-call | bytes 1 | tf_op jit(solution)/shard_map/mlp_out_own/pallas_call | solution.py:499
  234.5 2.2 merge_last.2
  239.1 2.4 merge_second.3
  242.4 2.0 collective-permute-start.29
  247.1 2.8 %collective-permute-done.31 = f32[8,768]{1,0:T(8,128)S(1)} collective-permute-done((f32[8,768]{1,0:T(8,128)}, f32[8,768]{1,0:T(8,128)S(1)}, u32[]{:S(2)}, u32[]{:S(2)}) %collective-permute-start.31) | collective-permute-done | bytes 24608 | tf_op jit(solution)/shard_map/ppermute | solution.py:525
  251.5 2.9 %collective-permute-done.32 = f32[8,768]{1,0:T(8,128)S(1)} collective-permute-done((f32[8,768]{1,0:T(8,128)S(1)}, f32[8,768]{1,0:T(8,128)S(1)}, u32[]{:S(2)}, u32[]{:S(2)}) %collective-permute-start.32) | collective-permute-done | bytes 24608 | tf_op jit(solution)/shard_map/ppermute | solution.py:525
  260.4 2.1 finish.1
  (67 shorter events, 40.0 us)
Async XLA Ops:
  7.2 101.8 %all-gather.2.cloned.1.call-start = ((), (), s32[]{:S(2)}) async-start(), calls=%async_computation | async-start | bytes 9732096 | tf_op jit(solution)/shard_map/all_gather | solution.py:642
  12.9 10.3 %collective-permute-start.2 = (bf16[208,384]{1,0:T(8,128)(2,1)}, bf16[208,384]{1,0:T(8,128)(2,1)S(1)}, u32[]{:S(2)}, u32[]{:S(2)}) collective-permute-start(bf16[208,384]{1,0:T(8,128)(2,1)} %get-tuple-element.143), channel_id=1, source_target_pairs={{0,8},{1,9},{2,10},{3,11},{4,12},{5,13},{6,14},{7,15},{8,0},{9,1},... | collective-permute-start | bytes 479240 | tf_op jit(solution)/shard_map/ppermute | solution.py:525
  15.9 17.4 %collective-permute-start.3 = (bf16[208,384]{1,0:T(8,128)(2,1)}, bf16[208,384]{1,0:T(8,128)(2,1)S(1)}, u32[]{:S(2)}, u32[]{:S(2)}) collective-permute-start(bf16[208,384]{1,0:T(8,128)(2,1)} %get-tuple-element.143), channel_id=1, source_target_pairs={{0,16},{1,17},{2,18},{3,19},{4,20},{5,21},{6,22},{7,23},{8,24},{9,... | collective-permute-start | bytes 479240 | tf_op jit(solution)/shard_map/ppermute | solution.py:525
  18.5 14.8 %collective-permute-start.4 = (bf16[208,384]{1,0:T(8,128)(2,1)}, bf16[208,384]{1,0:T(8,128)(2,1)S(1)}, u32[]{:S(2)}, u32[]{:S(2)}) collective-permute-start(bf16[208,384]{1,0:T(8,128)(2,1)} %get-tuple-element.143), channel_id=1, source_target_pairs={{0,24},{1,25},{2,26},{3,27},{4,28},{5,29},{6,30},{7,31},{8,16},{9,... | collective-permute-start | bytes 479240 | tf_op jit(solution)/shard_map/ppermute | solution.py:525
  35.1 22.7 %collective-permute-start.5 = (bf16[4,208,384]{2,1,0:T(8,128)(2,1)}, bf16[4,208,384]{2,1,0:T(8,128)(2,1)}, u32[]{:S(2)}, u32[]{:S(2)}) collective-permute-start(bf16[4,208,384]{2,1,0:T(8,128)(2,1)} %pad_maximum_fusion.refs_0_), channel_id=1, source_target_pairs={{0,2},{1,5},{2,0},{3,7},{4,6},{5,1},{6,4},{7,3},{8,10},{9,13},{10,... | collective-permute-start | bytes 1916936 | tf_op jit(solution)/shard_map/ppermute | solution.py:525
  36.6 21.7 %collective-permute-start.6 = (bf16[4,208,384]{2,1,0:T(8,128)(2,1)}, bf16[4,208,384]{2,1,0:T(8,128)(2,1)}, u32[]{:S(2)}, u32[]{:S(2)}) collective-permute-start(bf16[4,208,384]{2,1,0:T(8,128)(2,1)} %pad_maximum_fusion.refs_0_), channel_id=1, source_target_pairs={{0,4},{1,3},{2,6},{3,1},{4,0},{5,7},{6,2},{7,5},{8,12},{9,11},{10,... | collective-permute-start | bytes 1916936 | tf_op jit(solution)/shard_map/ppermute | solution.py:525
  57.8 10.6 %collective-permute-start.7 = (bf16[4,208,384]{2,1,0:T(8,128)(2,1)}, bf16[4,208,384]{2,1,0:T(8,128)(2,1)S(1)}, u32[]{:S(2)}, u32[]{:S(2)}) collective-permute-start(bf16[4,208,384]{2,1,0:T(8,128)(2,1)} %collective-permute-done.5.refs_1_), channel_id=1, source_target_pairs={{0,4},{1,3},{2,6},{3,1},{4,0},{5,7},{6,2},{7,5},{8,12},{9,11},{10,... | collective-permute-start | bytes 1916936 | tf_op jit(solution)/shard_map/ppermute | solution.py:525
  57.9 12.0 %collective-permute-start.8 = (bf16[4,208,384]{2,1,0:T(8,128)(2,1)}, bf16[4,208,384]{2,1,0:T(8,128)(2,1)}, u32[]{:S(2)}, u32[]{:S(2)}) collective-permute-start(bf16[4,208,384]{2,1,0:T(8,128)(2,1)} %pad_maximum_fusion.refs_0_), channel_id=1, source_target_pairs={{0,1},{1,0},{2,3},{3,2},{4,5},{5,4},{6,7},{7,6},{8,9},{9,8},{10,11... | collective-permute-start | bytes 1916936 | tf_op jit(solution)/shard_map/ppermute | solution.py:525
  57.9 12.0 %collective-permute-start.9 = (bf16[4,208,384]{2,1,0:T(8,128)(2,1)}, bf16[4,208,384]{2,1,0:T(8,128)(2,1)}, u32[]{:S(2)}, u32[]{:S(2)}) collective-permute-start(bf16[4,208,384]{2,1,0:T(8,128)(2,1)} %collective-permute-done.5.refs_1_), channel_id=1, source_target_pairs={{0,1},{1,0},{2,3},{3,2},{4,5},{5,4},{6,7},{7,6},{8,9},{9,8},{10,11... | collective-permute-start | bytes 1916936 | tf_op jit(solution)/shard_map/ppermute | solution.py:525
  58.4 11.5 %collective-permute-start.10 = (bf16[4,208,384]{2,1,0:T(8,128)(2,1)}, bf16[4,208,384]{2,1,0:T(8,128)(2,1)}, u32[]{:S(2)}, u32[]{:S(2)}) collective-permute-start(bf16[4,208,384]{2,1,0:T(8,128)(2,1)} %collective-permute-done.6.refs_2_), channel_id=1, source_target_pairs={{0,1},{1,0},{2,3},{3,2},{4,5},{5,4},{6,7},{7,6},{8,9},{9,8},{10,11... | collective-permute-start | bytes 1916936 | tf_op jit(solution)/shard_map/ppermute | solution.py:525
  69.3 3.1 %collective-permute-start.11 = (bf16[4,208,384]{2,1,0:T(8,128)(2,1)S(1)}, bf16[4,208,384]{2,1,0:T(8,128)(2,1)}, u32[]{:S(2)}, u32[]{:S(2)}) collective-permute-start(bf16[4,208,384]{2,1,0:T(8,128)(2,1)S(1)} %collective-permute-done.7.refs_3_), channel_id=1, source_target_pairs={{0,1},{1,0},{2,3},{3,2},{4,5},{5,4},{6,7},{7,6},{8,9},{9,8},{10,11... | collective-permute-start | bytes 1916936 | tf_op jit(solution)/shard_map/ppermute | solution.py:525
  69.3 26.8 %collective-permute-start.13 = (bf16[1024,768]{1,0:T(8,128)(2,1)}, bf16[1024,768]{1,0:T(8,128)(2,1)}, u32[]{:S(2)}, u32[]{:S(2)}) collective-permute-start(bf16[1024,768]{1,0:T(8,128)(2,1)} %get-tuple-element.145.refs_2_.cot_ref), channel_id=1, source_target_pairs={{0,1},{1,0},{2,3},{3,2},{4,5},{5,4},{6,7},{7,6},{8,9},{9,8},{10,11... | collective-permute-start | bytes 4718600 | tf_op jit(solution)/shard_map/ppermute | solution.py:525
  95.9 3.9 %collective-permute-start.12 = (bf16[1024,768]{1,0:T(8,128)(2,1)}, bf16[1024,768]{1,0:T(8,128)(2,1)}, u32[]{:S(2)}, u32[]{:S(2)}) collective-permute-start(bf16[1024,768]{1,0:T(8,128)(2,1)} %get-tuple-element.153.refs_0_), channel_id=1, source_target_pairs={{0,1},{1,0},{2,3},{3,2},{4,5},{5,4},{6,7},{7,6},{8,9},{9,8},{10,11... | collective-permute-start | bytes 4718600 | tf_op jit(solution)/shard_map/ppermute | solution.py:525
  143.3 3.8 %collective-permute-start.14 = (bf16[1024,768]{1,0:T(8,128)(2,1)}, bf16[1024,768]{1,0:T(8,128)(2,1)}, u32[]{:S(2)}, u32[]{:S(2)}) collective-permute-start(bf16[1024,768]{1,0:T(8,128)(2,1)} %get-tuple-element.162), channel_id=1, source_target_pairs={{0,1},{1,0},{2,3},{3,2},{4,5},{5,4},{6,7},{7,6},{8,9},{9,8},{10,11... | collective-permute-start | bytes 4718600 | tf_op jit(solution)/shard_map/ppermute | solution.py:525
  143.6 30.6 %collective-permute-start.16 = (bf16[4,2,96,768]{3,2,1,0:T(8,128)(2,1)}, bf16[4,2,96,768]{3,2,1,0:T(8,128)(2,1)}, u32[]{:S(2)}, u32[]{:S(2)}) collective-permute-start(bf16[4,2,96,768]{3,2,1,0:T(8,128)(2,1)} %get-tuple-element.167), channel_id=1, source_target_pairs={{0,2},{1,5},{2,0},{3,7},{4,6},{5,1},{6,4},{7,3},{8,10},{9,13},{10,... | collective-permute-start | bytes 3538952 | tf_op jit(solution)/shard_map/ppermute | solution.py:525
  145.1 29.2 %collective-permute-start.17 = (bf16[2,4,2,48,768]{4,3,2,1,0:T(8,128)(2,1)}, bf16[2,4,2,48,768]{4,3,2,1,0:T(8,128)(2,1)}, u32[]{:S(2)}, u32[]{:S(2)}) collective-permute-start(bf16[2,4,2,48,768]{4,3,2,1,0:T(8,128)(2,1)} %get-tuple-element.169), channel_id=1, source_target_pairs={{0,2},{1,5},{2,0},{3,7},{4,6},{5,1},{6,4},{7,3},{8,10},{9,13},{10,... | collective-permute-start | bytes 3538952 | tf_op jit(solution)/shard_map/ppermute | solution.py:525
  178.0 21.6 %collective-permute-start.19 = (bf16[4,192,768]{2,1,0:T(8,128)(2,1)}, bf16[4,192,768]{2,1,0:T(8,128)(2,1)}, u32[]{:S(2)}, u32[]{:S(2)}) collective-permute-start(bf16[4,192,768]{2,1,0:T(8,128)(2,1)} %get-tuple-element.182), channel_id=1, source_target_pairs={{0,4},{1,3},{2,6},{3,1},{4,0},{5,7},{6,2},{7,5},{8,12},{9,11},{10,... | collective-permute-start | bytes 3538952 | tf_op jit(solution)/shard_map/ppermute | solution.py:525
  179.5 43.5 %collective-permute-start.15 = (bf16[1024,768]{1,0:T(8,128)(2,1)}, bf16[1024,768]{1,0:T(8,128)(2,1)}, u32[]{:S(2)}, u32[]{:S(2)}) collective-permute-start(bf16[1024,768]{1,0:T(8,128)(2,1)} %mlp_out_other.1), channel_id=1, source_target_pairs={{0,1},{1,0},{2,3},{3,2},{4,5},{5,4},{6,7},{7,6},{8,9},{9,8},{10,11... | collective-permute-start | bytes 4718600 | tf_op jit(solution)/shard_map/ppermute | solution.py:525
  190.0 5.3 %collective-permute-start = (bf16[4,4,208,384]{3,2,1,0:T(8,128)(2,1)}, bf16[4,4,208,384]{3,2,1,0:T(8,128)(2,1)}, u32[]{:S(2)}, u32[]{:S(2)}) collective-permute-start(bf16[4,4,208,384]{3,2,1,0:T(8,128)(2,1)} %get-tuple-element.25), channel_id=1, source_target_pairs={{0,1},{1,0},{2,3},{3,2},{4,5},{5,4},{6,7},{7,6},{8,9},{9,8},{10,11... | collective-permute-start | bytes 7667720 | tf_op jit(solution)/shard_map/cond/branch_1_fun/ppermute | solution.py:525
  199.0 18.5 %collective-permute-start.18 = (bf16[4,2,208,384]{3,2,1,0:T(8,128)(2,1)}, bf16[4,2,208,384]{3,2,1,0:T(8,128)(2,1)}, u32[]{:S(2)}, u32[]{:S(2)}) collective-permute-start(bf16[4,2,208,384]{3,2,1,0:T(8,128)(2,1)} %get-tuple-element.180), channel_id=1, source_target_pairs={{0,2},{1,5},{2,0},{3,7},{4,6},{5,1},{6,4},{7,3},{8,10},{9,13},{10,... | collective-permute-start | bytes 3833864 | tf_op jit(solution)/shard_map/ppermute | solution.py:525
  202.7 31.8 %collective-permute-start.20 = (bf16[192,768]{1,0:T(8,128)(2,1)}, bf16[192,768]{1,0:T(8,128)(2,1)}, u32[]{:S(2)}, u32[]{:S(2)}) collective-permute-start(bf16[192,768]{1,0:T(8,128)(2,1)} %get-tuple-element.195), channel_id=1, source_target_pairs={{0,8},{1,9},{2,10},{3,11},{4,12},{5,13},{6,14},{7,15},{8,0},{9,1},... | collective-permute-start | bytes 884744 | tf_op jit(solution)/shard_map/ppermute | solution.py:525
  205.3 29.2 %collective-permute-start.21 = (bf16[192,768]{1,0:T(8,128)(2,1)}, bf16[192,768]{1,0:T(8,128)(2,1)}, u32[]{:S(2)}, u32[]{:S(2)}) collective-permute-start(bf16[192,768]{1,0:T(8,128)(2,1)} %get-tuple-element.196), channel_id=1, source_target_pairs={{0,16},{1,17},{2,18},{3,19},{4,20},{5,21},{6,22},{7,23},{8,24},{9,... | collective-permute-start | bytes 884744 | tf_op jit(solution)/shard_map/ppermute | solution.py:525
  206.2 28.3 %collective-permute-start.22 = (bf16[192,768]{1,0:T(8,128)(2,1)}, bf16[192,768]{1,0:T(8,128)(2,1)}, u32[]{:S(2)}, u32[]{:S(2)}) collective-permute-start(bf16[192,768]{1,0:T(8,128)(2,1)} %get-tuple-element.197), channel_id=1, source_target_pairs={{0,24},{1,25},{2,26},{3,27},{4,28},{5,29},{6,30},{7,31},{8,16},{9,... | collective-permute-start | bytes 884744 | tf_op jit(solution)/shard_map/ppermute | solution.py:525
  220.3 18.7 %collective-permute-start.26 = (bf16[4,208,384]{2,1,0:T(8,128)(2,1)}, bf16[4,208,384]{2,1,0:T(8,128)(2,1)}, u32[]{:S(2)}, u32[]{:S(2)}) collective-permute-start(bf16[4,208,384]{2,1,0:T(8,128)(2,1)} %get-tuple-element.206), channel_id=1, source_target_pairs={{0,4},{1,3},{2,6},{3,1},{4,0},{5,7},{6,2},{7,5},{8,12},{9,11},{10,... | collective-permute-start | bytes 1916936 | tf_op jit(solution)/shard_map/ppermute | solution.py:525
  223.0 8.3 %collective-permute-start.24 = (f32[8,768]{1,0:T(8,128)}, f32[8,768]{1,0:T(8,128)}, u32[]{:S(2)}, u32[]{:S(2)}) collective-permute-start(f32[8,768]{1,0:T(8,128)} %add.15), channel_id=1, source_target_pairs={{0,8},{1,9},{2,10},{3,11},{4,12},{5,13},{6,14},{7,15},{8,0},{9,1},... | collective-permute-start | bytes 73736 | tf_op jit(solution)/shard_map/ppermute | solution.py:525
  232.6 5.0 %collective-permute-start.27 = (f32[8,768]{1,0:T(8,128)}, f32[8,768]{1,0:T(8,128)}, u32[]{:S(2)}, u32[]{:S(2)}) collective-permute-start(f32[8,768]{1,0:T(8,128)} %add.16), channel_id=1, source_target_pairs={{0,16},{1,17},{2,18},{3,19},{4,20},{5,21},{6,22},{7,23},{8,24},{9,... | collective-permute-start | bytes 73736 | tf_op jit(solution)/shard_map/ppermute | solution.py:525
  241.4 13.6 %collective-permute-start.28 = (bf16[208,384]{1,0:T(8,128)(2,1)}, bf16[208,384]{1,0:T(8,128)(2,1)}, u32[]{:S(2)}, u32[]{:S(2)}) collective-permute-start(bf16[208,384]{1,0:T(8,128)(2,1)} %get-tuple-element.212), channel_id=1, source_target_pairs={{0,8},{1,9},{2,10},{3,11},{4,12},{5,13},{6,14},{7,15},{8,0},{9,1},... | collective-permute-start | bytes 479240 | tf_op jit(solution)/shard_map/ppermute | solution.py:525
  242.4 14.3 %collective-permute-start.29 = (bf16[208,384]{1,0:T(8,128)(2,1)}, bf16[208,384]{1,0:T(8,128)(2,1)}, u32[]{:S(2)}, u32[]{:S(2)}) collective-permute-start(bf16[208,384]{1,0:T(8,128)(2,1)} %get-tuple-element.213), channel_id=1, source_target_pairs={{0,16},{1,17},{2,18},{3,19},{4,20},{5,21},{6,22},{7,23},{8,24},{9,... | collective-permute-start | bytes 479240 | tf_op jit(solution)/shard_map/ppermute | solution.py:525
  244.4 12.3 %collective-permute-start.30 = (bf16[208,384]{1,0:T(8,128)(2,1)}, bf16[208,384]{1,0:T(8,128)(2,1)}, u32[]{:S(2)}, u32[]{:S(2)}) collective-permute-start(bf16[208,384]{1,0:T(8,128)(2,1)} %get-tuple-element.214), channel_id=1, source_target_pairs={{0,24},{1,25},{2,26},{3,27},{4,28},{5,29},{6,30},{7,31},{8,16},{9,... | collective-permute-start | bytes 479240 | tf_op jit(solution)/shard_map/ppermute | solution.py:525
  245.8 4.0 %collective-permute-start.31 = (f32[8,768]{1,0:T(8,128)}, f32[8,768]{1,0:T(8,128)S(1)}, u32[]{:S(2)}, u32[]{:S(2)}) collective-permute-start(f32[8,768]{1,0:T(8,128)} %add.17), channel_id=1, source_target_pairs={{0,2},{1,3},{2,0},{3,1},{4,6},{5,7},{6,4},{7,5},{8,10},{9,11},{10,... | collective-permute-start | bytes 73736 | tf_op jit(solution)/shard_map/ppermute | solution.py:525
  250.6 3.8 %collective-permute-start.32 = (f32[8,768]{1,0:T(8,128)S(1)}, f32[8,768]{1,0:T(8,128)S(1)}, u32[]{:S(2)}, u32[]{:S(2)}) collective-permute-start(f32[8,768]{1,0:T(8,128)S(1)} %add.18), channel_id=1, source_target_pairs={{0,4},{1,5},{2,6},{3,7},{4,0},{5,1},{6,2},{7,3},{8,12},{9,13},{10,... | collective-permute-start | bytes 73736 | tf_op jit(solution)/shard_map/ppermute | solution.py:525
  251.5 7.2 %collective-permute-start.25 = (f32[2,24,768]{2,1,0:T(8,128)}, f32[2,24,768]{2,1,0:T(8,128)}, u32[]{:S(2)}, u32[]{:S(2)}) collective-permute-start(f32[2,24,768]{2,1,0:T(8,128)} %get-tuple-element.205), channel_id=1, source_target_pairs={{0,1},{1,0},{2,3},{3,2},{4,5},{5,4},{6,7},{7,6},{8,9},{9,8},{10,11... | collective-permute-start | bytes 442376 | tf_op jit(solution)/shard_map/ppermute | solution.py:525
  (4 other events, 7.1 us)
Sparse Core Ops, SparseCore 0:
  13.0 95.9 all-gather.1

commit v6 on v5

--- a/solution.py
+++ b/solution.py
@@ -187,10 +187,6 @@
     n2_ref[...] = (hat * vec_ref[5:6, :] + vec_ref[6:7, :]).astype(BF16)
 
 
-def flat_rows(ref):
-    return ref[...].reshape(-1, ref.shape[-1])
-
-
 def spread(me, rows, put):
     layer, plane = me >> 3, (me >> 1) & 3
     each = rows.shape[0] // CHIPS
@@ -198,13 +194,40 @@
         put((chip & 3) ^ plane, (chip >> 2) ^ layer, rows[chip * each : (chip + 1) * each].astype(BF16))
 
 
-def mlp(sets, me_ref, *refs):
+def fetch_hidden(me, sources, wup_ref, wdown_ref, sem):
+    if len(sources) == 2:
+        for number in range(wup_ref.shape[0]):
+            pltpu.make_async_copy(sources[0].at[number], wup_ref.at[number], sem.at[number]).start()
+        pltpu.make_async_copy(sources[1], wdown_ref, sem.at[wup_ref.shape[0]]).start()
+        return
+    core, chip = me & 1, me >> 1
+    planes = (0, 1 + core, 2 - core, 3)
+    blocks, width = wup_ref.shape[:2]
+    each, deep = width // CHIPS, wdown_ref.shape[0] // CHIPS
+    for layer in range(4):
+        for index, plane in enumerate(planes):
+            owner = chip ^ (4 * layer + plane)
+            rows = pl.ds(pl.multiple_of(owner * each, 16), each)
+            side = sources[index].shape[2]
+            for part in range(sources[index].shape[1] // each):
+                number, cols = part * side // width, pl.ds(part * side % width, side)
+                pltpu.make_async_copy(
+                    sources[index].at[layer, pl.ds(part * each, each), :], wup_ref.at[number, rows, cols], sem.at[number]
+                ).start()
+            rows = pl.ds(pl.multiple_of(owner * deep, 16), deep)
+            source = sources[4 + layer // 2].at[2 * index + layer % 2]
+            pltpu.make_async_copy(source, wdown_ref.at[rows, :], sem.at[blocks]).start()
+
+
+def mlp(sets, count, me_ref, *refs):
     n2_hbm, cot_hbm = refs[:sets], refs[sets : 2 * sets]
-    bup_ref, wup_ref, wdown_ref = refs[2 * sets : 2 * sets + 3]
-    refs = refs[2 * sets + 3 :]
+    bup_ref = refs[2 * sets]
+    sources = refs[2 * sets + 1 : 2 * sets + 1 + count]
+    refs = refs[2 * sets + 1 + count :]
     act_hbm, gtwo_hbm, refs = refs[:sets], refs[sets : 2 * sets], refs[2 * sets :]
-    down_own, down_send, up_own, up_send, dbu_ref = refs[:5]
-    n2_ref, cot_ref, gacc, act_ref, gup_ref, low_ref, gdown_ref, gupw_ref, in_sem, act_sem, out_sem, grad_sem = refs[5:]
+    down_own, down_send, up_own, up_send, wdown_hbm, dbu_ref = refs[:6]
+    n2_ref, cot_ref, gacc, act_ref, gup_ref, low_ref, gdown_ref, gupw_ref = refs[6:14]
+    wup_all, wdown_all, in_sem, act_sem, out_sem, grad_sem, weight_sem = refs[14:]
     step = pl.program_id(0)
     last = pl.num_programs(0) - 1
     me = me_ref[0]
@@ -213,18 +236,28 @@
     def rows_of(index):
         return pl.ds(pl.multiple_of(index * rows, rows), rows)
 
+    blocks, width = wup_all.shape[:2]
+
     @pl.when(step == 0)
     def _():
+        fetch_hidden(me, sources, wup_all, wdown_all, weight_sem)
         for index in range(sets):
             at = pl.ds(index * rows, rows)
             pltpu.make_async_copy(n2_hbm[index], n2_ref.at[at, :], in_sem.at[0, index]).start()
             pltpu.make_async_copy(cot_hbm[index], cot_ref.at[at, :], in_sem.at[1, index]).start()
 
-    wup = flat_rows(wup_ref)
-    wdown = flat_rows(wdown_ref)
+    pltpu.make_async_copy(wup_all.at[step], wup_all.at[step], weight_sem.at[step]).wait()
+    write_down = pltpu.make_async_copy(wdown_all, wdown_hbm, weight_sem.at[blocks])
+
+    @pl.when(step == 0)
+    def _():
+        pltpu.make_async_copy(wdown_all, wdown_all, weight_sem.at[blocks]).wait()
+        write_down.start()
+
+    wup = wup_all[step]
+    wdown = wdown_all[pl.ds(pl.multiple_of(step * width, width), width), :]
     dbu_ref[...] = jnp.zeros_like(dbu_ref)
     slot = lax.rem(step, 2)
-    width = n2_ref.shape[1]
 
     @pl.loop(0, sets)
     def _(index):
@@ -310,6 +343,7 @@
     def _():
         for copy in results():
             copy.wait()
+        write_down.wait()
         for number in range(act_ref.shape[0]):
             for copy in activations(number):
                 copy.wait()
@@ -332,11 +366,11 @@
 
 
 def mlp_out_other(me_ref, act_ref, wdown_ref, out_ref):
-    out_ref[...] = dot_nn(act_ref[...], flat_rows(wdown_ref)).astype(BF16)
+    out_ref[...] = dot_nn(act_ref[...], wdown_ref[...]).astype(BF16)
 
 
 def mlp_out_own(me_ref, resid_ref, vec_ref, act_ref, take_ref, wdown_ref, out_ref):
-    half = dot_nn(act_ref[...], flat_rows(wdown_ref)) + take_ref[...].astype(F32)
+    half = dot_nn(act_ref[...], wdown_ref[...]) + take_ref[...].astype(F32)
     out_ref[...] = (resid_ref[...] + (half + vec_ref[7:8, :])).astype(BF16)
 
 
@@ -569,8 +603,8 @@
         put(4 + part, halves[0][:, at], halves[1][:, at])
 
 
-def join_shards(me_ref, keep_ref, take_ref, down_ref, *refs):
-    vectors, (near_ref, far_ref) = refs[:-2], refs[-2:]
+def join_shards(me_ref, keep_ref, take_ref, *refs):
+    vectors, near_ref = refs[:-1], refs[-1]
     me = me_ref[0]
     first = (me & 1) == 0
     parts, own, side = keep_ref.shape
@@ -585,9 +619,9 @@
 
     for index in range(4):
         near_ref[2 * own * index : 2 * own * (index + 1), :] = joined(index)
+    base = 8 * own + 16
     for index in range(folds):
-        far_ref[2 * own * (index // 2) : 2 * own * (index // 2 + 1), side * (index % 2) : side * (index % 2 + 1)] = joined(4 + index)
-    far_ref[folds * own :, :] = down_ref[...]
+        near_ref[base + 2 * own * index : base + 2 * own * (index + 1), :] = joined(4 + index)
     rows = []
     for ref in vectors:
         flat = ref[...].astype(F32).reshape(1, -1)
@@ -597,7 +631,7 @@
     short = pltpu.roll(rows, own * lax.rem(me, side // own), 1)
     long = pltpu.roll(rows, folds * own * lax.rem(me >> 1, side // (folds * own)), 1)
     index = lax.broadcasted_iota(jnp.int32, rows.shape, 0)
-    near_ref[8 * own :, :] = jnp.where(index < 8, short, long).astype(BF16)
+    near_ref[8 * own : base, :] = jnp.where(index < 8, short, long).astype(BF16)
 
 
 def across_layers(shard):
@@ -625,8 +659,7 @@
 ANY_SPEC = pl.BlockSpec(memory_space=pl.ANY)
 
 
-def gather_by_hand(me, weights, vectors, masked):
-    count = lax.axis_size("dp")
+def prepare(me, weights, vectors):
     own, width = weights[0].shape
     side = width // 2
     deep = weights[5].shape[0]
@@ -635,16 +668,17 @@
     keep, send = small_call(
         split_shards, (me & 1, *weights[:5]), [halves, halves], "split_shards", ins=[SMEM] + [VMEM_SPEC] * 5)
     take = swap(send, other_core)
-    near, far = small_call(
-        join_shards, (me, keep, take, weights[5], *vectors),
-        [(VMEM_SPEC, shaped(8 * own + 16, side)), (VMEM_SPEC, shaped(2 * deep, width))], "join_shards",
-        ins=[SMEM] + [VMEM_SPEC] * (3 + len(vectors)))
-    far = lax.all_gather(far, "dp", axis=0, tiled=True).reshape(count // 2, 2, 2 * deep, width)
-    near = across_layers(near)
-    cot, sum_down = masked(near)
-    far_plane = after(swap(near, first_plane), cot)
-    near = [near, far_plane, swap(near, second_plane), swap(far_plane, second_plane)]
-    return near + [swap(piece, other_core) for piece in near], far, cot, sum_down
+    return small_call(
+        join_shards, (me, keep, take, *vectors), [(VMEM_SPEC, shaped(8 * own + 16 + 2 * deep, side))], "join_shards",
+        ins=[SMEM] + [VMEM_SPEC] * (2 + len(vectors)))[0]
+
+
+def doubled(pieces, change):
+    return jnp.concatenate((pieces, swap(pieces, change)))
+
+
+def gather_down(pieces):
+    return doubled(doubled(pieces, first_plane), second_plane)
 
 
 def gather_plain(weights, vectors):
@@ -666,13 +700,13 @@
     whole = lax.all_gather(packed, "dp", axis=0, tiled=True).reshape(count, -1, width)
     square_all = [whole[:, index * own : (index + 1) * own, :].reshape(width, width) for index in range(4)]
     wup = whole[:, 4 * own : (4 + folds) * own, :].reshape(count, folds, own, width).transpose(0, 2, 1, 3)
-    wup = wup.reshape(CHIPS, width // CHIPS, 2, CHIPS // 2, 2, -1).transpose(0, 4, 2, 1, 3, 5).reshape(CHIPS, 2, -1, width)
+    wup = wup.reshape(width, 2, CHIPS // 2, 2, -1).transpose(3, 1, 0, 2, 4).reshape(2, 2, width, width)
     wdown = whole[:, (4 + folds) * own : (4 + 2 * folds) * own, :]
-    wdown = wdown.reshape(CHIPS, 2, -1, width)
+    wdown = wdown.reshape(CHIPS, 2, -1, width).transpose(1, 0, 2, 3).reshape(2, hidden // 2, width)
     last = whole[:, (4 + 2 * folds) * own, : flat.size].astype(F32)
     vec = last[:, : 8 * own].reshape(count, 8, own).transpose(1, 0, 2).reshape(8, width)
     bup = last[:, 8 * own :].reshape(CHIPS, 2, -1).transpose(1, 0, 2).reshape(2, 1, -1)
-    return (*square_all, jnp.concatenate((wup, wdown), axis=2), jnp.pad(vec, ((0, 8), (0, 0))), bup)
+    return (*square_all, (wup, wdown), jnp.pad(vec, ((0, 8), (0, 0))), bup)
 
 
 def merge_core(core_ref, keep_ref, take_ref, own_ref, send_ref):
@@ -870,30 +904,66 @@
             mask_grads, (tiles,), [SMEM, tile_rows], [low_rows, sums], [], "mask_grads", 0,
             lengths, after(grad_out, *earlier))
 
-    if by_hand:
-        near, far, cot, sum_down = gather_by_hand(me, weights, vectors, masked)
+    high_rows = (tile_rows, shaped(rows, width, dtype=F32))
+
+    def attend(q, k, v, vec, wo):
+        return call(
+            attention_forward, (tiles,), [SMEM, tile_rows, vec_spec, tile_rows, tile_rows, tile_rows, square],
+            [low_rows, (lse_spec, shaped(rows, LANES, dtype=F32)), high_rows, low_rows],
+            [], "attention_forward", 0, lengths, tokens, vec, q, k, v, wo)
+
+    def gather_near(near):
+        cot, sum_down = masked(near)
+        cot_other = swap(cot, other_core)
+        along = after(swap(near, first_plane), cot)
+        across = [swap(near, second_plane), swap(along, second_plane)]
+        along, across[0] = after((along, across[0]), *across[:1])
+        taken = [swap(near, other_core), swap(along, other_core)]
+        across = after(across, taken)
+        taken += [swap(piece, other_core) for piece in across]
+        return [along, *across, *taken], cot, cot_other, sum_down
+
+    def attend_by_hand(near, up_four):
+        up_along = swap(up_four, first_plane)
         n1, q, k, v, wq, wk, wv, wo, vec, bup = call_with(
             me, project, tiles, [tile_rows] + [ANY_SPEC] * 8, [low_rows] * 4 + [kept_square] * 4 + [kept_vec, kept_hidden],
             [pltpu.VMEM((count, 16, side), BF16), pltpu.SemaphoreType.DMA((5,))], "project", 0, tokens, *near)
-        cot_other = swap(cot, other_core)
+        up_four, up_along = after((up_four, up_along), n1)
+        up = [up_along, swap(up_four, second_plane), swap(up_along, second_plane)]
+        mixed, lse, resid, n2 = attend(q, k, v, vec, wo)
+        up = after(up, mixed)
+        n2_other = swap(after(n2, up), other_core)
+        return n1, q, k, v, wq, wk, wv, wo, vec, bup, mixed, lse, resid, n2, n2_other, up
+
+    if by_hand:
+        down_two = doubled(down_weight[None], other_layer(1))
+        first = prepare(me, weights, vectors)
+        moved = [swap(first, other_layer(r)) for r in (1, 2, 3)]
+        down_shard = fenced(gather_down, after(down_two, first))
+        pieces = [first] + after(moved, down_shard)
+        split = 8 * own + 16
+        near = jnp.stack([piece[:split] for piece in pieces])
+        up_four = jnp.stack([piece[split:] for piece in pieces])
+        near, up_four = after((near, up_four))
+        down = [down_shard, swap(after(down_shard, near, up_four), other_layer(2))]
+        near_moved, cot, cot_other, sum_down = fenced(gather_near, near)
+        near = [near] + near_moved
+        n1, q, k, v, wq, wk, wv, wo, vec, bup, mixed, lse, resid, n2, n2_other, up = fenced(
+            attend_by_hand, near, up_four)
+        hidden_weights = [(up_four, *up, *down)]
     else:
-        wq, wk, wv, wo, far, vec, bup = gather_plain(weights, vectors)
+        wq, wk, wv, wo, hidden_weights, vec, bup = gather_plain(weights, vectors)
+        hidden_weights = list(zip(*hidden_weights))
         cot, sum_down = masked()
         n1, q, k, v = call(
             project_rows, (tiles,), [tile_rows, vec_spec, square, square, square], [low_rows] * 4,
             [], "project", 0, tokens, vec, wq, wk, wv)
-    high_rows = (tile_rows, shaped(rows, width, dtype=F32))
-    mixed, lse, resid, n2 = call(
-        attention_forward, (tiles,), [SMEM, tile_rows, vec_spec, tile_rows, tile_rows, tile_rows, square],
-        [low_rows, (lse_spec, shaped(rows, LANES, dtype=F32)), high_rows, low_rows],
-        [], "attention_forward", 0, lengths, tokens, vec, q, k, v, wo)
+        mixed, lse, resid, n2 = attend(q, k, v, vec, wo)
 
     each = width // CHIPS
     deep = hidden // (2 * CHIPS)
     blocks = hidden // (2 * width)
     full_rows = whole_spec((rows, width))
-    up_spec = pl.BlockSpec((CHIPS, 1, each, width), lambda i, me: (0, me[0] & 1, i, 0))
-    down_spec = pl.BlockSpec((CHIPS // 2, 1, deep, width), lambda i, me: (i, me[0] & 1, 1, 0))
     hidden_spec = pl.BlockSpec((1, width), lambda i, me: (0, i))
     low_out, high_out = (ANY_SPEC, shaped(rows, width)), (ANY_SPEC, shaped(rows, width, dtype=F32))
     act_out = (ANY_SPEC, shaped(rows, blocks * width))
@@ -901,36 +971,36 @@
     up_part = (ANY_SPEC, shaped(blocks, 4, 2, each, width))
 
     act_spec = pl.BlockSpec((tile, blocks * width), lambda i, *me: (i, 0))
-    wide_spec = pl.BlockSpec(
-        (CHIPS, 1, deep, width), lambda i, me: (0, me[0] & 1, 1, 0), pipeline_mode=pl.Buffered(1))
-
-    def run_mlp(me, tokens_of, bup):
+    wide_spec = whole_spec((hidden // 2, width))
+
+    def run_mlp(me, tokens_of, bup, sources):
         sets = len(tokens_of[0])
         low, high = pltpu.VMEM((sets * rows, width), BF16), pltpu.VMEM((sets * rows, width), F32)
         weight = pltpu.VMEM((2, width, width), BF16)
         dma = pltpu.SemaphoreType.DMA((2, sets))
         return call_with(
-            me, functools.partial(mlp, sets), blocks, [ANY_SPEC] * (2 * sets) + [hidden_spec, up_spec, down_spec],
+            me, functools.partial(mlp, sets, len(sources)), blocks,
+            [ANY_SPEC] * (2 * sets) + [hidden_spec] + [ANY_SPEC] * len(sources),
             [act_out] * sets + [high_out] + [low_out] * (sets - 1) + [down_part] * 2 + [up_part] * 2
-            + [(hidden_spec, shaped(1, hidden // 2, dtype=F32))],
-            [low, low, high, pltpu.VMEM((blocks, sets * rows, width), BF16), low, low, weight, weight, dma,
-             pltpu.SemaphoreType.DMA((blocks, sets)), pltpu.SemaphoreType.DMA((sets,)), pltpu.SemaphoreType.DMA((4,))],
-            "mlp", 0, *tokens_of[0], *tokens_of[1], bup, far, far)
+            + [(ANY_SPEC, shaped(hidden // 2, width)), (hidden_spec, shaped(1, hidden // 2, dtype=F32))],
+            [low, low, high, pltpu.VMEM((blocks, sets * rows, width), BF16), low, low, weight, weight,
+             pltpu.VMEM((blocks, width, width), BF16), pltpu.VMEM((hidden // 2, width), BF16), dma,
+             pltpu.SemaphoreType.DMA((blocks, sets)), pltpu.SemaphoreType.DMA((sets,)), pltpu.SemaphoreType.DMA((4,)),
+             pltpu.SemaphoreType.DMA((blocks + 1,))],
+            "mlp", 0, *tokens_of[0], *tokens_of[1], bup, *sources)
 
     if by_hand:
-        cot_other = after(cot_other, mixed)
-        n2_other = swap(n2, other_core)
-        act_own, act_other, gtwo, gtwo_other, down_own, down_send, up_own, up_send, sum_up = run_mlp(
-            me, ((n2, n2_other), (cot, cot_other)), bup)
+        act_own, act_other, gtwo, gtwo_other, down_own, down_send, up_own, up_send, wdown, sum_up = run_mlp(
+            me, ((n2, n2_other), (cot, cot_other)), bup, hidden_weights[0])
         gtwo_take = swap(gtwo_other, other_core)
         parts = (-1, CHIPS // 4, 2)
         down_first = [piece.reshape(*parts, deep, width) for piece in (down_own, swap(down_send, first_plane))]
         up_first = [piece.reshape(*parts, each, width) for piece in (up_own, swap(up_send, first_plane))]
     else:
-        runs = [run_mlp(me + half, ((n2,), (cot,)), bup[half]) for half in range(2)]
+        runs = [run_mlp(me + half, ((n2,), (cot,)), bup[half], hidden_weights[half]) for half in range(2)]
         (act_own, gtwo), (act_other, gtwo_take) = ((run[0], run[1]) for run in runs)
         gtwo_take = gtwo_take.astype(BF16)
-        sum_up = jnp.concatenate([run[6] for run in runs], axis=1)
+        sum_up = jnp.concatenate([run[7] for run in runs], axis=1)
     grads_spec = pl.BlockSpec((4, tile, width), lambda i, *me: (0, i, 0))
     grads, gresid, sum_back = call(
         attention_backward, (tiles,),
@@ -954,7 +1024,7 @@
 
     if by_hand:
         (out_other,) = call_with(
-            me, mlp_out_other, tiles, [act_spec, wide_spec], [low_rows], [], "mlp_out_other", 0, after(act_other, grads), far)
+            me, mlp_out_other, tiles, [act_spec, wide_spec], [low_rows], [], "mlp_out_other", 0, after(act_other, grads), wdown)
         down_first, up_first = after((down_first, up_first), out_other)
         hidden_rest, hidden_take = scatter_second(*down_first, *up_first)
 
@@ -974,7 +1044,7 @@
         out_take = after(swap(out_other, other_core), square_second[0])
         (out,) = call_with(
             me, mlp_out_own, tiles, [tile_rows, vec_spec, act_spec, tile_rows, wide_spec], [low_rows], [],
-            "mlp_out_own", 0, resid, vec, act_own, out_take, far)
+            "mlp_out_own", 0, resid, vec, act_own, out_take, wdown)
         late = late + after(swap(late, other_layer(1)), out)
         hidden_layers = after(hidden_layers, late)
         g_down, up_keep, up_send = scatter_last(core, hidden_layers, own, blocks, deep)
@@ -1002,10 +1072,10 @@
         g_down, g_up, g_q, g_k, g_v, g_o, flat = reduce_plain(
             [run[2:4] for run in runs], [run[4:6] for run in runs], (square_keep, square_send), flat)
         (out_other,) = call_with(
-            me + 1, mlp_out_other, tiles, [act_spec, wide_spec], [low_rows], [], "mlp_out_other", 0, act_other, far)
+            me + 1, mlp_out_other, tiles, [act_spec, wide_spec], [low_rows], [], "mlp_out_other", 0, act_other, runs[1][6])
         (out,) = call_with(
             me, mlp_out_own, tiles, [tile_rows, vec_spec, act_spec, tile_rows, wide_spec], [low_rows], [],
-            "mlp_out_own", 0, resid, vec, act_own, out_other, far)
+            "mlp_out_own", 0, resid, vec, act_own, out_other, runs[0][6])
         g_flat = [flat[index * own : (index + 1) * own] for index in range(8)]
         g_ub = flat[8 * own :]
     g_gain, g_shift, g_qb, g_vb, g_ob, g_mg, g_ms, g_db = g_flat

time: 270 us -> 260 us (0.963)
  waiting for transfers between devices: 73.9 us -> 58.4 us
  starting transfers between devices: 31.1 us -> 45.1 us
  between operations: 14.2 us -> 0.96 us
    ppermute x34 -> x41, starting transfers between devices: 31 us -> 45.1 us  [swap(): return lax.ppermute(array, 'dp', flipped(lax.axis_size('dp'), change))]
    all_gather x1 -> x0, waiting for transfers between devices: 9.22 us -> none  [gather_by_hand(): lax.all_gather(far, 'dp', axis=0, tiled=True)]
    ppermute x34 -> x41, waiting for transfers between devices: 64.7 us -> 58.4 us  [swap(): return lax.ppermute(array, 'dp', flipped(lax.axis_size('dp'), change))]
  transfers between devices with their start and end apart: 35 -> 41, of which waited for: 15 -> 17; matrix products, arithmetic and copies ran while one was open for 3% -> 3% of each run, Pallas kernels for 36% -> 38%
where the time goes in v6:
time: 260 us; the launch traced here: 259 us
  Pallas kernels  143 us (55%)
  waiting for transfers between devices  58.4 us (22%)
  starting transfers between devices  45.1 us (17%)
  other arithmetic  9.63 us (4%)
    pallas_call x5, Pallas kernels, call_with(): pl.pallas_call(kernel, grid_spec=pltpu.PrefetchScalarGridSpec(num_scalar_...  69.9 us
    ppermute x41, waiting for transfers between devices, swap(): return lax.ppermute(array, 'dp', flipped(lax.axis_size('dp'), change))  58.4 us
    pallas_call x7, Pallas kernels, call(): pl.pallas_call(kernel, grid=grid, in_specs=ins, out_specs=out_specs, out_...  57.8 us
    ppermute x41, starting transfers between devices, swap(): return lax.ppermute(array, 'dp', flipped(lax.axis_size('dp'), change))  45.1 us
    pallas_call x7, Pallas kernels, small_call(): pl.pallas_call(kernel, in_specs=ins, out_specs=tuple((spec for spec, _ in...  15.6 us
  transfers between devices with their start and end apart: 41, of which 17 were waited for; matrix products, arithmetic and copies ran while one was open for 3% of the time, Pallas kernels for 38%

profile of v6, /device:TPU:0, one launch (start us, length us, event | category | flops | bytes accessed | tf_op | source)
XLA Modules:
  0.0 258.6 jit_solution(17762184317316958123)
XLA Ops:
  3.0 2.6 collective-permute-start.19
  9.1 2.6 %collective-permute-start.17 = (bf16[400,384]{1,0:T(8,128)(2,1)}, bf16[400,384]{1,0:T(8,128)(2,1)S(1)}, u32[]{:S(2)}, u32[]{:S(2)}) collective-permute-start(bf16[400,384]{1,0:T(8,128)(2,1)} %join_shards.1), channel_id=1, source_target_pairs={{0,16},{1,17},{2,18},{3,19},{4,20},{5,21},{6,22},{7,23},{8,24},{9,... | collective-permute-start | bytes 921608 | tf_op jit(solution)/shard_map/ppermute | solution.py:559
  13.8 18.0 %conditional.4 = (bf16[8,96,768]{2,1,0:T(8,128)(2,1)}) conditional(s32[]{:T(128)} %convert_element_type.2, () %tuple.65, bf16[2,96,768]{2,1,0:T(8,128)(2,1)S(1)} %pad_maximum_fusion.4), branch_computations={%region_0.0_spmd, %region_1.0_spmd} | conditional | flops 1474560 | bytes 7077976 | solution.py:798
  15.5 5.1 %collective-permute-done.13 = bf16[2,96,768]{2,1,0:T(8,128)(2,1)S(1)} collective-permute-done((bf16[2,96,768]{2,1,0:T(8,128)(2,1)S(1)}, bf16[2,96,768]{2,1,0:T(8,128)(2,1)S(1)}, u32[]{:S(2)}, u32[]{:S(2)}) %collective-permute-start.13) | collective-permute-done | bytes 294944 | tf_op jit(solution)/shard_map/cond/branch_1_fun/ppermute | solution.py:559
  22.4 8.2 %collective-permute-done.14 = bf16[4,96,768]{2,1,0:T(8,128)(2,1)S(1)} collective-permute-done((bf16[4,96,768]{2,1,0:T(8,128)(2,1)S(1)}, bf16[4,96,768]{2,1,0:T(8,128)(2,1)S(1)}, u32[]{:S(2)}, u32[]{:S(2)}) %collective-permute-start.14) | collective-permute-done | bytes 589856 | tf_op jit(solution)/shard_map/cond/branch_1_fun/ppermute | solution.py:559
  35.6 7.1 %collective-permute-start.20 = (bf16[8,96,768]{2,1,0:T(8,128)(2,1)}, bf16[8,96,768]{2,1,0:T(8,128)(2,1)}, u32[]{:S(2)}, u32[]{:S(2)}) collective-permute-start(bf16[8,96,768]{2,1,0:T(8,128)(2,1)} %get-tuple-element.410.refs_9_), channel_id=1, source_target_pairs={{0,16},{1,17},{2,18},{3,19},{4,20},{5,21},{6,22},{7,23},{8,24},{9,... | collective-permute-start | bytes 3538952 | tf_op jit(solution)/shard_map/ppermute | solution.py:559
  42.7 30.7 %conditional.5 = (bf16[4,208,384]{2,1,0:T(8,128)(2,1)}, bf16[4,208,384]{2,1,0:T(8,128)(2,1)}, bf16[4,208,384]{2,1,0:T(8,128)(2,1)}, bf16[4,208,384]{2,1,0:T(8,12...) conditional(s32[]{:T(128)} %convert_element_type.2, () %tuple.69, ...), branch_computations={%region_2.0_spmd, %region_3.0_spmd} | conditional | bytes 24183184 | solution.py:798
  45.7 3.8 %mask_grads.1 = (bf16[1024,768]{1,0:T(8,128)(2,1)}, f32[8,768]{1,0:T(8,128)}) custom-call(s32[4,5]{1,0:T(4,128)} %get-tuple-element.51.lengths_ref, bf16[1024,768]{1,0:T(8,128)(2,1)} %get-tuple-element.53.grad_ref), custom_call_target="tpu_custom_call" | custom-call | bytes 1 | tf_op jit(solution)/shard_map/cond/branch_1_fun/mask_grads/pallas_call | solution.py:518
  50.0 9.3 %collective-permute-done = bf16[4,208,384]{2,1,0:T(8,128)(2,1)} collective-permute-done((bf16[4,208,384]{2,1,0:T(8,128)(2,1)}, bf16[4,208,384]{2,1,0:T(8,128)(2,1)}, u32[]{:S(2)}, u32[]{:S(2)}) %collective-permute-start) | collective-permute-done | bytes 639008 | tf_op jit(solution)/shard_map/cond/branch_1_fun/ppermute | solution.py:559
  61.7 8.3 %collective-permute-done.2 = bf16[4,208,384]{2,1,0:T(8,128)(2,1)} collective-permute-done((bf16[4,208,384]{2,1,0:T(8,128)(2,1)}, bf16[4,208,384]{2,1,0:T(8,128)(2,1)}, u32[]{:S(2)}, u32[]{:S(2)}) %collective-permute-start.2) | collective-permute-done | bytes 639008 | tf_op jit(solution)/shard_map/cond/branch_1_fun/ppermute | solution.py:559
  73.4 32.0 %conditional.6 = (bf16[1024,768]{1,0:T(8,128)(2,1)}, bf16[1024,768]{1,0:T(8,128)(2,1)}, bf16[1024,768]{1,0:T(8,128)(2,1)}, bf16[1024,768]{1,0:T(8,128)(2,1)}, bf...) conditional(s32[]{:T(128)} %convert_element_type.2, () %tuple.64, ...), branch_computations={%region_4.0_spmd, %region_5.0_spmd} | conditional | bytes 21223612 | solution.py:798
  74.9 10.2 %project.1 = (bf16[1024,768]{1,0:T(8,128)(2,1)}, bf16[1024,768]{1,0:T(8,128)(2,1)}, bf16[1024,768]{1,0:T(8,128)(2,1)}, bf16[1024,768]{1,0:T(8,128)(2,1)}, bf16[7...) custom-call(s32[1]{0:T(128)} %get-tuple-element.61.me_ref, ...), custom_call_target="tpu_custom_call" | custom-call | bytes 1 | tf_op jit(solution)/shard_map/cond/branch_1_fun/project/pallas_call | solution.py:533
  87.1 13.2 %attention_forward.1 = (bf16[1024,768]{1,0:T(8,128)(2,1)}, f32[1024,128]{1,0:T(8,128)}, f32[1024,768]{1,0:T(8,128)}, bf16[1024,768]{1,0:T(8,128)(2,1)}) custom-call(s32[4,5]{1,0:T(4,128)} %get-tuple-element.81.lengths_ref, bf16[1024,768]{1,0:T(8,128)(2,1)} %get-tuple-element.62.x_ref, f32[16,768]{1,0:T(8,128)} %get-tuple-element.396.vec_ref, ...), custom_call_target="tpu_custom_call" | custom-call | bytes 1 | tf_op jit(solution)/shard_map/cond/branch_1_fun/attention_forward/pallas_call | solution.py:518
  101.6 3.7 %collective-permute-done.11 = bf16[1024,768]{1,0:T(8,128)(2,1)} collective-permute-done((bf16[1024,768]{1,0:T(8,128)(2,1)}, bf16[1024,768]{1,0:T(8,128)(2,1)}, u32[]{:S(2)}, u32[]{:S(2)}) %collective-permute-start.11) | collective-permute-done | bytes 1572896 | tf_op jit(solution)/shard_map/cond/branch_1_fun/ppermute | solution.py:559
  105.4 35.2 %mlp.1 = (bf16[1024,1536]{1,0:T(8,128)(2,1)}, bf16[1024,1536]{1,0:T(8,128)(2,1)}, f32[1024,768]{1,0:T(8,128)}, bf16[1024,768]{1,0:T(8,128)(2,1)}, bf16[4,2,96,76...) custom-call(s32[1]{0:T(128)} %bitcast.1.me_ref, ...), custom_call_target="tpu_custom_call" | custom-call | bytes 1 | tf_op jit(solution)/shard_map/mlp/pallas_call | solution.py:533
  144.5 20.7 %attention_backward.1 = (bf16[4,1024,768]{2,1,0:T(8,128)(2,1)}, f32[1024,768]{1,0:T(8,128)}, f32[8,768]{1,0:T(8,128)}) custom-call(s32[4,5]{1,0:T(4,128)} %lengths_ref.1, bf16[1024,768]{1,0:T(8,128)(2,1)} %get-tuple-element.261.q_ref, bf16[1024,768]{1,0:T(8,128)(2,1)} %get-tuple-element.262.k_ref, bf16[1024,768]{1,0:T(8,128)(2,1)} %get-tuple-element.263.v_ref, ...), custom_call_target="tpu_custom_call" | custom-call | bytes 1 | tf_op jit(solution)/shard_map/attention_backward/pallas_call | solution.py:518
  165.1 6.4 %mlp_out_other.1 = bf16[1024,768]{1,0:T(8,128)(2,1)} custom-call(s32[1]{0:T(128)} %bitcast.1.me_ref, bf16[1024,1536]{1,0:T(8,128)(2,1)} %get-tuple-element.269.act_ref, bf16[1536,768]{1,0:T(8,128)(2,1)} %get-tuple-element.270.wdown_ref), custom_call_target="tpu_custom_call" | custom-call | bytes 1 | tf_op jit(solution)/shard_map/mlp_out_other/pallas_call | solution.py:533
  171.6 3.8 %merge_first.2 = (f32[4,192,768]{2,1,0:T(8,128)}, bf16[4,192,768]{2,1,0:T(8,128)(2,1)}) custom-call(bf16[1,4,2,96,768]{4,3,2,1,0:T(8,128)(2,1)} %bitcast.22, bf16[1,4,2,96,768]{4,3,2,1,0:T(8,128)(2,1)} %bitcast.12.refs_1_, bf16[2,4,2,48,768]{4,3,2,1,0:T(8,128)(2,1)} %get-tuple-element.279.refs_2_, bf16[2,4,2,48,768]{4,3,2,1,0:T(8,128)(2,1)} %collective-permute-done.24.refs_3_), custom_call_target="tpu_custom_call" | custom-call | bytes 1 | tf_op jit(solution)/shard_map/merge_first/pallas_call | solution.py:518
  175.8 19.6 %conditional.7 = (bf16[1,4,2,208,384]{4,3,2,1,0:T(8,128)(2,1)}, bf16[4,2,208,384]{3,2,1,0:T(8,128)(2,1)}) conditional(s32[]{:T(128)} %convert_element_type.2, () %tuple.74, (s32[1]{0:T(128)}, bf16[1024,768]{1,0:T(8,128)(2,1)}, bf16[1024,768]{1,0:T(8,128)(2,1)}, bf16[4,1024,768]{2,1,0:T(8,128)(2,1)}, f32[8,768]{1,0:T(8,128)}, ...), branch_computations={%region_6.0_spmd, %region_7.0_spmd} | conditional | bytes 10223674 | solution.py:798
  175.8 10.6 %weight_grads.1 = (bf16[4,4,208,384]{3,2,1,0:T(8,128)(2,1)}, bf16[4,4,208,384]{3,2,1,0:T(8,128)(2,1)}) custom-call(s32[1]{0:T(128)} %get-tuple-element.94.me_ref, bf16[1024,768]{1,0:T(8,128)(2,1)} %get-tuple-element.95.n1_ref, bf16[1024,768]{1,0:T(8,128)(2,1)} %get-tuple-element.96.mixed_ref, bf16[4,1024,768]{2,1,0:T(8,128)(2,1)} %get-tuple-element.97.columns_ref, ...), custom_call_target="tpu_custom_call" | custom-call | bytes 1 | tf_op jit(solution)/shard_map/cond/branch_1_fun/weight_grads/pallas_call | solution.py:533
  186.9 4.8 %collective-permute-done.12.take_ref = bf16[4,4,208,384]{3,2,1,0:T(8,128)(2,1)} collective-permute-done((bf16[4,4,208,384]{3,2,1,0:T(8,128)(2,1)}, bf16[4,4,208,384]{3,2,1,0:T(8,128)(2,1)}, u32[]{:S(2)}, u32[]{:S(2)}) %collective-permute-start.12) | collective-permute-done | bytes 2555936 | tf_op jit(solution)/shard_map/cond/branch_1_fun/ppermute | solution.py:559
  191.7 3.7 %merge_core.1 = (bf16[4,2,208,384]{3,2,1,0:T(8,128)(2,1)}, bf16[4,2,208,384]{3,2,1,0:T(8,128)(2,1)}) custom-call(s32[1]{0:T(128)} %get-tuple-element.93.core_ref, bf16[4,4,208,384]{3,2,1,0:T(8,128)(2,1)} %get-tuple-element.101.keep_ref, bf16[4,4,208,384]{3,2,1,0:T(8,128)(2,1)} %collective-permute-done.12.take_ref), custom_call_target="tpu_custom_call" | custom-call | bytes 1 | tf_op jit(solution)/shard_map/cond/branch_1_fun/merge_core/pallas_call | solution.py:518
  196.7 3.2 %merge_second.2 = (f32[192,768]{1,0:T(8,128)}, bf16[192,768]{1,0:T(8,128)(2,1)}, bf16[192,768]{1,0:T(8,128)(2,1)}, bf16[192,768]{1,0:T(8,128)(2,1)}) custom-call(f32[4,192,768]{2,1,0:T(8,128)} %get-tuple-element.290.own_ref, bf16[4,192,768]{2,1,0:T(8,128)(2,1)} %collective-permute-done.26.take_ref), custom_call_target="tpu_custom_call" | custom-call | bytes 1 | tf_op jit(solution)/shard_map/merge_second/pallas_call | solution.py:646
  201.8 2.4 collective-permute-start.29
  204.2 9.8 %tokens_backward.1 = (bf16[1024,768]{1,0:T(8,128)(2,1)}, f32[8,768]{1,0:T(8,128)}) custom-call(bf16[1024,768]{1,0:T(8,128)(2,1)} %x_ref.1, f32[1024,768]{1,0:T(8,128)} %get-tuple-element.293.gresid_ref, f32[16,768]{1,0:T(8,128)} %get-tuple-element.249.vec_ref, bf16[4,1024,768]{2,1,0:T(8,128)(2,1)} %get-tuple-element.282.grads_ref, ...), custom_call_target="tpu_custom_call" | custom-call | flops 11500000256 | bytes 1 | tf_op jit(solution)/shard_map/tokens_backward/pallas_call | solution.py:518
  214.1 2.8 %merge_first.3 = (f32[4,208,384]{2,1,0:T(8,128)}, bf16[4,208,384]{2,1,0:T(8,128)(2,1)}) custom-call(bf16[1,4,2,208,384]{4,3,2,1,0:T(8,128)(2,1)} %get-tuple-element.286.refs_0_, bf16[1,4,2,208,384]{4,3,2,1,0:T(8,128)(2,1)} %bitcast.13.refs_1_), custom_call_target="tpu_custom_call" | custom-call | bytes 1 | tf_op jit(solution)/shard_map/merge_first/pallas_call | solution.py:518
  219.1 7.5 %mlp_out_own.1 = bf16[1024,768]{1,0:T(8,128)(2,1)} custom-call(s32[1]{0:T(128)} %bitcast.1.me_ref, f32[1024,768]{1,0:T(8,128)} %get-tuple-element.248.resid_ref, f32[16,768]{1,0:T(8,128)} %get-tuple-element.249.vec_ref, bf16[1024,1536]{1,0:T(8,128)(2,1)} %get-tuple-element.259.act_ref, bf16[1024,768]{1,0:T(8,128)(2,1)} %collective-permute-done.22.take_ref, ...), custom_call_target="tpu_custom_call" | custom-call | bytes 1 | tf_op jit(solution)/shard_map/mlp_out_own/pallas_call | solution.py:533
  234.3 2.4 merge_second.3
  238.8 2.3 collective-permute-start.37
  242.9 2.3 collective-permute-done.38
  247.1 2.6 collective-permute-done.39
  250.3 2.3 collective-permute-done.36.b_ref
  (91 shorter events, 60.8 us)
Async XLA Ops:
  3.0 9.8 %collective-permute-start.19 = (bf16[1,96,768]{2,1,0:T(8,128)(2,1)}, bf16[1,96,768]{2,1,0:T(8,128)(2,1)}, u32[]{:S(2)}, u32[]{:S(2)}) collective-permute-start(bf16[1,96,768]{2,1,0:T(8,128)(2,1)} %bitcast.23), channel_id=1, source_target_pairs={{0,8},{1,9},{2,10},{3,11},{4,12},{5,13},{6,14},{7,15},{8,0},{9,1},... | collective-permute-start | bytes 442376 | tf_op jit(solution)/shard_map/ppermute | solution.py:559
  7.4 24.4 %collective-permute-start.16 = (bf16[400,384]{1,0:T(8,128)(2,1)}, bf16[400,384]{1,0:T(8,128)(2,1)S(1)}, u32[]{:S(2)}, u32[]{:S(2)}) collective-permute-start(bf16[400,384]{1,0:T(8,128)(2,1)} %join_shards.1), channel_id=1, source_target_pairs={{0,8},{1,9},{2,10},{3,11},{4,12},{5,13},{6,14},{7,15},{8,0},{9,1},... | collective-permute-start | bytes 921608 | tf_op jit(solution)/shard_map/ppermute | solution.py:559
  9.1 24.4 %collective-permute-start.17 = (bf16[400,384]{1,0:T(8,128)(2,1)}, bf16[400,384]{1,0:T(8,128)(2,1)S(1)}, u32[]{:S(2)}, u32[]{:S(2)}) collective-permute-start(bf16[400,384]{1,0:T(8,128)(2,1)} %join_shards.1), channel_id=1, source_target_pairs={{0,16},{1,17},{2,18},{3,19},{4,20},{5,21},{6,22},{7,23},{8,24},{9,... | collective-permute-start | bytes 921608 | tf_op jit(solution)/shard_map/ppermute | solution.py:559
  11.7 21.8 %collective-permute-start.18 = (bf16[400,384]{1,0:T(8,128)(2,1)}, bf16[400,384]{1,0:T(8,128)(2,1)S(1)}, u32[]{:S(2)}, u32[]{:S(2)}) collective-permute-start(bf16[400,384]{1,0:T(8,128)(2,1)} %join_shards.1), channel_id=1, source_target_pairs={{0,24},{1,25},{2,26},{3,27},{4,28},{5,29},{6,30},{7,31},{8,16},{9,... | collective-permute-start | bytes 921608 | tf_op jit(solution)/shard_map/ppermute | solution.py:559
  13.8 6.8 %collective-permute-start.13 = (bf16[2,96,768]{2,1,0:T(8,128)(2,1)S(1)}, bf16[2,96,768]{2,1,0:T(8,128)(2,1)S(1)}, u32[]{:S(2)}, u32[]{:S(2)}) collective-permute-start(bf16[2,96,768]{2,1,0:T(8,128)(2,1)S(1)} %param.1), channel_id=1, source_target_pairs={{0,2},{1,5},{2,0},{3,7},{4,6},{5,1},{6,4},{7,3},{8,10},{9,13},{10,... | collective-permute-start | bytes 884744 | tf_op jit(solution)/shard_map/cond/branch_1_fun/ppermute | solution.py:559
  20.7 9.9 %collective-permute-start.14 = (bf16[4,96,768]{2,1,0:T(8,128)(2,1)S(1)}, bf16[4,96,768]{2,1,0:T(8,128)(2,1)S(1)}, u32[]{:S(2)}, u32[]{:S(2)}) collective-permute-start(bf16[4,96,768]{2,1,0:T(8,128)(2,1)S(1)} %pad_maximum_fusion.1), channel_id=1, source_target_pairs={{0,4},{1,3},{2,6},{3,1},{4,0},{5,7},{6,2},{7,5},{8,12},{9,11},{10,... | collective-permute-start | bytes 1769480 | tf_op jit(solution)/shard_map/cond/branch_1_fun/ppermute | solution.py:559
  35.6 69.8 %collective-permute-start.20 = (bf16[8,96,768]{2,1,0:T(8,128)(2,1)}, bf16[8,96,768]{2,1,0:T(8,128)(2,1)}, u32[]{:S(2)}, u32[]{:S(2)}) collective-permute-start(bf16[8,96,768]{2,1,0:T(8,128)(2,1)} %get-tuple-element.410.refs_9_), channel_id=1, source_target_pairs={{0,16},{1,17},{2,18},{3,19},{4,20},{5,21},{6,22},{7,23},{8,24},{9,... | collective-permute-start | bytes 3538952 | tf_op jit(solution)/shard_map/ppermute | solution.py:559
  42.7 16.6 %collective-permute-start = (bf16[4,208,384]{2,1,0:T(8,128)(2,1)}, bf16[4,208,384]{2,1,0:T(8,128)(2,1)}, u32[]{:S(2)}, u32[]{:S(2)}) collective-permute-start(bf16[4,208,384]{2,1,0:T(8,128)(2,1)} %get-tuple-element.50), channel_id=1, source_target_pairs={{0,2},{1,5},{2,0},{3,7},{4,6},{5,1},{6,4},{7,3},{8,10},{9,13},{10,... | collective-permute-start | bytes 1916936 | tf_op jit(solution)/shard_map/cond/branch_1_fun/ppermute | solution.py:559
  44.2 15.1 %collective-permute-start.1 = (bf16[4,208,384]{2,1,0:T(8,128)(2,1)}, bf16[4,208,384]{2,1,0:T(8,128)(2,1)}, u32[]{:S(2)}, u32[]{:S(2)}) collective-permute-start(bf16[4,208,384]{2,1,0:T(8,128)(2,1)} %get-tuple-element.50), channel_id=1, source_target_pairs={{0,4},{1,3},{2,6},{3,1},{4,0},{5,7},{6,2},{7,5},{8,12},{9,11},{10,... | collective-permute-start | bytes 1916936 | tf_op jit(solution)/shard_map/cond/branch_1_fun/ppermute | solution.py:559
  49.5 21.0 %collective-permute-start.7 = (bf16[1024,768]{1,0:T(8,128)(2,1)}, bf16[1024,768]{1,0:T(8,128)(2,1)}, u32[]{:S(2)}, u32[]{:S(2)}) collective-permute-start(bf16[1024,768]{1,0:T(8,128)(2,1)} %get-tuple-element.367), channel_id=1, source_target_pairs={{0,1},{1,0},{2,3},{3,2},{4,5},{5,4},{6,7},{7,6},{8,9},{9,8},{10,11... | collective-permute-start | bytes 4718600 | tf_op jit(solution)/shard_map/cond/branch_1_fun/ppermute | solution.py:559
  49.5 10.3 %collective-permute-start.3 = (bf16[4,208,384]{2,1,0:T(8,128)(2,1)}, bf16[4,208,384]{2,1,0:T(8,128)(2,1)}, u32[]{:S(2)}, u32[]{:S(2)}) collective-permute-start(bf16[4,208,384]{2,1,0:T(8,128)(2,1)} %get-tuple-element.50), channel_id=1, source_target_pairs={{0,1},{1,0},{2,3},{3,2},{4,5},{5,4},{6,7},{7,6},{8,9},{9,8},{10,11... | collective-permute-start | bytes 1916936 | tf_op jit(solution)/shard_map/cond/branch_1_fun/ppermute | solution.py:559
  59.3 10.7 %collective-permute-start.2 = (bf16[4,208,384]{2,1,0:T(8,128)(2,1)}, bf16[4,208,384]{2,1,0:T(8,128)(2,1)}, u32[]{:S(2)}, u32[]{:S(2)}) collective-permute-start(bf16[4,208,384]{2,1,0:T(8,128)(2,1)} %collective-permute-done), channel_id=1, source_target_pairs={{0,4},{1,3},{2,6},{3,1},{4,0},{5,7},{6,2},{7,5},{8,12},{9,11},{10,... | collective-permute-start | bytes 1916936 | tf_op jit(solution)/shard_map/cond/branch_1_fun/ppermute | solution.py:559
  73.4 11.7 %collective-permute-start.8 = (bf16[4,192,384]{2,1,0:T(8,128)(2,1)}, bf16[4,192,384]{2,1,0:T(8,128)(2,1)}, u32[]{:S(2)}, u32[]{:S(2)}) collective-permute-start(bf16[4,192,384]{2,1,0:T(8,128)(2,1)} %get-tuple-element.88), channel_id=1, source_target_pairs={{0,2},{1,5},{2,0},{3,7},{4,6},{5,1},{6,4},{7,3},{8,10},{9,13},{10,... | collective-permute-start | bytes 1769480 | tf_op jit(solution)/shard_map/cond/branch_1_fun/ppermute | solution.py:559
  85.1 15.3 %collective-permute-start.10 = (bf16[4,192,384]{2,1,0:T(8,128)(2,1)}, bf16[4,192,384]{2,1,0:T(8,128)(2,1)}, u32[]{:S(2)}, u32[]{:S(2)}) collective-permute-start(bf16[4,192,384]{2,1,0:T(8,128)(2,1)} %collective-permute-done.8), channel_id=1, source_target_pairs={{0,4},{1,3},{2,6},{3,1},{4,0},{5,7},{6,2},{7,5},{8,12},{9,11},{10,... | collective-permute-start | bytes 1769480 | tf_op jit(solution)/shard_map/cond/branch_1_fun/ppermute | solution.py:559
  85.6 16.0 %collective-permute-start.9 = (bf16[4,192,384]{2,1,0:T(8,128)(2,1)}, bf16[4,192,384]{2,1,0:T(8,128)(2,1)}, u32[]{:S(2)}, u32[]{:S(2)}) collective-permute-start(bf16[4,192,384]{2,1,0:T(8,128)(2,1)} %get-tuple-element.88), channel_id=1, source_target_pairs={{0,4},{1,3},{2,6},{3,1},{4,0},{5,7},{6,2},{7,5},{8,12},{9,11},{10,... | collective-permute-start | bytes 1769480 | tf_op jit(solution)/shard_map/cond/branch_1_fun/ppermute | solution.py:559
  140.8 30.7 %collective-permute-start.23 = (bf16[4,2,96,768]{3,2,1,0:T(8,128)(2,1)}, bf16[4,2,96,768]{3,2,1,0:T(8,128)(2,1)}, u32[]{:S(2)}, u32[]{:S(2)}) collective-permute-start(bf16[4,2,96,768]{3,2,1,0:T(8,128)(2,1)} %get-tuple-element.274), channel_id=1, source_target_pairs={{0,2},{1,5},{2,0},{3,7},{4,6},{5,1},{6,4},{7,3},{8,10},{9,13},{10,... | collective-permute-start | bytes 3538952 | tf_op jit(solution)/shard_map/ppermute | solution.py:559
  141.4 30.2 %collective-permute-start.24 = (bf16[2,4,2,48,768]{4,3,2,1,0:T(8,128)(2,1)}, bf16[2,4,2,48,768]{4,3,2,1,0:T(8,128)(2,1)}, u32[]{:S(2)}, u32[]{:S(2)}) collective-permute-start(bf16[2,4,2,48,768]{4,3,2,1,0:T(8,128)(2,1)} %get-tuple-element.276), channel_id=1, source_target_pairs={{0,2},{1,5},{2,0},{3,7},{4,6},{5,1},{6,4},{7,3},{8,10},{9,13},{10,... | collective-permute-start | bytes 3538952 | tf_op jit(solution)/shard_map/ppermute | solution.py:559
  175.3 21.4 %collective-permute-start.26 = (bf16[4,192,768]{2,1,0:T(8,128)(2,1)}, bf16[4,192,768]{2,1,0:T(8,128)(2,1)}, u32[]{:S(2)}, u32[]{:S(2)}) collective-permute-start(bf16[4,192,768]{2,1,0:T(8,128)(2,1)} %get-tuple-element.289), channel_id=1, source_target_pairs={{0,4},{1,3},{2,6},{3,1},{4,0},{5,7},{6,2},{7,5},{8,12},{9,11},{10,... | collective-permute-start | bytes 3538952 | tf_op jit(solution)/shard_map/ppermute | solution.py:559
  175.8 43.2 %collective-permute-start.22 = (bf16[1024,768]{1,0:T(8,128)(2,1)}, bf16[1024,768]{1,0:T(8,128)(2,1)}, u32[]{:S(2)}, u32[]{:S(2)}) collective-permute-start(bf16[1024,768]{1,0:T(8,128)(2,1)} %mlp_out_other.1), channel_id=1, source_target_pairs={{0,1},{1,0},{2,3},{3,2},{4,5},{5,4},{6,7},{7,6},{8,9},{9,8},{10,11... | collective-permute-start | bytes 4718600 | tf_op jit(solution)/shard_map/ppermute | solution.py:559
  186.4 5.3 %collective-permute-start.12 = (bf16[4,4,208,384]{3,2,1,0:T(8,128)(2,1)}, bf16[4,4,208,384]{3,2,1,0:T(8,128)(2,1)}, u32[]{:S(2)}, u32[]{:S(2)}) collective-permute-start(bf16[4,4,208,384]{3,2,1,0:T(8,128)(2,1)} %get-tuple-element.102), channel_id=1, source_target_pairs={{0,1},{1,0},{2,3},{3,2},{4,5},{5,4},{6,7},{7,6},{8,9},{9,8},{10,11... | collective-permute-start | bytes 7667720 | tf_op jit(solution)/shard_map/cond/branch_1_fun/ppermute | solution.py:559
  195.4 18.6 %collective-permute-start.25 = (bf16[4,2,208,384]{3,2,1,0:T(8,128)(2,1)}, bf16[4,2,208,384]{3,2,1,0:T(8,128)(2,1)}, u32[]{:S(2)}, u32[]{:S(2)}) collective-permute-start(bf16[4,2,208,384]{3,2,1,0:T(8,128)(2,1)} %get-tuple-element.287), channel_id=1, source_target_pairs={{0,2},{1,5},{2,0},{3,7},{4,6},{5,1},{6,4},{7,3},{8,10},{9,13},{10,... | collective-permute-start | bytes 3833864 | tf_op jit(solution)/shard_map/ppermute | solution.py:559
  199.8 30.1 %collective-permute-start.27 = (bf16[192,768]{1,0:T(8,128)(2,1)}, bf16[192,768]{1,0:T(8,128)(2,1)}, u32[]{:S(2)}, u32[]{:S(2)}) collective-permute-start(bf16[192,768]{1,0:T(8,128)(2,1)} %get-tuple-element.302), channel_id=1, source_target_pairs={{0,8},{1,9},{2,10},{3,11},{4,12},{5,13},{6,14},{7,15},{8,0},{9,1},... | collective-permute-start | bytes 884744 | tf_op jit(solution)/shard_map/ppermute | solution.py:559
  199.8 30.1 %collective-permute-start.28 = (bf16[192,768]{1,0:T(8,128)(2,1)}, bf16[192,768]{1,0:T(8,128)(2,1)}, u32[]{:S(2)}, u32[]{:S(2)}) collective-permute-start(bf16[192,768]{1,0:T(8,128)(2,1)} %get-tuple-element.303), channel_id=1, source_target_pairs={{0,16},{1,17},{2,18},{3,19},{4,20},{5,21},{6,22},{7,23},{8,24},{9,... | collective-permute-start | bytes 884744 | tf_op jit(solution)/shard_map/ppermute | solution.py:559
  201.8 28.1 %collective-permute-start.29 = (bf16[192,768]{1,0:T(8,128)(2,1)}, bf16[192,768]{1,0:T(8,128)(2,1)}, u32[]{:S(2)}, u32[]{:S(2)}) collective-permute-start(bf16[192,768]{1,0:T(8,128)(2,1)} %get-tuple-element.304), channel_id=1, source_target_pairs={{0,24},{1,25},{2,26},{3,27},{4,28},{5,29},{6,30},{7,31},{8,16},{9,... | collective-permute-start | bytes 884744 | tf_op jit(solution)/shard_map/ppermute | solution.py:559
  216.9 17.4 %collective-permute-start.33 = (bf16[4,208,384]{2,1,0:T(8,128)(2,1)}, bf16[4,208,384]{2,1,0:T(8,128)(2,1)}, u32[]{:S(2)}, u32[]{:S(2)}) collective-permute-start(bf16[4,208,384]{2,1,0:T(8,128)(2,1)} %get-tuple-element.313), channel_id=1, source_target_pairs={{0,4},{1,3},{2,6},{3,1},{4,0},{5,7},{6,2},{7,5},{8,12},{9,11},{10,... | collective-permute-start | bytes 1916936 | tf_op jit(solution)/shard_map/ppermute | solution.py:559
  219.1 7.5 %collective-permute-start.31 = (f32[8,768]{1,0:T(8,128)}, f32[8,768]{1,0:T(8,128)}, u32[]{:S(2)}, u32[]{:S(2)}) collective-permute-start(f32[8,768]{1,0:T(8,128)} %add.15), channel_id=1, source_target_pairs={{0,8},{1,9},{2,10},{3,11},{4,12},{5,13},{6,14},{7,15},{8,0},{9,1},... | collective-permute-start | bytes 73736 | tf_op jit(solution)/shard_map/ppermute | solution.py:559
  227.9 5.0 %collective-permute-start.34 = (f32[8,768]{1,0:T(8,128)}, f32[8,768]{1,0:T(8,128)}, u32[]{:S(2)}, u32[]{:S(2)}) collective-permute-start(f32[8,768]{1,0:T(8,128)} %add.16), channel_id=1, source_target_pairs={{0,16},{1,17},{2,18},{3,19},{4,20},{5,21},{6,22},{7,23},{8,24},{9,... | collective-permute-start | bytes 73736 | tf_op jit(solution)/shard_map/ppermute | solution.py:559
  236.7 13.6 %collective-permute-start.35 = (bf16[208,384]{1,0:T(8,128)(2,1)}, bf16[208,384]{1,0:T(8,128)(2,1)}, u32[]{:S(2)}, u32[]{:S(2)}) collective-permute-start(bf16[208,384]{1,0:T(8,128)(2,1)} %get-tuple-element.319), channel_id=1, source_target_pairs={{0,8},{1,9},{2,10},{3,11},{4,12},{5,13},{6,14},{7,15},{8,0},{9,1},... | collective-permute-start | bytes 479240 | tf_op jit(solution)/shard_map/ppermute | solution.py:559
  238.7 13.9 %collective-permute-start.36 = (bf16[208,384]{1,0:T(8,128)(2,1)}, bf16[208,384]{1,0:T(8,128)(2,1)}, u32[]{:S(2)}, u32[]{:S(2)}) collective-permute-start(bf16[208,384]{1,0:T(8,128)(2,1)} %get-tuple-element.320), channel_id=1, source_target_pairs={{0,16},{1,17},{2,18},{3,19},{4,20},{5,21},{6,22},{7,23},{8,24},{9,... | collective-permute-start | bytes 479240 | tf_op jit(solution)/shard_map/ppermute | solution.py:559
  238.8 13.8 %collective-permute-start.37 = (bf16[208,384]{1,0:T(8,128)(2,1)}, bf16[208,384]{1,0:T(8,128)(2,1)}, u32[]{:S(2)}, u32[]{:S(2)}) collective-permute-start(bf16[208,384]{1,0:T(8,128)(2,1)} %get-tuple-element.321), channel_id=1, source_target_pairs={{0,24},{1,25},{2,26},{3,27},{4,28},{5,29},{6,30},{7,31},{8,16},{9,... | collective-permute-start | bytes 479240 | tf_op jit(solution)/shard_map/ppermute | solution.py:559
  241.1 4.0 %collective-permute-start.38 = (f32[8,768]{1,0:T(8,128)}, f32[8,768]{1,0:T(8,128)S(1)}, u32[]{:S(2)}, u32[]{:S(2)}) collective-permute-start(f32[8,768]{1,0:T(8,128)} %add.17), channel_id=1, source_target_pairs={{0,2},{1,3},{2,0},{3,1},{4,6},{5,7},{6,4},{7,5},{8,10},{9,11},{10,... | collective-permute-start | bytes 73736 | tf_op jit(solution)/shard_map/ppermute | solution.py:559
  247.1 7.4 %collective-permute-start.32 = (f32[2,24,768]{2,1,0:T(8,128)}, f32[2,24,768]{2,1,0:T(8,128)}, u32[]{:S(2)}, u32[]{:S(2)}) collective-permute-start(f32[2,24,768]{2,1,0:T(8,128)} %get-tuple-element.312), channel_id=1, source_target_pairs={{0,1},{1,0},{2,3},{3,2},{4,5},{5,4},{6,7},{7,6},{8,9},{9,8},{10,11... | collective-permute-start | bytes 442376 | tf_op jit(solution)/shard_map/ppermute | solution.py:559
  (10 other events, 45.2 us)

commit v7 on v6

--- a/solution.py
+++ b/solution.py
@@ -16,6 +16,7 @@
 LONG = 10**11
 SHORT = 6 * 10**9
 MIDDLE = 115 * 10**8
+LATER = 9 * 10**9
 EPS = 1e-06
 MASKED = -1e30
 SCALE = HEAD_DIM**-0.5
@@ -77,48 +78,57 @@
     return jnp.where(keep, pair, jnp.zeros_like(pair))
 
 
-def fetch_weights(me, sources, weight_refs, parts_ref, sem):
+def fetch_weights(me, sources, stage_ref, sem):
     core, chip = me & 1, me >> 1
-    side = sources[0].shape[2]
-    each = weight_refs[0].shape[0] // CHIPS
+    side = sources[0].shape[3]
     for index, source in enumerate(sources):
         half = core if index < 4 else 1 - core
+        plane = (0, 1 + half, 2 - half, 3)[index % 4]
         cols = pl.ds(pl.multiple_of(half * side, LANES), side)
         for layer in range(4):
-            owner = chip ^ (4 * layer + (0, 1 + half, 2 - half, 3)[index % 4])
-            rows = pl.ds(pl.multiple_of(owner * each, 16), each)
-            for number, ref in enumerate(weight_refs):
-                pltpu.make_async_copy(
-                    source.at[layer, pl.ds(number * each, each), :], ref.at[rows, cols], sem.at[number]
-                ).start()
-            pltpu.make_async_copy(
-                source.at[layer, pl.ds(4 * each, 16), :], parts_ref.at[2 * owner + half], sem.at[4]
-            ).start()
+            owner = chip ^ (4 * layer + plane)
+            pltpu.make_async_copy(source.at[layer], stage_ref.at[owner, :, :, cols], sem.at[0]).start()
 
 
 def project(me_ref, x_ref, *refs):
     sources = refs[:8]
     n1_ref, q_ref, k_ref, v_ref = refs[8:12]
-    wq_ref, wk_ref, wv_ref, wo_ref, vec_ref, bup_ref, parts_ref, sem = refs[12:]
-    weights = (wq_ref, wk_ref, wv_ref, wo_ref)
+    outs, (vec_ref, bup_ref, weights_ref, stage_ref, sem, out_sem) = refs[12:16], refs[16:]
+    step = pl.program_id(0)
     core = me_ref[0] & 1
-
-    @pl.when(pl.program_id(0) == 0)
-    def _():
-        fetch_weights(me_ref[0], sources, weights, parts_ref, sem)
-        for number, ref in enumerate(weights + (parts_ref,)):
-            pltpu.make_async_copy(ref, ref, sem.at[number]).wait()
-        count, _, side = parts_ref.shape
-        group = count // 2
-        halves = [sum(parts_ref[half * group + index].astype(F32) for index in range(group)) for half in range(2)]
+    weights = [weights_ref.at[number] for number in range(4)]
+
+    def write(number):
+        return pltpu.make_async_copy(weights[number], outs[number], out_sem.at[number])
+
+    @pl.when(step == 0)
+    def _():
+        fetch_weights(me_ref[0], sources, stage_ref, sem)
+        pltpu.make_async_copy(stage_ref, stage_ref, sem.at[0]).wait()
+        width = stage_ref.shape[3]
+        side = width // 2
+        blocks = width // (16 * CHIPS)
+        for number in range(4):
+            weights[number][...] = stage_ref[:, number * blocks : (number + 1) * blocks].reshape(width, width)
+            write(number).start()
+        parts = [stage_ref[chip, 4 * blocks].astype(F32) for chip in range(CHIPS)]
+        halves = []
+        for half in range(2):
+            group = parts[half * CHIPS // 2 : (half + 1) * CHIPS // 2]
+            halves.append(sum(part[:, :side] + part[:, side:] for part in group))
         vec_ref[...] = jnp.concatenate(halves, axis=1)
         blocks = bup_ref.shape[1] // side
         group = CHIPS // blocks
         for block in range(blocks):
-            rows = sum(parts_ref[2 * (block * group + index) + core].astype(F32) for index in range(group))
-            bup_ref[:, block * side : (block + 1) * side] = rows[8:9]
-
-    project_rows(x_ref, vec_ref, wq_ref, wk_ref, wv_ref, n1_ref, q_ref, k_ref, v_ref)
+            rows = sum(parts[block * group : (block + 1) * group])
+            bup_ref[:, block * side : (block + 1) * side] = jnp.where(core == 0, rows[8:9, :side], rows[8:9, side:])
+
+    project_rows(x_ref, vec_ref, *weights[:3], n1_ref, q_ref, k_ref, v_ref)
+
+    @pl.when(step == pl.num_programs(0) - 1)
+    def _():
+        for number in range(4):
+            write(number).wait()
 
 
 def project_rows(x_ref, vec_ref, wq_ref, wk_ref, wv_ref, n1_ref, q_ref, k_ref, v_ref):
@@ -214,9 +224,16 @@
                 pltpu.make_async_copy(
                     sources[index].at[layer, pl.ds(part * each, each), :], wup_ref.at[number, rows, cols], sem.at[number]
                 ).start()
-            rows = pl.ds(pl.multiple_of(owner * deep, 16), deep)
             source = sources[4 + layer // 2].at[2 * index + layer % 2]
+            rows = pl.ds(pl.multiple_of(owner * deep, 16), source.shape[0])
             pltpu.make_async_copy(source, wdown_ref.at[rows, :], sem.at[blocks]).start()
+            rest = deep - source.shape[0]
+            rows = pl.ds(pl.multiple_of(owner * deep + source.shape[0], 16), rest)
+            for part in range(width // side):
+                at = pl.ds(sources[index].shape[1] - (width // side - part) * rest, rest)
+                pltpu.make_async_copy(
+                    sources[index].at[layer, at, :], wdown_ref.at[rows, pl.ds(part * side, side)], sem.at[blocks]
+                ).start()
 
 
 def mlp(sets, count, me_ref, *refs):
@@ -437,12 +454,23 @@
     dsum_ref[1:2, :] += column_sum(grads_ref[2].astype(F32))
 
 
-def weight_grads(me_ref, n1_ref, mixed_ref, columns_ref, sum_back_ref, sum_down_ref, sum_up_ref, send_ref, keep_ref):
+def weight_grads(me_ref, n1_ref, mixed_hbm, columns_ref, sum_back_ref, sum_down_ref, sum_up_ref, send_hbm, keep_hbm,
+                 send_ref, keep_ref, mixed_ref, in_sem, out_sem):
     step = pl.program_id(0)
     me = me_ref[0]
     first = (me & 1) == 0
     side = send_ref.shape[3]
     each = n1_ref.shape[1] // CHIPS
+    load = pltpu.make_async_copy(mixed_hbm, mixed_ref, in_sem.at[0])
+
+    def writes(number):
+        rows = pl.ds(number * each, each if number < 4 else 16)
+        for index, (ref, out) in enumerate(((send_ref, send_hbm), (keep_ref, keep_hbm))):
+            yield pltpu.make_async_copy(ref.at[:, :, rows, :], out.at[:, :, rows, :], out_sem.at[index, number])
+
+    @pl.when(step == 0)
+    def _():
+        load.start()
 
     def run(left, number):
         result = dot_tn(left, columns_ref[0])
@@ -462,9 +490,15 @@
     def _():
         run(n1_ref[...], step)
 
+    for number in range(3):
+
+        @pl.when(step == number)
+        def _():
+            for copy in writes(number):
+                copy.start()
+
     @pl.when(step == 3)
     def _():
-        run(mixed_ref[...], 3)
         nothing = jnp.zeros((2, n1_ref.shape[1]), F32)
         vecs = jnp.concatenate((nothing, sum_back_ref[0:5], sum_down_ref[0:1]), axis=0)
         for chip in range(CHIPS):
@@ -475,6 +509,15 @@
             at = ((chip >> 2) ^ (me >> 3), (chip & 3) ^ ((me >> 1) & 3))
             keep_ref[at[0], at[1], 4 * each :, :] = jnp.concatenate((short, last), axis=0).astype(BF16)
             send_ref[at[0], at[1], 4 * each :, :] = jnp.concatenate((short, jnp.zeros_like(last)), axis=0).astype(BF16)
+        for copy in writes(4):
+            copy.start()
+        load.wait()
+        run(mixed_ref[...], 3)
+        for copy in writes(3):
+            copy.start()
+        for number in range(5):
+            for copy in writes(number):
+                copy.wait()
 
 
 def tokens_backward(x_ref, gresid_ref, vec_ref, grads_ref, wq_ref, wk_ref, wv_ref, gtok_ref, dsum_ref):
@@ -537,7 +580,7 @@
             scratch_shapes=scratch),
         out_shape=out_shape,
         compiler_params=pltpu.CompilerParams(vmem_limit_bytes=VMEM, dimension_semantics=("arbitrary",)),
-        cost_estimate=cost(0),
+        cost_estimate=cost(flops),
         name=name,
     )(me, *args)
 
@@ -603,8 +646,8 @@
         put(4 + part, halves[0][:, at], halves[1][:, at])
 
 
-def join_shards(me_ref, keep_ref, take_ref, *refs):
-    vectors, near_ref = refs[:-1], refs[-1]
+def join_shards(me_ref, keep_ref, take_ref, down_ref, *refs):
+    vectors, (near_ref, up_ref) = refs[:-2], refs[-2:]
     me = me_ref[0]
     first = (me & 1) == 0
     parts, own, side = keep_ref.shape
@@ -619,9 +662,11 @@
 
     for index in range(4):
         near_ref[2 * own * index : 2 * own * (index + 1), :] = joined(index)
-    base = 8 * own + 16
     for index in range(folds):
-        near_ref[base + 2 * own * index : base + 2 * own * (index + 1), :] = joined(4 + index)
+        up_ref[2 * own * index : 2 * own * (index + 1), :] = joined(4 + index)
+    base = 2 * own * folds
+    up_ref[base : base + 16, :] = down_ref[-16:, :side]
+    up_ref[base + 16 :, :] = down_ref[-16:, side:]
     rows = []
     for ref in vectors:
         flat = ref[...].astype(F32).reshape(1, -1)
@@ -631,7 +676,7 @@
     short = pltpu.roll(rows, own * lax.rem(me, side // own), 1)
     long = pltpu.roll(rows, folds * own * lax.rem(me >> 1, side // (folds * own)), 1)
     index = lax.broadcasted_iota(jnp.int32, rows.shape, 0)
-    near_ref[8 * own : base, :] = jnp.where(index < 8, short, long).astype(BF16)
+    near_ref[8 * own :, :] = jnp.where(index < 8, short, long).astype(BF16)
 
 
 def across_layers(shard):
@@ -669,8 +714,9 @@
         split_shards, (me & 1, *weights[:5]), [halves, halves], "split_shards", ins=[SMEM] + [VMEM_SPEC] * 5)
     take = swap(send, other_core)
     return small_call(
-        join_shards, (me, keep, take, *vectors), [(VMEM_SPEC, shaped(8 * own + 16 + 2 * deep, side))], "join_shards",
-        ins=[SMEM] + [VMEM_SPEC] * (2 + len(vectors)))[0]
+        join_shards, (me, keep, take, weights[5], *vectors),
+        [(VMEM_SPEC, shaped(8 * own + 16, side)), (VMEM_SPEC, shaped(2 * deep + 32, side))], "join_shards",
+        ins=[SMEM] + [VMEM_SPEC] * (3 + len(vectors)))
 
 
 def doubled(pieces, change):
@@ -727,14 +773,14 @@
     for own_ref, take_ref in zip(pairs[::2], pairs[1::2]):
         for part in range(own_ref.shape[0]):
             at = slice(base, base + own_ref.shape[3])
-            rest_ref[:, at, :] = own_ref[part, :, 0].astype(F32) + take_ref[part, :, 0].astype(F32)
+            rest_ref[:, at, :] = (own_ref[part, :, 0].astype(F32) + take_ref[part, :, 0].astype(F32)).astype(BF16)
             send_ref[:, at, :] = (own_ref[part, :, 1].astype(F32) + take_ref[part, :, 1].astype(F32)).astype(BF16)
             base += own_ref.shape[3]
 
 
 def merge_second(own_ref, take_ref, rest_ref, *send_refs):
     for layer in range(4):
-        whole = own_ref[layer] + take_ref[layer].astype(F32)
+        whole = own_ref[layer].astype(F32) + take_ref[layer].astype(F32)
         if layer == 0:
             rest_ref[...] = whole
         else:
@@ -821,17 +867,21 @@
     ins = [pl.BlockSpec((piece.shape[0], count // steps, *piece.shape[2:]), lambda i: (0, i, 0, 0, 0)) for piece in pairs]
     out = pl.BlockSpec((count // steps, rows, side), lambda i: (i, 0, 0))
     rest, send = call(
-        merge_first, (steps,), ins, [(out, shaped(count, rows, side, dtype=F32)), (out, shaped(count, rows, side))], [],
+        merge_first, (steps,), ins, [(out, shaped(count, rows, side))] * 2, [],
         "merge_first", 0, *pairs)
     return rest, swap(send, second_plane)
 
 
-def scatter_layers(own, take):
+def merge_layers_of(own, take):
     _, rows, side = own.shape
     out = shaped(rows, side)
-    rest, *sends = small_call(
+    return small_call(
         merge_second, (own, take), [(VMEM_SPEC, shaped(rows, side, dtype=F32))] + [(VMEM_SPEC, out)] * 3,
         "merge_second", ins=[VMEM_SPEC] * 2)
+
+
+def scatter_layers(own, take):
+    rest, *sends = merge_layers_of(own, take)
     return [rest] + [swap(piece, other_layer(r + 1)) for r, piece in enumerate(sends)]
 
 
@@ -892,9 +942,11 @@
     vec_spec = whole_spec((16, width))
     sums = (kept_spec((8, width)), shaped(8, width, dtype=F32))
     low_rows = (tile_rows, shaped(rows, width))
+    fold = 2 if tiles % 2 == 0 else 1
+    wide_rows = rows_spec(fold * tile, width)
+    wide_low = (wide_rows, shaped(rows, width))
     lse_spec = rows_spec(tile, LANES)
     mac = 2 * rows * width * width
-    kept_square = (kept_spec((width, width)), shaped(width, width))
     kept_vec = (kept_spec((16, width)), shaped(16, width, dtype=F32))
     kept_hidden = (kept_spec((1, hidden // 2)), shaped(1, hidden // 2, dtype=F32))
     side = width // 2
@@ -912,44 +964,52 @@
             [low_rows, (lse_spec, shaped(rows, LANES, dtype=F32)), high_rows, low_rows],
             [], "attention_forward", 0, lengths, tokens, vec, q, k, v, wo)
 
-    def gather_near(near):
+    def gather_first(near):
         cot, sum_down = masked(near)
+        along = after(swap(near, first_plane), cot)
+        return along, swap(near, second_plane), cot, sum_down
+
+    def gather_second(near, along, across, cot, up_two, up_taken):
         cot_other = swap(cot, other_core)
-        along = after(swap(near, first_plane), cot)
-        across = [swap(near, second_plane), swap(along, second_plane)]
-        along, across[0] = after((along, across[0]), *across[:1])
+        corner = swap(along, second_plane)
         taken = [swap(near, other_core), swap(along, other_core)]
-        across = after(across, taken)
-        taken += [swap(piece, other_core) for piece in across]
-        return [along, *across, *taken], cot, cot_other, sum_down
-
-    def attend_by_hand(near, up_four):
-        up_along = swap(up_four, first_plane)
-        n1, q, k, v, wq, wk, wv, wo, vec, bup = call_with(
-            me, project, tiles, [tile_rows] + [ANY_SPEC] * 8, [low_rows] * 4 + [kept_square] * 4 + [kept_vec, kept_hidden],
-            [pltpu.VMEM((count, 16, side), BF16), pltpu.SemaphoreType.DMA((5,))], "project", 0, tokens, *near)
-        up_four, up_along = after((up_four, up_along), n1)
-        up = [up_along, swap(up_four, second_plane), swap(up_along, second_plane)]
+        across, corner_out = after((across, corner), taken)
+        taken += [swap(across, other_core), swap(corner_out, other_core)]
+        return corner, taken, cot_other, jnp.concatenate((up_two, up_taken))
+
+    def attend_by_hand(q, k, v, vec, wo, up_four, up_along):
+        up = [swap(up_four, second_plane), swap(up_along, second_plane)]
         mixed, lse, resid, n2 = attend(q, k, v, vec, wo)
         up = after(up, mixed)
         n2_other = swap(after(n2, up), other_core)
-        return n1, q, k, v, wq, wk, wv, wo, vec, bup, mixed, lse, resid, n2, n2_other, up
+        return mixed, lse, resid, n2, n2_other, up
 
     if by_hand:
-        down_two = doubled(down_weight[None], other_layer(1))
-        first = prepare(me, weights, vectors)
-        moved = [swap(first, other_layer(r)) for r in (1, 2, 3)]
-        down_shard = fenced(gather_down, after(down_two, first))
-        pieces = [first] + after(moved, down_shard)
-        split = 8 * own + 16
-        near = jnp.stack([piece[:split] for piece in pieces])
-        up_four = jnp.stack([piece[split:] for piece in pieces])
-        near, up_four = after((near, up_four))
-        down = [down_shard, swap(after(down_shard, near, up_four), other_layer(2))]
-        near_moved, cot, cot_other, sum_down = fenced(gather_near, near)
-        near = [near] + near_moved
-        n1, q, k, v, wq, wk, wv, wo, vec, bup, mixed, lse, resid, n2, n2_other, up = fenced(
-            attend_by_hand, near, up_four)
+        down_two = doubled(down_weight[None, :-16], other_layer(1))
+        near, up = prepare(me, weights, vectors)
+        near_moved = [swap(near, other_layer(r)) for r in (1, 2, 3)]
+        up_moved = swap(up, other_layer(1))
+        down_shard = fenced(gather_down, after(down_two, near))
+        near_moved, up_moved = after((near_moved, up_moved), down_shard)
+        near = jnp.stack([near] + near_moved)
+        up_two = jnp.stack((up, up_moved))
+        near, up_two = after((near, up_two))
+        up_moved = swap(up_two, other_layer(2))
+        along, across, cot, sum_down = fenced(gather_first, near)
+        up_taken = after(up_moved, along)
+        down = [down_shard, swap(after(down_shard, along), other_layer(2))]
+        corner, taken, cot_other, up_four = fenced(gather_second, near, along, across, cot, up_two, up_taken)
+        near = [near, along, across, corner] + taken
+        up_along = swap(up_four, first_plane)
+        n1, q, k, v, wq, wk, wv, wo, vec, bup = call_with(
+            me, project, tiles, [tile_rows] + [ANY_SPEC] * 8,
+            [low_rows] * 4 + [(ANY_SPEC, shaped(width, width))] * 4 + [kept_vec, kept_hidden],
+            [pltpu.VMEM((4, width, width), BF16), pltpu.VMEM((CHIPS, width // (4 * CHIPS) + 1, 16, width), BF16),
+             pltpu.SemaphoreType.DMA((1,)), pltpu.SemaphoreType.DMA((4,))],
+            "project", LATER, tokens, *[piece.reshape(4, -1, 16, side) for piece in near])
+        up_along = after(up_along, n1)
+        mixed, lse, resid, n2, n2_other, up_moved = fenced(attend_by_hand, q, k, v, vec, wo, up_four, up_along)
+        up = [up_along] + up_moved
         hidden_weights = [(up_four, *up, *down)]
     else:
         wq, wk, wv, wo, hidden_weights, vec, bup = gather_plain(weights, vectors)
@@ -970,7 +1030,7 @@
     down_part = (ANY_SPEC, shaped(4, 2, deep, width))
     up_part = (ANY_SPEC, shaped(blocks, 4, 2, each, width))
 
-    act_spec = pl.BlockSpec((tile, blocks * width), lambda i, *me: (i, 0))
+    act_spec = pl.BlockSpec((fold * tile, blocks * width), lambda i, *me: (i, 0))
     wide_spec = whole_spec((hidden // 2, width))
 
     def run_mlp(me, tokens_of, bup, sources):
@@ -1013,26 +1073,35 @@
 
     def run_weights(grads):
         return call_with(
-            me, weight_grads, 4, [full_rows] * 2 + [columns, sum_spec, sum_spec, whole_spec((1, sum_up.shape[1]))],
-            [(kept_spec(pair_shape), shaped(*pair_shape))] * 2, [], "weight_grads", 0,
+            me, weight_grads, 4, [full_rows, ANY_SPEC, columns, sum_spec, sum_spec, whole_spec((1, sum_up.shape[1]))],
+            [(ANY_SPEC, shaped(*pair_shape))] * 2,
+            [pltpu.VMEM(pair_shape, BF16)] * 2
+            + [pltpu.VMEM((rows, width), BF16), pltpu.SemaphoreType.DMA((1,)), pltpu.SemaphoreType.DMA((2, 5))],
+            "weight_grads", 0,
             n1, mixed, grads, sum_back, sum_down, sum_up)
 
     def run_tokens(gresid):
         return call(
-            tokens_backward, (tiles,), [tile_rows, tile_rows, vec_spec, grads_spec, square, square, square],
-            [low_rows, sums], [], "tokens_backward", MIDDLE, tokens, gresid, vec, grads, wq, wk, wv)
+            tokens_backward, (tiles // fold,),
+            [wide_rows, wide_rows, vec_spec, pl.BlockSpec((4, fold * tile, width), lambda i: (0, i, 0)), square, square, square],
+            [wide_low, sums], [], "tokens_backward", MIDDLE, tokens, gresid, vec, grads, wq, wk, wv)
 
     if by_hand:
         (out_other,) = call_with(
-            me, mlp_out_other, tiles, [act_spec, wide_spec], [low_rows], [], "mlp_out_other", 0, after(act_other, grads), wdown)
+            me, mlp_out_other, tiles // fold, [act_spec, wide_spec], [wide_low], [], "mlp_out_other", 0, after(act_other, grads), wdown)
         down_first, up_first = after((down_first, up_first), out_other)
         hidden_rest, hidden_take = scatter_second(*down_first, *up_first)
 
-        def weights_of_chip(grads):
+        def weights_of_chip(grads, out_take):
             square_send, square_keep = run_weights(grads)
-            return merge_core_of(core, square_keep, scatter_core(square_send))
-
-        square_own, square_send = fenced(weights_of_chip, after(grads, hidden_rest))
+            (out,) = call_with(
+                me, mlp_out_own, tiles // fold, [wide_rows, vec_spec, act_spec, wide_rows, wide_spec], [wide_low], [],
+                "mlp_out_own", 0, resid, vec, act_own, after(out_take, square_send), wdown)
+            square_take = after(scatter_core(square_send), out)
+            return *merge_core_of(core, square_keep, square_take), out
+
+        out_take = swap(out_other, other_core)
+        square_own, square_send, out = fenced(weights_of_chip, after(grads, hidden_rest), out_take)
         square_take = swap(square_send, first_plane).reshape(square_own.shape)
         hidden_rest, hidden_take = after((hidden_rest, hidden_take), square_own)
         hidden_layers = scatter_layers(hidden_rest, hidden_take)
@@ -1041,18 +1110,17 @@
         late = late + swap(late, other_core)
         square_second = scatter_second(square_own, square_take)
         late = after(late, square_second[0])
-        out_take = after(swap(out_other, other_core), square_second[0])
-        (out,) = call_with(
-            me, mlp_out_own, tiles, [tile_rows, vec_spec, act_spec, tile_rows, wide_spec], [low_rows], [],
-            "mlp_out_own", 0, resid, vec, act_own, out_take, wdown)
-        late = late + after(swap(late, other_layer(1)), out)
+        late = late + swap(late, other_layer(1))
         hidden_layers = after(hidden_layers, late)
         g_down, up_keep, up_send = scatter_last(core, hidden_layers, own, blocks, deep)
         up_take = scatter_core(up_send)
-        late = late + after(swap(late, other_layer(2)), g_down)
-        square_second = after(square_second, g_down, late)
-        square_layers = scatter_layers(*square_second)
-        late = late + after(swap(late, other_plane(1)), square_layers[0])
+        late_take = after(swap(late, other_layer(2)), g_down)
+        square_second = after(square_second, g_down)
+        rest, *sends = merge_layers_of(*square_second)
+        rest, sends, late_take = after((rest, sends, late_take))
+        square_layers = [rest] + [swap(piece, other_layer(r + 1)) for r, piece in enumerate(sends)]
+        late = late + late_take
+        late = late + after(swap(late, other_plane(1)), rest)
         late = late + swap(late, other_plane(2))
         square_layers = after(square_layers, late)
         square_keep, square_send, flat = scatter_last(core, square_layers, own, 4, 0)
@@ -1072,9 +1140,9 @@
         g_down, g_up, g_q, g_k, g_v, g_o, flat = reduce_plain(
             [run[2:4] for run in runs], [run[4:6] for run in runs], (square_keep, square_send), flat)
         (out_other,) = call_with(
-            me + 1, mlp_out_other, tiles, [act_spec, wide_spec], [low_rows], [], "mlp_out_other", 0, act_other, runs[1][6])
+            me + 1, mlp_out_other, tiles // fold, [act_spec, wide_spec], [wide_low], [], "mlp_out_other", 0, act_other, runs[1][6])
         (out,) = call_with(
-            me, mlp_out_own, tiles, [tile_rows, vec_spec, act_spec, tile_rows, wide_spec], [low_rows], [],
+            me, mlp_out_own, tiles // fold, [wide_rows, vec_spec, act_spec, wide_rows, wide_spec], [wide_low], [],
             "mlp_out_own", 0, resid, vec, act_own, out_other, runs[0][6])
         g_flat = [flat[index * own : (index + 1) * own] for index in range(8)]
         g_ub = flat[8 * own :]

time: 260 us -> 252 us (0.969)
  local copies, waits for them, and re-layouts: 1.1 us -> 4.72 us
  Pallas kernels: 143 us -> 140 us
  starting transfers between devices: 45.1 us -> 42.3 us
  waiting for transfers between devices: 58.4 us -> 55.7 us
    ppermute x41 -> x43, starting transfers between devices: 45.1 us -> 42.3 us  [swap(): return lax.ppermute(array, 'dp', flipped(lax.axis_size('dp'), change))]
    ppermute x41 -> x43, waiting for transfers between devices: 58.4 us -> 55.7 us  [swap(): return lax.ppermute(array, 'dp', flipped(lax.axis_size('dp'), change))]
  transfers between devices with their start and end apart: 41 -> 43, of which waited for: 17 -> 18; matrix products, arithmetic and copies ran while one was open for 3% -> 4% of each run, Pallas kernels for 38% -> 39%
where the time goes in v7:
time: 252 us
  Pallas kernels  140 us (56%)
  waiting for transfers between devices  55.7 us (22%)
  starting transfers between devices  42.3 us (17%)
  other arithmetic  7.73 us (3%)
  local copies, waits for them, and re-layouts  4.72 us (2%)
    pallas_call x5, Pallas kernels, call_with(): pl.pallas_call(kernel, grid_spec=pltpu.PrefetchScalarGridSpec(num_scalar_...  67.5 us
    pallas_call x7, Pallas kernels, call(): pl.pallas_call(kernel, grid=grid, in_specs=ins, out_specs=out_specs, out_...  57.5 us
    ppermute x43, waiting for transfers between devices, swap(): return lax.ppermute(array, 'dp', flipped(lax.axis_size('dp'), change))  55.7 us
    ppermute x43, starting transfers between devices, swap(): return lax.ppermute(array, 'dp', flipped(lax.axis_size('dp'), change))  42.3 us
    pallas_call x7, Pallas kernels, small_call(): pl.pallas_call(kernel, in_specs=ins, out_specs=tuple((spec for spec, _ in...  15.1 us
  transfers between devices with their start and end apart: 43, of which 18 were waited for; matrix products, arithmetic and copies ran while one was open for 4% of the time, Pallas kernels for 39%

profile of v7, /device:TPU:0, one launch (start us, length us, event | category | flops | bytes accessed | tf_op | source)
XLA Modules:
  0.0 251.6 jit_solution(7771244260104185695)
XLA Ops:
  4.5 2.6 %collective-permute-start.19 = (bf16[1,80,768]{2,1,0:T(8,128)(2,1)}, bf16[1,80,768]{2,1,0:T(8,128)(2,1)}, u32[]{:S(2)}, u32[]{:S(2)}) collective-permute-start(bf16[1,80,768]{2,1,0:T(8,128)(2,1)} %slice_bitcast_fusion), channel_id=1, source_target_pairs={{0,8},{1,9},{2,10},{3,11},{4,12},{5,13},{6,14},{7,15},{8,0},{9,1},... | collective-permute-start | bytes 368648 | tf_op jit(solution)/shard_map/ppermute | solution.py:602
  9.2 3.9 %collective-permute-start.17 = (bf16[208,384]{1,0:T(8,128)(2,1)}, bf16[208,384]{1,0:T(8,128)(2,1)S(1)}, u32[]{:S(2)}, u32[]{:S(2)}) collective-permute-start(bf16[208,384]{1,0:T(8,128)(2,1)} %get-tuple-element.262), channel_id=1, source_target_pairs={{0,24},{1,25},{2,26},{3,27},{4,28},{5,29},{6,30},{7,31},{8,16},{9,... | collective-permute-start | bytes 479240 | tf_op jit(solution)/shard_map/ppermute | solution.py:602
  14.7 15.3 %conditional.5 = (bf16[8,80,768]{2,1,0:T(8,128)(2,1)S(1)}) conditional(s32[]{:T(128)} %convert_element_type.2, () %tuple.85, bf16[2,80,768]{2,1,0:T(8,128)(2,1)S(1)} %pad_maximum_fusion.5), branch_computations={%region_0.0_spmd, %region_1.0_spmd} | conditional | flops 1228800 | bytes 5898328 | solution.py:844
  16.5 4.5 %collective-permute-done.6 = bf16[2,80,768]{2,1,0:T(8,128)(2,1)S(1)} collective-permute-done((bf16[2,80,768]{2,1,0:T(8,128)(2,1)S(1)}, bf16[2,80,768]{2,1,0:T(8,128)(2,1)S(1)}, u32[]{:S(2)}, u32[]{:S(2)}) %collective-permute-start.6) | collective-permute-done | bytes 245792 | tf_op jit(solution)/shard_map/cond/branch_1_fun/ppermute | solution.py:602
  22.8 7.1 %collective-permute-done.7 = bf16[4,80,768]{2,1,0:T(8,128)(2,1)S(1)} collective-permute-done((bf16[4,80,768]{2,1,0:T(8,128)(2,1)S(1)}, bf16[4,80,768]{2,1,0:T(8,128)(2,1)S(1)}, u32[]{:S(2)}, u32[]{:S(2)}) %collective-permute-start.7) | collective-permute-done | bytes 491552 | tf_op jit(solution)/shard_map/cond/branch_1_fun/ppermute | solution.py:602
  31.9 2.4 collective-permute-start.20
  34.3 17.4 %conditional.6 = (bf16[4,208,384]{2,1,0:T(8,128)(2,1)}, bf16[4,208,384]{2,1,0:T(8,128)(2,1)}, bf16[1024,768]{1,0:T(8,128)(2,1)S(1)}, f32[8,768]{1,0:T(8,128)}, b...) conditional(s32[]{:T(128)} %convert_element_type.2, () %tuple.89, ...), branch_computations={%region_2.0_spmd, %region_3.0_spmd} | conditional | bytes 13959325 | solution.py:844
  37.3 3.8 %mask_grads.1 = (bf16[1024,768]{1,0:T(8,128)(2,1)}, f32[8,768]{1,0:T(8,128)}) custom-call(s32[4,5]{1,0:T(4,128)} %get-tuple-element.73.lengths_ref, bf16[1024,768]{1,0:T(8,128)(2,1)} %get-tuple-element.75.grad_ref), custom_call_target="tpu_custom_call" | custom-call | bytes 1 | tf_op jit(solution)/shard_map/cond/branch_1_fun/mask_grads/pallas_call | solution.py:561
  41.1 8.4 %collective-permute-done.1 = bf16[4,208,384]{2,1,0:T(8,128)(2,1)} collective-permute-done((bf16[4,208,384]{2,1,0:T(8,128)(2,1)}, bf16[4,208,384]{2,1,0:T(8,128)(2,1)}, u32[]{:S(2)}, u32[]{:S(2)}) %collective-permute-start.1) | collective-permute-done | bytes 639008 | tf_op jit(solution)/shard_map/cond/branch_1_fun/ppermute | solution.py:602
  53.3 14.6 %conditional.7 = (bf16[1024,768]{1,0:T(8,128)(2,1)}, bf16[4,224,384]{2,1,0:T(8,128)(2,1)}, bf16[4,13,16,384]{3,2,1,0:T(8,128)(2,1)}, bf16[4,13,16,384]{3,2,1,0:T...) conditional(s32[]{:T(128)} %convert_element_type.2, () %tuple.91, ...), branch_computations={%region_4.0_spmd, %region_5.0_spmd} | conditional | flops 344064 | bytes 20447528 | solution.py:844
  58.5 6.0 %collective-permute-done.9 = bf16[4,208,384]{2,1,0:T(8,128)(2,1)} collective-permute-done((bf16[4,208,384]{2,1,0:T(8,128)(2,1)}, bf16[4,208,384]{2,1,0:T(8,128)(2,1)}, u32[]{:S(2)}, u32[]{:S(2)}) %collective-permute-start.9) | collective-permute-done | bytes 639008 | tf_op jit(solution)/shard_map/cond/branch_1_fun/ppermute | solution.py:602
  68.4 10.4 %project.1 = (bf16[1024,768]{1,0:T(8,128)(2,1)}, bf16[1024,768]{1,0:T(8,128)(2,1)}, bf16[1024,768]{1,0:T(8,128)(2,1)}, bf16[1024,768]{1,0:T(8,128)(2,1)}, bf16[7...) custom-call(s32[1]{0:T(128)} %bitcast.8.me_ref, ...), custom_call_target="tpu_custom_call" | custom-call | flops 8999999488 | bytes 1 | tf_op jit(solution)/shard_map/project/pallas_call | solution.py:576
  79.1 22.4 %conditional.8 = (bf16[1024,768]{1,0:T(8,128)(2,1)}, f32[1024,128]{1,0:T(8,128)}, f32[1024,768]{1,0:T(8,128)}, bf16[1024,768]{1,0:T(8,128)(2,1)}, bf16[1024,768]...) conditional(s32[]{:T(128)} %convert_element_type.2, () %tuple.94, ...), branch_computations={%region_6.0_spmd, %region_7.0_spmd} | conditional | bytes 11796657 | solution.py:844
  81.2 13.3 %attention_forward.1 = (bf16[1024,768]{1,0:T(8,128)(2,1)}, f32[1024,128]{1,0:T(8,128)}, f32[1024,768]{1,0:T(8,128)}, bf16[1024,768]{1,0:T(8,128)(2,1)}) custom-call(s32[4,5]{1,0:T(4,128)} %get-tuple-element.87.lengths_ref, bf16[1024,768]{1,0:T(8,128)(2,1)} %get-tuple-element.88.x_ref, f32[16,768]{1,0:T(8,128)} %get-tuple-element.89.vec_ref, ...), custom_call_target="tpu_custom_call" | custom-call | bytes 1 | tf_op jit(solution)/shard_map/cond/branch_1_fun/attention_forward/pallas_call | solution.py:561
  94.4 3.3 %collective-permute-done.3 = bf16[4,224,384]{2,1,0:T(8,128)(2,1)} collective-permute-done((bf16[4,224,384]{2,1,0:T(8,128)(2,1)}, bf16[4,224,384]{2,1,0:T(8,128)(2,1)}, u32[]{:S(2)}, u32[]{:S(2)}) %collective-permute-start.3) | collective-permute-done | bytes 688160 | tf_op jit(solution)/shard_map/cond/branch_1_fun/ppermute | solution.py:602
  97.8 3.7 %collective-permute-done.4 = bf16[1024,768]{1,0:T(8,128)(2,1)} collective-permute-done((bf16[1024,768]{1,0:T(8,128)(2,1)}, bf16[1024,768]{1,0:T(8,128)(2,1)}, u32[]{:S(2)}, u32[]{:S(2)}) %collective-permute-start.4) | collective-permute-done | bytes 1572896 | tf_op jit(solution)/shard_map/cond/branch_1_fun/ppermute | solution.py:602
  101.5 34.8 %mlp.1 = (bf16[1024,1536]{1,0:T(8,128)(2,1)}, bf16[1024,1536]{1,0:T(8,128)(2,1)}, f32[1024,768]{1,0:T(8,128)}, bf16[1024,768]{1,0:T(8,128)(2,1)}, bf16[4,2,96,76...) custom-call(s32[1]{0:T(128)} %bitcast.8.me_ref, ...), custom_call_target="tpu_custom_call" | custom-call | bytes 1 | tf_op jit(solution)/shard_map/mlp/pallas_call | solution.py:576
  140.1 20.6 %attention_backward.1 = (bf16[4,1024,768]{2,1,0:T(8,128)(2,1)}, f32[1024,768]{1,0:T(8,128)}, f32[8,768]{1,0:T(8,128)}) custom-call(s32[4,5]{1,0:T(4,128)} %lengths_ref.1, bf16[1024,768]{1,0:T(8,128)(2,1)} %get-tuple-element.283.q_ref, bf16[1024,768]{1,0:T(8,128)(2,1)} %get-tuple-element.284.k_ref, bf16[1024,768]{1,0:T(8,128)(2,1)} %get-tuple-element.285.v_ref, ...), custom_call_target="tpu_custom_call" | custom-call | bytes 1 | tf_op jit(solution)/shard_map/attention_backward/pallas_call | solution.py:561
  160.8 5.8 %mlp_out_other.1 = bf16[1024,768]{1,0:T(8,128)(2,1)} custom-call(s32[1]{0:T(128)} %bitcast.8.me_ref, bf16[1024,1536]{1,0:T(8,128)(2,1)} %get-tuple-element.307.act_ref, bf16[1536,768]{1,0:T(8,128)(2,1)} %get-tuple-element.308.wdown_ref), custom_call_target="tpu_custom_call" | custom-call | bytes 1 | tf_op jit(solution)/shard_map/mlp_out_other/pallas_call | solution.py:576
  166.7 3.6 %merge_first.2 = (bf16[4,192,768]{2,1,0:T(8,128)(2,1)}, bf16[4,192,768]{2,1,0:T(8,128)(2,1)}) custom-call(bf16[1,4,2,96,768]{4,3,2,1,0:T(8,128)(2,1)} %bitcast.21, bf16[1,4,2,96,768]{4,3,2,1,0:T(8,128)(2,1)} %bitcast.18.refs_1_, bf16[2,4,2,48,768]{4,3,2,1,0:T(8,128)(2,1)} %get-tuple-element.311.refs_2_, ...), custom_call_target="tpu_custom_call" | custom-call | bytes 1 | tf_op jit(solution)/shard_map/merge_first/pallas_call | solution.py:561
  171.9 20.3 %conditional.9 = (bf16[1,4,2,208,384]{4,3,2,1,0:T(8,128)(2,1)}, bf16[4,2,208,384]{3,2,1,0:T(8,128)(2,1)}, bf16[1024,768]{1,0:T(8,128)(2,1)}) conditional(s32[]{:T(128)} %convert_element_type.2, () %tuple.84, (s32[1]{0:T(128)}, bf16[1024,768]{1,0:T(8,128)(2,1)}, bf16[1024,768]{1,0:T(8,128)(2,1)}, bf16[4,1024,768]{2,1,0:T(8,128)(2,1)}, ...), branch_computations={%region_8.0_spmd, %region_9.0_spmd} | conditional | bytes 10223683 | solution.py:844
  171.9 9.4 %weight_grads.1 = (bf16[4,4,208,384]{3,2,1,0:T(8,128)(2,1)}, bf16[4,4,208,384]{3,2,1,0:T(8,128)(2,1)}) custom-call(s32[1]{0:T(128)} %get-tuple-element.104.me_ref, bf16[1024,768]{1,0:T(8,128)(2,1)} %get-tuple-element.105.n1_ref, bf16[1024,768]{1,0:T(8,128)(2,1)} %get-tuple-element.106.mixed_hbm, bf16[4,1024,768]{2,1,0:T(8,128)(2,1)} %get-tuple-element.107.columns_ref, ...), custom_call_target="tpu_custom_call" | custom-call | bytes 1 | tf_op jit(solution)/shard_map/cond/branch_1_fun/weight_grads/pallas_call | solution.py:576
  181.4 7.1 %mlp_out_own.1 = bf16[1024,768]{1,0:T(8,128)(2,1)} custom-call(s32[1]{0:T(128)} %get-tuple-element.104.me_ref, f32[1024,768]{1,0:T(8,128)} %get-tuple-element.113.resid_ref, f32[16,768]{1,0:T(8,128)} %get-tuple-element.114.vec_ref, bf16[1024,1536]{1,0:T(8,128)(2,1)} %get-tuple-element.115.act_ref, bf16[1024,768]{1,0:T(8,128)(2,1)} %get-tuple-element.117.take_ref, ...), custom_call_target="tpu_custom_call" | custom-call | bytes 1 | tf_op jit(solution)/shard_map/cond/branch_1_fun/mlp_out_own/pallas_call | solution.py:576
  188.4 3.7 %merge_core.1 = (bf16[4,2,208,384]{3,2,1,0:T(8,128)(2,1)}, bf16[4,2,208,384]{3,2,1,0:T(8,128)(2,1)}) custom-call(s32[1]{0:T(128)} %get-tuple-element.103.core_ref, bf16[4,4,208,384]{3,2,1,0:T(8,128)(2,1)} %get-tuple-element.111.keep_ref, bf16[4,4,208,384]{3,2,1,0:T(8,128)(2,1)} %collective-permute-done.5.take_ref), custom_call_target="tpu_custom_call" | custom-call | bytes 1 | tf_op jit(solution)/shard_map/cond/branch_1_fun/merge_core/pallas_call | solution.py:561
  193.5 2.8 %merge_second.2 = (f32[192,768]{1,0:T(8,128)}, bf16[192,768]{1,0:T(8,128)(2,1)}, bf16[192,768]{1,0:T(8,128)(2,1)}, bf16[192,768]{1,0:T(8,128)(2,1)}) custom-call(bf16[4,192,768]{2,1,0:T(8,128)(2,1)} %get-tuple-element.323.own_ref, bf16[4,192,768]{2,1,0:T(8,128)(2,1)} %collective-permute-done.27.take_ref), custom_call_target="tpu_custom_call" | custom-call | bytes 1 | tf_op jit(solution)/shard_map/merge_second/pallas_call | solution.py:691
  200.6 9.8 %tokens_backward.1 = (bf16[1024,768]{1,0:T(8,128)(2,1)}, f32[8,768]{1,0:T(8,128)}) custom-call(bf16[1024,768]{1,0:T(8,128)(2,1)} %x_ref.3, f32[1024,768]{1,0:T(8,128)} %get-tuple-element.326.gresid_ref, f32[16,768]{1,0:T(8,128)} %get-tuple-element.282.vec_ref, bf16[4,1024,768]{2,1,0:T(8,128)(2,1)} %get-tuple-element.314.grads_ref, ...), custom_call_target="tpu_custom_call" | custom-call | flops 11500000256 | bytes 1 | tf_op jit(solution)/shard_map/tokens_backward/pallas_call | solution.py:561
  210.5 2.6 %merge_first.3 = (bf16[4,208,384]{2,1,0:T(8,128)(2,1)}, bf16[4,208,384]{2,1,0:T(8,128)(2,1)}) custom-call(bf16[1,4,2,208,384]{4,3,2,1,0:T(8,128)(2,1)} %get-tuple-element.322.refs_0_, bf16[1,4,2,208,384]{4,3,2,1,0:T(8,128)(2,1)} %bitcast.19.refs_1_), custom_call_target="tpu_custom_call" | custom-call | bytes 1 | tf_op jit(solution)/shard_map/merge_first/pallas_call | solution.py:561
  217.6 2.5 %collective-permute-done.33 = f32[8,768]{1,0:T(8,128)S(1)} collective-permute-done((f32[8,768]{1,0:T(8,128)S(1)}, f32[8,768]{1,0:T(8,128)S(1)}, u32[]{:S(2)}, u32[]{:S(2)}) %collective-permute-start.33) | collective-permute-done | bytes 24608 | tf_op jit(solution)/shard_map/ppermute | solution.py:602
  224.0 3.7 %collective-permute-done.36 = f32[8,768]{1,0:T(8,128)} collective-permute-done((f32[8,768]{1,0:T(8,128)}, f32[8,768]{1,0:T(8,128)}, u32[]{:S(2)}, u32[]{:S(2)}) %collective-permute-start.36) | collective-permute-done | bytes 24608 | tf_op jit(solution)/shard_map/ppermute | solution.py:602
  229.9 2.5 collective-permute-start.37
  236.4 2.9 %collective-permute-done.40 = f32[8,768]{1,0:T(8,128)S(1)} collective-permute-done((f32[8,768]{1,0:T(8,128)S(1)}, f32[8,768]{1,0:T(8,128)S(1)}, u32[]{:S(2)}, u32[]{:S(2)}) %collective-permute-start.40) | collective-permute-done | bytes 24608 | tf_op jit(solution)/shard_map/ppermute | solution.py:602
  240.5 2.7 %collective-permute-done.41 = f32[8,768]{1,0:T(8,128)S(1)} collective-permute-done((f32[8,768]{1,0:T(8,128)S(1)}, f32[8,768]{1,0:T(8,128)S(1)}, u32[]{:S(2)}, u32[]{:S(2)}) %collective-permute-start.41) | collective-permute-done | bytes 24608 | tf_op jit(solution)/shard_map/ppermute | solution.py:602
  (106 shorter events, 66.6 us)
Async XLA Ops:
  4.5 9.1 %collective-permute-start.19 = (bf16[1,80,768]{2,1,0:T(8,128)(2,1)}, bf16[1,80,768]{2,1,0:T(8,128)(2,1)}, u32[]{:S(2)}, u32[]{:S(2)}) collective-permute-start(bf16[1,80,768]{2,1,0:T(8,128)(2,1)} %slice_bitcast_fusion), channel_id=1, source_target_pairs={{0,8},{1,9},{2,10},{3,11},{4,12},{5,13},{6,14},{7,15},{8,0},{9,1},... | collective-permute-start | bytes 368648 | tf_op jit(solution)/shard_map/ppermute | solution.py:602
  9.1 21.0 %collective-permute-start.18 = (bf16[224,384]{1,0:T(8,128)(2,1)}, bf16[224,384]{1,0:T(8,128)(2,1)S(1)}, u32[]{:S(2)}, u32[]{:S(2)}) collective-permute-start(bf16[224,384]{1,0:T(8,128)(2,1)} %get-tuple-element.263), channel_id=1, source_target_pairs={{0,8},{1,9},{2,10},{3,11},{4,12},{5,13},{6,14},{7,15},{8,0},{9,1},... | collective-permute-start | bytes 516104 | tf_op jit(solution)/shard_map/ppermute | solution.py:602
  9.2 20.8 %collective-permute-start.17 = (bf16[208,384]{1,0:T(8,128)(2,1)}, bf16[208,384]{1,0:T(8,128)(2,1)S(1)}, u32[]{:S(2)}, u32[]{:S(2)}) collective-permute-start(bf16[208,384]{1,0:T(8,128)(2,1)} %get-tuple-element.262), channel_id=1, source_target_pairs={{0,24},{1,25},{2,26},{3,27},{4,28},{5,29},{6,30},{7,31},{8,16},{9,... | collective-permute-start | bytes 479240 | tf_op jit(solution)/shard_map/ppermute | solution.py:602
  13.1 16.9 %collective-permute-start.16 = (bf16[208,384]{1,0:T(8,128)(2,1)}, bf16[208,384]{1,0:T(8,128)(2,1)S(1)}, u32[]{:S(2)}, u32[]{:S(2)}) collective-permute-start(bf16[208,384]{1,0:T(8,128)(2,1)} %get-tuple-element.262), channel_id=1, source_target_pairs={{0,16},{1,17},{2,18},{3,19},{4,20},{5,21},{6,22},{7,23},{8,24},{9,... | collective-permute-start | bytes 479240 | tf_op jit(solution)/shard_map/ppermute | solution.py:602
  13.1 16.9 %collective-permute-start.15 = (bf16[208,384]{1,0:T(8,128)(2,1)}, bf16[208,384]{1,0:T(8,128)(2,1)S(1)}, u32[]{:S(2)}, u32[]{:S(2)}) collective-permute-start(bf16[208,384]{1,0:T(8,128)(2,1)} %get-tuple-element.262), channel_id=1, source_target_pairs={{0,8},{1,9},{2,10},{3,11},{4,12},{5,13},{6,14},{7,15},{8,0},{9,1},... | collective-permute-start | bytes 479240 | tf_op jit(solution)/shard_map/ppermute | solution.py:602
  14.7 6.3 %collective-permute-start.6 = (bf16[2,80,768]{2,1,0:T(8,128)(2,1)S(1)}, bf16[2,80,768]{2,1,0:T(8,128)(2,1)S(1)}, u32[]{:S(2)}, u32[]{:S(2)}) collective-permute-start(bf16[2,80,768]{2,1,0:T(8,128)(2,1)S(1)} %param.1), channel_id=1, source_target_pairs={{0,2},{1,5},{2,0},{3,7},{4,6},{5,1},{6,4},{7,3},{8,10},{9,13},{10,... | collective-permute-start | bytes 737288 | tf_op jit(solution)/shard_map/cond/branch_1_fun/ppermute | solution.py:602
  21.0 8.9 %collective-permute-start.7 = (bf16[4,80,768]{2,1,0:T(8,128)(2,1)S(1)}, bf16[4,80,768]{2,1,0:T(8,128)(2,1)S(1)}, u32[]{:S(2)}, u32[]{:S(2)}) collective-permute-start(bf16[4,80,768]{2,1,0:T(8,128)(2,1)S(1)} %pad_maximum_fusion.1), channel_id=1, source_target_pairs={{0,4},{1,3},{2,6},{3,1},{4,0},{5,7},{6,2},{7,5},{8,12},{9,11},{10,... | collective-permute-start | bytes 1474568 | tf_op jit(solution)/shard_map/cond/branch_1_fun/ppermute | solution.py:602
  31.9 20.4 %collective-permute-start.20 = (bf16[2,224,384]{2,1,0:T(8,128)(2,1)}, bf16[2,224,384]{2,1,0:T(8,128)(2,1)}, u32[]{:S(2)}, u32[]{:S(2)}) collective-permute-start(bf16[2,224,384]{2,1,0:T(8,128)(2,1)} %pad_maximum_fusion.4), channel_id=1, source_target_pairs={{0,16},{1,17},{2,18},{3,19},{4,20},{5,21},{6,22},{7,23},{8,24},{9,... | collective-permute-start | bytes 1032200 | tf_op jit(solution)/shard_map/ppermute | solution.py:602
  34.3 15.2 %collective-permute-start.1 = (bf16[4,208,384]{2,1,0:T(8,128)(2,1)}, bf16[4,208,384]{2,1,0:T(8,128)(2,1)}, u32[]{:S(2)}, u32[]{:S(2)}) collective-permute-start(bf16[4,208,384]{2,1,0:T(8,128)(2,1)} %get-tuple-element.72), channel_id=1, source_target_pairs={{0,4},{1,3},{2,6},{3,1},{4,0},{5,7},{6,2},{7,5},{8,12},{9,11},{10,... | collective-permute-start | bytes 1916936 | tf_op jit(solution)/shard_map/cond/branch_1_fun/ppermute | solution.py:602
  35.8 14.8 %collective-permute-start = (bf16[4,208,384]{2,1,0:T(8,128)(2,1)}, bf16[4,208,384]{2,1,0:T(8,128)(2,1)}, u32[]{:S(2)}, u32[]{:S(2)}) collective-permute-start(bf16[4,208,384]{2,1,0:T(8,128)(2,1)} %get-tuple-element.72), channel_id=1, source_target_pairs={{0,2},{1,5},{2,0},{3,7},{4,6},{5,1},{6,4},{7,3},{8,10},{9,13},{10,... | collective-permute-start | bytes 1916936 | tf_op jit(solution)/shard_map/cond/branch_1_fun/ppermute | solution.py:602
  51.7 49.8 %collective-permute-start.22 = (bf16[8,80,768]{2,1,0:T(8,128)(2,1)}, bf16[8,80,768]{2,1,0:T(8,128)(2,1)}, u32[]{:S(2)}, u32[]{:S(2)}) collective-permute-start(bf16[8,80,768]{2,1,0:T(8,128)(2,1)} %copy-done.2), channel_id=1, source_target_pairs={{0,16},{1,17},{2,18},{3,19},{4,20},{5,21},{6,22},{7,23},{8,24},{9,... | collective-permute-start | bytes 2949128 | tf_op jit(solution)/shard_map/ppermute | solution.py:602
  53.3 14.6 %collective-permute-start.8 = (bf16[1024,768]{1,0:T(8,128)(2,1)S(1)}, bf16[1024,768]{1,0:T(8,128)(2,1)}, u32[]{:S(2)}, u32[]{:S(2)}) collective-permute-start(bf16[1024,768]{1,0:T(8,128)(2,1)S(1)} %get-tuple-element.79), channel_id=1, source_target_pairs={{0,1},{1,0},{2,3},{3,2},{4,5},{5,4},{6,7},{7,6},{8,9},{9,8},{10,11... | collective-permute-start | bytes 4718600 | tf_op jit(solution)/shard_map/cond/branch_1_fun/ppermute | solution.py:602
  53.8 4.7 %collective-permute-start.11 = (bf16[4,208,384]{2,1,0:T(8,128)(2,1)}, bf16[4,208,384]{2,1,0:T(8,128)(2,1)}, u32[]{:S(2)}, u32[]{:S(2)}) collective-permute-start(bf16[4,208,384]{2,1,0:T(8,128)(2,1)} %get-tuple-element.82), channel_id=1, source_target_pairs={{0,1},{1,0},{2,3},{3,2},{4,5},{5,4},{6,7},{7,6},{8,9},{9,8},{10,11... | collective-permute-start | bytes 1916936 | tf_op jit(solution)/shard_map/cond/branch_1_fun/ppermute | solution.py:602
  53.8 10.7 %collective-permute-start.9 = (bf16[4,208,384]{2,1,0:T(8,128)(2,1)}, bf16[4,208,384]{2,1,0:T(8,128)(2,1)}, u32[]{:S(2)}, u32[]{:S(2)}) collective-permute-start(bf16[4,208,384]{2,1,0:T(8,128)(2,1)} %get-tuple-element.82), channel_id=1, source_target_pairs={{0,4},{1,3},{2,6},{3,1},{4,0},{5,7},{6,2},{7,5},{8,12},{9,11},{10,... | collective-permute-start | bytes 1916936 | tf_op jit(solution)/shard_map/cond/branch_1_fun/ppermute | solution.py:602
  67.9 11.3 %collective-permute-start.21 = (bf16[4,224,384]{2,1,0:T(8,128)(2,1)}, bf16[4,224,384]{2,1,0:T(8,128)(2,1)}, u32[]{:S(2)}, u32[]{:S(2)}) collective-permute-start(bf16[4,224,384]{2,1,0:T(8,128)(2,1)} %get-tuple-element.287.refs_5_), channel_id=1, source_target_pairs={{0,2},{1,5},{2,0},{3,7},{4,6},{5,1},{6,4},{7,3},{8,10},{9,13},{10,... | collective-permute-start | bytes 2064392 | tf_op jit(solution)/shard_map/ppermute | solution.py:602
  79.1 15.3 %collective-permute-start.2 = (bf16[4,224,384]{2,1,0:T(8,128)(2,1)}, bf16[4,224,384]{2,1,0:T(8,128)(2,1)}, u32[]{:S(2)}, u32[]{:S(2)}) collective-permute-start(bf16[4,224,384]{2,1,0:T(8,128)(2,1)} %get-tuple-element.98), channel_id=1, source_target_pairs={{0,4},{1,3},{2,6},{3,1},{4,0},{5,7},{6,2},{7,5},{8,12},{9,11},{10,... | collective-permute-start | bytes 2064392 | tf_op jit(solution)/shard_map/cond/branch_1_fun/ppermute | solution.py:602
  80.6 17.1 %collective-permute-start.3 = (bf16[4,224,384]{2,1,0:T(8,128)(2,1)}, bf16[4,224,384]{2,1,0:T(8,128)(2,1)}, u32[]{:S(2)}, u32[]{:S(2)}) collective-permute-start(bf16[4,224,384]{2,1,0:T(8,128)(2,1)} %get-tuple-element.99), channel_id=1, source_target_pairs={{0,4},{1,3},{2,6},{3,1},{4,0},{5,7},{6,2},{7,5},{8,12},{9,11},{10,... | collective-permute-start | bytes 2064392 | tf_op jit(solution)/shard_map/cond/branch_1_fun/ppermute | solution.py:602
  136.5 30.3 %collective-permute-start.24 = (bf16[4,2,96,768]{3,2,1,0:T(8,128)(2,1)}, bf16[4,2,96,768]{3,2,1,0:T(8,128)(2,1)}, u32[]{:S(2)}, u32[]{:S(2)}) collective-permute-start(bf16[4,2,96,768]{3,2,1,0:T(8,128)(2,1)} %get-tuple-element.303), channel_id=1, source_target_pairs={{0,2},{1,5},{2,0},{3,7},{4,6},{5,1},{6,4},{7,3},{8,10},{9,13},{10,... | collective-permute-start | bytes 3538952 | tf_op jit(solution)/shard_map/ppermute | solution.py:602
  137.8 29.0 %collective-permute-start.25 = (bf16[2,4,2,48,768]{4,3,2,1,0:T(8,128)(2,1)}, bf16[2,4,2,48,768]{4,3,2,1,0:T(8,128)(2,1)}, u32[]{:S(2)}, u32[]{:S(2)}) collective-permute-start(bf16[2,4,2,48,768]{4,3,2,1,0:T(8,128)(2,1)} %get-tuple-element.305), channel_id=1, source_target_pairs={{0,2},{1,5},{2,0},{3,7},{4,6},{5,1},{6,4},{7,3},{8,10},{9,13},{10,... | collective-permute-start | bytes 3538952 | tf_op jit(solution)/shard_map/ppermute | solution.py:602
  166.6 5.3 %collective-permute-start.26 = (bf16[1024,768]{1,0:T(8,128)(2,1)}, bf16[1024,768]{1,0:T(8,128)(2,1)}, u32[]{:S(2)}, u32[]{:S(2)}) collective-permute-start(bf16[1024,768]{1,0:T(8,128)(2,1)} %mlp_out_other.1), channel_id=1, source_target_pairs={{0,1},{1,0},{2,3},{3,2},{4,5},{5,4},{6,7},{7,6},{8,9},{9,8},{10,11... | collective-permute-start | bytes 4718600 | tf_op jit(solution)/shard_map/ppermute | solution.py:602
  170.4 23.1 %collective-permute-start.27 = (bf16[4,192,768]{2,1,0:T(8,128)(2,1)}, bf16[4,192,768]{2,1,0:T(8,128)(2,1)}, u32[]{:S(2)}, u32[]{:S(2)}) collective-permute-start(bf16[4,192,768]{2,1,0:T(8,128)(2,1)} %get-tuple-element.321), channel_id=1, source_target_pairs={{0,4},{1,3},{2,6},{3,1},{4,0},{5,7},{6,2},{7,5},{8,12},{9,11},{10,... | collective-permute-start | bytes 3538952 | tf_op jit(solution)/shard_map/ppermute | solution.py:602
  181.3 7.2 %collective-permute-start.5 = (bf16[4,4,208,384]{3,2,1,0:T(8,128)(2,1)}, bf16[4,4,208,384]{3,2,1,0:T(8,128)(2,1)}, u32[]{:S(2)}, u32[]{:S(2)}) collective-permute-start(bf16[4,4,208,384]{3,2,1,0:T(8,128)(2,1)} %get-tuple-element.112), channel_id=1, source_target_pairs={{0,1},{1,0},{2,3},{3,2},{4,5},{5,4},{6,7},{7,6},{8,9},{9,8},{10,11... | collective-permute-start | bytes 7667720 | tf_op jit(solution)/shard_map/cond/branch_1_fun/ppermute | solution.py:602
  192.2 18.3 %collective-permute-start.32 = (bf16[4,2,208,384]{3,2,1,0:T(8,128)(2,1)}, bf16[4,2,208,384]{3,2,1,0:T(8,128)(2,1)}, u32[]{:S(2)}, u32[]{:S(2)}) collective-permute-start(bf16[4,2,208,384]{3,2,1,0:T(8,128)(2,1)} %get-tuple-element.335), channel_id=1, source_target_pairs={{0,2},{1,5},{2,0},{3,7},{4,6},{5,1},{6,4},{7,3},{8,10},{9,13},{10,... | collective-permute-start | bytes 3833864 | tf_op jit(solution)/shard_map/ppermute | solution.py:602
  196.3 25.6 %collective-permute-start.28 = (bf16[192,768]{1,0:T(8,128)(2,1)}, bf16[192,768]{1,0:T(8,128)(2,1)}, u32[]{:S(2)}, u32[]{:S(2)}) collective-permute-start(bf16[192,768]{1,0:T(8,128)(2,1)} %get-tuple-element.331), channel_id=1, source_target_pairs={{0,8},{1,9},{2,10},{3,11},{4,12},{5,13},{6,14},{7,15},{8,0},{9,1},... | collective-permute-start | bytes 884744 | tf_op jit(solution)/shard_map/ppermute | solution.py:602
  198.0 23.8 %collective-permute-start.29 = (bf16[192,768]{1,0:T(8,128)(2,1)}, bf16[192,768]{1,0:T(8,128)(2,1)}, u32[]{:S(2)}, u32[]{:S(2)}) collective-permute-start(bf16[192,768]{1,0:T(8,128)(2,1)} %get-tuple-element.332), channel_id=1, source_target_pairs={{0,16},{1,17},{2,18},{3,19},{4,20},{5,21},{6,22},{7,23},{8,24},{9,... | collective-permute-start | bytes 884744 | tf_op jit(solution)/shard_map/ppermute | solution.py:602
  199.6 22.3 %collective-permute-start.30 = (bf16[192,768]{1,0:T(8,128)(2,1)}, bf16[192,768]{1,0:T(8,128)(2,1)}, u32[]{:S(2)}, u32[]{:S(2)}) collective-permute-start(bf16[192,768]{1,0:T(8,128)(2,1)} %get-tuple-element.333), channel_id=1, source_target_pairs={{0,24},{1,25},{2,26},{3,27},{4,28},{5,29},{6,30},{7,31},{8,16},{9,... | collective-permute-start | bytes 884744 | tf_op jit(solution)/shard_map/ppermute | solution.py:602
  213.1 14.7 %collective-permute-start.35 = (bf16[4,208,384]{2,1,0:T(8,128)(2,1)}, bf16[4,208,384]{2,1,0:T(8,128)(2,1)}, u32[]{:S(2)}, u32[]{:S(2)}) collective-permute-start(bf16[4,208,384]{2,1,0:T(8,128)(2,1)} %get-tuple-element.345), channel_id=1, source_target_pairs={{0,4},{1,3},{2,6},{3,1},{4,0},{5,7},{6,2},{7,5},{8,12},{9,11},{10,... | collective-permute-start | bytes 1916936 | tf_op jit(solution)/shard_map/ppermute | solution.py:602
  220.7 7.0 %collective-permute-start.36 = (f32[8,768]{1,0:T(8,128)}, f32[8,768]{1,0:T(8,128)}, u32[]{:S(2)}, u32[]{:S(2)}) collective-permute-start(f32[8,768]{1,0:T(8,128)} %add.16), channel_id=1, source_target_pairs={{0,16},{1,17},{2,18},{3,19},{4,20},{5,21},{6,22},{7,23},{8,24},{9,... | collective-permute-start | bytes 73736 | tf_op jit(solution)/shard_map/ppermute | solution.py:602
  229.9 13.9 %collective-permute-start.37 = (bf16[208,384]{1,0:T(8,128)(2,1)}, bf16[208,384]{1,0:T(8,128)(2,1)}, u32[]{:S(2)}, u32[]{:S(2)}) collective-permute-start(bf16[208,384]{1,0:T(8,128)(2,1)} %get-tuple-element.355), channel_id=1, source_target_pairs={{0,8},{1,9},{2,10},{3,11},{4,12},{5,13},{6,14},{7,15},{8,0},{9,1},... | collective-permute-start | bytes 479240 | tf_op jit(solution)/shard_map/ppermute | solution.py:602
  232.4 13.2 %collective-permute-start.38 = (bf16[208,384]{1,0:T(8,128)(2,1)}, bf16[208,384]{1,0:T(8,128)(2,1)}, u32[]{:S(2)}, u32[]{:S(2)}) collective-permute-start(bf16[208,384]{1,0:T(8,128)(2,1)} %get-tuple-element.356), channel_id=1, source_target_pairs={{0,16},{1,17},{2,18},{3,19},{4,20},{5,21},{6,22},{7,23},{8,24},{9,... | collective-permute-start | bytes 479240 | tf_op jit(solution)/shard_map/ppermute | solution.py:602
  232.4 13.2 %collective-permute-start.39 = (bf16[208,384]{1,0:T(8,128)(2,1)}, bf16[208,384]{1,0:T(8,128)(2,1)}, u32[]{:S(2)}, u32[]{:S(2)}) collective-permute-start(bf16[208,384]{1,0:T(8,128)(2,1)} %get-tuple-element.357), channel_id=1, source_target_pairs={{0,24},{1,25},{2,26},{3,27},{4,28},{5,29},{6,30},{7,31},{8,16},{9,... | collective-permute-start | bytes 479240 | tf_op jit(solution)/shard_map/ppermute | solution.py:602
  240.5 7.0 %collective-permute-start.34 = (f32[2,24,768]{2,1,0:T(8,128)}, f32[2,24,768]{2,1,0:T(8,128)}, u32[]{:S(2)}, u32[]{:S(2)}) collective-permute-start(f32[2,24,768]{2,1,0:T(8,128)} %get-tuple-element.344), channel_id=1, source_target_pairs={{0,1},{1,0},{2,3},{3,2},{4,5},{5,4},{6,7},{7,6},{8,9},{9,8},{10,11... | collective-permute-start | bytes 442376 | tf_op jit(solution)/shard_map/ppermute | solution.py:602
  (18 other events, 87.9 us)

commit v8 on v7

--- a/solution.py
+++ b/solution.py
@@ -12,6 +12,7 @@
 PAIRS = 6
 LANES = 128
 CHIPS = 16
+PARTS = 2
 MERGE_STEPS = 2
 LONG = 10**11
 SHORT = 6 * 10**9
@@ -154,7 +155,7 @@
     dsum_ref[0:1, :] += column_sum(cot)
 
 
-def attention_forward(lengths_ref, x_ref, vec_ref, q_ref, k_ref, v_ref, wo_ref, mixed_ref, lse_ref, resid_ref, n2_ref):
+def attention_forward(lengths_ref, x_ref, vec_ref, q_ref, k_ref, v_ref, wo_ref, mixed_ref, lse_ref, resid_ref, *n2_refs):
     tile = pl.program_id(0)
     rows = q_ref.shape[0]
     slots = lengths_ref.shape[1]
@@ -194,7 +195,13 @@
     resid = x_ref[...].astype(F32) + (dot_nn(mixed_ref[...], wo_ref[...]) + vec_ref[4:5, :])
     resid_ref[...] = resid
     hat, _ = normalize(resid)
-    n2_ref[...] = (hat * vec_ref[5:6, :] + vec_ref[6:7, :]).astype(BF16)
+    normed = (hat * vec_ref[5:6, :] + vec_ref[6:7, :]).astype(BF16)
+    share = pl.num_programs(0) // len(n2_refs)
+    for number, ref in enumerate(n2_refs):
+
+        @pl.when(tile // share == number)
+        def _():
+            ref[...] = normed
 
 
 def spread(me, rows, put):
@@ -217,30 +224,31 @@
     for layer in range(4):
         for index, plane in enumerate(planes):
             owner = chip ^ (4 * layer + plane)
+            ref, at_layer = sources[min(index, 2)], layer + 4 * max(index - 2, 0)
             rows = pl.ds(pl.multiple_of(owner * each, 16), each)
-            side = sources[index].shape[2]
-            for part in range(sources[index].shape[1] // each):
+            side = ref.shape[2]
+            for part in range(ref.shape[1] // each):
                 number, cols = part * side // width, pl.ds(part * side % width, side)
                 pltpu.make_async_copy(
-                    sources[index].at[layer, pl.ds(part * each, each), :], wup_ref.at[number, rows, cols], sem.at[number]
+                    ref.at[at_layer, pl.ds(part * each, each), :], wup_ref.at[number, rows, cols], sem.at[number]
                 ).start()
-            source = sources[4 + layer // 2].at[2 * index + layer % 2]
+            source = sources[3 + layer // 2].at[2 * index + layer % 2]
             rows = pl.ds(pl.multiple_of(owner * deep, 16), source.shape[0])
             pltpu.make_async_copy(source, wdown_ref.at[rows, :], sem.at[blocks]).start()
             rest = deep - source.shape[0]
             rows = pl.ds(pl.multiple_of(owner * deep + source.shape[0], 16), rest)
             for part in range(width // side):
-                at = pl.ds(sources[index].shape[1] - (width // side - part) * rest, rest)
+                at = pl.ds(ref.shape[1] - (width // side - part) * rest, rest)
                 pltpu.make_async_copy(
-                    sources[index].at[layer, at, :], wdown_ref.at[rows, pl.ds(part * side, side)], sem.at[blocks]
+                    ref.at[at_layer, at, :], wdown_ref.at[rows, pl.ds(part * side, side)], sem.at[blocks]
                 ).start()
 
 
 def mlp(sets, count, me_ref, *refs):
-    n2_hbm, cot_hbm = refs[:sets], refs[sets : 2 * sets]
-    bup_ref = refs[2 * sets]
-    sources = refs[2 * sets + 1 : 2 * sets + 1 + count]
-    refs = refs[2 * sets + 1 + count :]
+    n2_hbm, refs = [refs[:PARTS], refs[PARTS : 2 * PARTS]][:sets], refs[PARTS * sets :]
+    cot_hbm, bup_ref = refs[:sets], refs[sets]
+    sources = refs[sets + 1 : sets + 1 + count]
+    refs = refs[sets + 1 + count :]
     act_hbm, gtwo_hbm, refs = refs[:sets], refs[sets : 2 * sets], refs[2 * sets :]
     down_own, down_send, up_own, up_send, wdown_hbm, dbu_ref = refs[:6]
     n2_ref, cot_ref, gacc, act_ref, gup_ref, low_ref, gdown_ref, gupw_ref = refs[6:14]
@@ -260,7 +268,10 @@
         fetch_hidden(me, sources, wup_all, wdown_all, weight_sem)
         for index in range(sets):
             at = pl.ds(index * rows, rows)
-            pltpu.make_async_copy(n2_hbm[index], n2_ref.at[at, :], in_sem.at[0, index]).start()
+            part = rows // len(n2_hbm[index])
+            for number, ref in enumerate(n2_hbm[index]):
+                piece = pl.ds(index * rows + number * part, part)
+                pltpu.make_async_copy(ref, n2_ref.at[piece, :], in_sem.at[0, index]).start()
             pltpu.make_async_copy(cot_hbm[index], cot_ref.at[at, :], in_sem.at[1, index]).start()
 
     pltpu.make_async_copy(wup_all.at[step], wup_all.at[step], weight_sem.at[step]).wait()
@@ -622,7 +633,8 @@
     return lambda core, chip: (core, chip ^ (4 * distance))
 
 
-def split_shards(core_ref, q_ref, k_ref, v_ref, o_ref, u_ref, keep_ref, send_ref):
+def split_shards(core_ref, q_ref, k_ref, v_ref, o_ref, u_ref, d_ref, keep_ref, send_ref, down_ref):
+    down_ref[...] = d_ref[: down_ref.shape[0], :]
     width = q_ref.shape[1]
     side = width // 2
     first = core_ref[0] == 0
@@ -710,13 +722,15 @@
     deep = weights[5].shape[0]
     folds = deep // own
     halves = (VMEM_SPEC, shaped(4 + folds, own, side))
-    keep, send = small_call(
-        split_shards, (me & 1, *weights[:5]), [halves, halves], "split_shards", ins=[SMEM] + [VMEM_SPEC] * 5)
+    keep, send, down = small_call(
+        split_shards, (me & 1, *weights), [halves, halves, (VMEM_SPEC, shaped(deep - 16, width))], "split_shards",
+        ins=[SMEM] + [VMEM_SPEC] * 6)
     take = swap(send, other_core)
-    return small_call(
+    near, up = small_call(
         join_shards, (me, keep, take, weights[5], *vectors),
         [(VMEM_SPEC, shaped(8 * own + 16, side)), (VMEM_SPEC, shaped(2 * deep + 32, side))], "join_shards",
         ins=[SMEM] + [VMEM_SPEC] * (3 + len(vectors)))
+    return near, up, down
 
 
 def doubled(pieces, change):
@@ -958,10 +972,17 @@
 
     high_rows = (tile_rows, shaped(rows, width, dtype=F32))
 
+    share = tiles // PARTS
+    normed_outs = [
+        (pl.BlockSpec((tile, width), lambda i, part=part: (jnp.clip(i - part * share, 0, share - 1), 0)),
+         shaped(share * tile, width))
+        for part in range(PARTS)
+    ]
+
     def attend(q, k, v, vec, wo):
         return call(
             attention_forward, (tiles,), [SMEM, tile_rows, vec_spec, tile_rows, tile_rows, tile_rows, square],
-            [low_rows, (lse_spec, shaped(rows, LANES, dtype=F32)), high_rows, low_rows],
+            [low_rows, (lse_spec, shaped(rows, LANES, dtype=F32)), high_rows] + normed_outs,
             [], "attention_forward", 0, lengths, tokens, vec, q, k, v, wo)
 
     def gather_first(near):
@@ -978,15 +999,15 @@
         return corner, taken, cot_other, jnp.concatenate((up_two, up_taken))
 
     def attend_by_hand(q, k, v, vec, wo, up_four, up_along):
-        up = [swap(up_four, second_plane), swap(up_along, second_plane)]
-        mixed, lse, resid, n2 = attend(q, k, v, vec, wo)
-        up = after(up, mixed)
-        n2_other = swap(after(n2, up), other_core)
+        up = swap(jnp.concatenate((up_four, up_along)), second_plane)
+        mixed, lse, resid, *n2 = attend(q, k, v, vec, wo)
+        n2_other = [swap(piece, other_core) for piece in n2]
         return mixed, lse, resid, n2, n2_other, up
 
     if by_hand:
-        down_two = doubled(down_weight[None, :-16], other_layer(1))
-        near, up = prepare(me, weights, vectors)
+        near, up, down = prepare(me, weights, vectors)
+        down = after(down, near)[None]
+        down_two = doubled(down, other_layer(1))
         near_moved = [swap(near, other_layer(r)) for r in (1, 2, 3)]
         up_moved = swap(up, other_layer(1))
         down_shard = fenced(gather_down, after(down_two, near))
@@ -997,7 +1018,7 @@
         up_moved = swap(up_two, other_layer(2))
         along, across, cot, sum_down = fenced(gather_first, near)
         up_taken = after(up_moved, along)
-        down = [down_shard, swap(after(down_shard, along), other_layer(2))]
+        down = [down_shard, swap(after(down_shard, up_taken), other_layer(2))]
         corner, taken, cot_other, up_four = fenced(gather_second, near, along, across, cot, up_two, up_taken)
         near = [near, along, across, corner] + taken
         up_along = swap(up_four, first_plane)
@@ -1006,10 +1027,10 @@
             [low_rows] * 4 + [(ANY_SPEC, shaped(width, width))] * 4 + [kept_vec, kept_hidden],
             [pltpu.VMEM((4, width, width), BF16), pltpu.VMEM((CHIPS, width // (4 * CHIPS) + 1, 16, width), BF16),
              pltpu.SemaphoreType.DMA((1,)), pltpu.SemaphoreType.DMA((4,))],
-            "project", LATER, tokens, *[piece.reshape(4, -1, 16, side) for piece in near])
+            "project", LATER, tokens, *[piece.reshape(4, -1, 16, side) for piece in after(near)])
         up_along = after(up_along, n1)
         mixed, lse, resid, n2, n2_other, up_moved = fenced(attend_by_hand, q, k, v, vec, wo, up_four, up_along)
-        up = [up_along] + up_moved
+        up = [up_along, up_moved]
         hidden_weights = [(up_four, *up, *down)]
     else:
         wq, wk, wv, wo, hidden_weights, vec, bup = gather_plain(weights, vectors)
@@ -1018,7 +1039,7 @@
         n1, q, k, v = call(
             project_rows, (tiles,), [tile_rows, vec_spec, square, square, square], [low_rows] * 4,
             [], "project", 0, tokens, vec, wq, wk, wv)
-        mixed, lse, resid, n2 = attend(q, k, v, vec, wo)
+        mixed, lse, resid, *n2 = attend(q, k, v, vec, wo)
 
     each = width // CHIPS
     deep = hidden // (2 * CHIPS)
@@ -1034,13 +1055,13 @@
     wide_spec = whole_spec((hidden // 2, width))
 
     def run_mlp(me, tokens_of, bup, sources):
-        sets = len(tokens_of[0])
+        sets = len(tokens_of[1])
         low, high = pltpu.VMEM((sets * rows, width), BF16), pltpu.VMEM((sets * rows, width), F32)
         weight = pltpu.VMEM((2, width, width), BF16)
         dma = pltpu.SemaphoreType.DMA((2, sets))
         return call_with(
             me, functools.partial(mlp, sets, len(sources)), blocks,
-            [ANY_SPEC] * (2 * sets) + [hidden_spec] + [ANY_SPEC] * len(sources),
+            [ANY_SPEC] * (PARTS * sets + sets) + [hidden_spec] + [ANY_SPEC] * len(sources),
             [act_out] * sets + [high_out] + [low_out] * (sets - 1) + [down_part] * 2 + [up_part] * 2
             + [(ANY_SPEC, shaped(hidden // 2, width)), (hidden_spec, shaped(1, hidden // 2, dtype=F32))],
             [low, low, high, pltpu.VMEM((blocks, sets * rows, width), BF16), low, low, weight, weight,
@@ -1051,13 +1072,13 @@
 
     if by_hand:
         act_own, act_other, gtwo, gtwo_other, down_own, down_send, up_own, up_send, wdown, sum_up = run_mlp(
-            me, ((n2, n2_other), (cot, cot_other)), bup, hidden_weights[0])
+            me, ((*n2, *n2_other), (cot, cot_other)), bup, hidden_weights[0])
         gtwo_take = swap(gtwo_other, other_core)
         parts = (-1, CHIPS // 4, 2)
         down_first = [piece.reshape(*parts, deep, width) for piece in (down_own, swap(down_send, first_plane))]
         up_first = [piece.reshape(*parts, each, width) for piece in (up_own, swap(up_send, first_plane))]
     else:
-        runs = [run_mlp(me + half, ((n2,), (cot,)), bup[half], hidden_weights[half]) for half in range(2)]
+        runs = [run_mlp(me + half, (n2, (cot,)), bup[half], hidden_weights[half]) for half in range(2)]
         (act_own, gtwo), (act_other, gtwo_take) = ((run[0], run[1]) for run in runs)
         gtwo_take = gtwo_take.astype(BF16)
         sum_up = jnp.concatenate([run[7] for run in runs], axis=1)
@@ -1117,7 +1138,8 @@
         late_take = after(swap(late, other_layer(2)), g_down)
         square_second = after(square_second, g_down)
         rest, *sends = merge_layers_of(*square_second)
-        rest, sends, late_take = after((rest, sends, late_take))
+        late_take = after(late_take, rest)
+        sends = after(sends, late_take)
         square_layers = [rest] + [swap(piece, other_layer(r + 1)) for r, piece in enumerate(sends)]
         late = late + late_take
         late = late + after(swap(late, other_plane(1)), rest)

time: 252 us -> 250 us (level)
  local copies, waits for them, and re-layouts: 4.72 us -> 0.02 us
    concatenate x0 -> x1, other arithmetic: none -> 2.62 us  [attend_by_hand(): up = swap(jnp.concatenate((up_four, up_along)), second_plane)]
  transfers between devices with their start and end apart: 43 -> 43, of which waited for: 18 -> 19; matrix products, arithmetic and copies ran while one was open for 4% -> 3% of each run, Pallas kernels for 39% -> 39%
where the time goes in v8:
time: 250 us; the launch traced here: 249 us
  Pallas kernels  141 us (56%)
  waiting for transfers between devices  54.8 us (22%)
  starting transfers between devices  41.4 us (17%)
  other arithmetic  10.2 us (4%)
    pallas_call x5, Pallas kernels, call_with(): pl.pallas_call(kernel, grid_spec=pltpu.PrefetchScalarGridSpec(num_scalar_...  67.6 us
    pallas_call x7, Pallas kernels, call(): pl.pallas_call(kernel, grid=grid, in_specs=ins, out_specs=out_specs, out_...  58.2 us
    ppermute x43, waiting for transfers between devices, swap(): return lax.ppermute(array, 'dp', flipped(lax.axis_size('dp'), change))  54.8 us
    ppermute x43, starting transfers between devices, swap(): return lax.ppermute(array, 'dp', flipped(lax.axis_size('dp'), change))  41.4 us
    pallas_call x7, Pallas kernels, small_call(): pl.pallas_call(kernel, in_specs=ins, out_specs=tuple((spec for spec, _ in...  15.2 us
  transfers between devices with their start and end apart: 43, of which 19 were waited for; matrix products, arithmetic and copies ran while one was open for 3% of the time, Pallas kernels for 39%

profile of v8, /device:TPU:0, one launch (start us, length us, event | category | flops | bytes accessed | tf_op | source)
XLA Modules:
  0.0 248.6 jit_solution(14638857994602826137)
XLA Ops:
  6.4 2.9 %collective-permute-start.19 = (bf16[1,80,768]{2,1,0:T(8,128)(2,1)}, bf16[1,80,768]{2,1,0:T(8,128)(2,1)S(1)}, u32[]{:S(2)}, u32[]{:S(2)}) collective-permute-start(bf16[1,80,768]{2,1,0:T(8,128)(2,1)} %bitcast.27), channel_id=1, source_target_pairs={{0,8},{1,9},{2,10},{3,11},{4,12},{5,13},{6,14},{7,15},{8,0},{9,1},... | collective-permute-start | bytes 368648 | tf_op jit(solution)/shard_map/ppermute | solution.py:613
  9.4 4.0 %collective-permute-start.17 = (bf16[208,384]{1,0:T(8,128)(2,1)}, bf16[208,384]{1,0:T(8,128)(2,1)S(1)}, u32[]{:S(2)}, u32[]{:S(2)}) collective-permute-start(bf16[208,384]{1,0:T(8,128)(2,1)} %get-tuple-element.263), channel_id=1, source_target_pairs={{0,24},{1,25},{2,26},{3,27},{4,28},{5,29},{6,30},{7,31},{8,16},{9,... | collective-permute-start | bytes 479240 | tf_op jit(solution)/shard_map/ppermute | solution.py:613
  14.9 15.3 %conditional.5 = (bf16[8,80,768]{2,1,0:T(8,128)(2,1)S(1)}) conditional(s32[]{:T(128)} %convert_element_type.2, () %tuple.74, bf16[2,80,768]{2,1,0:T(8,128)(2,1)S(1)} %pad_maximum_fusion.6), branch_computations={%region_0.0_spmd, %region_1.0_spmd} | conditional | flops 1228800 | bytes 5898328 | solution.py:858
  16.7 4.5 %collective-permute-done.3 = bf16[2,80,768]{2,1,0:T(8,128)(2,1)S(1)} collective-permute-done((bf16[2,80,768]{2,1,0:T(8,128)(2,1)S(1)}, bf16[2,80,768]{2,1,0:T(8,128)(2,1)S(1)}, u32[]{:S(2)}, u32[]{:S(2)}) %collective-permute-start.3) | collective-permute-done | bytes 245792 | tf_op jit(solution)/shard_map/cond/branch_1_fun/ppermute | solution.py:613
  23.0 7.1 %collective-permute-done.4 = bf16[4,80,768]{2,1,0:T(8,128)(2,1)S(1)} collective-permute-done((bf16[4,80,768]{2,1,0:T(8,128)(2,1)S(1)}, bf16[4,80,768]{2,1,0:T(8,128)(2,1)S(1)}, u32[]{:S(2)}, u32[]{:S(2)}) %collective-permute-start.4) | collective-permute-done | bytes 491552 | tf_op jit(solution)/shard_map/cond/branch_1_fun/ppermute | solution.py:613
  32.1 2.8 %collective-permute-start.20 = (bf16[2,224,384]{2,1,0:T(8,128)(2,1)}, bf16[2,224,384]{2,1,0:T(8,128)(2,1)}, u32[]{:S(2)}, u32[]{:S(2)}) collective-permute-start(bf16[2,224,384]{2,1,0:T(8,128)(2,1)} %pad_maximum_fusion.5), channel_id=1, source_target_pairs={{0,16},{1,17},{2,18},{3,19},{4,20},{5,21},{6,22},{7,23},{8,24},{9,... | collective-permute-start | bytes 1032200 | tf_op jit(solution)/shard_map/ppermute | solution.py:613
  34.9 14.5 %conditional.6 = (bf16[4,208,384]{2,1,0:T(8,128)(2,1)}, bf16[4,208,384]{2,1,0:T(8,128)(2,1)}, bf16[1024,768]{1,0:T(8,128)(2,1)}, f32[8,768]{1,0:T(8,128)}) conditional(s32[]{:T(128)} %convert_element_type.2, () %tuple.79, (bf16[4,208,384]{2,1,0:T(8,128)(2,1)}, bf16[1024,768]{1,0:T(8,128)(2,1)}, s32[4,5]{1,0:T(4,128)}) %tuple.80), branch_computations={%region_2.0_spmd, %region_3.0_spmd} | conditional | bytes 5111921 | solution.py:858
  37.9 3.8 %mask_grads.1 = (bf16[1024,768]{1,0:T(8,128)(2,1)}, f32[8,768]{1,0:T(8,128)}) custom-call(s32[4,5]{1,0:T(4,128)} %get-tuple-element.67.lengths_ref, bf16[1024,768]{1,0:T(8,128)(2,1)} %get-tuple-element.69.grad_ref), custom_call_target="tpu_custom_call" | custom-call | bytes 1 | tf_op jit(solution)/shard_map/cond/branch_1_fun/mask_grads/pallas_call | solution.py:572
  41.7 7.7 %collective-permute-done = bf16[4,208,384]{2,1,0:T(8,128)(2,1)} collective-permute-done((bf16[4,208,384]{2,1,0:T(8,128)(2,1)}, bf16[4,208,384]{2,1,0:T(8,128)(2,1)}, u32[]{:S(2)}, u32[]{:S(2)}) %collective-permute-start) | collective-permute-done | bytes 639008 | tf_op jit(solution)/shard_map/cond/branch_1_fun/ppermute | solution.py:613
  49.9 14.6 %conditional.7 = (bf16[4,208,384]{2,1,0:T(8,128)(2,1)}, bf16[4,208,384]{2,1,0:T(8,128)(2,1)}, bf16[4,208,384]{2,1,0:T(8,128)(2,1)}, bf16[4,208,384]{2,1,0:T(8,12...) conditional(s32[]{:T(128)} %convert_element_type.2, () %tuple.81, ...), branch_computations={%region_4.0_spmd, %region_5.0_spmd} | conditional | flops 344064 | bytes 20447528 | solution.py:858
  50.9 3.6 %collective-permute-done.6 = bf16[4,208,384]{2,1,0:T(8,128)(2,1)} collective-permute-done((bf16[4,208,384]{2,1,0:T(8,128)(2,1)}, bf16[4,208,384]{2,1,0:T(8,128)(2,1)}, u32[]{:S(2)}, u32[]{:S(2)}) %collective-permute-start.6) | collective-permute-done | bytes 639008 | tf_op jit(solution)/shard_map/cond/branch_1_fun/ppermute | solution.py:613
  55.5 5.7 %collective-permute-done.5 = bf16[4,208,384]{2,1,0:T(8,128)(2,1)} collective-permute-done((bf16[4,208,384]{2,1,0:T(8,128)(2,1)}, bf16[4,208,384]{2,1,0:T(8,128)(2,1)}, u32[]{:S(2)}, u32[]{:S(2)}) %collective-permute-start.5) | collective-permute-done | bytes 639008 | tf_op jit(solution)/shard_map/cond/branch_1_fun/ppermute | solution.py:613
  66.0 10.4 %project.1 = (bf16[1024,768]{1,0:T(8,128)(2,1)}, bf16[1024,768]{1,0:T(8,128)(2,1)}, bf16[1024,768]{1,0:T(8,128)(2,1)}, bf16[1024,768]{1,0:T(8,128)(2,1)}, bf16[7...) custom-call(s32[1]{0:T(128)} %bitcast.1.me_ref, ...), custom_call_target="tpu_custom_call" | custom-call | flops 8999999488 | bytes 1 | tf_op jit(solution)/shard_map/project/pallas_call | solution.py:587
  76.4 21.3 %conditional.8 = (bf16[1024,768]{1,0:T(8,128)(2,1)}, f32[1024,128]{1,0:T(8,128)}, f32[1024,768]{1,0:T(8,128)}, bf16[512,768]{1,0:T(8,128)(2,1)}, bf16[512,768]{1...) conditional(s32[]{:T(128)} %convert_element_type.2, () %tuple.85, ...), branch_computations={%region_6.0_spmd, %region_7.0_spmd} | conditional | flops 688128 | bytes 14549177 | solution.py:858
  76.4 2.6 %pad_maximum_fusion.3 = bf16[8,224,384]{2,1,0:T(8,128)(2,1)} fusion(bf16[4,224,384]{2,1,0:T(8,128)(2,1)} %get-tuple-element.94, bf16[4,224,384]{2,1,0:T(8,128)(2,1)} %get-tuple-element.93), kind=kLoop, calls=%fused_computation.3 | loop fusion | flops 688128 | bytes 2752512 | tf_op jit(solution)/shard_map/cond/branch_1_fun/concatenate | solution.py:1002
  79.5 14.0 %attention_forward.1 = (bf16[1024,768]{1,0:T(8,128)(2,1)}, f32[1024,128]{1,0:T(8,128)}, f32[1024,768]{1,0:T(8,128)}, bf16[512,768]{1,0:T(8,128)(2,1)}, bf16[512,768]{1,0:T(8,128)(2,1)}) custom-call(s32[4,5]{1,0:T(4,128)} %get-tuple-element.81.lengths_ref, bf16[1024,768]{1,0:T(8,128)(2,1)} %get-tuple-element.82.x_ref, f32[16,768]{1,0:T(8,128)} %get-tuple-element.83.vec_ref, ...), custom_call_target="tpu_custom_call" | custom-call | bytes 1 | tf_op jit(solution)/shard_map/cond/branch_1_fun/attention_forward/pallas_call | solution.py:572
  97.7 34.9 %mlp.1 = (bf16[1024,1536]{1,0:T(8,128)(2,1)}, bf16[1024,1536]{1,0:T(8,128)(2,1)}, f32[1024,768]{1,0:T(8,128)}, bf16[1024,768]{1,0:T(8,128)(2,1)}, bf16[4,2,96,76...) custom-call(s32[1]{0:T(128)} %bitcast.1.me_ref, ...), custom_call_target="tpu_custom_call" | custom-call | bytes 1 | tf_op jit(solution)/shard_map/mlp/pallas_call | solution.py:587
  136.4 20.7 %attention_backward.1 = (bf16[4,1024,768]{2,1,0:T(8,128)(2,1)}, f32[1024,768]{1,0:T(8,128)}, f32[8,768]{1,0:T(8,128)}) custom-call(s32[4,5]{1,0:T(4,128)} %lengths_ref.1, bf16[1024,768]{1,0:T(8,128)(2,1)} %get-tuple-element.293.q_ref, bf16[1024,768]{1,0:T(8,128)(2,1)} %get-tuple-element.294.k_ref, bf16[1024,768]{1,0:T(8,128)(2,1)} %get-tuple-element.295.v_ref, ...), custom_call_target="tpu_custom_call" | custom-call | bytes 1 | tf_op jit(solution)/shard_map/attention_backward/pallas_call | solution.py:572
  157.0 5.8 %mlp_out_other.1 = bf16[1024,768]{1,0:T(8,128)(2,1)} custom-call(s32[1]{0:T(128)} %bitcast.1.me_ref, bf16[1024,1536]{1,0:T(8,128)(2,1)} %get-tuple-element.318.act_ref, bf16[1536,768]{1,0:T(8,128)(2,1)} %get-tuple-element.319.wdown_ref), custom_call_target="tpu_custom_call" | custom-call | bytes 1 | tf_op jit(solution)/shard_map/mlp_out_other/pallas_call | solution.py:587
  163.0 3.6 %merge_first.2 = (bf16[4,192,768]{2,1,0:T(8,128)(2,1)}, bf16[4,192,768]{2,1,0:T(8,128)(2,1)}) custom-call(bf16[1,4,2,96,768]{4,3,2,1,0:T(8,128)(2,1)} %bitcast.20, bf16[1,4,2,96,768]{4,3,2,1,0:T(8,128)(2,1)} %bitcast.18.refs_1_, bf16[2,4,2,48,768]{4,3,2,1,0:T(8,128)(2,1)} %get-tuple-element.322.refs_2_, ...), custom_call_target="tpu_custom_call" | custom-call | bytes 1 | tf_op jit(solution)/shard_map/merge_first/pallas_call | solution.py:572
  168.0 20.3 %conditional.9 = (bf16[1,4,2,208,384]{4,3,2,1,0:T(8,128)(2,1)}, bf16[4,2,208,384]{3,2,1,0:T(8,128)(2,1)}, bf16[1024,768]{1,0:T(8,128)(2,1)}) conditional(s32[]{:T(128)} %convert_element_type.2, () %tuple.73, (s32[1]{0:T(128)}, bf16[1024,768]{1,0:T(8,128)(2,1)}, bf16[1024,768]{1,0:T(8,128)(2,1)}, bf16[4,1024,768]{2,1,0:T(8,128)(2,1)}, ...), branch_computations={%region_8.0_spmd, %region_9.0_spmd} | conditional | bytes 10223683 | solution.py:858
  168.0 9.5 %weight_grads.1 = (bf16[4,4,208,384]{3,2,1,0:T(8,128)(2,1)}, bf16[4,4,208,384]{3,2,1,0:T(8,128)(2,1)}) custom-call(s32[1]{0:T(128)} %get-tuple-element.96.me_ref, bf16[1024,768]{1,0:T(8,128)(2,1)} %get-tuple-element.97.n1_ref, bf16[1024,768]{1,0:T(8,128)(2,1)} %get-tuple-element.98.mixed_hbm, bf16[4,1024,768]{2,1,0:T(8,128)(2,1)} %get-tuple-element.99.columns_ref, ...), custom_call_target="tpu_custom_call" | custom-call | bytes 1 | tf_op jit(solution)/shard_map/cond/branch_1_fun/weight_grads/pallas_call | solution.py:587
  177.6 7.1 %mlp_out_own.1 = bf16[1024,768]{1,0:T(8,128)(2,1)} custom-call(s32[1]{0:T(128)} %get-tuple-element.96.me_ref, f32[1024,768]{1,0:T(8,128)} %get-tuple-element.105.resid_ref, f32[16,768]{1,0:T(8,128)} %get-tuple-element.106.vec_ref, bf16[1024,1536]{1,0:T(8,128)(2,1)} %get-tuple-element.107.act_ref, bf16[1024,768]{1,0:T(8,128)(2,1)} %get-tuple-element.109.take_ref, ...), custom_call_target="tpu_custom_call" | custom-call | bytes 1 | tf_op jit(solution)/shard_map/cond/branch_1_fun/mlp_out_own/pallas_call | solution.py:587
  184.7 3.7 %merge_core.1 = (bf16[4,2,208,384]{3,2,1,0:T(8,128)(2,1)}, bf16[4,2,208,384]{3,2,1,0:T(8,128)(2,1)}) custom-call(s32[1]{0:T(128)} %get-tuple-element.95.core_ref, bf16[4,4,208,384]{3,2,1,0:T(8,128)(2,1)} %get-tuple-element.103.keep_ref, bf16[4,4,208,384]{3,2,1,0:T(8,128)(2,1)} %collective-permute-done.2.take_ref), custom_call_target="tpu_custom_call" | custom-call | bytes 1 | tf_op jit(solution)/shard_map/cond/branch_1_fun/merge_core/pallas_call | solution.py:572
  189.1 2.8 %merge_second.2 = (f32[192,768]{1,0:T(8,128)}, bf16[192,768]{1,0:T(8,128)(2,1)}, bf16[192,768]{1,0:T(8,128)(2,1)}, bf16[192,768]{1,0:T(8,128)(2,1)}) custom-call(bf16[4,192,768]{2,1,0:T(8,128)(2,1)} %get-tuple-element.334.own_ref, bf16[4,192,768]{2,1,0:T(8,128)(2,1)} %collective-permute-done.27.take_ref), custom_call_target="tpu_custom_call" | custom-call | bytes 1 | tf_op jit(solution)/shard_map/merge_second/pallas_call | solution.py:703
  192.0 2.6 %collective-permute-start.28 = (bf16[192,768]{1,0:T(8,128)(2,1)}, bf16[192,768]{1,0:T(8,128)(2,1)}, u32[]{:S(2)}, u32[]{:S(2)}) collective-permute-start(bf16[192,768]{1,0:T(8,128)(2,1)} %get-tuple-element.342), channel_id=1, source_target_pairs={{0,8},{1,9},{2,10},{3,11},{4,12},{5,13},{6,14},{7,15},{8,0},{9,1},... | collective-permute-start | bytes 884744 | tf_op jit(solution)/shard_map/ppermute | solution.py:613
  197.0 9.9 %tokens_backward.1 = (bf16[1024,768]{1,0:T(8,128)(2,1)}, f32[8,768]{1,0:T(8,128)}) custom-call(bf16[1024,768]{1,0:T(8,128)(2,1)} %x_ref.3, f32[1024,768]{1,0:T(8,128)} %get-tuple-element.337.gresid_ref, f32[16,768]{1,0:T(8,128)} %get-tuple-element.292.vec_ref, bf16[4,1024,768]{2,1,0:T(8,128)(2,1)} %get-tuple-element.325.grads_ref, ...), custom_call_target="tpu_custom_call" | custom-call | flops 11500000256 | bytes 1 | tf_op jit(solution)/shard_map/tokens_backward/pallas_call | solution.py:572
  206.8 2.6 %merge_first.3 = (bf16[4,208,384]{2,1,0:T(8,128)(2,1)}, bf16[4,208,384]{2,1,0:T(8,128)(2,1)}) custom-call(bf16[1,4,2,208,384]{4,3,2,1,0:T(8,128)(2,1)} %get-tuple-element.333.refs_0_, bf16[1,4,2,208,384]{4,3,2,1,0:T(8,128)(2,1)} %bitcast.19.refs_1_), custom_call_target="tpu_custom_call" | custom-call | bytes 1 | tf_op jit(solution)/shard_map/merge_first/pallas_call | solution.py:572
  214.0 3.1 %collective-permute-done.33 = f32[8,768]{1,0:T(8,128)S(1)} collective-permute-done((f32[8,768]{1,0:T(8,128)S(1)}, f32[8,768]{1,0:T(8,128)S(1)}, u32[]{:S(2)}, u32[]{:S(2)}) %collective-permute-start.33) | collective-permute-done | bytes 24608 | tf_op jit(solution)/shard_map/ppermute | solution.py:613
  221.0 3.6 %collective-permute-done.36 = f32[8,768]{1,0:T(8,128)} collective-permute-done((f32[8,768]{1,0:T(8,128)}, f32[8,768]{1,0:T(8,128)}, u32[]{:S(2)}, u32[]{:S(2)}) %collective-permute-start.36) | collective-permute-done | bytes 24608 | tf_op jit(solution)/shard_map/ppermute | solution.py:613
  233.3 3.0 %collective-permute-done.40 = f32[8,768]{1,0:T(8,128)S(1)} collective-permute-done((f32[8,768]{1,0:T(8,128)S(1)}, f32[8,768]{1,0:T(8,128)S(1)}, u32[]{:S(2)}, u32[]{:S(2)}) %collective-permute-start.40) | collective-permute-done | bytes 24608 | tf_op jit(solution)/shard_map/ppermute | solution.py:613
  236.9 3.2 %collective-permute-done.41 = f32[8,768]{1,0:T(8,128)S(1)} collective-permute-done((f32[8,768]{1,0:T(8,128)S(1)}, f32[8,768]{1,0:T(8,128)S(1)}, u32[]{:S(2)}, u32[]{:S(2)}) %collective-permute-start.41) | collective-permute-done | bytes 24608 | tf_op jit(solution)/shard_map/ppermute | solution.py:613
  (96 shorter events, 62.5 us)
Async XLA Ops:
  6.4 7.6 %collective-permute-start.19 = (bf16[1,80,768]{2,1,0:T(8,128)(2,1)}, bf16[1,80,768]{2,1,0:T(8,128)(2,1)S(1)}, u32[]{:S(2)}, u32[]{:S(2)}) collective-permute-start(bf16[1,80,768]{2,1,0:T(8,128)(2,1)} %bitcast.27), channel_id=1, source_target_pairs={{0,8},{1,9},{2,10},{3,11},{4,12},{5,13},{6,14},{7,15},{8,0},{9,1},... | collective-permute-start | bytes 368648 | tf_op jit(solution)/shard_map/ppermute | solution.py:613
  9.3 20.9 %collective-permute-start.18 = (bf16[224,384]{1,0:T(8,128)(2,1)}, bf16[224,384]{1,0:T(8,128)(2,1)S(1)}, u32[]{:S(2)}, u32[]{:S(2)}) collective-permute-start(bf16[224,384]{1,0:T(8,128)(2,1)} %get-tuple-element.264), channel_id=1, source_target_pairs={{0,8},{1,9},{2,10},{3,11},{4,12},{5,13},{6,14},{7,15},{8,0},{9,1},... | collective-permute-start | bytes 516104 | tf_op jit(solution)/shard_map/ppermute | solution.py:613
  9.4 20.8 %collective-permute-start.17 = (bf16[208,384]{1,0:T(8,128)(2,1)}, bf16[208,384]{1,0:T(8,128)(2,1)S(1)}, u32[]{:S(2)}, u32[]{:S(2)}) collective-permute-start(bf16[208,384]{1,0:T(8,128)(2,1)} %get-tuple-element.263), channel_id=1, source_target_pairs={{0,24},{1,25},{2,26},{3,27},{4,28},{5,29},{6,30},{7,31},{8,16},{9,... | collective-permute-start | bytes 479240 | tf_op jit(solution)/shard_map/ppermute | solution.py:613
  13.4 16.9 %collective-permute-start.16 = (bf16[208,384]{1,0:T(8,128)(2,1)}, bf16[208,384]{1,0:T(8,128)(2,1)S(1)}, u32[]{:S(2)}, u32[]{:S(2)}) collective-permute-start(bf16[208,384]{1,0:T(8,128)(2,1)} %get-tuple-element.263), channel_id=1, source_target_pairs={{0,16},{1,17},{2,18},{3,19},{4,20},{5,21},{6,22},{7,23},{8,24},{9,... | collective-permute-start | bytes 479240 | tf_op jit(solution)/shard_map/ppermute | solution.py:613
  13.4 16.9 %collective-permute-start.15 = (bf16[208,384]{1,0:T(8,128)(2,1)}, bf16[208,384]{1,0:T(8,128)(2,1)S(1)}, u32[]{:S(2)}, u32[]{:S(2)}) collective-permute-start(bf16[208,384]{1,0:T(8,128)(2,1)} %get-tuple-element.263), channel_id=1, source_target_pairs={{0,8},{1,9},{2,10},{3,11},{4,12},{5,13},{6,14},{7,15},{8,0},{9,1},... | collective-permute-start | bytes 479240 | tf_op jit(solution)/shard_map/ppermute | solution.py:613
  14.9 6.3 %collective-permute-start.3 = (bf16[2,80,768]{2,1,0:T(8,128)(2,1)S(1)}, bf16[2,80,768]{2,1,0:T(8,128)(2,1)S(1)}, u32[]{:S(2)}, u32[]{:S(2)}) collective-permute-start(bf16[2,80,768]{2,1,0:T(8,128)(2,1)S(1)} %param.1), channel_id=1, source_target_pairs={{0,2},{1,5},{2,0},{3,7},{4,6},{5,1},{6,4},{7,3},{8,10},{9,13},{10,... | collective-permute-start | bytes 737288 | tf_op jit(solution)/shard_map/cond/branch_1_fun/ppermute | solution.py:613
  21.2 8.9 %collective-permute-start.4 = (bf16[4,80,768]{2,1,0:T(8,128)(2,1)S(1)}, bf16[4,80,768]{2,1,0:T(8,128)(2,1)S(1)}, u32[]{:S(2)}, u32[]{:S(2)}) collective-permute-start(bf16[4,80,768]{2,1,0:T(8,128)(2,1)S(1)} %pad_maximum_fusion.1), channel_id=1, source_target_pairs={{0,4},{1,3},{2,6},{3,1},{4,0},{5,7},{6,2},{7,5},{8,12},{9,11},{10,... | collective-permute-start | bytes 1474568 | tf_op jit(solution)/shard_map/cond/branch_1_fun/ppermute | solution.py:613
  32.1 17.3 %collective-permute-start.20 = (bf16[2,224,384]{2,1,0:T(8,128)(2,1)}, bf16[2,224,384]{2,1,0:T(8,128)(2,1)}, u32[]{:S(2)}, u32[]{:S(2)}) collective-permute-start(bf16[2,224,384]{2,1,0:T(8,128)(2,1)} %pad_maximum_fusion.5), channel_id=1, source_target_pairs={{0,16},{1,17},{2,18},{3,19},{4,20},{5,21},{6,22},{7,23},{8,24},{9,... | collective-permute-start | bytes 1032200 | tf_op jit(solution)/shard_map/ppermute | solution.py:613
  34.9 14.5 %collective-permute-start = (bf16[4,208,384]{2,1,0:T(8,128)(2,1)}, bf16[4,208,384]{2,1,0:T(8,128)(2,1)}, u32[]{:S(2)}, u32[]{:S(2)}) collective-permute-start(bf16[4,208,384]{2,1,0:T(8,128)(2,1)} %get-tuple-element.66), channel_id=1, source_target_pairs={{0,2},{1,5},{2,0},{3,7},{4,6},{5,1},{6,4},{7,3},{8,10},{9,13},{10,... | collective-permute-start | bytes 1916936 | tf_op jit(solution)/shard_map/cond/branch_1_fun/ppermute | solution.py:613
  36.4 13.0 %collective-permute-start.1 = (bf16[4,208,384]{2,1,0:T(8,128)(2,1)}, bf16[4,208,384]{2,1,0:T(8,128)(2,1)}, u32[]{:S(2)}, u32[]{:S(2)}) collective-permute-start(bf16[4,208,384]{2,1,0:T(8,128)(2,1)} %get-tuple-element.66), channel_id=1, source_target_pairs={{0,4},{1,3},{2,6},{3,1},{4,0},{5,7},{6,2},{7,5},{8,12},{9,11},{10,... | collective-permute-start | bytes 1916936 | tf_op jit(solution)/shard_map/cond/branch_1_fun/ppermute | solution.py:613
  49.4 48.3 %collective-permute-start.22 = (bf16[8,80,768]{2,1,0:T(8,128)(2,1)}, bf16[8,80,768]{2,1,0:T(8,128)(2,1)}, u32[]{:S(2)}, u32[]{:S(2)}) collective-permute-start(bf16[8,80,768]{2,1,0:T(8,128)(2,1)} %copy-done), channel_id=1, source_target_pairs={{0,16},{1,17},{2,18},{3,19},{4,20},{5,21},{6,22},{7,23},{8,24},{9,... | collective-permute-start | bytes 2949128 | tf_op jit(solution)/shard_map/ppermute | solution.py:613
  49.9 14.6 %collective-permute-start.10 = (bf16[1024,768]{1,0:T(8,128)(2,1)}, bf16[1024,768]{1,0:T(8,128)(2,1)}, u32[]{:S(2)}, u32[]{:S(2)}) collective-permute-start(bf16[1024,768]{1,0:T(8,128)(2,1)} %get-tuple-element.78), channel_id=1, source_target_pairs={{0,1},{1,0},{2,3},{3,2},{4,5},{5,4},{6,7},{7,6},{8,9},{9,8},{10,11... | collective-permute-start | bytes 4718600 | tf_op jit(solution)/shard_map/cond/branch_1_fun/ppermute | solution.py:613
  50.4 5.1 %collective-permute-start.7 = (bf16[4,208,384]{2,1,0:T(8,128)(2,1)}, bf16[4,208,384]{2,1,0:T(8,128)(2,1)}, u32[]{:S(2)}, u32[]{:S(2)}) collective-permute-start(bf16[4,208,384]{2,1,0:T(8,128)(2,1)} %get-tuple-element.73), channel_id=1, source_target_pairs={{0,1},{1,0},{2,3},{3,2},{4,5},{5,4},{6,7},{7,6},{8,9},{9,8},{10,11... | collective-permute-start | bytes 1916936 | tf_op jit(solution)/shard_map/cond/branch_1_fun/ppermute | solution.py:613
  50.4 10.7 %collective-permute-start.5 = (bf16[4,208,384]{2,1,0:T(8,128)(2,1)}, bf16[4,208,384]{2,1,0:T(8,128)(2,1)}, u32[]{:S(2)}, u32[]{:S(2)}) collective-permute-start(bf16[4,208,384]{2,1,0:T(8,128)(2,1)} %get-tuple-element.73), channel_id=1, source_target_pairs={{0,4},{1,3},{2,6},{3,1},{4,0},{5,7},{6,2},{7,5},{8,12},{9,11},{10,... | collective-permute-start | bytes 1916936 | tf_op jit(solution)/shard_map/cond/branch_1_fun/ppermute | solution.py:613
  64.5 11.9 %collective-permute-start.21 = (bf16[4,224,384]{2,1,0:T(8,128)(2,1)}, bf16[4,224,384]{2,1,0:T(8,128)(2,1)}, u32[]{:S(2)}, u32[]{:S(2)}) collective-permute-start(bf16[4,224,384]{2,1,0:T(8,128)(2,1)} %get-tuple-element.297.refs_7_), channel_id=1, source_target_pairs={{0,2},{1,5},{2,0},{3,7},{4,6},{5,1},{6,4},{7,3},{8,10},{9,13},{10,... | collective-permute-start | bytes 2064392 | tf_op jit(solution)/shard_map/ppermute | solution.py:613
  79.0 18.6 %collective-permute-start.13 = (bf16[8,224,384]{2,1,0:T(8,128)(2,1)}, bf16[8,224,384]{2,1,0:T(8,128)(2,1)}, u32[]{:S(2)}, u32[]{:S(2)}) collective-permute-start(bf16[8,224,384]{2,1,0:T(8,128)(2,1)} %pad_maximum_fusion.3), channel_id=1, source_target_pairs={{0,4},{1,3},{2,6},{3,1},{4,0},{5,7},{6,2},{7,5},{8,12},{9,11},{10,... | collective-permute-start | bytes 4128776 | tf_op jit(solution)/shard_map/cond/branch_1_fun/ppermute | solution.py:613
  132.6 30.4 %collective-permute-start.24 = (bf16[4,2,96,768]{3,2,1,0:T(8,128)(2,1)}, bf16[4,2,96,768]{3,2,1,0:T(8,128)(2,1)}, u32[]{:S(2)}, u32[]{:S(2)}) collective-permute-start(bf16[4,2,96,768]{3,2,1,0:T(8,128)(2,1)} %get-tuple-element.314), channel_id=1, source_target_pairs={{0,2},{1,5},{2,0},{3,7},{4,6},{5,1},{6,4},{7,3},{8,10},{9,13},{10,... | collective-permute-start | bytes 3538952 | tf_op jit(solution)/shard_map/ppermute | solution.py:613
  133.5 29.5 %collective-permute-start.25 = (bf16[2,4,2,48,768]{4,3,2,1,0:T(8,128)(2,1)}, bf16[2,4,2,48,768]{4,3,2,1,0:T(8,128)(2,1)}, u32[]{:S(2)}, u32[]{:S(2)}) collective-permute-start(bf16[2,4,2,48,768]{4,3,2,1,0:T(8,128)(2,1)} %get-tuple-element.316), channel_id=1, source_target_pairs={{0,2},{1,5},{2,0},{3,7},{4,6},{5,1},{6,4},{7,3},{8,10},{9,13},{10,... | collective-permute-start | bytes 3538952 | tf_op jit(solution)/shard_map/ppermute | solution.py:613
  162.9 5.2 %collective-permute-start.26 = (bf16[1024,768]{1,0:T(8,128)(2,1)}, bf16[1024,768]{1,0:T(8,128)(2,1)}, u32[]{:S(2)}, u32[]{:S(2)}) collective-permute-start(bf16[1024,768]{1,0:T(8,128)(2,1)} %mlp_out_other.1), channel_id=1, source_target_pairs={{0,1},{1,0},{2,3},{3,2},{4,5},{5,4},{6,7},{7,6},{8,9},{9,8},{10,11... | collective-permute-start | bytes 4718600 | tf_op jit(solution)/shard_map/ppermute | solution.py:613
  166.6 22.5 %collective-permute-start.27 = (bf16[4,192,768]{2,1,0:T(8,128)(2,1)}, bf16[4,192,768]{2,1,0:T(8,128)(2,1)}, u32[]{:S(2)}, u32[]{:S(2)}) collective-permute-start(bf16[4,192,768]{2,1,0:T(8,128)(2,1)} %get-tuple-element.332), channel_id=1, source_target_pairs={{0,4},{1,3},{2,6},{3,1},{4,0},{5,7},{6,2},{7,5},{8,12},{9,11},{10,... | collective-permute-start | bytes 3538952 | tf_op jit(solution)/shard_map/ppermute | solution.py:613
  177.5 7.2 %collective-permute-start.2 = (bf16[4,4,208,384]{3,2,1,0:T(8,128)(2,1)}, bf16[4,4,208,384]{3,2,1,0:T(8,128)(2,1)}, u32[]{:S(2)}, u32[]{:S(2)}) collective-permute-start(bf16[4,4,208,384]{3,2,1,0:T(8,128)(2,1)} %get-tuple-element.104), channel_id=1, source_target_pairs={{0,1},{1,0},{2,3},{3,2},{4,5},{5,4},{6,7},{7,6},{8,9},{9,8},{10,11... | collective-permute-start | bytes 7667720 | tf_op jit(solution)/shard_map/cond/branch_1_fun/ppermute | solution.py:613
  188.3 18.5 %collective-permute-start.32 = (bf16[4,2,208,384]{3,2,1,0:T(8,128)(2,1)}, bf16[4,2,208,384]{3,2,1,0:T(8,128)(2,1)}, u32[]{:S(2)}, u32[]{:S(2)}) collective-permute-start(bf16[4,2,208,384]{3,2,1,0:T(8,128)(2,1)} %get-tuple-element.346), channel_id=1, source_target_pairs={{0,2},{1,5},{2,0},{3,7},{4,6},{5,1},{6,4},{7,3},{8,10},{9,13},{10,... | collective-permute-start | bytes 3833864 | tf_op jit(solution)/shard_map/ppermute | solution.py:613
  192.0 26.8 %collective-permute-start.28 = (bf16[192,768]{1,0:T(8,128)(2,1)}, bf16[192,768]{1,0:T(8,128)(2,1)}, u32[]{:S(2)}, u32[]{:S(2)}) collective-permute-start(bf16[192,768]{1,0:T(8,128)(2,1)} %get-tuple-element.342), channel_id=1, source_target_pairs={{0,8},{1,9},{2,10},{3,11},{4,12},{5,13},{6,14},{7,15},{8,0},{9,1},... | collective-permute-start | bytes 884744 | tf_op jit(solution)/shard_map/ppermute | solution.py:613
  194.6 24.2 %collective-permute-start.29 = (bf16[192,768]{1,0:T(8,128)(2,1)}, bf16[192,768]{1,0:T(8,128)(2,1)}, u32[]{:S(2)}, u32[]{:S(2)}) collective-permute-start(bf16[192,768]{1,0:T(8,128)(2,1)} %get-tuple-element.343), channel_id=1, source_target_pairs={{0,16},{1,17},{2,18},{3,19},{4,20},{5,21},{6,22},{7,23},{8,24},{9,... | collective-permute-start | bytes 884744 | tf_op jit(solution)/shard_map/ppermute | solution.py:613
  196.1 22.7 %collective-permute-start.30 = (bf16[192,768]{1,0:T(8,128)(2,1)}, bf16[192,768]{1,0:T(8,128)(2,1)}, u32[]{:S(2)}, u32[]{:S(2)}) collective-permute-start(bf16[192,768]{1,0:T(8,128)(2,1)} %get-tuple-element.344), channel_id=1, source_target_pairs={{0,24},{1,25},{2,26},{3,27},{4,28},{5,29},{6,30},{7,31},{8,16},{9,... | collective-permute-start | bytes 884744 | tf_op jit(solution)/shard_map/ppermute | solution.py:613
  209.5 15.2 %collective-permute-start.35 = (bf16[4,208,384]{2,1,0:T(8,128)(2,1)}, bf16[4,208,384]{2,1,0:T(8,128)(2,1)}, u32[]{:S(2)}, u32[]{:S(2)}) collective-permute-start(bf16[4,208,384]{2,1,0:T(8,128)(2,1)} %get-tuple-element.356), channel_id=1, source_target_pairs={{0,4},{1,3},{2,6},{3,1},{4,0},{5,7},{6,2},{7,5},{8,12},{9,11},{10,... | collective-permute-start | bytes 1916936 | tf_op jit(solution)/shard_map/ppermute | solution.py:613
  212.4 4.7 %collective-permute-start.33 = (f32[8,768]{1,0:T(8,128)S(1)}, f32[8,768]{1,0:T(8,128)S(1)}, u32[]{:S(2)}, u32[]{:S(2)}) collective-permute-start(f32[8,768]{1,0:T(8,128)S(1)} %add.15), channel_id=1, source_target_pairs={{0,8},{1,9},{2,10},{3,11},{4,12},{5,13},{6,14},{7,15},{8,0},{9,1},... | collective-permute-start | bytes 73736 | tf_op jit(solution)/shard_map/ppermute | solution.py:613
  217.7 6.9 %collective-permute-start.36 = (f32[8,768]{1,0:T(8,128)}, f32[8,768]{1,0:T(8,128)}, u32[]{:S(2)}, u32[]{:S(2)}) collective-permute-start(f32[8,768]{1,0:T(8,128)} %add.16), channel_id=1, source_target_pairs={{0,16},{1,17},{2,18},{3,19},{4,20},{5,21},{6,22},{7,23},{8,24},{9,... | collective-permute-start | bytes 73736 | tf_op jit(solution)/shard_map/ppermute | solution.py:613
  226.8 13.9 %collective-permute-start.37 = (bf16[208,384]{1,0:T(8,128)(2,1)}, bf16[208,384]{1,0:T(8,128)(2,1)}, u32[]{:S(2)}, u32[]{:S(2)}) collective-permute-start(bf16[208,384]{1,0:T(8,128)(2,1)} %get-tuple-element.366), channel_id=1, source_target_pairs={{0,8},{1,9},{2,10},{3,11},{4,12},{5,13},{6,14},{7,15},{8,0},{9,1},... | collective-permute-start | bytes 479240 | tf_op jit(solution)/shard_map/ppermute | solution.py:613
  229.3 13.3 %collective-permute-start.38 = (bf16[208,384]{1,0:T(8,128)(2,1)}, bf16[208,384]{1,0:T(8,128)(2,1)}, u32[]{:S(2)}, u32[]{:S(2)}) collective-permute-start(bf16[208,384]{1,0:T(8,128)(2,1)} %get-tuple-element.367), channel_id=1, source_target_pairs={{0,16},{1,17},{2,18},{3,19},{4,20},{5,21},{6,22},{7,23},{8,24},{9,... | collective-permute-start | bytes 479240 | tf_op jit(solution)/shard_map/ppermute | solution.py:613
  229.3 13.3 %collective-permute-start.39 = (bf16[208,384]{1,0:T(8,128)(2,1)}, bf16[208,384]{1,0:T(8,128)(2,1)}, u32[]{:S(2)}, u32[]{:S(2)}) collective-permute-start(bf16[208,384]{1,0:T(8,128)(2,1)} %get-tuple-element.368), channel_id=1, source_target_pairs={{0,24},{1,25},{2,26},{3,27},{4,28},{5,29},{6,30},{7,31},{8,16},{9,... | collective-permute-start | bytes 479240 | tf_op jit(solution)/shard_map/ppermute | solution.py:613
  236.9 7.7 %collective-permute-start.34 = (f32[2,24,768]{2,1,0:T(8,128)}, f32[2,24,768]{2,1,0:T(8,128)}, u32[]{:S(2)}, u32[]{:S(2)}) collective-permute-start(f32[2,24,768]{2,1,0:T(8,128)} %get-tuple-element.355), channel_id=1, source_target_pairs={{0,1},{1,0},{2,3},{3,2},{4,5},{5,4},{6,7},{7,6},{8,9},{9,8},{10,11... | collective-permute-start | bytes 442376 | tf_op jit(solution)/shard_map/ppermute | solution.py:613
  (14 other events, 69.6 us)

commit v9 on v7

--- a/solution.py
+++ b/solution.py
@@ -622,7 +622,8 @@
     return lambda core, chip: (core, chip ^ (4 * distance))
 
 
-def split_shards(core_ref, q_ref, k_ref, v_ref, o_ref, u_ref, keep_ref, send_ref):
+def split_shards(core_ref, q_ref, k_ref, v_ref, o_ref, u_ref, d_ref, keep_ref, send_ref, down_ref):
+    down_ref[...] = d_ref[: down_ref.shape[0], :]
     width = q_ref.shape[1]
     side = width // 2
     first = core_ref[0] == 0
@@ -710,13 +711,15 @@
     deep = weights[5].shape[0]
     folds = deep // own
     halves = (VMEM_SPEC, shaped(4 + folds, own, side))
-    keep, send = small_call(
-        split_shards, (me & 1, *weights[:5]), [halves, halves], "split_shards", ins=[SMEM] + [VMEM_SPEC] * 5)
+    keep, send, down = small_call(
+        split_shards, (me & 1, *weights), [halves, halves, (VMEM_SPEC, shaped(deep - 16, width))], "split_shards",
+        ins=[SMEM] + [VMEM_SPEC] * 6)
     take = swap(send, other_core)
-    return small_call(
+    near, up = small_call(
         join_shards, (me, keep, take, weights[5], *vectors),
         [(VMEM_SPEC, shaped(8 * own + 16, side)), (VMEM_SPEC, shaped(2 * deep + 32, side))], "join_shards",
         ins=[SMEM] + [VMEM_SPEC] * (3 + len(vectors)))
+    return near, up, down
 
 
 def doubled(pieces, change):
@@ -980,13 +983,14 @@
     def attend_by_hand(q, k, v, vec, wo, up_four, up_along):
         up = [swap(up_four, second_plane), swap(up_along, second_plane)]
         mixed, lse, resid, n2 = attend(q, k, v, vec, wo)
-        up = after(up, mixed)
-        n2_other = swap(after(n2, up), other_core)
+        n2_other = fenced(scatter_core, n2)
+        up = after(up, n2_other)
         return mixed, lse, resid, n2, n2_other, up
 
     if by_hand:
-        down_two = doubled(down_weight[None, :-16], other_layer(1))
-        near, up = prepare(me, weights, vectors)
+        near, up, down = prepare(me, weights, vectors)
+        down = after(down, near)[None]
+        down_two = doubled(down, other_layer(1))
         near_moved = [swap(near, other_layer(r)) for r in (1, 2, 3)]
         up_moved = swap(up, other_layer(1))
         down_shard = fenced(gather_down, after(down_two, near))
@@ -997,7 +1001,7 @@
         up_moved = swap(up_two, other_layer(2))
         along, across, cot, sum_down = fenced(gather_first, near)
         up_taken = after(up_moved, along)
-        down = [down_shard, swap(after(down_shard, along), other_layer(2))]
+        down = [down_shard, swap(after(down_shard, up_taken), other_layer(2))]
         corner, taken, cot_other, up_four = fenced(gather_second, near, along, across, cot, up_two, up_taken)
         near = [near, along, across, corner] + taken
         up_along = swap(up_four, first_plane)
@@ -1006,7 +1010,7 @@
             [low_rows] * 4 + [(ANY_SPEC, shaped(width, width))] * 4 + [kept_vec, kept_hidden],
             [pltpu.VMEM((4, width, width), BF16), pltpu.VMEM((CHIPS, width // (4 * CHIPS) + 1, 16, width), BF16),
              pltpu.SemaphoreType.DMA((1,)), pltpu.SemaphoreType.DMA((4,))],
-            "project", LATER, tokens, *[piece.reshape(4, -1, 16, side) for piece in near])
+            "project", LATER, tokens, *[piece.reshape(4, -1, 16, side) for piece in after(near)])
         up_along = after(up_along, n1)
         mixed, lse, resid, n2, n2_other, up_moved = fenced(attend_by_hand, q, k, v, vec, wo, up_four, up_along)
         up = [up_along] + up_moved
@@ -1117,7 +1121,8 @@
         late_take = after(swap(late, other_layer(2)), g_down)
         square_second = after(square_second, g_down)
         rest, *sends = merge_layers_of(*square_second)
-        rest, sends, late_take = after((rest, sends, late_take))
+        late_take = after(late_take, rest)
+        sends = after(sends, late_take)
         square_layers = [rest] + [swap(piece, other_layer(r + 1)) for r, piece in enumerate(sends)]
         late = late + late_take
         late = late + after(swap(late, other_plane(1)), rest)

time: 252 us -> 247 us (0.980)
  local copies, waits for them, and re-layouts: 4.72 us -> 0.02 us
  transfers between devices with their start and end apart: 43 -> 43, of which waited for: 18 -> 17; matrix products, arithmetic and copies ran while one was open for 4% -> 2% of each run, Pallas kernels for 39% -> 39%
where the time goes in v9:
time: 247 us; the launch traced here: 246 us
  Pallas kernels  140 us (57%)
  waiting for transfers between devices  54.1 us (22%)
  starting transfers between devices  43 us (17%)
  other arithmetic  7.71 us (3%)
    pallas_call x5, Pallas kernels, call_with(): pl.pallas_call(kernel, grid_spec=pltpu.PrefetchScalarGridSpec(num_scalar_...  67.7 us
    pallas_call x7, Pallas kernels, call(): pl.pallas_call(kernel, grid=grid, in_specs=ins, out_specs=out_specs, out_...  57.5 us
    ppermute x43, waiting for transfers between devices, swap(): return lax.ppermute(array, 'dp', flipped(lax.axis_size('dp'), change))  54.1 us
    ppermute x43, starting transfers between devices, swap(): return lax.ppermute(array, 'dp', flipped(lax.axis_size('dp'), change))  43 us
    pallas_call x7, Pallas kernels, small_call(): pl.pallas_call(kernel, in_specs=ins, out_specs=tuple((spec for spec, _ in...  15.2 us
  transfers between devices with their start and end apart: 43, of which 17 were waited for; matrix products, arithmetic and copies ran while one was open for 2% of the time, Pallas kernels for 39%

profile of v9, /device:TPU:0, one launch (start us, length us, event | category | flops | bytes accessed | tf_op | source)
XLA Modules:
  0.0 246.2 jit_solution(14407522021934377041)
XLA Ops:
  6.4 2.9 %collective-permute-start.19 = (bf16[1,80,768]{2,1,0:T(8,128)(2,1)}, bf16[1,80,768]{2,1,0:T(8,128)(2,1)S(1)}, u32[]{:S(2)}, u32[]{:S(2)}) collective-permute-start(bf16[1,80,768]{2,1,0:T(8,128)(2,1)} %bitcast.27), channel_id=1, source_target_pairs={{0,8},{1,9},{2,10},{3,11},{4,12},{5,13},{6,14},{7,15},{8,0},{9,1},... | collective-permute-start | bytes 368648 | tf_op jit(solution)/shard_map/ppermute | solution.py:602
  9.4 4.0 %collective-permute-start.17 = (bf16[208,384]{1,0:T(8,128)(2,1)}, bf16[208,384]{1,0:T(8,128)(2,1)S(1)}, u32[]{:S(2)}, u32[]{:S(2)}) collective-permute-start(bf16[208,384]{1,0:T(8,128)(2,1)} %get-tuple-element.267), channel_id=1, source_target_pairs={{0,24},{1,25},{2,26},{3,27},{4,28},{5,29},{6,30},{7,31},{8,16},{9,... | collective-permute-start | bytes 479240 | tf_op jit(solution)/shard_map/ppermute | solution.py:602
  14.9 15.3 %conditional.6 = (bf16[8,80,768]{2,1,0:T(8,128)(2,1)S(1)}) conditional(s32[]{:T(128)} %convert_element_type.4, () %tuple.81, bf16[2,80,768]{2,1,0:T(8,128)(2,1)S(1)} %pad_maximum_fusion.5), branch_computations={%region_0.0_spmd, %region_1.0_spmd} | conditional | flops 1228800 | bytes 5898328 | solution.py:847
  16.7 4.5 %collective-permute-done.6 = bf16[2,80,768]{2,1,0:T(8,128)(2,1)S(1)} collective-permute-done((bf16[2,80,768]{2,1,0:T(8,128)(2,1)S(1)}, bf16[2,80,768]{2,1,0:T(8,128)(2,1)S(1)}, u32[]{:S(2)}, u32[]{:S(2)}) %collective-permute-start.6) | collective-permute-done | bytes 245792 | tf_op jit(solution)/shard_map/cond/branch_1_fun/ppermute | solution.py:602
  23.0 7.1 %collective-permute-done.7 = bf16[4,80,768]{2,1,0:T(8,128)(2,1)S(1)} collective-permute-done((bf16[4,80,768]{2,1,0:T(8,128)(2,1)S(1)}, bf16[4,80,768]{2,1,0:T(8,128)(2,1)S(1)}, u32[]{:S(2)}, u32[]{:S(2)}) %collective-permute-start.7) | collective-permute-done | bytes 491552 | tf_op jit(solution)/shard_map/cond/branch_1_fun/ppermute | solution.py:602
  32.2 2.8 %collective-permute-start.20 = (bf16[2,224,384]{2,1,0:T(8,128)(2,1)}, bf16[2,224,384]{2,1,0:T(8,128)(2,1)}, u32[]{:S(2)}, u32[]{:S(2)}) collective-permute-start(bf16[2,224,384]{2,1,0:T(8,128)(2,1)} %pad_maximum_fusion.4), channel_id=1, source_target_pairs={{0,16},{1,17},{2,18},{3,19},{4,20},{5,21},{6,22},{7,23},{8,24},{9,... | collective-permute-start | bytes 1032200 | tf_op jit(solution)/shard_map/ppermute | solution.py:602
  34.9 14.5 %conditional.7 = (bf16[4,208,384]{2,1,0:T(8,128)(2,1)}, bf16[4,208,384]{2,1,0:T(8,128)(2,1)}, bf16[1024,768]{1,0:T(8,128)(2,1)}, f32[8,768]{1,0:T(8,128)}) conditional(s32[]{:T(128)} %convert_element_type.4, () %tuple.86, (bf16[4,208,384]{2,1,0:T(8,128)(2,1)}, bf16[1024,768]{1,0:T(8,128)(2,1)}, s32[4,5]{1,0:T(4,128)}) %tuple.87), branch_computations={%region_2.0_spmd, %region_3.0_spmd} | conditional | bytes 5111921 | solution.py:847
  37.9 3.8 %mask_grads.1 = (bf16[1024,768]{1,0:T(8,128)(2,1)}, f32[8,768]{1,0:T(8,128)}) custom-call(s32[4,5]{1,0:T(4,128)} %get-tuple-element.71.lengths_ref, bf16[1024,768]{1,0:T(8,128)(2,1)} %get-tuple-element.73.grad_ref), custom_call_target="tpu_custom_call" | custom-call | bytes 1 | tf_op jit(solution)/shard_map/cond/branch_1_fun/mask_grads/pallas_call | solution.py:561
  41.8 7.7 %collective-permute-done = bf16[4,208,384]{2,1,0:T(8,128)(2,1)} collective-permute-done((bf16[4,208,384]{2,1,0:T(8,128)(2,1)}, bf16[4,208,384]{2,1,0:T(8,128)(2,1)}, u32[]{:S(2)}, u32[]{:S(2)}) %collective-permute-start) | collective-permute-done | bytes 639008 | tf_op jit(solution)/shard_map/cond/branch_1_fun/ppermute | solution.py:602
  50.0 14.6 %conditional.8 = (bf16[4,208,384]{2,1,0:T(8,128)(2,1)}, bf16[4,208,384]{2,1,0:T(8,128)(2,1)}, bf16[4,208,384]{2,1,0:T(8,128)(2,1)}, bf16[4,208,384]{2,1,0:T(8,12...) conditional(s32[]{:T(128)} %convert_element_type.4, () %tuple.88, ...), branch_computations={%region_4.0_spmd, %region_5.0_spmd} | conditional | flops 344064 | bytes 20447528 | solution.py:847
  51.0 3.6 %collective-permute-done.9 = bf16[4,208,384]{2,1,0:T(8,128)(2,1)} collective-permute-done((bf16[4,208,384]{2,1,0:T(8,128)(2,1)}, bf16[4,208,384]{2,1,0:T(8,128)(2,1)}, u32[]{:S(2)}, u32[]{:S(2)}) %collective-permute-start.9) | collective-permute-done | bytes 639008 | tf_op jit(solution)/shard_map/cond/branch_1_fun/ppermute | solution.py:602
  55.6 5.7 %collective-permute-done.8 = bf16[4,208,384]{2,1,0:T(8,128)(2,1)} collective-permute-done((bf16[4,208,384]{2,1,0:T(8,128)(2,1)}, bf16[4,208,384]{2,1,0:T(8,128)(2,1)}, u32[]{:S(2)}, u32[]{:S(2)}) %collective-permute-start.8) | collective-permute-done | bytes 639008 | tf_op jit(solution)/shard_map/cond/branch_1_fun/ppermute | solution.py:602
  66.0 10.4 %project.1 = (bf16[1024,768]{1,0:T(8,128)(2,1)}, bf16[1024,768]{1,0:T(8,128)(2,1)}, bf16[1024,768]{1,0:T(8,128)(2,1)}, bf16[1024,768]{1,0:T(8,128)(2,1)}, bf16[7...) custom-call(s32[1]{0:T(128)} %bitcast.1.me_ref, ...), custom_call_target="tpu_custom_call" | custom-call | flops 8999999488 | bytes 1 | tf_op jit(solution)/shard_map/project/pallas_call | solution.py:576
  76.5 19.2 %conditional.9 = (bf16[1024,768]{1,0:T(8,128)(2,1)}, f32[1024,128]{1,0:T(8,128)}, f32[1024,768]{1,0:T(8,128)}, bf16[1024,768]{1,0:T(8,128)(2,1)}, bf16[1024,768]...) conditional(s32[]{:T(128)} %convert_element_type.4, () %tuple.92, ...), branch_computations={%region_6.0_spmd, %region_7.0_spmd} | conditional | flops 4 | bytes 11796699 | solution.py:847
  78.6 13.2 %attention_forward.1 = (bf16[1024,768]{1,0:T(8,128)(2,1)}, f32[1024,128]{1,0:T(8,128)}, f32[1024,768]{1,0:T(8,128)}, bf16[1024,768]{1,0:T(8,128)(2,1)}) custom-call(s32[4,5]{1,0:T(4,128)} %get-tuple-element.85.lengths_ref, bf16[1024,768]{1,0:T(8,128)(2,1)} %get-tuple-element.86.x_ref, f32[16,768]{1,0:T(8,128)} %get-tuple-element.87.vec_ref, ...), custom_call_target="tpu_custom_call" | custom-call | bytes 1 | tf_op jit(solution)/shard_map/cond/branch_1_fun/attention_forward/pallas_call | solution.py:561
  91.8 3.8 %conditional = (bf16[1024,768]{1,0:T(8,128)(2,1)}) conditional(s32[]{:T(128)} %convert_element_type.0, () %tuple.40, bf16[1024,768]{1,0:T(8,128)(2,1)} %get-tuple-element.428), branch_computations={%region_8.0_spmd, %region_9.0_spmd} | conditional | bytes 6291504 | solution.py:847
  91.9 3.7 %collective-permute-done.2 = bf16[1024,768]{1,0:T(8,128)(2,1)} collective-permute-done((bf16[1024,768]{1,0:T(8,128)(2,1)}, bf16[1024,768]{1,0:T(8,128)(2,1)}, u32[]{:S(2)}, u32[]{:S(2)}) %collective-permute-start.2) | collective-permute-done | bytes 1572896 | tf_op jit(solution)/shard_map/cond/branch_1_fun/cond/branch_1_fun/ppermute | solution.py:602
  95.6 35.0 %mlp.1 = (bf16[1024,1536]{1,0:T(8,128)(2,1)}, bf16[1024,1536]{1,0:T(8,128)(2,1)}, f32[1024,768]{1,0:T(8,128)}, bf16[1024,768]{1,0:T(8,128)(2,1)}, bf16[4,2,96,76...) custom-call(s32[1]{0:T(128)} %bitcast.1.me_ref, ...), custom_call_target="tpu_custom_call" | custom-call | bytes 1 | tf_op jit(solution)/shard_map/mlp/pallas_call | solution.py:576
  134.4 20.7 %attention_backward.1 = (bf16[4,1024,768]{2,1,0:T(8,128)(2,1)}, f32[1024,768]{1,0:T(8,128)}, f32[8,768]{1,0:T(8,128)}) custom-call(s32[4,5]{1,0:T(4,128)} %lengths_ref.1, bf16[1024,768]{1,0:T(8,128)(2,1)} %get-tuple-element.297.q_ref, bf16[1024,768]{1,0:T(8,128)(2,1)} %get-tuple-element.298.k_ref, bf16[1024,768]{1,0:T(8,128)(2,1)} %get-tuple-element.299.v_ref, ...), custom_call_target="tpu_custom_call" | custom-call | bytes 1 | tf_op jit(solution)/shard_map/attention_backward/pallas_call | solution.py:561
  155.1 5.8 %mlp_out_other.1 = bf16[1024,768]{1,0:T(8,128)(2,1)} custom-call(s32[1]{0:T(128)} %bitcast.1.me_ref, bf16[1024,1536]{1,0:T(8,128)(2,1)} %get-tuple-element.321.act_ref, bf16[1536,768]{1,0:T(8,128)(2,1)} %get-tuple-element.322.wdown_ref), custom_call_target="tpu_custom_call" | custom-call | bytes 1 | tf_op jit(solution)/shard_map/mlp_out_other/pallas_call | solution.py:576
  161.1 3.6 %merge_first.2 = (bf16[4,192,768]{2,1,0:T(8,128)(2,1)}, bf16[4,192,768]{2,1,0:T(8,128)(2,1)}) custom-call(bf16[1,4,2,96,768]{4,3,2,1,0:T(8,128)(2,1)} %bitcast.20, bf16[1,4,2,96,768]{4,3,2,1,0:T(8,128)(2,1)} %bitcast.18.refs_1_, bf16[2,4,2,48,768]{4,3,2,1,0:T(8,128)(2,1)} %get-tuple-element.325.refs_2_, ...), custom_call_target="tpu_custom_call" | custom-call | bytes 1 | tf_op jit(solution)/shard_map/merge_first/pallas_call | solution.py:561
  165.2 20.5 %conditional.10 = (bf16[1,4,2,208,384]{4,3,2,1,0:T(8,128)(2,1)}, bf16[4,2,208,384]{3,2,1,0:T(8,128)(2,1)}, bf16[1024,768]{1,0:T(8,128)(2,1)}) conditional(s32[]{:T(128)} %convert_element_type.4, () %tuple.80, (s32[1]{0:T(128)}, bf16[1024,768]{1,0:T(8,128)(2,1)}, bf16[1024,768]{1,0:T(8,128)(2,1)}, bf16[4,1024,768]{2,1,0:T(8,128)(2,1)}, ...), branch_computations={%region_10.0_spmd, %region_11.0_spmd} | conditional | bytes 10223683 | solution.py:847
  165.2 9.4 %weight_grads.1 = (bf16[4,4,208,384]{3,2,1,0:T(8,128)(2,1)}, bf16[4,4,208,384]{3,2,1,0:T(8,128)(2,1)}) custom-call(s32[1]{0:T(128)} %get-tuple-element.101.me_ref, bf16[1024,768]{1,0:T(8,128)(2,1)} %get-tuple-element.102.n1_ref, bf16[1024,768]{1,0:T(8,128)(2,1)} %get-tuple-element.103.mixed_hbm, bf16[4,1024,768]{2,1,0:T(8,128)(2,1)} %get-tuple-element.104.columns_ref, ...), custom_call_target="tpu_custom_call" | custom-call | bytes 1 | tf_op jit(solution)/shard_map/cond/branch_1_fun/weight_grads/pallas_call | solution.py:576
  175.0 7.1 %mlp_out_own.1 = bf16[1024,768]{1,0:T(8,128)(2,1)} custom-call(s32[1]{0:T(128)} %get-tuple-element.101.me_ref, f32[1024,768]{1,0:T(8,128)} %get-tuple-element.110.resid_ref, f32[16,768]{1,0:T(8,128)} %get-tuple-element.111.vec_ref, bf16[1024,1536]{1,0:T(8,128)(2,1)} %get-tuple-element.112.act_ref, bf16[1024,768]{1,0:T(8,128)(2,1)} %get-tuple-element.114.take_ref, ...), custom_call_target="tpu_custom_call" | custom-call | bytes 1 | tf_op jit(solution)/shard_map/cond/branch_1_fun/mlp_out_own/pallas_call | solution.py:576
  182.1 3.7 %merge_core.1 = (bf16[4,2,208,384]{3,2,1,0:T(8,128)(2,1)}, bf16[4,2,208,384]{3,2,1,0:T(8,128)(2,1)}) custom-call(s32[1]{0:T(128)} %get-tuple-element.100.core_ref, bf16[4,4,208,384]{3,2,1,0:T(8,128)(2,1)} %get-tuple-element.108.keep_ref, bf16[4,4,208,384]{3,2,1,0:T(8,128)(2,1)} %collective-permute-done.5.take_ref), custom_call_target="tpu_custom_call" | custom-call | bytes 1 | tf_op jit(solution)/shard_map/cond/branch_1_fun/merge_core/pallas_call | solution.py:561
  187.0 2.8 %merge_second.2 = (f32[192,768]{1,0:T(8,128)}, bf16[192,768]{1,0:T(8,128)(2,1)}, bf16[192,768]{1,0:T(8,128)(2,1)}, bf16[192,768]{1,0:T(8,128)(2,1)}) custom-call(bf16[4,192,768]{2,1,0:T(8,128)(2,1)} %get-tuple-element.337.own_ref, bf16[4,192,768]{2,1,0:T(8,128)(2,1)} %collective-permute-done.27.take_ref), custom_call_target="tpu_custom_call" | custom-call | bytes 1 | tf_op jit(solution)/shard_map/merge_second/pallas_call | solution.py:692
  194.3 9.9 %tokens_backward.1 = (bf16[1024,768]{1,0:T(8,128)(2,1)}, f32[8,768]{1,0:T(8,128)}) custom-call(bf16[1024,768]{1,0:T(8,128)(2,1)} %x_ref.3, f32[1024,768]{1,0:T(8,128)} %get-tuple-element.340.gresid_ref, f32[16,768]{1,0:T(8,128)} %get-tuple-element.296.vec_ref, bf16[4,1024,768]{2,1,0:T(8,128)(2,1)} %get-tuple-element.328.grads_ref, ...), custom_call_target="tpu_custom_call" | custom-call | flops 11500000256 | bytes 1 | tf_op jit(solution)/shard_map/tokens_backward/pallas_call | solution.py:561
  204.2 2.6 %merge_first.3 = (bf16[4,208,384]{2,1,0:T(8,128)(2,1)}, bf16[4,208,384]{2,1,0:T(8,128)(2,1)}) custom-call(bf16[1,4,2,208,384]{4,3,2,1,0:T(8,128)(2,1)} %get-tuple-element.336.refs_0_, bf16[1,4,2,208,384]{4,3,2,1,0:T(8,128)(2,1)} %bitcast.19.refs_1_), custom_call_target="tpu_custom_call" | custom-call | bytes 1 | tf_op jit(solution)/shard_map/merge_first/pallas_call | solution.py:561
  211.5 3.3 %collective-permute-done.33 = f32[8,768]{1,0:T(8,128)S(1)} collective-permute-done((f32[8,768]{1,0:T(8,128)S(1)}, f32[8,768]{1,0:T(8,128)S(1)}, u32[]{:S(2)}, u32[]{:S(2)}) %collective-permute-start.33) | collective-permute-done | bytes 24608 | tf_op jit(solution)/shard_map/ppermute | solution.py:602
  218.4 3.4 %collective-permute-done.36 = f32[8,768]{1,0:T(8,128)} collective-permute-done((f32[8,768]{1,0:T(8,128)}, f32[8,768]{1,0:T(8,128)}, u32[]{:S(2)}, u32[]{:S(2)}) %collective-permute-start.36) | collective-permute-done | bytes 24608 | tf_op jit(solution)/shard_map/ppermute | solution.py:602
  224.0 2.5 %collective-permute-start.37 = (bf16[208,384]{1,0:T(8,128)(2,1)}, bf16[208,384]{1,0:T(8,128)(2,1)}, u32[]{:S(2)}, u32[]{:S(2)}) collective-permute-start(bf16[208,384]{1,0:T(8,128)(2,1)} %get-tuple-element.369), channel_id=1, source_target_pairs={{0,8},{1,9},{2,10},{3,11},{4,12},{5,13},{6,14},{7,15},{8,0},{9,1},... | collective-permute-start | bytes 479240 | tf_op jit(solution)/shard_map/ppermute | solution.py:602
  230.7 2.7 %collective-permute-done.40 = f32[8,768]{1,0:T(8,128)S(1)} collective-permute-done((f32[8,768]{1,0:T(8,128)S(1)}, f32[8,768]{1,0:T(8,128)S(1)}, u32[]{:S(2)}, u32[]{:S(2)}) %collective-permute-start.40) | collective-permute-done | bytes 24608 | tf_op jit(solution)/shard_map/ppermute | solution.py:602
  (96 shorter events, 63.4 us)
Async XLA Ops:
  6.4 7.6 %collective-permute-start.19 = (bf16[1,80,768]{2,1,0:T(8,128)(2,1)}, bf16[1,80,768]{2,1,0:T(8,128)(2,1)S(1)}, u32[]{:S(2)}, u32[]{:S(2)}) collective-permute-start(bf16[1,80,768]{2,1,0:T(8,128)(2,1)} %bitcast.27), channel_id=1, source_target_pairs={{0,8},{1,9},{2,10},{3,11},{4,12},{5,13},{6,14},{7,15},{8,0},{9,1},... | collective-permute-start | bytes 368648 | tf_op jit(solution)/shard_map/ppermute | solution.py:602
  9.3 20.9 %collective-permute-start.18 = (bf16[224,384]{1,0:T(8,128)(2,1)}, bf16[224,384]{1,0:T(8,128)(2,1)S(1)}, u32[]{:S(2)}, u32[]{:S(2)}) collective-permute-start(bf16[224,384]{1,0:T(8,128)(2,1)} %get-tuple-element.268), channel_id=1, source_target_pairs={{0,8},{1,9},{2,10},{3,11},{4,12},{5,13},{6,14},{7,15},{8,0},{9,1},... | collective-permute-start | bytes 516104 | tf_op jit(solution)/shard_map/ppermute | solution.py:602
  9.4 20.8 %collective-permute-start.17 = (bf16[208,384]{1,0:T(8,128)(2,1)}, bf16[208,384]{1,0:T(8,128)(2,1)S(1)}, u32[]{:S(2)}, u32[]{:S(2)}) collective-permute-start(bf16[208,384]{1,0:T(8,128)(2,1)} %get-tuple-element.267), channel_id=1, source_target_pairs={{0,24},{1,25},{2,26},{3,27},{4,28},{5,29},{6,30},{7,31},{8,16},{9,... | collective-permute-start | bytes 479240 | tf_op jit(solution)/shard_map/ppermute | solution.py:602
  13.4 16.9 %collective-permute-start.16 = (bf16[208,384]{1,0:T(8,128)(2,1)}, bf16[208,384]{1,0:T(8,128)(2,1)S(1)}, u32[]{:S(2)}, u32[]{:S(2)}) collective-permute-start(bf16[208,384]{1,0:T(8,128)(2,1)} %get-tuple-element.267), channel_id=1, source_target_pairs={{0,16},{1,17},{2,18},{3,19},{4,20},{5,21},{6,22},{7,23},{8,24},{9,... | collective-permute-start | bytes 479240 | tf_op jit(solution)/shard_map/ppermute | solution.py:602
  13.4 16.9 %collective-permute-start.15 = (bf16[208,384]{1,0:T(8,128)(2,1)}, bf16[208,384]{1,0:T(8,128)(2,1)S(1)}, u32[]{:S(2)}, u32[]{:S(2)}) collective-permute-start(bf16[208,384]{1,0:T(8,128)(2,1)} %get-tuple-element.267), channel_id=1, source_target_pairs={{0,8},{1,9},{2,10},{3,11},{4,12},{5,13},{6,14},{7,15},{8,0},{9,1},... | collective-permute-start | bytes 479240 | tf_op jit(solution)/shard_map/ppermute | solution.py:602
  14.9 6.3 %collective-permute-start.6 = (bf16[2,80,768]{2,1,0:T(8,128)(2,1)S(1)}, bf16[2,80,768]{2,1,0:T(8,128)(2,1)S(1)}, u32[]{:S(2)}, u32[]{:S(2)}) collective-permute-start(bf16[2,80,768]{2,1,0:T(8,128)(2,1)S(1)} %param.1), channel_id=1, source_target_pairs={{0,2},{1,5},{2,0},{3,7},{4,6},{5,1},{6,4},{7,3},{8,10},{9,13},{10,... | collective-permute-start | bytes 737288 | tf_op jit(solution)/shard_map/cond/branch_1_fun/ppermute | solution.py:602
  21.2 8.9 %collective-permute-start.7 = (bf16[4,80,768]{2,1,0:T(8,128)(2,1)S(1)}, bf16[4,80,768]{2,1,0:T(8,128)(2,1)S(1)}, u32[]{:S(2)}, u32[]{:S(2)}) collective-permute-start(bf16[4,80,768]{2,1,0:T(8,128)(2,1)S(1)} %pad_maximum_fusion.1), channel_id=1, source_target_pairs={{0,4},{1,3},{2,6},{3,1},{4,0},{5,7},{6,2},{7,5},{8,12},{9,11},{10,... | collective-permute-start | bytes 1474568 | tf_op jit(solution)/shard_map/cond/branch_1_fun/ppermute | solution.py:602
  32.2 17.3 %collective-permute-start.20 = (bf16[2,224,384]{2,1,0:T(8,128)(2,1)}, bf16[2,224,384]{2,1,0:T(8,128)(2,1)}, u32[]{:S(2)}, u32[]{:S(2)}) collective-permute-start(bf16[2,224,384]{2,1,0:T(8,128)(2,1)} %pad_maximum_fusion.4), channel_id=1, source_target_pairs={{0,16},{1,17},{2,18},{3,19},{4,20},{5,21},{6,22},{7,23},{8,24},{9,... | collective-permute-start | bytes 1032200 | tf_op jit(solution)/shard_map/ppermute | solution.py:602
  34.9 14.5 %collective-permute-start = (bf16[4,208,384]{2,1,0:T(8,128)(2,1)}, bf16[4,208,384]{2,1,0:T(8,128)(2,1)}, u32[]{:S(2)}, u32[]{:S(2)}) collective-permute-start(bf16[4,208,384]{2,1,0:T(8,128)(2,1)} %get-tuple-element.70), channel_id=1, source_target_pairs={{0,2},{1,5},{2,0},{3,7},{4,6},{5,1},{6,4},{7,3},{8,10},{9,13},{10,... | collective-permute-start | bytes 1916936 | tf_op jit(solution)/shard_map/cond/branch_1_fun/ppermute | solution.py:602
  36.4 13.0 %collective-permute-start.1 = (bf16[4,208,384]{2,1,0:T(8,128)(2,1)}, bf16[4,208,384]{2,1,0:T(8,128)(2,1)}, u32[]{:S(2)}, u32[]{:S(2)}) collective-permute-start(bf16[4,208,384]{2,1,0:T(8,128)(2,1)} %get-tuple-element.70), channel_id=1, source_target_pairs={{0,4},{1,3},{2,6},{3,1},{4,0},{5,7},{6,2},{7,5},{8,12},{9,11},{10,... | collective-permute-start | bytes 1916936 | tf_op jit(solution)/shard_map/cond/branch_1_fun/ppermute | solution.py:602
  49.4 46.2 %collective-permute-start.22 = (bf16[8,80,768]{2,1,0:T(8,128)(2,1)}, bf16[8,80,768]{2,1,0:T(8,128)(2,1)}, u32[]{:S(2)}, u32[]{:S(2)}) collective-permute-start(bf16[8,80,768]{2,1,0:T(8,128)(2,1)} %copy-done), channel_id=1, source_target_pairs={{0,16},{1,17},{2,18},{3,19},{4,20},{5,21},{6,22},{7,23},{8,24},{9,... | collective-permute-start | bytes 2949128 | tf_op jit(solution)/shard_map/ppermute | solution.py:602
  50.0 14.6 %collective-permute-start.13 = (bf16[1024,768]{1,0:T(8,128)(2,1)}, bf16[1024,768]{1,0:T(8,128)(2,1)}, u32[]{:S(2)}, u32[]{:S(2)}) collective-permute-start(bf16[1024,768]{1,0:T(8,128)(2,1)} %get-tuple-element.82), channel_id=1, source_target_pairs={{0,1},{1,0},{2,3},{3,2},{4,5},{5,4},{6,7},{7,6},{8,9},{9,8},{10,11... | collective-permute-start | bytes 4718600 | tf_op jit(solution)/shard_map/cond/branch_1_fun/ppermute | solution.py:602
  50.0 4.7 %collective-permute-start.9 = (bf16[4,208,384]{2,1,0:T(8,128)(2,1)}, bf16[4,208,384]{2,1,0:T(8,128)(2,1)}, u32[]{:S(2)}, u32[]{:S(2)}) collective-permute-start(bf16[4,208,384]{2,1,0:T(8,128)(2,1)} %get-tuple-element.78), channel_id=1, source_target_pairs={{0,1},{1,0},{2,3},{3,2},{4,5},{5,4},{6,7},{7,6},{8,9},{9,8},{10,11... | collective-permute-start | bytes 1916936 | tf_op jit(solution)/shard_map/cond/branch_1_fun/ppermute | solution.py:602
  50.5 5.1 %collective-permute-start.10 = (bf16[4,208,384]{2,1,0:T(8,128)(2,1)}, bf16[4,208,384]{2,1,0:T(8,128)(2,1)}, u32[]{:S(2)}, u32[]{:S(2)}) collective-permute-start(bf16[4,208,384]{2,1,0:T(8,128)(2,1)} %get-tuple-element.77), channel_id=1, source_target_pairs={{0,1},{1,0},{2,3},{3,2},{4,5},{5,4},{6,7},{7,6},{8,9},{9,8},{10,11... | collective-permute-start | bytes 1916936 | tf_op jit(solution)/shard_map/cond/branch_1_fun/ppermute | solution.py:602
  50.5 10.7 %collective-permute-start.8 = (bf16[4,208,384]{2,1,0:T(8,128)(2,1)}, bf16[4,208,384]{2,1,0:T(8,128)(2,1)}, u32[]{:S(2)}, u32[]{:S(2)}) collective-permute-start(bf16[4,208,384]{2,1,0:T(8,128)(2,1)} %get-tuple-element.77), channel_id=1, source_target_pairs={{0,4},{1,3},{2,6},{3,1},{4,0},{5,7},{6,2},{7,5},{8,12},{9,11},{10,... | collective-permute-start | bytes 1916936 | tf_op jit(solution)/shard_map/cond/branch_1_fun/ppermute | solution.py:602
  64.6 11.9 %collective-permute-start.21 = (bf16[4,224,384]{2,1,0:T(8,128)(2,1)}, bf16[4,224,384]{2,1,0:T(8,128)(2,1)}, u32[]{:S(2)}, u32[]{:S(2)}) collective-permute-start(bf16[4,224,384]{2,1,0:T(8,128)(2,1)} %get-tuple-element.301.refs_5_), channel_id=1, source_target_pairs={{0,2},{1,5},{2,0},{3,7},{4,6},{5,1},{6,4},{7,3},{8,10},{9,13},{10,... | collective-permute-start | bytes 2064392 | tf_op jit(solution)/shard_map/ppermute | solution.py:602
  76.5 19.1 %collective-permute-start.3 = (bf16[4,224,384]{2,1,0:T(8,128)(2,1)}, bf16[4,224,384]{2,1,0:T(8,128)(2,1)}, u32[]{:S(2)}, u32[]{:S(2)}) collective-permute-start(bf16[4,224,384]{2,1,0:T(8,128)(2,1)} %get-tuple-element.96), channel_id=1, source_target_pairs={{0,4},{1,3},{2,6},{3,1},{4,0},{5,7},{6,2},{7,5},{8,12},{9,11},{10,... | collective-permute-start | bytes 2064392 | tf_op jit(solution)/shard_map/cond/branch_1_fun/ppermute | solution.py:602
  77.0 18.6 %collective-permute-start.4 = (bf16[4,224,384]{2,1,0:T(8,128)(2,1)}, bf16[4,224,384]{2,1,0:T(8,128)(2,1)}, u32[]{:S(2)}, u32[]{:S(2)}) collective-permute-start(bf16[4,224,384]{2,1,0:T(8,128)(2,1)} %get-tuple-element.97), channel_id=1, source_target_pairs={{0,4},{1,3},{2,6},{3,1},{4,0},{5,7},{6,2},{7,5},{8,12},{9,11},{10,... | collective-permute-start | bytes 2064392 | tf_op jit(solution)/shard_map/cond/branch_1_fun/ppermute | solution.py:602
  130.8 30.3 %collective-permute-start.24 = (bf16[4,2,96,768]{3,2,1,0:T(8,128)(2,1)}, bf16[4,2,96,768]{3,2,1,0:T(8,128)(2,1)}, u32[]{:S(2)}, u32[]{:S(2)}) collective-permute-start(bf16[4,2,96,768]{3,2,1,0:T(8,128)(2,1)} %get-tuple-element.317), channel_id=1, source_target_pairs={{0,2},{1,5},{2,0},{3,7},{4,6},{5,1},{6,4},{7,3},{8,10},{9,13},{10,... | collective-permute-start | bytes 3538952 | tf_op jit(solution)/shard_map/ppermute | solution.py:602
  131.6 29.5 %collective-permute-start.25 = (bf16[2,4,2,48,768]{4,3,2,1,0:T(8,128)(2,1)}, bf16[2,4,2,48,768]{4,3,2,1,0:T(8,128)(2,1)}, u32[]{:S(2)}, u32[]{:S(2)}) collective-permute-start(bf16[2,4,2,48,768]{4,3,2,1,0:T(8,128)(2,1)} %get-tuple-element.319), channel_id=1, source_target_pairs={{0,2},{1,5},{2,0},{3,7},{4,6},{5,1},{6,4},{7,3},{8,10},{9,13},{10,... | collective-permute-start | bytes 3538952 | tf_op jit(solution)/shard_map/ppermute | solution.py:602
  164.7 22.3 %collective-permute-start.27 = (bf16[4,192,768]{2,1,0:T(8,128)(2,1)}, bf16[4,192,768]{2,1,0:T(8,128)(2,1)}, u32[]{:S(2)}, u32[]{:S(2)}) collective-permute-start(bf16[4,192,768]{2,1,0:T(8,128)(2,1)} %get-tuple-element.335), channel_id=1, source_target_pairs={{0,4},{1,3},{2,6},{3,1},{4,0},{5,7},{6,2},{7,5},{8,12},{9,11},{10,... | collective-permute-start | bytes 3538952 | tf_op jit(solution)/shard_map/ppermute | solution.py:602
  174.6 7.5 %collective-permute-start.5 = (bf16[4,4,208,384]{3,2,1,0:T(8,128)(2,1)}, bf16[4,4,208,384]{3,2,1,0:T(8,128)(2,1)}, u32[]{:S(2)}, u32[]{:S(2)}) collective-permute-start(bf16[4,4,208,384]{3,2,1,0:T(8,128)(2,1)} %get-tuple-element.109), channel_id=1, source_target_pairs={{0,1},{1,0},{2,3},{3,2},{4,5},{5,4},{6,7},{7,6},{8,9},{9,8},{10,11... | collective-permute-start | bytes 7667720 | tf_op jit(solution)/shard_map/cond/branch_1_fun/ppermute | solution.py:602
  185.8 18.4 %collective-permute-start.32 = (bf16[4,2,208,384]{3,2,1,0:T(8,128)(2,1)}, bf16[4,2,208,384]{3,2,1,0:T(8,128)(2,1)}, u32[]{:S(2)}, u32[]{:S(2)}) collective-permute-start(bf16[4,2,208,384]{3,2,1,0:T(8,128)(2,1)} %get-tuple-element.349), channel_id=1, source_target_pairs={{0,2},{1,5},{2,0},{3,7},{4,6},{5,1},{6,4},{7,3},{8,10},{9,13},{10,... | collective-permute-start | bytes 3833864 | tf_op jit(solution)/shard_map/ppermute | solution.py:602
  189.9 26.3 %collective-permute-start.28 = (bf16[192,768]{1,0:T(8,128)(2,1)}, bf16[192,768]{1,0:T(8,128)(2,1)}, u32[]{:S(2)}, u32[]{:S(2)}) collective-permute-start(bf16[192,768]{1,0:T(8,128)(2,1)} %get-tuple-element.345), channel_id=1, source_target_pairs={{0,8},{1,9},{2,10},{3,11},{4,12},{5,13},{6,14},{7,15},{8,0},{9,1},... | collective-permute-start | bytes 884744 | tf_op jit(solution)/shard_map/ppermute | solution.py:602
  191.9 24.2 %collective-permute-start.29 = (bf16[192,768]{1,0:T(8,128)(2,1)}, bf16[192,768]{1,0:T(8,128)(2,1)}, u32[]{:S(2)}, u32[]{:S(2)}) collective-permute-start(bf16[192,768]{1,0:T(8,128)(2,1)} %get-tuple-element.346), channel_id=1, source_target_pairs={{0,16},{1,17},{2,18},{3,19},{4,20},{5,21},{6,22},{7,23},{8,24},{9,... | collective-permute-start | bytes 884744 | tf_op jit(solution)/shard_map/ppermute | solution.py:602
  194.0 22.2 %collective-permute-start.30 = (bf16[192,768]{1,0:T(8,128)(2,1)}, bf16[192,768]{1,0:T(8,128)(2,1)}, u32[]{:S(2)}, u32[]{:S(2)}) collective-permute-start(bf16[192,768]{1,0:T(8,128)(2,1)} %get-tuple-element.347), channel_id=1, source_target_pairs={{0,24},{1,25},{2,26},{3,27},{4,28},{5,29},{6,30},{7,31},{8,16},{9,... | collective-permute-start | bytes 884744 | tf_op jit(solution)/shard_map/ppermute | solution.py:602
  206.8 15.0 %collective-permute-start.35 = (bf16[4,208,384]{2,1,0:T(8,128)(2,1)}, bf16[4,208,384]{2,1,0:T(8,128)(2,1)}, u32[]{:S(2)}, u32[]{:S(2)}) collective-permute-start(bf16[4,208,384]{2,1,0:T(8,128)(2,1)} %get-tuple-element.359), channel_id=1, source_target_pairs={{0,4},{1,3},{2,6},{3,1},{4,0},{5,7},{6,2},{7,5},{8,12},{9,11},{10,... | collective-permute-start | bytes 1916936 | tf_op jit(solution)/shard_map/ppermute | solution.py:602
  215.4 6.4 %collective-permute-start.36 = (f32[8,768]{1,0:T(8,128)}, f32[8,768]{1,0:T(8,128)}, u32[]{:S(2)}, u32[]{:S(2)}) collective-permute-start(f32[8,768]{1,0:T(8,128)} %add.16), channel_id=1, source_target_pairs={{0,16},{1,17},{2,18},{3,19},{4,20},{5,21},{6,22},{7,23},{8,24},{9,... | collective-permute-start | bytes 73736 | tf_op jit(solution)/shard_map/ppermute | solution.py:602
  224.0 13.9 %collective-permute-start.37 = (bf16[208,384]{1,0:T(8,128)(2,1)}, bf16[208,384]{1,0:T(8,128)(2,1)}, u32[]{:S(2)}, u32[]{:S(2)}) collective-permute-start(bf16[208,384]{1,0:T(8,128)(2,1)} %get-tuple-element.369), channel_id=1, source_target_pairs={{0,8},{1,9},{2,10},{3,11},{4,12},{5,13},{6,14},{7,15},{8,0},{9,1},... | collective-permute-start | bytes 479240 | tf_op jit(solution)/shard_map/ppermute | solution.py:602
  226.5 13.8 %collective-permute-start.38 = (bf16[208,384]{1,0:T(8,128)(2,1)}, bf16[208,384]{1,0:T(8,128)(2,1)}, u32[]{:S(2)}, u32[]{:S(2)}) collective-permute-start(bf16[208,384]{1,0:T(8,128)(2,1)} %get-tuple-element.370), channel_id=1, source_target_pairs={{0,16},{1,17},{2,18},{3,19},{4,20},{5,21},{6,22},{7,23},{8,24},{9,... | collective-permute-start | bytes 479240 | tf_op jit(solution)/shard_map/ppermute | solution.py:602
  227.0 13.2 %collective-permute-start.39 = (bf16[208,384]{1,0:T(8,128)(2,1)}, bf16[208,384]{1,0:T(8,128)(2,1)}, u32[]{:S(2)}, u32[]{:S(2)}) collective-permute-start(bf16[208,384]{1,0:T(8,128)(2,1)} %get-tuple-element.371), channel_id=1, source_target_pairs={{0,24},{1,25},{2,26},{3,27},{4,28},{5,29},{6,30},{7,31},{8,16},{9,... | collective-permute-start | bytes 479240 | tf_op jit(solution)/shard_map/ppermute | solution.py:602
  235.0 7.3 %collective-permute-start.34 = (f32[2,24,768]{2,1,0:T(8,128)}, f32[2,24,768]{2,1,0:T(8,128)}, u32[]{:S(2)}, u32[]{:S(2)}) collective-permute-start(f32[2,24,768]{2,1,0:T(8,128)} %get-tuple-element.358), channel_id=1, source_target_pairs={{0,1},{1,0},{2,3},{3,2},{4,5},{5,4},{6,7},{7,6},{8,9},{9,8},{10,11... | collective-permute-start | bytes 442376 | tf_op jit(solution)/shard_map/ppermute | solution.py:602
  (14 other events, 71.3 us)

commit v10 on v9

--- a/solution.py
+++ b/solution.py
@@ -174,7 +174,7 @@
         top = jnp.max(scores, axis=-1, keepdims=True)
         weights = jnp.exp(scores - top)
         sums = jnp.sum(weights, axis=-1, keepdims=True)
-        return (weights * (1.0 / sums)).astype(BF16), top + jnp.log(sums)
+        return (weights.astype(BF16), 1.0 / sums), top + jnp.log(sums)
 
     raw = {}
     probs = {}
@@ -188,7 +188,7 @@
             probs[turn - 1] = [pair[0] for pair in both]
         if turn >= 2:
             vp = v_ref[:, at(turn - 2)]
-            parts = [dot_nn(probs[turn - 2][side], half_of(vp, side)) for side in range(2)]
+            parts = [dot_nn(probs[turn - 2][side][0], half_of(vp, side)) * probs[turn - 2][side][1] for side in range(2)]
             mixed_ref[:, at(turn - 2)] = (parts[0] + parts[1]).astype(BF16)
     lse_ref[...] = lse
     resid = x_ref[...].astype(F32) + (dot_nn(mixed_ref[...], wo_ref[...]) + vec_ref[4:5, :])

time: 247 us -> 246 us (level)
  transfers between devices with their start and end apart: 43 -> 43, of which waited for: 17 -> 18; matrix products, arithmetic and copies ran while one was open for 2% -> 2% of each run, Pallas kernels for 39% -> 39%
where the time goes in v10:
time: 246 us
  Pallas kernels  138 us (56%)
  waiting for transfers between devices  55.4 us (23%)
  starting transfers between devices  42.9 us (17%)
  other arithmetic  7.74 us (3%)
    pallas_call x5, Pallas kernels, call_with(): pl.pallas_call(kernel, grid_spec=pltpu.PrefetchScalarGridSpec(num_scalar_...  67.5 us
    pallas_call x7, Pallas kernels, call(): pl.pallas_call(kernel, grid=grid, in_specs=ins, out_specs=out_specs, out_...  55.7 us
    ppermute x43, waiting for transfers between devices, swap(): return lax.ppermute(array, 'dp', flipped(lax.axis_size('dp'), change))  55.4 us
    ppermute x43, starting transfers between devices, swap(): return lax.ppermute(array, 'dp', flipped(lax.axis_size('dp'), change))  42.9 us
    pallas_call x7, Pallas kernels, small_call(): pl.pallas_call(kernel, in_specs=ins, out_specs=tuple((spec for spec, _ in...  15.2 us
  transfers between devices with their start and end apart: 43, of which 18 were waited for; matrix products, arithmetic and copies ran while one was open for 2% of the time, Pallas kernels for 39%

profile of v10, /device:TPU:0, one launch (start us, length us, event | category | flops | bytes accessed | tf_op | source)
XLA Modules:
  0.0 245.6 jit_solution(7938674657621458662)
XLA Ops:
  6.4 2.9 %collective-permute-start.19 = (bf16[1,80,768]{2,1,0:T(8,128)(2,1)}, bf16[1,80,768]{2,1,0:T(8,128)(2,1)S(1)}, u32[]{:S(2)}, u32[]{:S(2)}) collective-permute-start(bf16[1,80,768]{2,1,0:T(8,128)(2,1)} %bitcast.27), channel_id=1, source_target_pairs={{0,8},{1,9},{2,10},{3,11},{4,12},{5,13},{6,14},{7,15},{8,0},{9,1},... | collective-permute-start | bytes 368648 | tf_op jit(solution)/shard_map/ppermute | solution.py:602
  9.4 4.0 %collective-permute-start.17 = (bf16[208,384]{1,0:T(8,128)(2,1)}, bf16[208,384]{1,0:T(8,128)(2,1)S(1)}, u32[]{:S(2)}, u32[]{:S(2)}) collective-permute-start(bf16[208,384]{1,0:T(8,128)(2,1)} %get-tuple-element.267), channel_id=1, source_target_pairs={{0,24},{1,25},{2,26},{3,27},{4,28},{5,29},{6,30},{7,31},{8,16},{9,... | collective-permute-start | bytes 479240 | tf_op jit(solution)/shard_map/ppermute | solution.py:602
  14.9 15.3 %conditional.6 = (bf16[8,80,768]{2,1,0:T(8,128)(2,1)S(1)}) conditional(s32[]{:T(128)} %convert_element_type.4, () %tuple.81, bf16[2,80,768]{2,1,0:T(8,128)(2,1)S(1)} %pad_maximum_fusion.5), branch_computations={%region_0.0_spmd, %region_1.0_spmd} | conditional | flops 1228800 | bytes 5898328 | solution.py:847
  16.7 4.5 %collective-permute-done.6 = bf16[2,80,768]{2,1,0:T(8,128)(2,1)S(1)} collective-permute-done((bf16[2,80,768]{2,1,0:T(8,128)(2,1)S(1)}, bf16[2,80,768]{2,1,0:T(8,128)(2,1)S(1)}, u32[]{:S(2)}, u32[]{:S(2)}) %collective-permute-start.6) | collective-permute-done | bytes 245792 | tf_op jit(solution)/shard_map/cond/branch_1_fun/ppermute | solution.py:602
  23.0 7.1 %collective-permute-done.7 = bf16[4,80,768]{2,1,0:T(8,128)(2,1)S(1)} collective-permute-done((bf16[4,80,768]{2,1,0:T(8,128)(2,1)S(1)}, bf16[4,80,768]{2,1,0:T(8,128)(2,1)S(1)}, u32[]{:S(2)}, u32[]{:S(2)}) %collective-permute-start.7) | collective-permute-done | bytes 491552 | tf_op jit(solution)/shard_map/cond/branch_1_fun/ppermute | solution.py:602
  32.2 2.8 %collective-permute-start.20 = (bf16[2,224,384]{2,1,0:T(8,128)(2,1)}, bf16[2,224,384]{2,1,0:T(8,128)(2,1)}, u32[]{:S(2)}, u32[]{:S(2)}) collective-permute-start(bf16[2,224,384]{2,1,0:T(8,128)(2,1)} %pad_maximum_fusion.4), channel_id=1, source_target_pairs={{0,16},{1,17},{2,18},{3,19},{4,20},{5,21},{6,22},{7,23},{8,24},{9,... | collective-permute-start | bytes 1032200 | tf_op jit(solution)/shard_map/ppermute | solution.py:602
  35.0 14.5 %conditional.7 = (bf16[4,208,384]{2,1,0:T(8,128)(2,1)}, bf16[4,208,384]{2,1,0:T(8,128)(2,1)}, bf16[1024,768]{1,0:T(8,128)(2,1)}, f32[8,768]{1,0:T(8,128)}) conditional(s32[]{:T(128)} %convert_element_type.4, () %tuple.86, (bf16[4,208,384]{2,1,0:T(8,128)(2,1)}, bf16[1024,768]{1,0:T(8,128)(2,1)}, s32[4,5]{1,0:T(4,128)}) %tuple.87), branch_computations={%region_2.0_spmd, %region_3.0_spmd} | conditional | bytes 5111921 | solution.py:847
  38.0 3.8 %mask_grads.1 = (bf16[1024,768]{1,0:T(8,128)(2,1)}, f32[8,768]{1,0:T(8,128)}) custom-call(s32[4,5]{1,0:T(4,128)} %get-tuple-element.71.lengths_ref, bf16[1024,768]{1,0:T(8,128)(2,1)} %get-tuple-element.73.grad_ref), custom_call_target="tpu_custom_call" | custom-call | bytes 1 | tf_op jit(solution)/shard_map/cond/branch_1_fun/mask_grads/pallas_call | solution.py:561
  41.8 7.7 %collective-permute-done = bf16[4,208,384]{2,1,0:T(8,128)(2,1)} collective-permute-done((bf16[4,208,384]{2,1,0:T(8,128)(2,1)}, bf16[4,208,384]{2,1,0:T(8,128)(2,1)}, u32[]{:S(2)}, u32[]{:S(2)}) %collective-permute-start) | collective-permute-done | bytes 639008 | tf_op jit(solution)/shard_map/cond/branch_1_fun/ppermute | solution.py:602
  50.0 14.6 %conditional.8 = (bf16[4,208,384]{2,1,0:T(8,128)(2,1)}, bf16[4,208,384]{2,1,0:T(8,128)(2,1)}, bf16[4,208,384]{2,1,0:T(8,128)(2,1)}, bf16[4,208,384]{2,1,0:T(8,12...) conditional(s32[]{:T(128)} %convert_element_type.4, () %tuple.88, ...), branch_computations={%region_4.0_spmd, %region_5.0_spmd} | conditional | flops 344064 | bytes 20447528 | solution.py:847
  51.0 3.6 %collective-permute-done.9 = bf16[4,208,384]{2,1,0:T(8,128)(2,1)} collective-permute-done((bf16[4,208,384]{2,1,0:T(8,128)(2,1)}, bf16[4,208,384]{2,1,0:T(8,128)(2,1)}, u32[]{:S(2)}, u32[]{:S(2)}) %collective-permute-start.9) | collective-permute-done | bytes 639008 | tf_op jit(solution)/shard_map/cond/branch_1_fun/ppermute | solution.py:602
  55.6 5.7 %collective-permute-done.8 = bf16[4,208,384]{2,1,0:T(8,128)(2,1)} collective-permute-done((bf16[4,208,384]{2,1,0:T(8,128)(2,1)}, bf16[4,208,384]{2,1,0:T(8,128)(2,1)}, u32[]{:S(2)}, u32[]{:S(2)}) %collective-permute-start.8) | collective-permute-done | bytes 639008 | tf_op jit(solution)/shard_map/cond/branch_1_fun/ppermute | solution.py:602
  66.1 10.4 %project.1 = (bf16[1024,768]{1,0:T(8,128)(2,1)}, bf16[1024,768]{1,0:T(8,128)(2,1)}, bf16[1024,768]{1,0:T(8,128)(2,1)}, bf16[1024,768]{1,0:T(8,128)(2,1)}, bf16[7...) custom-call(s32[1]{0:T(128)} %bitcast.1.me_ref, ...), custom_call_target="tpu_custom_call" | custom-call | flops 8999999488 | bytes 1 | tf_op jit(solution)/shard_map/project/pallas_call | solution.py:576
  76.5 18.7 %conditional.9 = (bf16[1024,768]{1,0:T(8,128)(2,1)}, f32[1024,128]{1,0:T(8,128)}, f32[1024,768]{1,0:T(8,128)}, bf16[1024,768]{1,0:T(8,128)(2,1)}, bf16[1024,768]...) conditional(s32[]{:T(128)} %convert_element_type.4, () %tuple.92, ...), branch_computations={%region_6.0_spmd, %region_7.0_spmd} | conditional | flops 4 | bytes 11796699 | solution.py:847
  78.6 11.5 %attention_forward.1 = (bf16[1024,768]{1,0:T(8,128)(2,1)}, f32[1024,128]{1,0:T(8,128)}, f32[1024,768]{1,0:T(8,128)}, bf16[1024,768]{1,0:T(8,128)(2,1)}) custom-call(s32[4,5]{1,0:T(4,128)} %get-tuple-element.85.lengths_ref, bf16[1024,768]{1,0:T(8,128)(2,1)} %get-tuple-element.86.x_ref, f32[16,768]{1,0:T(8,128)} %get-tuple-element.87.vec_ref, ...), custom_call_target="tpu_custom_call" | custom-call | bytes 1 | tf_op jit(solution)/shard_map/cond/branch_1_fun/attention_forward/pallas_call | solution.py:561
  90.1 3.8 %conditional = (bf16[1024,768]{1,0:T(8,128)(2,1)}) conditional(s32[]{:T(128)} %convert_element_type.0, () %tuple.40, bf16[1024,768]{1,0:T(8,128)(2,1)} %get-tuple-element.428), branch_computations={%region_8.0_spmd, %region_9.0_spmd} | conditional | bytes 6291504 | solution.py:847
  90.2 3.7 %collective-permute-done.2 = bf16[1024,768]{1,0:T(8,128)(2,1)} collective-permute-done((bf16[1024,768]{1,0:T(8,128)(2,1)}, bf16[1024,768]{1,0:T(8,128)(2,1)}, u32[]{:S(2)}, u32[]{:S(2)}) %collective-permute-start.2) | collective-permute-done | bytes 1572896 | tf_op jit(solution)/shard_map/cond/branch_1_fun/cond/branch_1_fun/ppermute | solution.py:602
  95.2 34.8 %mlp.1 = (bf16[1024,1536]{1,0:T(8,128)(2,1)}, bf16[1024,1536]{1,0:T(8,128)(2,1)}, f32[1024,768]{1,0:T(8,128)}, bf16[1024,768]{1,0:T(8,128)(2,1)}, bf16[4,2,96,76...) custom-call(s32[1]{0:T(128)} %bitcast.1.me_ref, ...), custom_call_target="tpu_custom_call" | custom-call | bytes 1 | tf_op jit(solution)/shard_map/mlp/pallas_call | solution.py:576
  133.8 20.7 %attention_backward.1 = (bf16[4,1024,768]{2,1,0:T(8,128)(2,1)}, f32[1024,768]{1,0:T(8,128)}, f32[8,768]{1,0:T(8,128)}) custom-call(s32[4,5]{1,0:T(4,128)} %lengths_ref.1, bf16[1024,768]{1,0:T(8,128)(2,1)} %get-tuple-element.297.q_ref, bf16[1024,768]{1,0:T(8,128)(2,1)} %get-tuple-element.298.k_ref, bf16[1024,768]{1,0:T(8,128)(2,1)} %get-tuple-element.299.v_ref, ...), custom_call_target="tpu_custom_call" | custom-call | bytes 1 | tf_op jit(solution)/shard_map/attention_backward/pallas_call | solution.py:561
  154.5 5.8 %mlp_out_other.1 = bf16[1024,768]{1,0:T(8,128)(2,1)} custom-call(s32[1]{0:T(128)} %bitcast.1.me_ref, bf16[1024,1536]{1,0:T(8,128)(2,1)} %get-tuple-element.321.act_ref, bf16[1536,768]{1,0:T(8,128)(2,1)} %get-tuple-element.322.wdown_ref), custom_call_target="tpu_custom_call" | custom-call | bytes 1 | tf_op jit(solution)/shard_map/mlp_out_other/pallas_call | solution.py:576
  160.4 3.6 %merge_first.2 = (bf16[4,192,768]{2,1,0:T(8,128)(2,1)}, bf16[4,192,768]{2,1,0:T(8,128)(2,1)}) custom-call(bf16[1,4,2,96,768]{4,3,2,1,0:T(8,128)(2,1)} %bitcast.20, bf16[1,4,2,96,768]{4,3,2,1,0:T(8,128)(2,1)} %bitcast.18.refs_1_, bf16[2,4,2,48,768]{4,3,2,1,0:T(8,128)(2,1)} %get-tuple-element.325.refs_2_, ...), custom_call_target="tpu_custom_call" | custom-call | bytes 1 | tf_op jit(solution)/shard_map/merge_first/pallas_call | solution.py:561
  164.6 20.5 %conditional.10 = (bf16[1,4,2,208,384]{4,3,2,1,0:T(8,128)(2,1)}, bf16[4,2,208,384]{3,2,1,0:T(8,128)(2,1)}, bf16[1024,768]{1,0:T(8,128)(2,1)}) conditional(s32[]{:T(128)} %convert_element_type.4, () %tuple.80, (s32[1]{0:T(128)}, bf16[1024,768]{1,0:T(8,128)(2,1)}, bf16[1024,768]{1,0:T(8,128)(2,1)}, bf16[4,1024,768]{2,1,0:T(8,128)(2,1)}, ...), branch_computations={%region_10.0_spmd, %region_11.0_spmd} | conditional | bytes 10223683 | solution.py:847
  164.6 9.4 %weight_grads.1 = (bf16[4,4,208,384]{3,2,1,0:T(8,128)(2,1)}, bf16[4,4,208,384]{3,2,1,0:T(8,128)(2,1)}) custom-call(s32[1]{0:T(128)} %get-tuple-element.101.me_ref, bf16[1024,768]{1,0:T(8,128)(2,1)} %get-tuple-element.102.n1_ref, bf16[1024,768]{1,0:T(8,128)(2,1)} %get-tuple-element.103.mixed_hbm, bf16[4,1024,768]{2,1,0:T(8,128)(2,1)} %get-tuple-element.104.columns_ref, ...), custom_call_target="tpu_custom_call" | custom-call | bytes 1 | tf_op jit(solution)/shard_map/cond/branch_1_fun/weight_grads/pallas_call | solution.py:576
  174.4 7.1 %mlp_out_own.1 = bf16[1024,768]{1,0:T(8,128)(2,1)} custom-call(s32[1]{0:T(128)} %get-tuple-element.101.me_ref, f32[1024,768]{1,0:T(8,128)} %get-tuple-element.110.resid_ref, f32[16,768]{1,0:T(8,128)} %get-tuple-element.111.vec_ref, bf16[1024,1536]{1,0:T(8,128)(2,1)} %get-tuple-element.112.act_ref, bf16[1024,768]{1,0:T(8,128)(2,1)} %get-tuple-element.114.take_ref, ...), custom_call_target="tpu_custom_call" | custom-call | bytes 1 | tf_op jit(solution)/shard_map/cond/branch_1_fun/mlp_out_own/pallas_call | solution.py:576
  181.5 3.7 %merge_core.1 = (bf16[4,2,208,384]{3,2,1,0:T(8,128)(2,1)}, bf16[4,2,208,384]{3,2,1,0:T(8,128)(2,1)}) custom-call(s32[1]{0:T(128)} %get-tuple-element.100.core_ref, bf16[4,4,208,384]{3,2,1,0:T(8,128)(2,1)} %get-tuple-element.108.keep_ref, bf16[4,4,208,384]{3,2,1,0:T(8,128)(2,1)} %collective-permute-done.5.take_ref), custom_call_target="tpu_custom_call" | custom-call | bytes 1 | tf_op jit(solution)/shard_map/cond/branch_1_fun/merge_core/pallas_call | solution.py:561
  186.4 2.8 %merge_second.2 = (f32[192,768]{1,0:T(8,128)}, bf16[192,768]{1,0:T(8,128)(2,1)}, bf16[192,768]{1,0:T(8,128)(2,1)}, bf16[192,768]{1,0:T(8,128)(2,1)}) custom-call(bf16[4,192,768]{2,1,0:T(8,128)(2,1)} %get-tuple-element.337.own_ref, bf16[4,192,768]{2,1,0:T(8,128)(2,1)} %collective-permute-done.27.take_ref), custom_call_target="tpu_custom_call" | custom-call | bytes 1 | tf_op jit(solution)/shard_map/merge_second/pallas_call | solution.py:692
  193.7 9.8 %tokens_backward.1 = (bf16[1024,768]{1,0:T(8,128)(2,1)}, f32[8,768]{1,0:T(8,128)}) custom-call(bf16[1024,768]{1,0:T(8,128)(2,1)} %x_ref.3, f32[1024,768]{1,0:T(8,128)} %get-tuple-element.340.gresid_ref, f32[16,768]{1,0:T(8,128)} %get-tuple-element.296.vec_ref, bf16[4,1024,768]{2,1,0:T(8,128)(2,1)} %get-tuple-element.328.grads_ref, ...), custom_call_target="tpu_custom_call" | custom-call | flops 11500000256 | bytes 1 | tf_op jit(solution)/shard_map/tokens_backward/pallas_call | solution.py:561
  203.5 2.6 %merge_first.3 = (bf16[4,208,384]{2,1,0:T(8,128)(2,1)}, bf16[4,208,384]{2,1,0:T(8,128)(2,1)}) custom-call(bf16[1,4,2,208,384]{4,3,2,1,0:T(8,128)(2,1)} %get-tuple-element.336.refs_0_, bf16[1,4,2,208,384]{4,3,2,1,0:T(8,128)(2,1)} %bitcast.19.refs_1_), custom_call_target="tpu_custom_call" | custom-call | bytes 1 | tf_op jit(solution)/shard_map/merge_first/pallas_call | solution.py:561
  210.8 3.2 %collective-permute-done.33 = f32[8,768]{1,0:T(8,128)S(1)} collective-permute-done((f32[8,768]{1,0:T(8,128)S(1)}, f32[8,768]{1,0:T(8,128)S(1)}, u32[]{:S(2)}, u32[]{:S(2)}) %collective-permute-start.33) | collective-permute-done | bytes 24608 | tf_op jit(solution)/shard_map/ppermute | solution.py:602
  217.7 3.4 %collective-permute-done.36 = f32[8,768]{1,0:T(8,128)} collective-permute-done((f32[8,768]{1,0:T(8,128)}, f32[8,768]{1,0:T(8,128)}, u32[]{:S(2)}, u32[]{:S(2)}) %collective-permute-start.36) | collective-permute-done | bytes 24608 | tf_op jit(solution)/shard_map/ppermute | solution.py:602
  223.3 2.5 %collective-permute-start.37 = (bf16[208,384]{1,0:T(8,128)(2,1)}, bf16[208,384]{1,0:T(8,128)(2,1)}, u32[]{:S(2)}, u32[]{:S(2)}) collective-permute-start(bf16[208,384]{1,0:T(8,128)(2,1)} %get-tuple-element.369), channel_id=1, source_target_pairs={{0,8},{1,9},{2,10},{3,11},{4,12},{5,13},{6,14},{7,15},{8,0},{9,1},... | collective-permute-start | bytes 479240 | tf_op jit(solution)/shard_map/ppermute | solution.py:602
  230.1 2.7 %collective-permute-done.40 = f32[8,768]{1,0:T(8,128)S(1)} collective-permute-done((f32[8,768]{1,0:T(8,128)S(1)}, f32[8,768]{1,0:T(8,128)S(1)}, u32[]{:S(2)}, u32[]{:S(2)}) %collective-permute-start.40) | collective-permute-done | bytes 24608 | tf_op jit(solution)/shard_map/ppermute | solution.py:602
  (96 shorter events, 64.7 us)
Async XLA Ops:
  6.4 7.6 %collective-permute-start.19 = (bf16[1,80,768]{2,1,0:T(8,128)(2,1)}, bf16[1,80,768]{2,1,0:T(8,128)(2,1)S(1)}, u32[]{:S(2)}, u32[]{:S(2)}) collective-permute-start(bf16[1,80,768]{2,1,0:T(8,128)(2,1)} %bitcast.27), channel_id=1, source_target_pairs={{0,8},{1,9},{2,10},{3,11},{4,12},{5,13},{6,14},{7,15},{8,0},{9,1},... | collective-permute-start | bytes 368648 | tf_op jit(solution)/shard_map/ppermute | solution.py:602
  9.3 20.9 %collective-permute-start.18 = (bf16[224,384]{1,0:T(8,128)(2,1)}, bf16[224,384]{1,0:T(8,128)(2,1)S(1)}, u32[]{:S(2)}, u32[]{:S(2)}) collective-permute-start(bf16[224,384]{1,0:T(8,128)(2,1)} %get-tuple-element.268), channel_id=1, source_target_pairs={{0,8},{1,9},{2,10},{3,11},{4,12},{5,13},{6,14},{7,15},{8,0},{9,1},... | collective-permute-start | bytes 516104 | tf_op jit(solution)/shard_map/ppermute | solution.py:602
  9.4 20.8 %collective-permute-start.17 = (bf16[208,384]{1,0:T(8,128)(2,1)}, bf16[208,384]{1,0:T(8,128)(2,1)S(1)}, u32[]{:S(2)}, u32[]{:S(2)}) collective-permute-start(bf16[208,384]{1,0:T(8,128)(2,1)} %get-tuple-element.267), channel_id=1, source_target_pairs={{0,24},{1,25},{2,26},{3,27},{4,28},{5,29},{6,30},{7,31},{8,16},{9,... | collective-permute-start | bytes 479240 | tf_op jit(solution)/shard_map/ppermute | solution.py:602
  13.4 16.9 %collective-permute-start.16 = (bf16[208,384]{1,0:T(8,128)(2,1)}, bf16[208,384]{1,0:T(8,128)(2,1)S(1)}, u32[]{:S(2)}, u32[]{:S(2)}) collective-permute-start(bf16[208,384]{1,0:T(8,128)(2,1)} %get-tuple-element.267), channel_id=1, source_target_pairs={{0,16},{1,17},{2,18},{3,19},{4,20},{5,21},{6,22},{7,23},{8,24},{9,... | collective-permute-start | bytes 479240 | tf_op jit(solution)/shard_map/ppermute | solution.py:602
  13.4 16.9 %collective-permute-start.15 = (bf16[208,384]{1,0:T(8,128)(2,1)}, bf16[208,384]{1,0:T(8,128)(2,1)S(1)}, u32[]{:S(2)}, u32[]{:S(2)}) collective-permute-start(bf16[208,384]{1,0:T(8,128)(2,1)} %get-tuple-element.267), channel_id=1, source_target_pairs={{0,8},{1,9},{2,10},{3,11},{4,12},{5,13},{6,14},{7,15},{8,0},{9,1},... | collective-permute-start | bytes 479240 | tf_op jit(solution)/shard_map/ppermute | solution.py:602
  14.9 6.3 %collective-permute-start.6 = (bf16[2,80,768]{2,1,0:T(8,128)(2,1)S(1)}, bf16[2,80,768]{2,1,0:T(8,128)(2,1)S(1)}, u32[]{:S(2)}, u32[]{:S(2)}) collective-permute-start(bf16[2,80,768]{2,1,0:T(8,128)(2,1)S(1)} %param.1), channel_id=1, source_target_pairs={{0,2},{1,5},{2,0},{3,7},{4,6},{5,1},{6,4},{7,3},{8,10},{9,13},{10,... | collective-permute-start | bytes 737288 | tf_op jit(solution)/shard_map/cond/branch_1_fun/ppermute | solution.py:602
  21.2 8.9 %collective-permute-start.7 = (bf16[4,80,768]{2,1,0:T(8,128)(2,1)S(1)}, bf16[4,80,768]{2,1,0:T(8,128)(2,1)S(1)}, u32[]{:S(2)}, u32[]{:S(2)}) collective-permute-start(bf16[4,80,768]{2,1,0:T(8,128)(2,1)S(1)} %pad_maximum_fusion.1), channel_id=1, source_target_pairs={{0,4},{1,3},{2,6},{3,1},{4,0},{5,7},{6,2},{7,5},{8,12},{9,11},{10,... | collective-permute-start | bytes 1474568 | tf_op jit(solution)/shard_map/cond/branch_1_fun/ppermute | solution.py:602
  32.2 17.3 %collective-permute-start.20 = (bf16[2,224,384]{2,1,0:T(8,128)(2,1)}, bf16[2,224,384]{2,1,0:T(8,128)(2,1)}, u32[]{:S(2)}, u32[]{:S(2)}) collective-permute-start(bf16[2,224,384]{2,1,0:T(8,128)(2,1)} %pad_maximum_fusion.4), channel_id=1, source_target_pairs={{0,16},{1,17},{2,18},{3,19},{4,20},{5,21},{6,22},{7,23},{8,24},{9,... | collective-permute-start | bytes 1032200 | tf_op jit(solution)/shard_map/ppermute | solution.py:602
  35.0 14.5 %collective-permute-start = (bf16[4,208,384]{2,1,0:T(8,128)(2,1)}, bf16[4,208,384]{2,1,0:T(8,128)(2,1)}, u32[]{:S(2)}, u32[]{:S(2)}) collective-permute-start(bf16[4,208,384]{2,1,0:T(8,128)(2,1)} %get-tuple-element.70), channel_id=1, source_target_pairs={{0,2},{1,5},{2,0},{3,7},{4,6},{5,1},{6,4},{7,3},{8,10},{9,13},{10,... | collective-permute-start | bytes 1916936 | tf_op jit(solution)/shard_map/cond/branch_1_fun/ppermute | solution.py:602
  36.5 13.0 %collective-permute-start.1 = (bf16[4,208,384]{2,1,0:T(8,128)(2,1)}, bf16[4,208,384]{2,1,0:T(8,128)(2,1)}, u32[]{:S(2)}, u32[]{:S(2)}) collective-permute-start(bf16[4,208,384]{2,1,0:T(8,128)(2,1)} %get-tuple-element.70), channel_id=1, source_target_pairs={{0,4},{1,3},{2,6},{3,1},{4,0},{5,7},{6,2},{7,5},{8,12},{9,11},{10,... | collective-permute-start | bytes 1916936 | tf_op jit(solution)/shard_map/cond/branch_1_fun/ppermute | solution.py:602
  49.4 45.8 %collective-permute-start.22 = (bf16[8,80,768]{2,1,0:T(8,128)(2,1)}, bf16[8,80,768]{2,1,0:T(8,128)(2,1)}, u32[]{:S(2)}, u32[]{:S(2)}) collective-permute-start(bf16[8,80,768]{2,1,0:T(8,128)(2,1)} %copy-done), channel_id=1, source_target_pairs={{0,16},{1,17},{2,18},{3,19},{4,20},{5,21},{6,22},{7,23},{8,24},{9,... | collective-permute-start | bytes 2949128 | tf_op jit(solution)/shard_map/ppermute | solution.py:602
  50.0 14.6 %collective-permute-start.13 = (bf16[1024,768]{1,0:T(8,128)(2,1)}, bf16[1024,768]{1,0:T(8,128)(2,1)}, u32[]{:S(2)}, u32[]{:S(2)}) collective-permute-start(bf16[1024,768]{1,0:T(8,128)(2,1)} %get-tuple-element.82), channel_id=1, source_target_pairs={{0,1},{1,0},{2,3},{3,2},{4,5},{5,4},{6,7},{7,6},{8,9},{9,8},{10,11... | collective-permute-start | bytes 4718600 | tf_op jit(solution)/shard_map/cond/branch_1_fun/ppermute | solution.py:602
  50.0 4.7 %collective-permute-start.9 = (bf16[4,208,384]{2,1,0:T(8,128)(2,1)}, bf16[4,208,384]{2,1,0:T(8,128)(2,1)}, u32[]{:S(2)}, u32[]{:S(2)}) collective-permute-start(bf16[4,208,384]{2,1,0:T(8,128)(2,1)} %get-tuple-element.78), channel_id=1, source_target_pairs={{0,1},{1,0},{2,3},{3,2},{4,5},{5,4},{6,7},{7,6},{8,9},{9,8},{10,11... | collective-permute-start | bytes 1916936 | tf_op jit(solution)/shard_map/cond/branch_1_fun/ppermute | solution.py:602
  50.5 5.1 %collective-permute-start.10 = (bf16[4,208,384]{2,1,0:T(8,128)(2,1)}, bf16[4,208,384]{2,1,0:T(8,128)(2,1)}, u32[]{:S(2)}, u32[]{:S(2)}) collective-permute-start(bf16[4,208,384]{2,1,0:T(8,128)(2,1)} %get-tuple-element.77), channel_id=1, source_target_pairs={{0,1},{1,0},{2,3},{3,2},{4,5},{5,4},{6,7},{7,6},{8,9},{9,8},{10,11... | collective-permute-start | bytes 1916936 | tf_op jit(solution)/shard_map/cond/branch_1_fun/ppermute | solution.py:602
  50.5 10.7 %collective-permute-start.8 = (bf16[4,208,384]{2,1,0:T(8,128)(2,1)}, bf16[4,208,384]{2,1,0:T(8,128)(2,1)}, u32[]{:S(2)}, u32[]{:S(2)}) collective-permute-start(bf16[4,208,384]{2,1,0:T(8,128)(2,1)} %get-tuple-element.77), channel_id=1, source_target_pairs={{0,4},{1,3},{2,6},{3,1},{4,0},{5,7},{6,2},{7,5},{8,12},{9,11},{10,... | collective-permute-start | bytes 1916936 | tf_op jit(solution)/shard_map/cond/branch_1_fun/ppermute | solution.py:602
  64.6 11.9 %collective-permute-start.21 = (bf16[4,224,384]{2,1,0:T(8,128)(2,1)}, bf16[4,224,384]{2,1,0:T(8,128)(2,1)}, u32[]{:S(2)}, u32[]{:S(2)}) collective-permute-start(bf16[4,224,384]{2,1,0:T(8,128)(2,1)} %get-tuple-element.301.refs_5_), channel_id=1, source_target_pairs={{0,2},{1,5},{2,0},{3,7},{4,6},{5,1},{6,4},{7,3},{8,10},{9,13},{10,... | collective-permute-start | bytes 2064392 | tf_op jit(solution)/shard_map/ppermute | solution.py:602
  76.5 17.5 %collective-permute-start.3 = (bf16[4,224,384]{2,1,0:T(8,128)(2,1)}, bf16[4,224,384]{2,1,0:T(8,128)(2,1)}, u32[]{:S(2)}, u32[]{:S(2)}) collective-permute-start(bf16[4,224,384]{2,1,0:T(8,128)(2,1)} %get-tuple-element.96), channel_id=1, source_target_pairs={{0,4},{1,3},{2,6},{3,1},{4,0},{5,7},{6,2},{7,5},{8,12},{9,11},{10,... | collective-permute-start | bytes 2064392 | tf_op jit(solution)/shard_map/cond/branch_1_fun/ppermute | solution.py:602
  77.1 18.1 %collective-permute-start.4 = (bf16[4,224,384]{2,1,0:T(8,128)(2,1)}, bf16[4,224,384]{2,1,0:T(8,128)(2,1)}, u32[]{:S(2)}, u32[]{:S(2)}) collective-permute-start(bf16[4,224,384]{2,1,0:T(8,128)(2,1)} %get-tuple-element.97), channel_id=1, source_target_pairs={{0,4},{1,3},{2,6},{3,1},{4,0},{5,7},{6,2},{7,5},{8,12},{9,11},{10,... | collective-permute-start | bytes 2064392 | tf_op jit(solution)/shard_map/cond/branch_1_fun/ppermute | solution.py:602
  130.1 30.4 %collective-permute-start.24 = (bf16[4,2,96,768]{3,2,1,0:T(8,128)(2,1)}, bf16[4,2,96,768]{3,2,1,0:T(8,128)(2,1)}, u32[]{:S(2)}, u32[]{:S(2)}) collective-permute-start(bf16[4,2,96,768]{3,2,1,0:T(8,128)(2,1)} %get-tuple-element.317), channel_id=1, source_target_pairs={{0,2},{1,5},{2,0},{3,7},{4,6},{5,1},{6,4},{7,3},{8,10},{9,13},{10,... | collective-permute-start | bytes 3538952 | tf_op jit(solution)/shard_map/ppermute | solution.py:602
  130.9 29.6 %collective-permute-start.25 = (bf16[2,4,2,48,768]{4,3,2,1,0:T(8,128)(2,1)}, bf16[2,4,2,48,768]{4,3,2,1,0:T(8,128)(2,1)}, u32[]{:S(2)}, u32[]{:S(2)}) collective-permute-start(bf16[2,4,2,48,768]{4,3,2,1,0:T(8,128)(2,1)} %get-tuple-element.319), channel_id=1, source_target_pairs={{0,2},{1,5},{2,0},{3,7},{4,6},{5,1},{6,4},{7,3},{8,10},{9,13},{10,... | collective-permute-start | bytes 3538952 | tf_op jit(solution)/shard_map/ppermute | solution.py:602
  164.1 22.3 %collective-permute-start.27 = (bf16[4,192,768]{2,1,0:T(8,128)(2,1)}, bf16[4,192,768]{2,1,0:T(8,128)(2,1)}, u32[]{:S(2)}, u32[]{:S(2)}) collective-permute-start(bf16[4,192,768]{2,1,0:T(8,128)(2,1)} %get-tuple-element.335), channel_id=1, source_target_pairs={{0,4},{1,3},{2,6},{3,1},{4,0},{5,7},{6,2},{7,5},{8,12},{9,11},{10,... | collective-permute-start | bytes 3538952 | tf_op jit(solution)/shard_map/ppermute | solution.py:602
  174.0 7.5 %collective-permute-start.5 = (bf16[4,4,208,384]{3,2,1,0:T(8,128)(2,1)}, bf16[4,4,208,384]{3,2,1,0:T(8,128)(2,1)}, u32[]{:S(2)}, u32[]{:S(2)}) collective-permute-start(bf16[4,4,208,384]{3,2,1,0:T(8,128)(2,1)} %get-tuple-element.109), channel_id=1, source_target_pairs={{0,1},{1,0},{2,3},{3,2},{4,5},{5,4},{6,7},{7,6},{8,9},{9,8},{10,11... | collective-permute-start | bytes 7667720 | tf_op jit(solution)/shard_map/cond/branch_1_fun/ppermute | solution.py:602
  185.1 18.4 %collective-permute-start.32 = (bf16[4,2,208,384]{3,2,1,0:T(8,128)(2,1)}, bf16[4,2,208,384]{3,2,1,0:T(8,128)(2,1)}, u32[]{:S(2)}, u32[]{:S(2)}) collective-permute-start(bf16[4,2,208,384]{3,2,1,0:T(8,128)(2,1)} %get-tuple-element.349), channel_id=1, source_target_pairs={{0,2},{1,5},{2,0},{3,7},{4,6},{5,1},{6,4},{7,3},{8,10},{9,13},{10,... | collective-permute-start | bytes 3833864 | tf_op jit(solution)/shard_map/ppermute | solution.py:602
  189.2 26.2 %collective-permute-start.28 = (bf16[192,768]{1,0:T(8,128)(2,1)}, bf16[192,768]{1,0:T(8,128)(2,1)}, u32[]{:S(2)}, u32[]{:S(2)}) collective-permute-start(bf16[192,768]{1,0:T(8,128)(2,1)} %get-tuple-element.345), channel_id=1, source_target_pairs={{0,8},{1,9},{2,10},{3,11},{4,12},{5,13},{6,14},{7,15},{8,0},{9,1},... | collective-permute-start | bytes 884744 | tf_op jit(solution)/shard_map/ppermute | solution.py:602
  191.3 24.2 %collective-permute-start.29 = (bf16[192,768]{1,0:T(8,128)(2,1)}, bf16[192,768]{1,0:T(8,128)(2,1)}, u32[]{:S(2)}, u32[]{:S(2)}) collective-permute-start(bf16[192,768]{1,0:T(8,128)(2,1)} %get-tuple-element.346), channel_id=1, source_target_pairs={{0,16},{1,17},{2,18},{3,19},{4,20},{5,21},{6,22},{7,23},{8,24},{9,... | collective-permute-start | bytes 884744 | tf_op jit(solution)/shard_map/ppermute | solution.py:602
  193.3 22.1 %collective-permute-start.30 = (bf16[192,768]{1,0:T(8,128)(2,1)}, bf16[192,768]{1,0:T(8,128)(2,1)}, u32[]{:S(2)}, u32[]{:S(2)}) collective-permute-start(bf16[192,768]{1,0:T(8,128)(2,1)} %get-tuple-element.347), channel_id=1, source_target_pairs={{0,24},{1,25},{2,26},{3,27},{4,28},{5,29},{6,30},{7,31},{8,16},{9,... | collective-permute-start | bytes 884744 | tf_op jit(solution)/shard_map/ppermute | solution.py:602
  206.1 15.0 %collective-permute-start.35 = (bf16[4,208,384]{2,1,0:T(8,128)(2,1)}, bf16[4,208,384]{2,1,0:T(8,128)(2,1)}, u32[]{:S(2)}, u32[]{:S(2)}) collective-permute-start(bf16[4,208,384]{2,1,0:T(8,128)(2,1)} %get-tuple-element.359), channel_id=1, source_target_pairs={{0,4},{1,3},{2,6},{3,1},{4,0},{5,7},{6,2},{7,5},{8,12},{9,11},{10,... | collective-permute-start | bytes 1916936 | tf_op jit(solution)/shard_map/ppermute | solution.py:602
  214.7 6.4 %collective-permute-start.36 = (f32[8,768]{1,0:T(8,128)}, f32[8,768]{1,0:T(8,128)}, u32[]{:S(2)}, u32[]{:S(2)}) collective-permute-start(f32[8,768]{1,0:T(8,128)} %add.16), channel_id=1, source_target_pairs={{0,16},{1,17},{2,18},{3,19},{4,20},{5,21},{6,22},{7,23},{8,24},{9,... | collective-permute-start | bytes 73736 | tf_op jit(solution)/shard_map/ppermute | solution.py:602
  223.3 13.9 %collective-permute-start.37 = (bf16[208,384]{1,0:T(8,128)(2,1)}, bf16[208,384]{1,0:T(8,128)(2,1)}, u32[]{:S(2)}, u32[]{:S(2)}) collective-permute-start(bf16[208,384]{1,0:T(8,128)(2,1)} %get-tuple-element.369), channel_id=1, source_target_pairs={{0,8},{1,9},{2,10},{3,11},{4,12},{5,13},{6,14},{7,15},{8,0},{9,1},... | collective-permute-start | bytes 479240 | tf_op jit(solution)/shard_map/ppermute | solution.py:602
  225.8 13.8 %collective-permute-start.38 = (bf16[208,384]{1,0:T(8,128)(2,1)}, bf16[208,384]{1,0:T(8,128)(2,1)}, u32[]{:S(2)}, u32[]{:S(2)}) collective-permute-start(bf16[208,384]{1,0:T(8,128)(2,1)} %get-tuple-element.370), channel_id=1, source_target_pairs={{0,16},{1,17},{2,18},{3,19},{4,20},{5,21},{6,22},{7,23},{8,24},{9,... | collective-permute-start | bytes 479240 | tf_op jit(solution)/shard_map/ppermute | solution.py:602
  226.4 13.3 %collective-permute-start.39 = (bf16[208,384]{1,0:T(8,128)(2,1)}, bf16[208,384]{1,0:T(8,128)(2,1)}, u32[]{:S(2)}, u32[]{:S(2)}) collective-permute-start(bf16[208,384]{1,0:T(8,128)(2,1)} %get-tuple-element.371), channel_id=1, source_target_pairs={{0,24},{1,25},{2,26},{3,27},{4,28},{5,29},{6,30},{7,31},{8,16},{9,... | collective-permute-start | bytes 479240 | tf_op jit(solution)/shard_map/ppermute | solution.py:602
  234.3 7.3 %collective-permute-start.34 = (f32[2,24,768]{2,1,0:T(8,128)}, f32[2,24,768]{2,1,0:T(8,128)}, u32[]{:S(2)}, u32[]{:S(2)}) collective-permute-start(f32[2,24,768]{2,1,0:T(8,128)} %get-tuple-element.358), channel_id=1, source_target_pairs={{0,1},{1,0},{2,3},{3,2},{4,5},{5,4},{6,7},{7,6},{8,9},{9,8},{10,11... | collective-permute-start | bytes 442376 | tf_op jit(solution)/shard_map/ppermute | solution.py:602
  (14 other events, 71.3 us)

commit v11 on v10

--- a/solution.py
+++ b/solution.py
@@ -1096,16 +1096,12 @@
         down_first, up_first = after((down_first, up_first), out_other)
         hidden_rest, hidden_take = scatter_second(*down_first, *up_first)
 
-        def weights_of_chip(grads, out_take):
+        def weights_of_chip(grads):
             square_send, square_keep = run_weights(grads)
-            (out,) = call_with(
-                me, mlp_out_own, tiles // fold, [wide_rows, vec_spec, act_spec, wide_rows, wide_spec], [wide_low], [],
-                "mlp_out_own", 0, resid, vec, act_own, after(out_take, square_send), wdown)
-            square_take = after(scatter_core(square_send), out)
-            return *merge_core_of(core, square_keep, square_take), out
+            return merge_core_of(core, square_keep, scatter_core(square_send))
 
         out_take = swap(out_other, other_core)
-        square_own, square_send, out = fenced(weights_of_chip, after(grads, hidden_rest), out_take)
+        square_own, square_send = fenced(weights_of_chip, after(grads, hidden_rest))
         square_take = swap(square_send, first_plane).reshape(square_own.shape)
         hidden_rest, hidden_take = after((hidden_rest, hidden_take), square_own)
         hidden_layers = scatter_layers(hidden_rest, hidden_take)
@@ -1114,7 +1110,10 @@
         late = late + swap(late, other_core)
         square_second = scatter_second(square_own, square_take)
         late = after(late, square_second[0])
-        late = late + swap(late, other_layer(1))
+        (out,) = call_with(
+            me, mlp_out_own, tiles // fold, [wide_rows, vec_spec, act_spec, wide_rows, wide_spec], [wide_low], [],
+            "mlp_out_own", 0, resid, vec, act_own, after(out_take, square_second[0]), wdown)
+        late = late + after(swap(late, other_layer(1)), out)
         hidden_layers = after(hidden_layers, late)
         g_down, up_keep, up_send = scatter_last(core, hidden_layers, own, blocks, deep)
         up_take = scatter_core(up_send)

time: 246 us -> 246 us (level)
  waiting for transfers between devices: 55.4 us -> 52.4 us
    ppermute x43, waiting for transfers between devices: 55.4 us -> 52.4 us  [swap(): return lax.ppermute(array, 'dp', flipped(lax.axis_size('dp'), change))]
  transfers between devices with their start and end apart: 43 -> 43, of which waited for: 18 -> 17; matrix products, arithmetic and copies ran while one was open for 2% -> 3% of each run, Pallas kernels for 39% -> 37%
where the time goes in v11:
time: 246 us; the launch traced here: 245 us
  Pallas kernels  138 us (56%)
  waiting for transfers between devices  52.4 us (21%)
  starting transfers between devices  44 us (18%)
  other arithmetic  9.11 us (4%)
    pallas_call x5, Pallas kernels, call_with(): pl.pallas_call(kernel, grid_spec=pltpu.PrefetchScalarGridSpec(num_scalar_...  67.5 us
    pallas_call x7, Pallas kernels, call(): pl.pallas_call(kernel, grid=grid, in_specs=ins, out_specs=out_specs, out_...  55.8 us
    ppermute x43, waiting for transfers between devices, swap(): return lax.ppermute(array, 'dp', flipped(lax.axis_size('dp'), change))  52.4 us
    ppermute x43, starting transfers between devices, swap(): return lax.ppermute(array, 'dp', flipped(lax.axis_size('dp'), change))  44 us
    pallas_call x7, Pallas kernels, small_call(): pl.pallas_call(kernel, in_specs=ins, out_specs=tuple((spec for spec, _ in...  15.2 us
  transfers between devices with their start and end apart: 43, of which 17 were waited for; matrix products, arithmetic and copies ran while one was open for 3% of the time, Pallas kernels for 37%

profile of v11, /device:TPU:0, one launch (start us, length us, event | category | flops | bytes accessed | tf_op | source)
XLA Modules:
  0.0 245.0 jit_solution(13121361726833631499)
XLA Ops:
  6.4 2.9 %collective-permute-start.19 = (bf16[1,80,768]{2,1,0:T(8,128)(2,1)}, bf16[1,80,768]{2,1,0:T(8,128)(2,1)S(1)}, u32[]{:S(2)}, u32[]{:S(2)}) collective-permute-start(bf16[1,80,768]{2,1,0:T(8,128)(2,1)} %bitcast.27), channel_id=1, source_target_pairs={{0,8},{1,9},{2,10},{3,11},{4,12},{5,13},{6,14},{7,15},{8,0},{9,1},... | collective-permute-start | bytes 368648 | tf_op jit(solution)/shard_map/ppermute | solution.py:602
  9.4 4.0 %collective-permute-start.17 = (bf16[208,384]{1,0:T(8,128)(2,1)}, bf16[208,384]{1,0:T(8,128)(2,1)S(1)}, u32[]{:S(2)}, u32[]{:S(2)}) collective-permute-start(bf16[208,384]{1,0:T(8,128)(2,1)} %get-tuple-element.251), channel_id=1, source_target_pairs={{0,24},{1,25},{2,26},{3,27},{4,28},{5,29},{6,30},{7,31},{8,16},{9,... | collective-permute-start | bytes 479240 | tf_op jit(solution)/shard_map/ppermute | solution.py:602
  14.9 15.3 %conditional.6 = (bf16[8,80,768]{2,1,0:T(8,128)(2,1)S(1)}) conditional(s32[]{:T(128)} %convert_element_type.4, () %tuple.81, bf16[2,80,768]{2,1,0:T(8,128)(2,1)S(1)} %pad_maximum_fusion.5), branch_computations={%region_0.0_spmd, %region_1.0_spmd} | conditional | flops 1228800 | bytes 5898328 | solution.py:847
  16.7 4.5 %collective-permute-done.6 = bf16[2,80,768]{2,1,0:T(8,128)(2,1)S(1)} collective-permute-done((bf16[2,80,768]{2,1,0:T(8,128)(2,1)S(1)}, bf16[2,80,768]{2,1,0:T(8,128)(2,1)S(1)}, u32[]{:S(2)}, u32[]{:S(2)}) %collective-permute-start.6) | collective-permute-done | bytes 245792 | tf_op jit(solution)/shard_map/cond/branch_1_fun/ppermute | solution.py:602
  23.0 7.1 %collective-permute-done.7 = bf16[4,80,768]{2,1,0:T(8,128)(2,1)S(1)} collective-permute-done((bf16[4,80,768]{2,1,0:T(8,128)(2,1)S(1)}, bf16[4,80,768]{2,1,0:T(8,128)(2,1)S(1)}, u32[]{:S(2)}, u32[]{:S(2)}) %collective-permute-start.7) | collective-permute-done | bytes 491552 | tf_op jit(solution)/shard_map/cond/branch_1_fun/ppermute | solution.py:602
  32.2 2.8 %collective-permute-start.20 = (bf16[2,224,384]{2,1,0:T(8,128)(2,1)}, bf16[2,224,384]{2,1,0:T(8,128)(2,1)}, u32[]{:S(2)}, u32[]{:S(2)}) collective-permute-start(bf16[2,224,384]{2,1,0:T(8,128)(2,1)} %pad_maximum_fusion.4), channel_id=1, source_target_pairs={{0,16},{1,17},{2,18},{3,19},{4,20},{5,21},{6,22},{7,23},{8,24},{9,... | collective-permute-start | bytes 1032200 | tf_op jit(solution)/shard_map/ppermute | solution.py:602
  35.0 14.5 %conditional.7 = (bf16[4,208,384]{2,1,0:T(8,128)(2,1)}, bf16[4,208,384]{2,1,0:T(8,128)(2,1)}, bf16[1024,768]{1,0:T(8,128)(2,1)}, f32[8,768]{1,0:T(8,128)}) conditional(s32[]{:T(128)} %convert_element_type.4, () %tuple.86, (bf16[4,208,384]{2,1,0:T(8,128)(2,1)}, bf16[1024,768]{1,0:T(8,128)(2,1)}, s32[4,5]{1,0:T(4,128)}) %tuple.87), branch_computations={%region_2.0_spmd, %region_3.0_spmd} | conditional | bytes 5111921 | solution.py:847
  38.0 3.8 %mask_grads.1 = (bf16[1024,768]{1,0:T(8,128)(2,1)}, f32[8,768]{1,0:T(8,128)}) custom-call(s32[4,5]{1,0:T(4,128)} %get-tuple-element.61.lengths_ref, bf16[1024,768]{1,0:T(8,128)(2,1)} %get-tuple-element.63.grad_ref), custom_call_target="tpu_custom_call" | custom-call | bytes 1 | tf_op jit(solution)/shard_map/cond/branch_1_fun/mask_grads/pallas_call | solution.py:561
  41.8 7.7 %collective-permute-done = bf16[4,208,384]{2,1,0:T(8,128)(2,1)} collective-permute-done((bf16[4,208,384]{2,1,0:T(8,128)(2,1)}, bf16[4,208,384]{2,1,0:T(8,128)(2,1)}, u32[]{:S(2)}, u32[]{:S(2)}) %collective-permute-start) | collective-permute-done | bytes 639008 | tf_op jit(solution)/shard_map/cond/branch_1_fun/ppermute | solution.py:602
  50.0 14.6 %conditional.8 = (bf16[4,208,384]{2,1,0:T(8,128)(2,1)}, bf16[4,208,384]{2,1,0:T(8,128)(2,1)}, bf16[4,208,384]{2,1,0:T(8,128)(2,1)}, bf16[4,208,384]{2,1,0:T(8,12...) conditional(s32[]{:T(128)} %convert_element_type.4, () %tuple.88, ...), branch_computations={%region_4.0_spmd, %region_5.0_spmd} | conditional | flops 344064 | bytes 20447528 | solution.py:847
  51.0 3.6 %collective-permute-done.9 = bf16[4,208,384]{2,1,0:T(8,128)(2,1)} collective-permute-done((bf16[4,208,384]{2,1,0:T(8,128)(2,1)}, bf16[4,208,384]{2,1,0:T(8,128)(2,1)}, u32[]{:S(2)}, u32[]{:S(2)}) %collective-permute-start.9) | collective-permute-done | bytes 639008 | tf_op jit(solution)/shard_map/cond/branch_1_fun/ppermute | solution.py:602
  55.6 5.7 %collective-permute-done.8 = bf16[4,208,384]{2,1,0:T(8,128)(2,1)} collective-permute-done((bf16[4,208,384]{2,1,0:T(8,128)(2,1)}, bf16[4,208,384]{2,1,0:T(8,128)(2,1)}, u32[]{:S(2)}, u32[]{:S(2)}) %collective-permute-start.8) | collective-permute-done | bytes 639008 | tf_op jit(solution)/shard_map/cond/branch_1_fun/ppermute | solution.py:602
  66.1 10.4 %project.1 = (bf16[1024,768]{1,0:T(8,128)(2,1)}, bf16[1024,768]{1,0:T(8,128)(2,1)}, bf16[1024,768]{1,0:T(8,128)(2,1)}, bf16[1024,768]{1,0:T(8,128)(2,1)}, bf16[7...) custom-call(s32[1]{0:T(128)} %bitcast.1.me_ref, ...), custom_call_target="tpu_custom_call" | custom-call | flops 8999999488 | bytes 1 | tf_op jit(solution)/shard_map/project/pallas_call | solution.py:576
  76.5 18.7 %conditional.9 = (bf16[1024,768]{1,0:T(8,128)(2,1)}, f32[1024,128]{1,0:T(8,128)}, f32[1024,768]{1,0:T(8,128)}, bf16[1024,768]{1,0:T(8,128)(2,1)}, bf16[1024,768]...) conditional(s32[]{:T(128)} %convert_element_type.4, () %tuple.80, ...), branch_computations={%region_6.0_spmd, %region_7.0_spmd} | conditional | flops 4 | bytes 11796699 | solution.py:847
  78.6 11.5 %attention_forward.1 = (bf16[1024,768]{1,0:T(8,128)(2,1)}, f32[1024,128]{1,0:T(8,128)}, f32[1024,768]{1,0:T(8,128)}, bf16[1024,768]{1,0:T(8,128)(2,1)}) custom-call(s32[4,5]{1,0:T(4,128)} %get-tuple-element.75.lengths_ref, bf16[1024,768]{1,0:T(8,128)(2,1)} %get-tuple-element.76.x_ref, f32[16,768]{1,0:T(8,128)} %get-tuple-element.77.vec_ref, ...), custom_call_target="tpu_custom_call" | custom-call | bytes 1 | tf_op jit(solution)/shard_map/cond/branch_1_fun/attention_forward/pallas_call | solution.py:561
  90.1 3.8 %conditional = (bf16[1024,768]{1,0:T(8,128)(2,1)}) conditional(s32[]{:T(128)} %convert_element_type.0, () %tuple.40, bf16[1024,768]{1,0:T(8,128)(2,1)} %get-tuple-element.413), branch_computations={%region_8.0_spmd, %region_9.0_spmd} | conditional | bytes 6291504 | solution.py:847
  90.2 3.7 %collective-permute-done.2 = bf16[1024,768]{1,0:T(8,128)(2,1)} collective-permute-done((bf16[1024,768]{1,0:T(8,128)(2,1)}, bf16[1024,768]{1,0:T(8,128)(2,1)}, u32[]{:S(2)}, u32[]{:S(2)}) %collective-permute-start.2) | collective-permute-done | bytes 1572896 | tf_op jit(solution)/shard_map/cond/branch_1_fun/cond/branch_1_fun/ppermute | solution.py:602
  95.2 34.8 %mlp.1 = (bf16[1024,1536]{1,0:T(8,128)(2,1)}, bf16[1024,1536]{1,0:T(8,128)(2,1)}, f32[1024,768]{1,0:T(8,128)}, bf16[1024,768]{1,0:T(8,128)(2,1)}, bf16[4,2,96,76...) custom-call(s32[1]{0:T(128)} %bitcast.1.me_ref, ...), custom_call_target="tpu_custom_call" | custom-call | bytes 1 | tf_op jit(solution)/shard_map/mlp/pallas_call | solution.py:576
  133.8 20.7 %attention_backward.1 = (bf16[4,1024,768]{2,1,0:T(8,128)(2,1)}, f32[1024,768]{1,0:T(8,128)}, f32[8,768]{1,0:T(8,128)}) custom-call(s32[4,5]{1,0:T(4,128)} %lengths_ref.1, bf16[1024,768]{1,0:T(8,128)(2,1)} %get-tuple-element.280.q_ref, bf16[1024,768]{1,0:T(8,128)(2,1)} %get-tuple-element.281.k_ref, bf16[1024,768]{1,0:T(8,128)(2,1)} %get-tuple-element.282.v_ref, ...), custom_call_target="tpu_custom_call" | custom-call | bytes 1 | tf_op jit(solution)/shard_map/attention_backward/pallas_call | solution.py:561
  154.5 5.8 %mlp_out_other.1 = bf16[1024,768]{1,0:T(8,128)(2,1)} custom-call(s32[1]{0:T(128)} %bitcast.1.me_ref, bf16[1024,1536]{1,0:T(8,128)(2,1)} %get-tuple-element.301.act_ref, bf16[1536,768]{1,0:T(8,128)(2,1)} %get-tuple-element.302.wdown_ref), custom_call_target="tpu_custom_call" | custom-call | bytes 1 | tf_op jit(solution)/shard_map/mlp_out_other/pallas_call | solution.py:576
  160.4 3.6 %merge_first.2 = (bf16[4,192,768]{2,1,0:T(8,128)(2,1)}, bf16[4,192,768]{2,1,0:T(8,128)(2,1)}) custom-call(bf16[1,4,2,96,768]{4,3,2,1,0:T(8,128)(2,1)} %bitcast.20, bf16[1,4,2,96,768]{4,3,2,1,0:T(8,128)(2,1)} %bitcast.18.refs_1_, bf16[2,4,2,48,768]{4,3,2,1,0:T(8,128)(2,1)} %get-tuple-element.310.refs_2_, ...), custom_call_target="tpu_custom_call" | custom-call | bytes 1 | tf_op jit(solution)/shard_map/merge_first/pallas_call | solution.py:561
  164.6 18.4 %conditional.10 = (bf16[1,4,2,208,384]{4,3,2,1,0:T(8,128)(2,1)}, bf16[4,2,208,384]{3,2,1,0:T(8,128)(2,1)}) conditional(s32[]{:T(128)} %convert_element_type.4, () %tuple.96, (s32[1]{0:T(128)}, bf16[1024,768]{1,0:T(8,128)(2,1)}, bf16[1024,768]{1,0:T(8,128)(2,1)}, bf16[4,1024,768]{2,1,0:T(8,128)(2,1)}, f32[8,768]{1,0:T(8,128)}, ...), branch_computations={%region_10.0_spmd, %region_11.0_spmd} | conditional | bytes 10223674 | solution.py:847
  164.6 9.4 %weight_grads.1 = (bf16[4,4,208,384]{3,2,1,0:T(8,128)(2,1)}, bf16[4,4,208,384]{3,2,1,0:T(8,128)(2,1)}) custom-call(s32[1]{0:T(128)} %get-tuple-element.91.me_ref, bf16[1024,768]{1,0:T(8,128)(2,1)} %get-tuple-element.92.n1_ref, bf16[1024,768]{1,0:T(8,128)(2,1)} %get-tuple-element.93.mixed_hbm, bf16[4,1024,768]{2,1,0:T(8,128)(2,1)} %get-tuple-element.94.columns_ref, ...), custom_call_target="tpu_custom_call" | custom-call | bytes 1 | tf_op jit(solution)/shard_map/cond/branch_1_fun/weight_grads/pallas_call | solution.py:576
  174.4 4.8 %collective-permute-done.5.take_ref = bf16[4,4,208,384]{3,2,1,0:T(8,128)(2,1)} collective-permute-done((bf16[4,4,208,384]{3,2,1,0:T(8,128)(2,1)}, bf16[4,4,208,384]{3,2,1,0:T(8,128)(2,1)}, u32[]{:S(2)}, u32[]{:S(2)}) %collective-permute-start.5) | collective-permute-done | bytes 2555936 | tf_op jit(solution)/shard_map/cond/branch_1_fun/ppermute | solution.py:602
  179.2 3.7 %merge_core.1 = (bf16[4,2,208,384]{3,2,1,0:T(8,128)(2,1)}, bf16[4,2,208,384]{3,2,1,0:T(8,128)(2,1)}) custom-call(s32[1]{0:T(128)} %get-tuple-element.90.core_ref, bf16[4,4,208,384]{3,2,1,0:T(8,128)(2,1)} %get-tuple-element.98.keep_ref, bf16[4,4,208,384]{3,2,1,0:T(8,128)(2,1)} %collective-permute-done.5.take_ref), custom_call_target="tpu_custom_call" | custom-call | bytes 1 | tf_op jit(solution)/shard_map/cond/branch_1_fun/merge_core/pallas_call | solution.py:561
  184.2 2.8 %merge_second.2 = (f32[192,768]{1,0:T(8,128)}, bf16[192,768]{1,0:T(8,128)(2,1)}, bf16[192,768]{1,0:T(8,128)(2,1)}, bf16[192,768]{1,0:T(8,128)(2,1)}) custom-call(bf16[4,192,768]{2,1,0:T(8,128)(2,1)} %get-tuple-element.321.own_ref, bf16[4,192,768]{2,1,0:T(8,128)(2,1)} %collective-permute-done.28.take_ref), custom_call_target="tpu_custom_call" | custom-call | bytes 1 | tf_op jit(solution)/shard_map/merge_second/pallas_call | solution.py:692
  191.7 9.8 %tokens_backward.1 = (bf16[1024,768]{1,0:T(8,128)(2,1)}, f32[8,768]{1,0:T(8,128)}) custom-call(bf16[1024,768]{1,0:T(8,128)(2,1)} %x_ref.3, f32[1024,768]{1,0:T(8,128)} %get-tuple-element.324.gresid_ref, f32[16,768]{1,0:T(8,128)} %get-tuple-element.279.vec_ref, bf16[4,1024,768]{2,1,0:T(8,128)(2,1)} %get-tuple-element.313.grads_ref, ...), custom_call_target="tpu_custom_call" | custom-call | flops 11500000256 | bytes 1 | tf_op jit(solution)/shard_map/tokens_backward/pallas_call | solution.py:561
  201.6 2.6 %merge_first.3 = (bf16[4,208,384]{2,1,0:T(8,128)(2,1)}, bf16[4,208,384]{2,1,0:T(8,128)(2,1)}) custom-call(bf16[1,4,2,208,384]{4,3,2,1,0:T(8,128)(2,1)} %get-tuple-element.317.refs_0_, bf16[1,4,2,208,384]{4,3,2,1,0:T(8,128)(2,1)} %bitcast.19.refs_1_), custom_call_target="tpu_custom_call" | custom-call | bytes 1 | tf_op jit(solution)/shard_map/merge_first/pallas_call | solution.py:561
  207.9 7.1 %mlp_out_own.1 = bf16[1024,768]{1,0:T(8,128)(2,1)} custom-call(s32[1]{0:T(128)} %bitcast.1.me_ref, f32[1024,768]{1,0:T(8,128)} %get-tuple-element.287.resid_ref, f32[16,768]{1,0:T(8,128)} %get-tuple-element.279.vec_ref, bf16[1024,1536]{1,0:T(8,128)(2,1)} %get-tuple-element.295.act_ref, bf16[1024,768]{1,0:T(8,128)(2,1)} %collective-permute-done.24.take_ref, ...), custom_call_target="tpu_custom_call" | custom-call | bytes 1 | tf_op jit(solution)/shard_map/mlp_out_own/pallas_call | solution.py:576
  216.3 2.5 %collective-permute-start.36 = (f32[8,768]{1,0:T(8,128)}, f32[8,768]{1,0:T(8,128)}, u32[]{:S(2)}, u32[]{:S(2)}) collective-permute-start(f32[8,768]{1,0:T(8,128)} %add.16), channel_id=1, source_target_pairs={{0,16},{1,17},{2,18},{3,19},{4,20},{5,21},{6,22},{7,23},{8,24},{9,... | collective-permute-start | bytes 73736 | tf_op jit(solution)/shard_map/ppermute | solution.py:602
  230.1 2.7 %collective-permute-done.40 = f32[8,768]{1,0:T(8,128)S(1)} collective-permute-done((f32[8,768]{1,0:T(8,128)S(1)}, f32[8,768]{1,0:T(8,128)S(1)}, u32[]{:S(2)}, u32[]{:S(2)}) %collective-permute-start.40) | collective-permute-done | bytes 24608 | tf_op jit(solution)/shard_map/ppermute | solution.py:602
  234.1 2.6 %collective-permute-done.41 = f32[8,768]{1,0:T(8,128)S(1)} collective-permute-done((f32[8,768]{1,0:T(8,128)S(1)}, f32[8,768]{1,0:T(8,128)S(1)}, u32[]{:S(2)}, u32[]{:S(2)}) %collective-permute-start.41) | collective-permute-done | bytes 24608 | tf_op jit(solution)/shard_map/ppermute | solution.py:602
  (96 shorter events, 63.3 us)
Async XLA Ops:
  6.4 7.6 %collective-permute-start.19 = (bf16[1,80,768]{2,1,0:T(8,128)(2,1)}, bf16[1,80,768]{2,1,0:T(8,128)(2,1)S(1)}, u32[]{:S(2)}, u32[]{:S(2)}) collective-permute-start(bf16[1,80,768]{2,1,0:T(8,128)(2,1)} %bitcast.27), channel_id=1, source_target_pairs={{0,8},{1,9},{2,10},{3,11},{4,12},{5,13},{6,14},{7,15},{8,0},{9,1},... | collective-permute-start | bytes 368648 | tf_op jit(solution)/shard_map/ppermute | solution.py:602
  9.3 20.9 %collective-permute-start.18 = (bf16[224,384]{1,0:T(8,128)(2,1)}, bf16[224,384]{1,0:T(8,128)(2,1)S(1)}, u32[]{:S(2)}, u32[]{:S(2)}) collective-permute-start(bf16[224,384]{1,0:T(8,128)(2,1)} %get-tuple-element.252), channel_id=1, source_target_pairs={{0,8},{1,9},{2,10},{3,11},{4,12},{5,13},{6,14},{7,15},{8,0},{9,1},... | collective-permute-start | bytes 516104 | tf_op jit(solution)/shard_map/ppermute | solution.py:602
  9.4 20.8 %collective-permute-start.17 = (bf16[208,384]{1,0:T(8,128)(2,1)}, bf16[208,384]{1,0:T(8,128)(2,1)S(1)}, u32[]{:S(2)}, u32[]{:S(2)}) collective-permute-start(bf16[208,384]{1,0:T(8,128)(2,1)} %get-tuple-element.251), channel_id=1, source_target_pairs={{0,24},{1,25},{2,26},{3,27},{4,28},{5,29},{6,30},{7,31},{8,16},{9,... | collective-permute-start | bytes 479240 | tf_op jit(solution)/shard_map/ppermute | solution.py:602
  13.4 16.9 %collective-permute-start.16 = (bf16[208,384]{1,0:T(8,128)(2,1)}, bf16[208,384]{1,0:T(8,128)(2,1)S(1)}, u32[]{:S(2)}, u32[]{:S(2)}) collective-permute-start(bf16[208,384]{1,0:T(8,128)(2,1)} %get-tuple-element.251), channel_id=1, source_target_pairs={{0,16},{1,17},{2,18},{3,19},{4,20},{5,21},{6,22},{7,23},{8,24},{9,... | collective-permute-start | bytes 479240 | tf_op jit(solution)/shard_map/ppermute | solution.py:602
  13.4 16.9 %collective-permute-start.15 = (bf16[208,384]{1,0:T(8,128)(2,1)}, bf16[208,384]{1,0:T(8,128)(2,1)S(1)}, u32[]{:S(2)}, u32[]{:S(2)}) collective-permute-start(bf16[208,384]{1,0:T(8,128)(2,1)} %get-tuple-element.251), channel_id=1, source_target_pairs={{0,8},{1,9},{2,10},{3,11},{4,12},{5,13},{6,14},{7,15},{8,0},{9,1},... | collective-permute-start | bytes 479240 | tf_op jit(solution)/shard_map/ppermute | solution.py:602
  14.9 6.3 %collective-permute-start.6 = (bf16[2,80,768]{2,1,0:T(8,128)(2,1)S(1)}, bf16[2,80,768]{2,1,0:T(8,128)(2,1)S(1)}, u32[]{:S(2)}, u32[]{:S(2)}) collective-permute-start(bf16[2,80,768]{2,1,0:T(8,128)(2,1)S(1)} %param.1), channel_id=1, source_target_pairs={{0,2},{1,5},{2,0},{3,7},{4,6},{5,1},{6,4},{7,3},{8,10},{9,13},{10,... | collective-permute-start | bytes 737288 | tf_op jit(solution)/shard_map/cond/branch_1_fun/ppermute | solution.py:602
  21.2 8.9 %collective-permute-start.7 = (bf16[4,80,768]{2,1,0:T(8,128)(2,1)S(1)}, bf16[4,80,768]{2,1,0:T(8,128)(2,1)S(1)}, u32[]{:S(2)}, u32[]{:S(2)}) collective-permute-start(bf16[4,80,768]{2,1,0:T(8,128)(2,1)S(1)} %pad_maximum_fusion.1), channel_id=1, source_target_pairs={{0,4},{1,3},{2,6},{3,1},{4,0},{5,7},{6,2},{7,5},{8,12},{9,11},{10,... | collective-permute-start | bytes 1474568 | tf_op jit(solution)/shard_map/cond/branch_1_fun/ppermute | solution.py:602
  32.2 17.3 %collective-permute-start.20 = (bf16[2,224,384]{2,1,0:T(8,128)(2,1)}, bf16[2,224,384]{2,1,0:T(8,128)(2,1)}, u32[]{:S(2)}, u32[]{:S(2)}) collective-permute-start(bf16[2,224,384]{2,1,0:T(8,128)(2,1)} %pad_maximum_fusion.4), channel_id=1, source_target_pairs={{0,16},{1,17},{2,18},{3,19},{4,20},{5,21},{6,22},{7,23},{8,24},{9,... | collective-permute-start | bytes 1032200 | tf_op jit(solution)/shard_map/ppermute | solution.py:602
  35.0 14.5 %collective-permute-start = (bf16[4,208,384]{2,1,0:T(8,128)(2,1)}, bf16[4,208,384]{2,1,0:T(8,128)(2,1)}, u32[]{:S(2)}, u32[]{:S(2)}) collective-permute-start(bf16[4,208,384]{2,1,0:T(8,128)(2,1)} %get-tuple-element.60), channel_id=1, source_target_pairs={{0,2},{1,5},{2,0},{3,7},{4,6},{5,1},{6,4},{7,3},{8,10},{9,13},{10,... | collective-permute-start | bytes 1916936 | tf_op jit(solution)/shard_map/cond/branch_1_fun/ppermute | solution.py:602
  36.5 13.0 %collective-permute-start.1 = (bf16[4,208,384]{2,1,0:T(8,128)(2,1)}, bf16[4,208,384]{2,1,0:T(8,128)(2,1)}, u32[]{:S(2)}, u32[]{:S(2)}) collective-permute-start(bf16[4,208,384]{2,1,0:T(8,128)(2,1)} %get-tuple-element.60), channel_id=1, source_target_pairs={{0,4},{1,3},{2,6},{3,1},{4,0},{5,7},{6,2},{7,5},{8,12},{9,11},{10,... | collective-permute-start | bytes 1916936 | tf_op jit(solution)/shard_map/cond/branch_1_fun/ppermute | solution.py:602
  49.4 45.8 %collective-permute-start.22 = (bf16[8,80,768]{2,1,0:T(8,128)(2,1)}, bf16[8,80,768]{2,1,0:T(8,128)(2,1)}, u32[]{:S(2)}, u32[]{:S(2)}) collective-permute-start(bf16[8,80,768]{2,1,0:T(8,128)(2,1)} %copy-done), channel_id=1, source_target_pairs={{0,16},{1,17},{2,18},{3,19},{4,20},{5,21},{6,22},{7,23},{8,24},{9,... | collective-permute-start | bytes 2949128 | tf_op jit(solution)/shard_map/ppermute | solution.py:602
  50.0 14.6 %collective-permute-start.13 = (bf16[1024,768]{1,0:T(8,128)(2,1)}, bf16[1024,768]{1,0:T(8,128)(2,1)}, u32[]{:S(2)}, u32[]{:S(2)}) collective-permute-start(bf16[1024,768]{1,0:T(8,128)(2,1)} %get-tuple-element.72), channel_id=1, source_target_pairs={{0,1},{1,0},{2,3},{3,2},{4,5},{5,4},{6,7},{7,6},{8,9},{9,8},{10,11... | collective-permute-start | bytes 4718600 | tf_op jit(solution)/shard_map/cond/branch_1_fun/ppermute | solution.py:602
  50.5 10.7 %collective-permute-start.8 = (bf16[4,208,384]{2,1,0:T(8,128)(2,1)}, bf16[4,208,384]{2,1,0:T(8,128)(2,1)}, u32[]{:S(2)}, u32[]{:S(2)}) collective-permute-start(bf16[4,208,384]{2,1,0:T(8,128)(2,1)} %get-tuple-element.67), channel_id=1, source_target_pairs={{0,4},{1,3},{2,6},{3,1},{4,0},{5,7},{6,2},{7,5},{8,12},{9,11},{10,... | collective-permute-start | bytes 1916936 | tf_op jit(solution)/shard_map/cond/branch_1_fun/ppermute | solution.py:602
  64.6 11.9 %collective-permute-start.21 = (bf16[4,224,384]{2,1,0:T(8,128)(2,1)}, bf16[4,224,384]{2,1,0:T(8,128)(2,1)}, u32[]{:S(2)}, u32[]{:S(2)}) collective-permute-start(bf16[4,224,384]{2,1,0:T(8,128)(2,1)} %get-tuple-element.284.refs_5_), channel_id=1, source_target_pairs={{0,2},{1,5},{2,0},{3,7},{4,6},{5,1},{6,4},{7,3},{8,10},{9,13},{10,... | collective-permute-start | bytes 2064392 | tf_op jit(solution)/shard_map/ppermute | solution.py:602
  76.5 17.5 %collective-permute-start.3 = (bf16[4,224,384]{2,1,0:T(8,128)(2,1)}, bf16[4,224,384]{2,1,0:T(8,128)(2,1)}, u32[]{:S(2)}, u32[]{:S(2)}) collective-permute-start(bf16[4,224,384]{2,1,0:T(8,128)(2,1)} %get-tuple-element.86), channel_id=1, source_target_pairs={{0,4},{1,3},{2,6},{3,1},{4,0},{5,7},{6,2},{7,5},{8,12},{9,11},{10,... | collective-permute-start | bytes 2064392 | tf_op jit(solution)/shard_map/cond/branch_1_fun/ppermute | solution.py:602
  77.1 18.1 %collective-permute-start.4 = (bf16[4,224,384]{2,1,0:T(8,128)(2,1)}, bf16[4,224,384]{2,1,0:T(8,128)(2,1)}, u32[]{:S(2)}, u32[]{:S(2)}) collective-permute-start(bf16[4,224,384]{2,1,0:T(8,128)(2,1)} %get-tuple-element.87), channel_id=1, source_target_pairs={{0,4},{1,3},{2,6},{3,1},{4,0},{5,7},{6,2},{7,5},{8,12},{9,11},{10,... | collective-permute-start | bytes 2064392 | tf_op jit(solution)/shard_map/cond/branch_1_fun/ppermute | solution.py:602
  130.1 30.3 %collective-permute-start.25 = (bf16[4,2,96,768]{3,2,1,0:T(8,128)(2,1)}, bf16[4,2,96,768]{3,2,1,0:T(8,128)(2,1)}, u32[]{:S(2)}, u32[]{:S(2)}) collective-permute-start(bf16[4,2,96,768]{3,2,1,0:T(8,128)(2,1)} %get-tuple-element.305), channel_id=1, source_target_pairs={{0,2},{1,5},{2,0},{3,7},{4,6},{5,1},{6,4},{7,3},{8,10},{9,13},{10,... | collective-permute-start | bytes 3538952 | tf_op jit(solution)/shard_map/ppermute | solution.py:602
  130.9 29.5 %collective-permute-start.26 = (bf16[2,4,2,48,768]{4,3,2,1,0:T(8,128)(2,1)}, bf16[2,4,2,48,768]{4,3,2,1,0:T(8,128)(2,1)}, u32[]{:S(2)}, u32[]{:S(2)}) collective-permute-start(bf16[2,4,2,48,768]{4,3,2,1,0:T(8,128)(2,1)} %get-tuple-element.307), channel_id=1, source_target_pairs={{0,2},{1,5},{2,0},{3,7},{4,6},{5,1},{6,4},{7,3},{8,10},{9,13},{10,... | collective-permute-start | bytes 3538952 | tf_op jit(solution)/shard_map/ppermute | solution.py:602
  163.9 20.2 %collective-permute-start.28 = (bf16[4,192,768]{2,1,0:T(8,128)(2,1)}, bf16[4,192,768]{2,1,0:T(8,128)(2,1)}, u32[]{:S(2)}, u32[]{:S(2)}) collective-permute-start(bf16[4,192,768]{2,1,0:T(8,128)(2,1)} %get-tuple-element.320), channel_id=1, source_target_pairs={{0,4},{1,3},{2,6},{3,1},{4,0},{5,7},{6,2},{7,5},{8,12},{9,11},{10,... | collective-permute-start | bytes 3538952 | tf_op jit(solution)/shard_map/ppermute | solution.py:602
  164.5 42.2 %collective-permute-start.24 = (bf16[1024,768]{1,0:T(8,128)(2,1)}, bf16[1024,768]{1,0:T(8,128)(2,1)}, u32[]{:S(2)}, u32[]{:S(2)}) collective-permute-start(bf16[1024,768]{1,0:T(8,128)(2,1)} %mlp_out_other.1), channel_id=1, source_target_pairs={{0,1},{1,0},{2,3},{3,2},{4,5},{5,4},{6,7},{7,6},{8,9},{9,8},{10,11... | collective-permute-start | bytes 4718600 | tf_op jit(solution)/shard_map/ppermute | solution.py:602
  174.0 5.3 %collective-permute-start.5 = (bf16[4,4,208,384]{3,2,1,0:T(8,128)(2,1)}, bf16[4,4,208,384]{3,2,1,0:T(8,128)(2,1)}, u32[]{:S(2)}, u32[]{:S(2)}) collective-permute-start(bf16[4,4,208,384]{3,2,1,0:T(8,128)(2,1)} %get-tuple-element.99), channel_id=1, source_target_pairs={{0,1},{1,0},{2,3},{3,2},{4,5},{5,4},{6,7},{7,6},{8,9},{9,8},{10,11... | collective-permute-start | bytes 7667720 | tf_op jit(solution)/shard_map/cond/branch_1_fun/ppermute | solution.py:602
  182.9 18.6 %collective-permute-start.27 = (bf16[4,2,208,384]{3,2,1,0:T(8,128)(2,1)}, bf16[4,2,208,384]{3,2,1,0:T(8,128)(2,1)}, u32[]{:S(2)}, u32[]{:S(2)}) collective-permute-start(bf16[4,2,208,384]{3,2,1,0:T(8,128)(2,1)} %get-tuple-element.318), channel_id=1, source_target_pairs={{0,2},{1,5},{2,0},{3,7},{4,6},{5,1},{6,4},{7,3},{8,10},{9,13},{10,... | collective-permute-start | bytes 3833864 | tf_op jit(solution)/shard_map/ppermute | solution.py:602
  187.0 31.9 %collective-permute-start.29 = (bf16[192,768]{1,0:T(8,128)(2,1)}, bf16[192,768]{1,0:T(8,128)(2,1)}, u32[]{:S(2)}, u32[]{:S(2)}) collective-permute-start(bf16[192,768]{1,0:T(8,128)(2,1)} %get-tuple-element.333), channel_id=1, source_target_pairs={{0,8},{1,9},{2,10},{3,11},{4,12},{5,13},{6,14},{7,15},{8,0},{9,1},... | collective-permute-start | bytes 884744 | tf_op jit(solution)/shard_map/ppermute | solution.py:602
  189.4 29.5 %collective-permute-start.30 = (bf16[192,768]{1,0:T(8,128)(2,1)}, bf16[192,768]{1,0:T(8,128)(2,1)}, u32[]{:S(2)}, u32[]{:S(2)}) collective-permute-start(bf16[192,768]{1,0:T(8,128)(2,1)} %get-tuple-element.334), channel_id=1, source_target_pairs={{0,16},{1,17},{2,18},{3,19},{4,20},{5,21},{6,22},{7,23},{8,24},{9,... | collective-permute-start | bytes 884744 | tf_op jit(solution)/shard_map/ppermute | solution.py:602
  191.1 27.8 %collective-permute-start.31 = (bf16[192,768]{1,0:T(8,128)(2,1)}, bf16[192,768]{1,0:T(8,128)(2,1)}, u32[]{:S(2)}, u32[]{:S(2)}) collective-permute-start(bf16[192,768]{1,0:T(8,128)(2,1)} %get-tuple-element.335), channel_id=1, source_target_pairs={{0,24},{1,25},{2,26},{3,27},{4,28},{5,29},{6,30},{7,31},{8,16},{9,... | collective-permute-start | bytes 884744 | tf_op jit(solution)/shard_map/ppermute | solution.py:602
  204.3 17.4 %collective-permute-start.35 = (bf16[4,208,384]{2,1,0:T(8,128)(2,1)}, bf16[4,208,384]{2,1,0:T(8,128)(2,1)}, u32[]{:S(2)}, u32[]{:S(2)}) collective-permute-start(bf16[4,208,384]{2,1,0:T(8,128)(2,1)} %get-tuple-element.344), channel_id=1, source_target_pairs={{0,4},{1,3},{2,6},{3,1},{4,0},{5,7},{6,2},{7,5},{8,12},{9,11},{10,... | collective-permute-start | bytes 1916936 | tf_op jit(solution)/shard_map/ppermute | solution.py:602
  206.6 8.3 %collective-permute-start.33 = (f32[8,768]{1,0:T(8,128)}, f32[8,768]{1,0:T(8,128)}, u32[]{:S(2)}, u32[]{:S(2)}) collective-permute-start(f32[8,768]{1,0:T(8,128)} %add.15), channel_id=1, source_target_pairs={{0,8},{1,9},{2,10},{3,11},{4,12},{5,13},{6,14},{7,15},{8,0},{9,1},... | collective-permute-start | bytes 73736 | tf_op jit(solution)/shard_map/ppermute | solution.py:602
  216.3 5.3 %collective-permute-start.36 = (f32[8,768]{1,0:T(8,128)}, f32[8,768]{1,0:T(8,128)}, u32[]{:S(2)}, u32[]{:S(2)}) collective-permute-start(f32[8,768]{1,0:T(8,128)} %add.16), channel_id=1, source_target_pairs={{0,16},{1,17},{2,18},{3,19},{4,20},{5,21},{6,22},{7,23},{8,24},{9,... | collective-permute-start | bytes 73736 | tf_op jit(solution)/shard_map/ppermute | solution.py:602
  223.8 13.4 %collective-permute-start.37 = (bf16[208,384]{1,0:T(8,128)(2,1)}, bf16[208,384]{1,0:T(8,128)(2,1)}, u32[]{:S(2)}, u32[]{:S(2)}) collective-permute-start(bf16[208,384]{1,0:T(8,128)(2,1)} %get-tuple-element.354), channel_id=1, source_target_pairs={{0,8},{1,9},{2,10},{3,11},{4,12},{5,13},{6,14},{7,15},{8,0},{9,1},... | collective-permute-start | bytes 479240 | tf_op jit(solution)/shard_map/ppermute | solution.py:602
  224.3 14.7 %collective-permute-start.38 = (bf16[208,384]{1,0:T(8,128)(2,1)}, bf16[208,384]{1,0:T(8,128)(2,1)}, u32[]{:S(2)}, u32[]{:S(2)}) collective-permute-start(bf16[208,384]{1,0:T(8,128)(2,1)} %get-tuple-element.355), channel_id=1, source_target_pairs={{0,16},{1,17},{2,18},{3,19},{4,20},{5,21},{6,22},{7,23},{8,24},{9,... | collective-permute-start | bytes 479240 | tf_op jit(solution)/shard_map/ppermute | solution.py:602
  226.4 12.6 %collective-permute-start.39 = (bf16[208,384]{1,0:T(8,128)(2,1)}, bf16[208,384]{1,0:T(8,128)(2,1)}, u32[]{:S(2)}, u32[]{:S(2)}) collective-permute-start(bf16[208,384]{1,0:T(8,128)(2,1)} %get-tuple-element.356), channel_id=1, source_target_pairs={{0,24},{1,25},{2,26},{3,27},{4,28},{5,29},{6,30},{7,31},{8,16},{9,... | collective-permute-start | bytes 479240 | tf_op jit(solution)/shard_map/ppermute | solution.py:602
  234.1 6.9 %collective-permute-start.34 = (f32[2,24,768]{2,1,0:T(8,128)}, f32[2,24,768]{2,1,0:T(8,128)}, u32[]{:S(2)}, u32[]{:S(2)}) collective-permute-start(f32[2,24,768]{2,1,0:T(8,128)} %get-tuple-element.343), channel_id=1, source_target_pairs={{0,1},{1,0},{2,3},{3,2},{4,5},{5,4},{6,7},{7,6},{8,9},{9,8},{10,11... | collective-permute-start | bytes 442376 | tf_op jit(solution)/shard_map/ppermute | solution.py:602
  (14 other events, 73.6 us)
